TPU v7x, 32 devices: a whole 2x2x4 slice. The times are simulated.
32 devices in a mesh: grp: 4 (over y, core), pair: 8 (over z, x).
Axes of the slice: x: 2, y: 2, z: 4, core: 2. Of those that a mesh axis runs over, the one named last changes fastest.
Arguments:
- amplitudes: bfloat16 [4, 32, 1024, 1024], P('grp', 'pair'), may hold values from -6 to 6
- vv_fock: bfloat16 [1024, 1024], replicated, may hold values from -0.1875 to 0.1875
- cycle_panels: bfloat16 [2, 1024, 2048], P(None, 'pair', 'grp'), may hold values from -0.125 to 0.125
- row_energy: float32 [2], replicated, may hold values from -2 to -0.5
- col_energy: float32 [64], P('grp'), may hold values from -2 to -0.5
- virt_energy: float32 [1024], replicated, may hold values from 0.2 to 3
Outputs:
- new_amplitudes: bfloat16 [4, 32, 1024, 1024], P('grp', 'pair')
All inputs are finite; a program needn't handle non-finite values.
Results may differ from a plain program's by a relative error of at most 0.0049.
Values may be sent and summed in bfloat16 or wider, within the bound.
No kernel may reach another device: no remote copies, remote signals or barrier semaphores. Data moves between devices by JAX's collectives and lax.ppermute only.
A program may use at most 128 MiB of HBM per device.

v0:
```python
import jax
import jax.numpy as jnp
from jax import lax
from jax.sharding import PartitionSpec as P


def column_cycle(column_block, occ_count, virt_count, shard_rows):
    panel_part = shard_rows.reshape(occ_count, shard_rows.shape[1], occ_count, virt_count)
    return jnp.einsum(
        "ibkc,kjac->ijab", panel_part, column_block, preferred_element_type=jnp.float32
    )


def shards(amplitudes, vv_fock, cycle_panels, row_energy, col_energy, virt_energy):
    dressed = (
        jnp.einsum("ac,gpcb->gpab", vv_fock, amplitudes, preferred_element_type=jnp.float32)
        + jnp.einsum("gpac,bc->gpab", amplitudes, vv_fock, preferred_element_type=jnp.float32)
    ).astype(jnp.bfloat16)
    panels = lax.all_gather(cycle_panels, "grp", axis=2, tiled=True)
    own_index = lax.axis_index("pair")
    per_dev = dressed.shape[1]
    virt_count = dressed.shape[2]
    occ_count = panels.shape[0]
    group_j = col_energy.shape[0]
    gathered = lax.all_to_all(dressed, "pair", split_axis=2, concat_axis=1, tiled=True)
    slice_a = gathered.shape[2]
    column_block = gathered.reshape(occ_count, group_j, slice_a, virt_count)
    cycle_term = column_cycle(
        column_block, occ_count, virt_count, lax.all_gather(panels, "pair", axis=1, tiled=True)
    )
    cycle_flat = cycle_term.reshape(1, occ_count * group_j, slice_a, virt_count)
    pair_cycle = lax.all_to_all(cycle_flat, "pair", split_axis=1, concat_axis=2, tiled=True)
    first_pair = own_index * per_dev
    pair_ids = first_pair + jnp.arange(per_dev, dtype=jnp.int32)
    pair_occ = pair_ids // group_j
    occ_row = jnp.sum(
        jnp.where(
            pair_occ[:, None] == jnp.arange(occ_count, dtype=jnp.int32)[None, :],
            row_energy[None, :],
            0.0,
        ),
        axis=1,
    )
    occ_col = lax.dynamic_slice_in_dim(col_energy, first_pair % group_j, per_dev)
    divisor = (
        virt_energy[None, :, None]
        + virt_energy[None, None, :]
        - occ_row[:, None, None]
        - occ_col[:, None, None]
    )
    return ((dressed[0].astype(jnp.float32) + pair_cycle[0]) / divisor).astype(jnp.bfloat16)[None]


def solution(mesh):
    in_specs = (P("grp", "pair", None, None), P(), P(None, "pair", "grp"), P(), P("grp"), P())
    out_specs = P("grp", "pair", None, None)
    return jax.shard_map(shards, mesh=mesh, in_specs=in_specs, out_specs=out_specs, check_vma=False)
```

profile of v0, /device:TPU:0, one launch (start us, length us, event | category | flops | bytes accessed | tf_op | source)
XLA Modules:
  0.0 825.4 jit_solution(4374700401762639664)
XLA Ops:
  6.5 0.0 copy-start
  6.5 0.0 all-gather.3.cloned.1.call-start
  6.5 1.9 copy.46
  8.5 0.0 all-gather.3.cloned.1.call-update
  8.5 0.0 copy-done
  8.5 14.6 %fusion.3 = f32[4,1024,1024]{2,1,0:T(8,128)} fusion(bf16[1,4,1024,1024]{3,2,1,0:T(8,128)(2,1)} %param.6, bf16[1024,1024]{1,0:T(8,128)(2,1)S(1)} %copy-done), kind=kOutput, calls=%fused_computation.6 | convolution fusion | flops 8589934592 | bytes 27262976 | tf_op jit(solution)/shard_map/ac,gpcb->gpab/dot_general | solution.py:16
  23.1 16.5 %fusion = bf16[1,4,1024,1024]{2,3,1,0:T(8,128)(2,1)} fusion(f32[4,1024,1024]{2,1,0:T(8,128)} %fusion.3, bf16[1,4,1024,1024]{3,2,1,0:T(8,128)(2,1)} %param.6, bf16[1024,1024]{1,0:T(8,128)(2,1)S(1)} %copy-done), kind=kOutput, calls=%fused_computation.1 | convolution fusion | flops 8598323200 | bytes 35651584 | tf_op jit(solution)/shard_map/gpac,bc->gpab/dot_general | solution.py:17
  39.6 14.9 %copy.43 = bf16[1,4,1024,1024]{3,1,0,2:T(4,128)(2,1)} copy(bf16[1,4,1024,1024]{2,3,1,0:T(8,128)(2,1)} %fusion) | data formatting | bytes 16777216 | tf_op jit(solution)/shard_map/convert_element_type | solution.py:18
  54.4 7.2 all-to-all-start
  61.7 0.2 all-gather.5.cloned.1.call-start
  61.9 0.0 all-gather.3.cloned.1.call-done
  61.9 0.5 all-gather.5.cloned.1.call-update
  62.4 283.6 %all-to-all-done = bf16[1,4,1024,1024]{3,1,0,2:T(4,128)(2,1)} async-done(((bf16[1,4,1024,1024]{3,1,0,2:T(4,128)(2,1)}), bf16[1,4,1024,1024]{3,1,0,2:T(4,128)(2,1)}, u32[]{:S(2)}, u32[]{:S(2)}) %all-to-all-start) | async-done | bytes 8388640 | tf_op jit(solution)/shard_map/all_to_all | solution.py:25
  346.0 9.5 %copy.44 = bf16[1,4,1024,1024]{3,2,1,0:T(8,128)(2,1)} copy(bf16[1,4,1024,1024]{3,1,0,2:T(4,128)(2,1)} %all-to-all-done) | data formatting | bytes 16777216 | tf_op jit(solution)/shard_map/all_to_all | solution.py:25
  355.5 8.2 copy.45
  363.7 0.0 all-gather.5.cloned.1.call-done
  363.7 21.5 %convolution_bitcast_fusion = f32[2,16,128,1024]{3,2,0,1:T(8,128)S(1)} fusion(bf16[2,1024,2,1024,1]{1,3,2,0,4:T(8,128)(2,1)} %bitcast.46, bf16[2,16,128,1024,1]{3,2,1,0,4:T(8,128)(2,1)} %bitcast.45), kind=kOutput, calls=%fused_computation.3 | convolution fusion | flops 17179869184 | bytes 33554432 | tf_op jit(solution)/shard_map/ibkc,kjac->ijab/dot_general | solution.py:9
  385.2 6.1 copy.49
  391.2 0.0 copy-start.3
  391.2 0.0 copy-start.4
  391.2 0.0 copy-start.2
  391.2 5.9 all-to-all-start.1
  397.1 0.0 copy-done.3
  397.1 0.1 dynamic_slice.3
  397.2 0.0 copy-done.4
  397.2 0.1 fusion.7
  397.3 0.0 copy-done.2
  397.3 2.4 broadcast_add_fusion
  399.7 359.3 %all-to-all-done.1 = f32[1,32,128,1024]{3,2,0,1:T(8,128)} async-done(((f32[1,32,128,1024]{3,2,0,1:T(8,128)}), f32[1,32,128,1024]{3,2,0,1:T(8,128)}, u32[]{:S(2)}, u32[]{:S(2)}) %all-to-all-start.1) | async-done | bytes 16777248 | tf_op jit(solution)/shard_map/all_to_all | solution.py:32
  759.1 16.5 %copy.51 = f32[1,4,8,128,1024]{3,2,4,1,0:T(8,128)} copy(f32[1,4,8,128,1024]{4,3,1,2,0:T(8,128)} %bitcast.17) | data formatting | bytes 33554432 | tf_op jit(solution)/shard_map/all_to_all | solution.py:32
  775.6 18.0 %squeeze.4 = f32[1,4,1024,1024]{2,3,1,0:T(8,128)} reshape(f32[1,4,8,128,1024]{3,2,4,1,0:T(8,128)} %copy.51) | data formatting | bytes 33554432 | tf_op jit(solution)/shard_map/squeeze | solution.py:51
  793.6 0.0 copy-start.1
  793.6 13.6 %divide_convert_fusion = bf16[1,4,1024,1024]{2,3,1,0:T(8,128)(2,1)} fusion(f32[1,4,1024,1024]{2,3,1,0:T(8,128)} %squeeze.4, bf16[1,4,1024,1024]{2,3,1,0:T(8,128)(2,1)} %fusion, f32[4]{0:T(128)S(1)} %dynamic_slice.3, f32[4]{0:T(128)S(1)} %fusion.7, f32[1024,1024]{0,1:T(8,128)} %broadcast_add_fusion), kind=kLoop, calls=%fused_computation.2 | loop fusion | flops 25165824 | bytes 37748768 | tf_op jit(solution)/shard_map/convert_element_type | solution.py:51
  807.2 11.3 %copy.52 = bf16[1,4,1024,1024]{3,2,1,0:T(8,128)(2,1)} copy(bf16[1,4,1024,1024]{2,3,1,0:T(8,128)(2,1)} %divide_convert_fusion) | data formatting | bytes 16777216 | tf_op jit(solution)/shard_map/convert_element_type | solution.py:51
  818.5 0.0 copy-done.1
  (1 shorter events, 0.0 us)
Async XLA Ops:
  6.5 2.0 copy-start
  6.5 55.4 %all-gather.3.cloned.1.call-start = ((), (), s32[]{:S(2)}) async-start(), calls=%async_computation.2 | async-start | bytes 1310720 | tf_op jit(solution)/shard_map/all_gather | solution.py:19
  54.4 291.6 %all-to-all-start = ((bf16[1,4,1024,1024]{3,1,0,2:T(4,128)(2,1)}), bf16[1,4,1024,1024]{3,1,0,2:T(4,128)(2,1)}, u32[]{:S(2)}, u32[]{:S(2)}) async-start(bf16[1,4,1024,1024]{3,1,0,2:T(4,128)(2,1)} %copy.43), calls=%async_computation | async-start | bytes 16777216 | tf_op jit(solution)/shard_map/all_to_all | solution.py:25
  61.7 302.0 %all-gather.5.cloned.1.call-start = ((), (), s32[]{:S(2)}) async-start(), calls=%async_computation.3 | async-start | bytes 9437184 | tf_op jit(solution)/shard_map/all_gather | solution.py:29
  391.2 5.9 copy-start.3
  391.2 6.0 copy-start.4
  391.2 6.1 copy-start.2
  391.2 367.8 %all-to-all-start.1 = ((f32[1,32,128,1024]{3,2,0,1:T(8,128)}), f32[1,32,128,1024]{3,2,0,1:T(8,128)}, u32[]{:S(2)}, u32[]{:S(2)}) async-start(f32[1,32,128,1024]{3,2,0,1:T(8,128)} %bitcast.43), calls=%async_computation.1 | async-start | bytes 33554432 | tf_op jit(solution)/shard_map/all_to_all | solution.py:32
  793.6 25.0 %copy-start.1 = (bf16[1024,1024]{1,0:T(8,128)(2,1)S(1)}, bf16[1024,1024]{1,0:T(8,128)(2,1)}, u32[]{:S(2)}) copy-start(bf16[1024,1024]{1,0:T(8,128)(2,1)} %param.7) | copy-start | bytes 6291460
Sparse Core Ops, SparseCore 0:
  8.9 19.4 all-gather.2
  64.5 271.4 all-gather.4
where the time goes:
time: 827 us; the launch traced here: 825 us
  waiting for transfers between devices  643 us (78%)
  local copies, waits for them, and re-layouts  86.5 us (10%)
  matrix products  52.5 us (6%)
  other arithmetic  16.1 us (2%)
  between operations  13.5 us (2%)
  starting transfers between devices  13.3 us (2%)
    all_to_all x1, waiting for transfers between devices, shards(): lax.all_to_all(cycle_flat, 'pair', split_axis=1, concat_axis=2, tiled=True)  359 us
    all_to_all x1, waiting for transfers between devices, shards(): lax.all_to_all(dressed, 'pair', split_axis=2, concat_axis=1, tiled=True)  284 us
    dot_general x1, matrix products, column_cycle(): jnp.einsum('ibkc,kjac->ijab', panel_part, column_block, preferred_element...  21.5 us
    squeeze x1, local copies, waits for them, and re-layouts, shards(): pair_cycle[0]  18 us
    all_to_all x2, local copies, waits for them, and re-layouts, shards(): lax.all_to_all(dressed, 'pair', split_axis=2, concat_axis=1, tiled=True)  17.7 us
    all_to_all x1, local copies, waits for them, and re-layouts, shards(): lax.all_to_all(cycle_flat, 'pair', split_axis=1, concat_axis=2, tiled=True)  16.5 us
  transfers between devices with their start and end apart: 4, of which 2 were waited for; matrix products, arithmetic and copies ran while one was open for 8% of the time, Pallas kernels for 0%

commit v1 on v0

v1 whole, which is shorter than its diff:
```python
import jax
import jax.numpy as jnp
from jax import lax
from jax.sharding import Mesh, PartitionSpec as P

ROWS = 256
SWAP = [(0, 1), (1, 0)]


def shards(amplitudes, vv_fock, cycle_panels, row_energy, col_energy, virt_energy):
    amps = amplitudes[0]
    per_dev, virt_count, _ = amps.shape
    group_j = col_energy.shape[0]
    half = lax.axis_index("half")
    rest = lax.axis_index("rest")
    rows = min(ROWS, virt_count)

    kept = lax.dynamic_index_in_dim(cycle_panels, half, 0, keepdims=False)
    given = lax.dynamic_index_in_dim(cycle_panels, 1 - half, 0, keepdims=False)
    got = lax.ppermute(given, "half", SWAP)

    chunks = [(p, a) for p in range(per_dev) for a in range(0, virt_count, rows)]
    own, other = [], []
    for p, a in chunks:
        piece = (
            jnp.dot(vv_fock[a : a + rows], amps[p], preferred_element_type=jnp.float32)
            + lax.dot_general(
                amps[p, a : a + rows], vv_fock, (((1,), (1,)), ((), ())), preferred_element_type=jnp.float32
            )
        ).astype(jnp.bfloat16)
        own.append(piece)
        other.append(lax.ppermute(piece, "half", SWAP))

    first = jnp.where(half == 0, kept, got)
    second = jnp.where(half == 0, got, kept)
    panel = lax.all_gather(jnp.stack([first, second]), "grp", axis=2, tiled=True)
    panel = lax.all_gather(panel, "rest", axis=1, tiled=True)
    panel = panel.reshape(virt_count, 2, virt_count)
    own_panel = lax.dynamic_index_in_dim(panel, half, 1, keepdims=False)
    other_panel = lax.dynamic_index_in_dim(panel, 1 - half, 1, keepdims=False)

    row = lax.dynamic_index_in_dim(row_energy, half, 0, keepdims=False)
    out = jnp.zeros(amps.shape, jnp.bfloat16)
    for (p, a), mine, theirs in zip(chunks, own, other):
        nt = (((1,), (1,)), ((), ()))
        total = (
            mine.astype(jnp.float32)
            + lax.dot_general(mine, own_panel, nt, preferred_element_type=jnp.float32)
            + lax.dot_general(theirs, other_panel, nt, preferred_element_type=jnp.float32)
        )
        col = lax.dynamic_index_in_dim(col_energy, (rest * per_dev + p) % group_j, 0, keepdims=False)
        divisor = ((virt_energy[a : a + rows, None] + virt_energy[None, :]) - row) - col
        out = lax.dynamic_update_slice(out, (total / divisor).astype(jnp.bfloat16)[None], (p, a, 0))
    return out[None]


def solution(mesh):
    n_grp, n_pair = mesh.shape["grp"], mesh.shape["pair"]
    split = Mesh(mesh.devices.reshape(n_grp, 2, n_pair // 2), ("grp", "half", "rest"))
    pair = ("half", "rest")
    in_specs = (P("grp", pair, None, None), P(), P(None, pair, "grp"), P(), P("grp"), P())
    out_specs = P("grp", pair, None, None)
    return jax.shard_map(shards, mesh=split, in_specs=in_specs, out_specs=out_specs, check_vma=False)
```

time: 827 us -> 446 us (0.54)
  waiting for transfers between devices: 643 us -> 275 us
  local copies, waits for them, and re-layouts: 86.5 us -> 23.9 us
  matrix products: 52.5 us -> 110 us
  other arithmetic: 16.1 us -> 0.76 us
    all_to_all x2 -> x0, waiting for transfers between devices: 643 us -> none  [the longest x1 359 us: shards(): lax.all_to_all(cycle_flat, 'pair', split_axis=1, concat_axis=2, tiled=True)]
    ppermute x0 -> x17, waiting for transfers between devices: none -> 193 us  [the longest x16 193 us: shards(): other.append(lax.ppermute(piece, 'half', SWAP))]
    all_gather x2, waiting for transfers between devices: 0.02 us -> 82.1 us  [the longest x1 79.8 us: shards(): panel = lax.all_gather(panel, 'rest', axis=1, tiled=True)]
    dot_general x3 -> x64, matrix products: 52.5 us -> 110 us  [the longest x16 38.1 us: shards(): lax.dot_general(theirs, other_panel, nt, preferred_element_type=jnp.float32)]
    all_to_all x3 -> x0, local copies, waits for them, and re-layouts: 34.2 us -> none  [the longest x2 17.7 us: shards(): lax.all_to_all(dressed, 'pair', split_axis=2, concat_axis=1, tiled=True)]
    convert_element_type x2 -> x0, local copies, waits for them, and re-layouts: 26.2 us -> none  [the longest x1 14.9 us: shards(): dressed = (jnp.einsum('ac,gpcb->gpab', vv_fock, amplitudes, preferred_ele...]
    squeeze x1, local copies, waits for them, and re-layouts: 18 us -> 1.06 us  [shards(): given = lax.dynamic_index_in_dim(cycle_panels, 1 - half, 0, keepdims=False)]
    ppermute x0 -> x17, starting transfers between devices: none -> 16.1 us  [the longest x16 12 us: shards(): other.append(lax.ppermute(piece, 'half', SWAP))]
  transfers between devices with their start and end apart: 4 -> 19, of which waited for: 2 -> 13; matrix products, arithmetic and copies ran while one was open for 8% -> 30% of each run, Pallas kernels for 0% -> 0%
where the time goes in v1:
time: 446 us; the launch traced here: 441 us
  waiting for transfers between devices  275 us (62%)
  matrix products  110 us (25%)
  local copies, waits for them, and re-layouts  23.9 us (5%)
  starting transfers between devices  16.3 us (4%)
  between operations  14.3 us (3%)
    ppermute x16, waiting for transfers between devices, shards(): other.append(lax.ppermute(piece, 'half', SWAP))  193 us
    all_gather x1, waiting for transfers between devices, shards(): panel = lax.all_gather(panel, 'rest', axis=1, tiled=True)  79.8 us
    dot_general x16, matrix products, shards(): lax.dot_general(theirs, other_panel, nt, preferred_element_type=jnp.float32)  38.1 us
    dot_general x16, matrix products, shards(): jnp.dot(vv_fock[a:a + rows], amps[p], preferred_element_type=jnp.float32)  27.2 us
    dot_general x16, matrix products, shards(): lax.dot_general(amps[p, a:a + rows], vv_fock, (((1,), (1,)), ((), ())), p...  26.5 us
    dot_general x16, matrix products, shards(): lax.dot_general(mine, own_panel, nt, preferred_element_type=jnp.float32)  18.6 us
    ppermute x16, starting transfers between devices, shards(): other.append(lax.ppermute(piece, 'half', SWAP))  12 us
    dynamic_slice x1, local copies, waits for them, and re-layouts, shards(): other_panel = lax.dynamic_index_in_dim(panel, 1 - half, 1, keepdims=False)  10.3 us
  transfers between devices with their start and end apart: 19, of which 13 were waited for; matrix products, arithmetic and copies ran while one was open for 30% of the time, Pallas kernels for 0%

profile of v1, /device:TPU:0, one launch (start us, length us, event | category | flops | bytes accessed | tf_op | source)
XLA Modules:
  0.0 440.8 jit_solution(7256142142692195584)
XLA Ops:
  7.6 4.1 collective-permute-start
  11.7 2.6 fusion.508
  14.4 3.6 fusion.301
  18.0 1.8 fusion.507
  21.4 2.9 collective-permute-start.2
  25.0 1.6 fusion.295
  27.3 1.6 fusion.292
  28.9 2.9 collective-permute-start.4
  32.8 1.8 fusion.504
  34.6 3.2 fusion.289
  39.0 2.8 fusion.503
  41.8 2.7 fusion.502
  44.6 1.8 fusion.501
  46.4 2.3 all-gather.3.cloned.1.call-done
  48.8 1.9 fusion.500
  50.7 1.8 fusion.499
  52.5 1.9 fusion.498
  54.5 1.8 fusion.497
  56.2 1.8 fusion.496
  60.9 1.5 fusion.286
  62.4 1.5 fusion.283
  65.5 1.5 fusion.277
  67.0 1.6 fusion.274
  68.6 1.5 fusion.271
  70.1 1.9 fusion.268
  72.0 1.6 fusion.265
  73.6 1.5 fusion.262
  76.6 79.8 %all-gather.5.cloned.1.call-done = bf16[2,512,2048]{2,1,0:T(8,128)(2,1)} async-done(((bf16[2,128,2048]{2,1,0:T(8,128)(2,1)}), bf16[2,512,2048]{2,1,0:T(8,128)(2,1)}) %all-gather.5.cloned.1.call-update) | async-done | bytes 4194320 | tf_op jit(solution)/shard_map/all_gather | solution.py:37
  156.4 7.8 %reshape.61 = bf16[1024,2,1024]{2,1,0:T(2,128)(2,1)} reshape(bf16[2,512,2048]{2,1,0:T(8,128)(2,1)} %all-gather.5.cloned.1.call-done) | data formatting | bytes 8388608 | tf_op jit(solution)/shard_map/reshape | solution.py:38
  164.2 10.3 %constant_dynamic-slice_fusion = (bf16[1024,1,1024]{2,1,0:T(2,128)(2,1)S(1)}, bf16[1024,1,1024]{2,1,0:T(2,128)(2,1)S(1)}) fusion(bf16[1024,2,1024]{2,1,0:T(2,128)(2,1)} %reshape.61, s32[]{:T(128)S(6)} %select_n.94, s32[]{:T(128)S(6)} %select_n.93), kind=kLoop, calls=%fused_computation.298 | loop fusion | bytes 8388616 | tf_op jit(solution)/shard_map/jit(dynamic_index_in_dim)/dynamic_slice | solution.py:40
  176.1 2.0 fusion.144
  178.1 2.0 fusion.147
  180.3 3.0 fusion.400
  184.4 3.0 collective-permute-start.7
  187.4 3.0 fusion.406
  190.5 2.0 fusion.150
  192.5 2.1 fusion.153
  194.6 3.1 fusion.412
  197.8 3.0 collective-permute-start.9
  200.7 3.0 fusion.418
  203.8 2.0 fusion.156
  206.8 3.1 fusion.424
  210.0 42.2 %collective-permute-done.6 = bf16[256,1024]{1,0:T(8,128)(2,1)S(1)} collective-permute-done((bf16[256,1024]{1,0:T(8,128)(2,1)S(1)}, bf16[256,1024]{1,0:T(8,128)(2,1)S(1)}, u32[]{:S(2)}, u32[]{:S(2)}) %collective-permute-start.6) | collective-permute-done | bytes 524320 | tf_op jit(solution)/shard_map/ppermute | solution.py:32
  252.1 2.1 fusion.430
  255.9 18.7 %collective-permute-done.7 = bf16[256,1024]{1,0:T(8,128)(2,1)S(1)} collective-permute-done((bf16[256,1024]{1,0:T(8,128)(2,1)S(1)}, bf16[256,1024]{1,0:T(8,128)(2,1)S(1)}, u32[]{:S(2)}, u32[]{:S(2)}) %collective-permute-start.7) | collective-permute-done | bytes 524320 | tf_op jit(solution)/shard_map/ppermute | solution.py:32
  274.6 2.1 fusion.436
  276.7 20.4 %collective-permute-done.8 = bf16[256,1024]{1,0:T(8,128)(2,1)S(1)} collective-permute-done((bf16[256,1024]{1,0:T(8,128)(2,1)S(1)}, bf16[256,1024]{1,0:T(8,128)(2,1)S(1)}, u32[]{:S(2)}, u32[]{:S(2)}) %collective-permute-start.8) | collective-permute-done | bytes 524320 | tf_op jit(solution)/shard_map/ppermute | solution.py:32
  297.1 2.0 fusion.442
  300.7 18.9 %collective-permute-done.9 = bf16[256,1024]{1,0:T(8,128)(2,1)S(1)} collective-permute-done((bf16[256,1024]{1,0:T(8,128)(2,1)S(1)}, bf16[256,1024]{1,0:T(8,128)(2,1)S(1)}, u32[]{:S(2)}, u32[]{:S(2)}) %collective-permute-start.9) | collective-permute-done | bytes 524320 | tf_op jit(solution)/shard_map/ppermute | solution.py:32
  319.6 2.0 fusion.448
  321.6 20.4 %collective-permute-done.10 = bf16[256,1024]{1,0:T(8,128)(2,1)S(1)} collective-permute-done((bf16[256,1024]{1,0:T(8,128)(2,1)S(1)}, bf16[256,1024]{1,0:T(8,128)(2,1)S(1)}, u32[]{:S(2)}, u32[]{:S(2)}) %collective-permute-start.10) | collective-permute-done | bytes 524320 | tf_op jit(solution)/shard_map/ppermute | solution.py:32
  342.0 2.0 fusion.454
  345.6 18.9 %collective-permute-done.11 = bf16[256,1024]{1,0:T(8,128)(2,1)S(1)} collective-permute-done((bf16[256,1024]{1,0:T(8,128)(2,1)S(1)}, bf16[256,1024]{1,0:T(8,128)(2,1)S(1)}, u32[]{:S(2)}, u32[]{:S(2)}) %collective-permute-start.11) | collective-permute-done | bytes 524320 | tf_op jit(solution)/shard_map/ppermute | solution.py:32
  364.5 2.0 fusion.460
  366.5 20.4 %collective-permute-done.12 = bf16[256,1024]{1,0:T(8,128)(2,1)S(1)} collective-permute-done((bf16[256,1024]{1,0:T(8,128)(2,1)S(1)}, bf16[256,1024]{1,0:T(8,128)(2,1)S(1)}, u32[]{:S(2)}, u32[]{:S(2)}) %collective-permute-start.12) | collective-permute-done | bytes 524320 | tf_op jit(solution)/shard_map/ppermute | solution.py:32
  387.0 2.0 fusion.466
  390.5 7.7 %collective-permute-done.13 = bf16[256,1024]{1,0:T(8,128)(2,1)S(1)} collective-permute-done((bf16[256,1024]{1,0:T(8,128)(2,1)S(1)}, bf16[256,1024]{1,0:T(8,128)(2,1)S(1)}, u32[]{:S(2)}, u32[]{:S(2)}) %collective-permute-start.13) | collective-permute-done | bytes 524320 | tf_op jit(solution)/shard_map/ppermute | solution.py:32
  398.2 1.9 fusion.472
  400.1 9.3 %collective-permute-done.14 = bf16[256,1024]{1,0:T(8,128)(2,1)S(1)} collective-permute-done((bf16[256,1024]{1,0:T(8,128)(2,1)S(1)}, bf16[256,1024]{1,0:T(8,128)(2,1)S(1)}, u32[]{:S(2)}, u32[]{:S(2)}) %collective-permute-start.14) | collective-permute-done | bytes 524320 | tf_op jit(solution)/shard_map/ppermute | solution.py:32
  409.4 1.9 fusion.478
  413.0 7.7 %collective-permute-done.15 = bf16[256,1024]{1,0:T(8,128)(2,1)S(1)} collective-permute-done((bf16[256,1024]{1,0:T(8,128)(2,1)S(1)}, bf16[256,1024]{1,0:T(8,128)(2,1)S(1)}, u32[]{:S(2)}, u32[]{:S(2)}) %collective-permute-start.15) | collective-permute-done | bytes 524320 | tf_op jit(solution)/shard_map/ppermute | solution.py:32
  420.7 1.9 fusion.484
  422.6 8.4 %collective-permute-done.16 = bf16[256,1024]{1,0:T(8,128)(2,1)S(1)} collective-permute-done((bf16[256,1024]{1,0:T(8,128)(2,1)S(1)}, bf16[256,1024]{1,0:T(8,128)(2,1)S(1)}, u32[]{:S(2)}, u32[]{:S(2)}) %collective-permute-start.16) | collective-permute-done | bytes 524320 | tf_op jit(solution)/shard_map/ppermute | solution.py:32
  431.0 2.7 fusion.490
  (92 shorter events, 23.9 us)
Async XLA Ops:
  6.5 7.8 %copy-start = (bf16[1024,1024]{1,0:T(8,128)(2,1)S(1)}, bf16[1024,1024]{1,0:T(8,128)(2,1)}, u32[]{:S(2)}) copy-start(bf16[1024,1024]{1,0:T(8,128)(2,1)} %param.7) | copy-start | bytes 6291460
  6.5 42.2 %all-gather.3.cloned.1.call-start = ((), (), s32[]{:S(2)}) async-start(), calls=%async_computation | async-start | bytes 1310720 | tf_op jit(solution)/shard_map/all_gather | solution.py:36
  7.6 24.2 %collective-permute-start = (bf16[128,512]{1,0:T(8,128)(2,1)S(1)}, bf16[128,512]{1,0:T(8,128)(2,1)S(1)}, u32[]{:S(2)}, u32[]{:S(2)}) collective-permute-start(bf16[128,512]{1,0:T(8,128)(2,1)S(1)} %dynamic-slice_bitcast_fusion), channel_id=1, source_target_pairs={{0,4},{4,0},{1,5},{5,1},{2,6},{6,2},{3,7},{7,3},{8,12},{12,8},{9,1... | collective-permute-start | bytes 393224 | tf_op jit(solution)/shard_map/ppermute | solution.py:20
  11.7 8.1 %copy-start.1 = (bf16[1,4,1024,1024]{3,2,1,0:T(8,128)(2,1)S(1)}, bf16[1,4,1024,1024]{3,2,1,0:T(8,128)(2,1)}, u32[]{:S(2)}) copy-start(bf16[1,4,1024,1024]{3,2,1,0:T(8,128)(2,1)} %param.6) | copy-start | bytes 25165828
  18.0 162.2 %collective-permute-start.1 = (bf16[256,1024]{1,0:T(8,128)(2,1)}, bf16[256,1024]{1,0:T(8,128)(2,1)}, u32[]{:S(2)}, u32[]{:S(2)}) collective-permute-start(bf16[256,1024]{1,0:T(8,128)(2,1)} %fusion.301), channel_id=1, source_target_pairs={{0,4},{4,0},{1,5},{5,1},{2,6},{6,2},{3,7},{7,3},{8,12},{12,8},{9,1... | collective-permute-start | bytes 1572872 | tf_op jit(solution)/shard_map/ppermute | solution.py:32
  21.4 163.1 %collective-permute-start.2 = (bf16[256,1024]{1,0:T(8,128)(2,1)}, bf16[256,1024]{1,0:T(8,128)(2,1)}, u32[]{:S(2)}, u32[]{:S(2)}) collective-permute-start(bf16[256,1024]{1,0:T(8,128)(2,1)} %fusion.298), channel_id=1, source_target_pairs={{0,4},{4,0},{1,5},{5,1},{2,6},{6,2},{3,7},{7,3},{8,12},{12,8},{9,1... | collective-permute-start | bytes 1572872 | tf_op jit(solution)/shard_map/ppermute | solution.py:32
  26.6 168.0 %collective-permute-start.3 = (bf16[256,1024]{1,0:T(8,128)(2,1)}, bf16[256,1024]{1,0:T(8,128)(2,1)}, u32[]{:S(2)}, u32[]{:S(2)}) collective-permute-start(bf16[256,1024]{1,0:T(8,128)(2,1)} %fusion.295), channel_id=1, source_target_pairs={{0,4},{4,0},{1,5},{5,1},{2,6},{6,2},{3,7},{7,3},{8,12},{12,8},{9,1... | collective-permute-start | bytes 1572872 | tf_op jit(solution)/shard_map/ppermute | solution.py:32
  27.3 4.5 %copy-start.5 = (bf16[2,128,512]{2,1,0:T(8,128)(2,1)S(1)}, bf16[2,128,512]{2,1,0:T(8,128)(2,1)}, u32[]{:S(2)}) copy-start(bf16[2,128,512]{2,1,0:T(8,128)(2,1)} %param.8) | copy-start | bytes 786436
  28.9 168.8 %collective-permute-start.4 = (bf16[256,1024]{1,0:T(8,128)(2,1)}, bf16[256,1024]{1,0:T(8,128)(2,1)}, u32[]{:S(2)}, u32[]{:S(2)}) collective-permute-start(bf16[256,1024]{1,0:T(8,128)(2,1)} %fusion.292), channel_id=1, source_target_pairs={{0,4},{4,0},{1,5},{5,1},{2,6},{6,2},{3,7},{7,3},{8,12},{12,8},{9,1... | collective-permute-start | bytes 1572872 | tf_op jit(solution)/shard_map/ppermute | solution.py:32
  32.6 123.8 %all-gather.5.cloned.1.call-start = ((), (), s32[]{:S(2)}) async-start(), calls=%async_computation.1 | async-start | bytes 5242880 | tf_op jit(solution)/shard_map/all_gather | solution.py:37
  34.6 3.2 copy-start.17
  34.6 3.8 copy-start.6
  37.8 168.8 %collective-permute-start.5 = (bf16[256,1024]{1,0:T(8,128)(2,1)}, bf16[256,1024]{1,0:T(8,128)(2,1)}, u32[]{:S(2)}, u32[]{:S(2)}) collective-permute-start(bf16[256,1024]{1,0:T(8,128)(2,1)} %fusion.289), channel_id=1, source_target_pairs={{0,4},{4,0},{1,5},{5,1},{2,6},{6,2},{3,7},{7,3},{8,12},{12,8},{9,1... | collective-permute-start | bytes 1572872 | tf_op jit(solution)/shard_map/ppermute | solution.py:32
  44.6 4.1 copy-start.7
  48.7 9.3 %slice-start = ((s8[8388608]{0:T(1024)(128)(4,1)}), s8[4194304]{0:T(1024)(128)(4,1)S(1)}, s32[]{:S(2)}) async-start(s8[8388608]{0:T(1024)(128)(4,1)} %bitcast.548), calls=%async_computation.2 | async-start | bytes 8388608
  52.5 5.6 %slice-start.1 = ((s8[8388608]{0:T(1024)(128)(4,1)}), s8[4194304]{0:T(1024)(128)(4,1)S(1)}, s32[]{:S(2)}) async-start(s8[8388608]{0:T(1024)(128)(4,1)} %bitcast.548), calls=%async_computation.3 | async-start | bytes 8388608
  59.6 1.3 copy-start.4
  60.9 1.5 copy-start.3
  178.1 2.1 copy-start.16
  180.2 71.9 %collective-permute-start.6 = (bf16[256,1024]{1,0:T(8,128)(2,1)S(1)}, bf16[256,1024]{1,0:T(8,128)(2,1)S(1)}, u32[]{:S(2)}, u32[]{:S(2)}) collective-permute-start(bf16[256,1024]{1,0:T(8,128)(2,1)S(1)} %copy-done.16), channel_id=1, source_target_pairs={{0,4},{4,0},{1,5},{5,1},{2,6},{6,2},{3,7},{7,3},{8,12},{12,8},{9,1... | collective-permute-start | bytes 1572872 | tf_op jit(solution)/shard_map/ppermute | solution.py:32
  183.3 1.1 copy-start.15
  184.4 90.2 %collective-permute-start.7 = (bf16[256,1024]{1,0:T(8,128)(2,1)S(1)}, bf16[256,1024]{1,0:T(8,128)(2,1)S(1)}, u32[]{:S(2)}, u32[]{:S(2)}) collective-permute-start(bf16[256,1024]{1,0:T(8,128)(2,1)S(1)} %copy-done.15), channel_id=1, source_target_pairs={{0,4},{4,0},{1,5},{5,1},{2,6},{6,2},{3,7},{7,3},{8,12},{12,8},{9,1... | collective-permute-start | bytes 1572872 | tf_op jit(solution)/shard_map/ppermute | solution.py:32
  192.5 2.1 copy-start.14
  194.5 102.5 %collective-permute-start.8 = (bf16[256,1024]{1,0:T(8,128)(2,1)S(1)}, bf16[256,1024]{1,0:T(8,128)(2,1)S(1)}, u32[]{:S(2)}, u32[]{:S(2)}) collective-permute-start(bf16[256,1024]{1,0:T(8,128)(2,1)S(1)} %copy-done.14), channel_id=1, source_target_pairs={{0,4},{4,0},{1,5},{5,1},{2,6},{6,2},{3,7},{7,3},{8,12},{12,8},{9,1... | collective-permute-start | bytes 1572872 | tf_op jit(solution)/shard_map/ppermute | solution.py:32
  194.6 3.1 copy-start.13
  197.8 121.8 %collective-permute-start.9 = (bf16[256,1024]{1,0:T(8,128)(2,1)S(1)}, bf16[256,1024]{1,0:T(8,128)(2,1)S(1)}, u32[]{:S(2)}, u32[]{:S(2)}) collective-permute-start(bf16[256,1024]{1,0:T(8,128)(2,1)S(1)} %copy-done.13), channel_id=1, source_target_pairs={{0,4},{4,0},{1,5},{5,1},{2,6},{6,2},{3,7},{7,3},{8,12},{12,8},{9,1... | collective-permute-start | bytes 1572872 | tf_op jit(solution)/shard_map/ppermute | solution.py:32
  205.8 1.0 copy-start.12
  206.8 135.2 %collective-permute-start.10 = (bf16[256,1024]{1,0:T(8,128)(2,1)S(1)}, bf16[256,1024]{1,0:T(8,128)(2,1)S(1)}, u32[]{:S(2)}, u32[]{:S(2)}) collective-permute-start(bf16[256,1024]{1,0:T(8,128)(2,1)S(1)} %copy-done.12), channel_id=1, source_target_pairs={{0,4},{4,0},{1,5},{5,1},{2,6},{6,2},{3,7},{7,3},{8,12},{12,8},{9,1... | collective-permute-start | bytes 1572872 | tf_op jit(solution)/shard_map/ppermute | solution.py:32
  206.8 45.3 %copy-start.11 = (bf16[256,1024]{1,0:T(8,128)(2,1)S(1)}, bf16[256,1024]{1,0:T(8,128)(2,1)}, u32[]{:S(2)}) copy-start(bf16[256,1024]{1,0:T(8,128)(2,1)} %fusion.271) | copy-start | bytes 1572868
  252.1 112.4 %collective-permute-start.11 = (bf16[256,1024]{1,0:T(8,128)(2,1)S(1)}, bf16[256,1024]{1,0:T(8,128)(2,1)S(1)}, u32[]{:S(2)}, u32[]{:S(2)}) collective-permute-start(bf16[256,1024]{1,0:T(8,128)(2,1)S(1)} %copy-done.11), channel_id=1, source_target_pairs={{0,4},{4,0},{1,5},{5,1},{2,6},{6,2},{3,7},{7,3},{8,12},{12,8},{9,1... | collective-permute-start | bytes 1572872 | tf_op jit(solution)/shard_map/ppermute | solution.py:32
  255.0 19.6 %copy-start.10 = (bf16[256,1024]{1,0:T(8,128)(2,1)S(1)}, bf16[256,1024]{1,0:T(8,128)(2,1)}, u32[]{:S(2)}) copy-start(bf16[256,1024]{1,0:T(8,128)(2,1)} %fusion.268) | copy-start | bytes 1572868
  255.9 41.2 %copy-start.9 = (bf16[256,1024]{1,0:T(8,128)(2,1)S(1)}, bf16[256,1024]{1,0:T(8,128)(2,1)}, u32[]{:S(2)}) copy-start(bf16[256,1024]{1,0:T(8,128)(2,1)} %fusion.265) | copy-start | bytes 1572868
  274.6 112.4 %collective-permute-start.12 = (bf16[256,1024]{1,0:T(8,128)(2,1)S(1)}, bf16[256,1024]{1,0:T(8,128)(2,1)S(1)}, u32[]{:S(2)}, u32[]{:S(2)}) collective-permute-start(bf16[256,1024]{1,0:T(8,128)(2,1)S(1)} %copy-done.10), channel_id=1, source_target_pairs={{0,4},{4,0},{1,5},{5,1},{2,6},{6,2},{3,7},{7,3},{8,12},{12,8},{9,1... | collective-permute-start | bytes 1572872 | tf_op jit(solution)/shard_map/ppermute | solution.py:32
  297.1 101.1 %collective-permute-start.13 = (bf16[256,1024]{1,0:T(8,128)(2,1)S(1)}, bf16[256,1024]{1,0:T(8,128)(2,1)S(1)}, u32[]{:S(2)}, u32[]{:S(2)}) collective-permute-start(bf16[256,1024]{1,0:T(8,128)(2,1)S(1)} %copy-done.9), channel_id=1, source_target_pairs={{0,4},{4,0},{1,5},{5,1},{2,6},{6,2},{3,7},{7,3},{8,12},{12,8},{9,1... | collective-permute-start | bytes 1572872 | tf_op jit(solution)/shard_map/ppermute | solution.py:32
  299.9 19.7 %copy-start.8 = (bf16[256,1024]{1,0:T(8,128)(2,1)S(1)}, bf16[256,1024]{1,0:T(8,128)(2,1)}, u32[]{:S(2)}) copy-start(bf16[256,1024]{1,0:T(8,128)(2,1)} %fusion.262) | copy-start | bytes 1572868
  319.6 89.9 %collective-permute-start.14 = (bf16[256,1024]{1,0:T(8,128)(2,1)S(1)}, bf16[256,1024]{1,0:T(8,128)(2,1)S(1)}, u32[]{:S(2)}, u32[]{:S(2)}) collective-permute-start(bf16[256,1024]{1,0:T(8,128)(2,1)S(1)} %copy-done.8), channel_id=1, source_target_pairs={{0,4},{4,0},{1,5},{5,1},{2,6},{6,2},{3,7},{7,3},{8,12},{12,8},{9,1... | collective-permute-start | bytes 1572872 | tf_op jit(solution)/shard_map/ppermute | solution.py:32
  342.0 78.6 %collective-permute-start.15 = (bf16[256,1024]{1,0:T(8,128)(2,1)S(1)}, bf16[256,1024]{1,0:T(8,128)(2,1)S(1)}, u32[]{:S(2)}, u32[]{:S(2)}) collective-permute-start(bf16[256,1024]{1,0:T(8,128)(2,1)S(1)} %fusion.259), channel_id=1, source_target_pairs={{0,4},{4,0},{1,5},{5,1},{2,6},{6,2},{3,7},{7,3},{8,12},{12,8},{9,1... | collective-permute-start | bytes 1572872 | tf_op jit(solution)/shard_map/ppermute | solution.py:32
  364.5 66.5 %collective-permute-start.16 = (bf16[256,1024]{1,0:T(8,128)(2,1)S(1)}, bf16[256,1024]{1,0:T(8,128)(2,1)S(1)}, u32[]{:S(2)}, u32[]{:S(2)}) collective-permute-start(bf16[256,1024]{1,0:T(8,128)(2,1)S(1)} %fusion.256), channel_id=1, source_target_pairs={{0,4},{4,0},{1,5},{5,1},{2,6},{6,2},{3,7},{7,3},{8,12},{12,8},{9,1... | collective-permute-start | bytes 1572872 | tf_op jit(solution)/shard_map/ppermute | solution.py:32
  422.6 8.4 %copy-start.2 = (bf16[1,4,1024,1024]{3,2,1,0:T(8,128)(2,1)}, bf16[1,4,1024,1024]{3,2,1,0:T(8,128)(2,1)S(1)}, u32[]{:S(2)}) copy-start(bf16[1,4,1024,1024]{3,2,1,0:T(8,128)(2,1)S(1)} %fusion.484) | copy-start | bytes 25165828
Sparse Core Ops, SparseCore 0:
  32.7 15.9 all-gather.2
  50.2 106.1 all-gather.4

commit v2 on v1

v2 whole, which is shorter than its diff:
```python
import jax
import jax.numpy as jnp
from jax import lax
from jax.sharding import Mesh, PartitionSpec as P

ROWS = 256
DEPTH = 3
SWAP = [(0, 1), (1, 0)]
NT = (((1,), (1,)), ((), ()))


def after(value, event):
    return lax.optimization_barrier((value, event))[0]


def shards(amplitudes, vv_fock, cycle_panels, row_energy, col_energy, virt_energy):
    amps = amplitudes[0]
    per_dev, virt_count, _ = amps.shape
    group_j = col_energy.shape[0]
    n_grp, n_rest = lax.axis_size("grp"), lax.axis_size("rest")
    half, rest = (lax.axis_index(name) for name in ("half", "rest"))
    rows = min(ROWS, virt_count)

    kept = lax.dynamic_index_in_dim(cycle_panels, half, 0, keepdims=False)
    given = lax.dynamic_index_in_dim(cycle_panels, 1 - half, 0, keepdims=False)
    got = lax.ppermute(given, "half", SWAP)
    block = jnp.where(half == 0, jnp.stack([kept, got]), jnp.stack([got, kept]))[None]
    for axis, size in (("rest", n_rest), ("grp", n_grp)):
        step = size // 2
        while step:
            swapped = lax.ppermute(block, axis, [(i, i ^ step) for i in range(size)])
            low = lax.axis_index(axis) & step == 0
            block = jnp.where(low, jnp.concatenate([block, swapped]), jnp.concatenate([swapped, block]))
            step //= 2

    chunks = [(p, a) for p in range(per_dev) for a in range(0, virt_count, rows)]
    own, other = [], []
    for n, (p, a) in enumerate(chunks):
        whole, fock = amps[p], vv_fock
        if n >= DEPTH:
            whole, fock = after((whole, fock), other[n - DEPTH])
        piece = (
            jnp.dot(fock[a : a + rows], whole, preferred_element_type=jnp.float32)
            + lax.dot_general(whole[a : a + rows], fock, NT, preferred_element_type=jnp.float32)
        ).astype(jnp.bfloat16)
        own.append(piece)
        other.append(lax.ppermute(piece, "half", SWAP))

    block = after(block, other[min(len(chunks) - 1, 5)])
    bits = (n_rest * n_grp).bit_length() - 1
    panel = block.reshape(*(2,) * bits, *block.shape[1:])
    panel = panel.transpose(*range(bits)[::-1], bits, bits + 1, bits + 2)
    panel = panel.reshape(n_rest, n_grp, *block.shape[1:])
    panel = panel.transpose(2, 0, 3, 1, 4).reshape(virt_count, 2, virt_count)
    own_panel = lax.dynamic_index_in_dim(panel, half, 1, keepdims=False)
    other_panel = lax.dynamic_index_in_dim(panel, 1 - half, 1, keepdims=False)

    row = lax.dynamic_index_in_dim(row_energy, half, 0, keepdims=False)
    out = jnp.zeros(amps.shape, jnp.bfloat16)
    for (p, a), mine, theirs in zip(chunks, own, other):
        total = (
            mine.astype(jnp.float32)
            + lax.dot_general(mine, own_panel, NT, preferred_element_type=jnp.float32)
            + lax.dot_general(theirs, other_panel, NT, preferred_element_type=jnp.float32)
        )
        col = lax.dynamic_index_in_dim(col_energy, (rest * per_dev + p) % group_j, 0, keepdims=False)
        divisor = ((virt_energy[a : a + rows, None] + virt_energy[None, :]) - row) - col
        out = lax.dynamic_update_slice(out, (total / divisor).astype(jnp.bfloat16)[None], (p, a, 0))
    return out[None]


def solution(mesh):
    n_grp, n_pair = mesh.shape["grp"], mesh.shape["pair"]
    split = Mesh(mesh.devices.reshape(n_grp, 2, n_pair // 2), ("grp", "half", "rest"))
    pair = ("half", "rest")
    in_specs = (P("grp", pair, None, None), P(), P(None, pair, "grp"), P(), P("grp"), P())
    out_specs = P("grp", pair, None, None)
    return jax.shard_map(shards, mesh=split, in_specs=in_specs, out_specs=out_specs, check_vma=False)
```

time: 446 us -> 438 us (0.982)
  starting transfers between devices: 16.3 us -> 41.1 us
  waiting for transfers between devices: 275 us -> 252 us
  between operations: 14.3 us -> 1.35 us
  local copies, waits for them, and re-layouts: 23.9 us -> 35 us
  matrix products: 110 us -> 99.7 us
    all_gather x2 -> x0, waiting for transfers between devices: 82.1 us -> none  [the longest x1 79.8 us: shards(): panel = lax.all_gather(panel, 'rest', axis=1, tiled=True)]
    ppermute x0 -> x4, waiting for transfers between devices: none -> 33.4 us  [shards(): swapped = lax.ppermute(block, axis, [(i, i ^ step) for i in range(size)])]
    ppermute x0 -> x4, starting transfers between devices: none -> 27.6 us  [shards(): swapped = lax.ppermute(block, axis, [(i, i ^ step) for i in range(size)])]
    ppermute x16, waiting for transfers between devices: 193 us -> 218 us  [shards(): other.append(lax.ppermute(piece, 'half', SWAP))]
    dot_general x64, matrix products: 110 us -> 99.7 us  [the longest x16 39.9 us: shards(): lax.dot_general(theirs, other_panel, NT, preferred_element_type=jnp.float32)]
    dynamic_slice x1 -> x0, local copies, waits for them, and re-layouts: 10.3 us -> none  [shards(): other_panel = lax.dynamic_index_in_dim(panel, 1 - half, 1, keepdims=False)]
    transpose x0 -> x2, local copies, waits for them, and re-layouts: none -> 10.1 us  [the longest x1 7.59 us: shards(): panel = panel.transpose(2, 0, 3, 1, 4).reshape(virt_count, 2, virt_count)]
    unnamed x42 -> x110, local copies, waits for them, and re-layouts: 2.51 us -> 7.9 us
  transfers between devices with their start and end apart: 19 -> 21, of which waited for: 13 -> 11; matrix products, arithmetic and copies ran while one was open for 30% -> 29% of each run, Pallas kernels for 0% -> 0%
where the time goes in v2:
time: 438 us; the launch traced here: 433 us
  waiting for transfers between devices  252 us (58%)
  matrix products  99.7 us (23%)
  starting transfers between devices  41.1 us (9%)
  local copies, waits for them, and re-layouts  35 us (8%)
    ppermute x16, waiting for transfers between devices, shards(): other.append(lax.ppermute(piece, 'half', SWAP))  218 us
    dot_general x16, matrix products, shards(): lax.dot_general(theirs, other_panel, NT, preferred_element_type=jnp.float32)  39.9 us
    ppermute x4, waiting for transfers between devices, shards(): swapped = lax.ppermute(block, axis, [(i, i ^ step) for i in range(size)])  33.4 us
    ppermute x4, starting transfers between devices, shards(): swapped = lax.ppermute(block, axis, [(i, i ^ step) for i in range(size)])  27.6 us
    dot_general x16, matrix products, shards(): lax.dot_general(mine, own_panel, NT, preferred_element_type=jnp.float32)  23.9 us
    dot_general x16, matrix products, shards(): jnp.dot(fock[a:a + rows], whole, preferred_element_type=jnp.float32)  19 us
    dot_general x16, matrix products, shards(): lax.dot_general(whole[a:a + rows], fock, NT, preferred_element_type=jnp.f...  16.9 us
    ppermute x16, starting transfers between devices, shards(): other.append(lax.ppermute(piece, 'half', SWAP))  9.4 us
  transfers between devices with their start and end apart: 21, of which 11 were waited for; matrix products, arithmetic and copies ran while one was open for 29% of the time, Pallas kernels for 0%

profile of v2, /device:TPU:0, one launch (start us, length us, event | category | flops | bytes accessed | tf_op | source)
XLA Modules:
  0.0 432.8 jit_solution(12234856665735994783)
XLA Ops:
  0.0 1.0 dynamic-slice_bitcast_fusion.1
  1.0 4.1 collective-permute-start
  5.1 2.5 fusion.411
  7.6 1.8 fusion.161
  9.6 2.3 fusion.414
  11.9 1.8 fusion.160
  13.7 2.9 collective-permute-start.7
  16.6 2.3 fusion.405
  18.9 2.6 fusion.163
  22.3 1.0 maximum_select_fusion.4
  23.3 24.4 %collective-permute-start.1 = (bf16[1,2,128,512]{3,2,1,0:T(8,128)(2,1)S(1)}, bf16[1,2,128,512]{3,2,1,0:T(8,128)(2,1)}, u32[]{:S(2)}, u32[]{:S(2)}) collective-permute-start(bf16[1,2,128,512]{3,2,1,0:T(8,128)(2,1)S(1)} %maximum_select_fusion.4), channel_id=1, source_target_pairs={{0,2},{1,3},{2,0},{3,1},{4,6},{5,7},{6,4},{7,5},{8,10},{9,11},{10,... | collective-permute-start | bytes 786440 | tf_op jit(solution)/shard_map/ppermute | solution.py:31
  47.7 6.1 %slice_bitcast_fusion = (bf16[1024,1024]{1,0:T(8,128)(2,1)}, bf16[1024,1024]{1,0:T(8,128)(2,1)}, bf16[1024,1024]{1,0:T(8,128)(2,1)}, bf16[1024,1024]{1,0:T(8,128)(2,1)}) fusion(bf16[1,4,1024,1024]{3,2,1,0:T(8,128)(2,1)} %param.6), kind=kLoop, calls=%fused_computation.67 | loop fusion | bytes 16777216 | tf_op jit(solution)/shard_map/squeeze | solution.py:39
  55.1 30.5 %collective-permute-done.1 = bf16[1,2,128,512]{3,2,1,0:T(8,128)(2,1)} collective-permute-done((bf16[1,2,128,512]{3,2,1,0:T(8,128)(2,1)S(1)}, bf16[1,2,128,512]{3,2,1,0:T(8,128)(2,1)}, u32[]{:S(2)}, u32[]{:S(2)}) %collective-permute-start.1) | collective-permute-done | bytes 262176 | tf_op jit(solution)/shard_map/ppermute | solution.py:31
  85.6 1.1 maximum_select_fusion.3
  86.8 1.6 collective-permute-start.2
  88.4 1.8 fusion.407
  93.3 2.2 collective-permute-start.9
  97.0 0.8 collective-permute-start.10
  97.8 2.9 collective-permute-done.2
  100.9 1.6 collective-permute-start.3
  102.5 47.8 %collective-permute-done.9 = bf16[256,1024]{1,0:T(8,128)(2,1)S(1)} collective-permute-done((bf16[256,1024]{1,0:T(8,128)(2,1)S(1)}, bf16[256,1024]{1,0:T(8,128)(2,1)S(1)}, u32[]{:S(2)}, u32[]{:S(2)}) %collective-permute-start.9) | collective-permute-done | bytes 524320 | tf_op jit(solution)/shard_map/ppermute | solution.py:47
  151.9 20.9 %collective-permute-done.10 = bf16[256,1024]{1,0:T(8,128)(2,1)S(1)} collective-permute-done((bf16[256,1024]{1,0:T(8,128)(2,1)S(1)}, bf16[256,1024]{1,0:T(8,128)(2,1)S(1)}, u32[]{:S(2)}, u32[]{:S(2)}) %collective-permute-start.10) | collective-permute-done | bytes 524320 | tf_op jit(solution)/shard_map/ppermute | solution.py:47
  172.8 0.8 copy-done.34
  177.4 2.2 collective-permute-start.13
  179.7 26.8 %collective-permute-done.11 = bf16[256,1024]{1,0:T(8,128)(2,1)S(1)} collective-permute-done((bf16[256,1024]{1,0:T(8,128)(2,1)S(1)}, bf16[256,1024]{1,0:T(8,128)(2,1)S(1)}, u32[]{:S(2)}, u32[]{:S(2)}) %collective-permute-start.11) | collective-permute-done | bytes 524320 | tf_op jit(solution)/shard_map/ppermute | solution.py:47
  208.1 20.9 %collective-permute-done.12 = bf16[256,1024]{1,0:T(8,128)(2,1)S(1)} collective-permute-done((bf16[256,1024]{1,0:T(8,128)(2,1)S(1)}, bf16[256,1024]{1,0:T(8,128)(2,1)S(1)}, u32[]{:S(2)}, u32[]{:S(2)}) %collective-permute-start.12) | collective-permute-done | bytes 524320 | tf_op jit(solution)/shard_map/ppermute | solution.py:47
  230.5 20.9 %collective-permute-done.13 = bf16[256,1024]{1,0:T(8,128)(2,1)S(1)} collective-permute-done((bf16[256,1024]{1,0:T(8,128)(2,1)S(1)}, bf16[256,1024]{1,0:T(8,128)(2,1)S(1)}, u32[]{:S(2)}, u32[]{:S(2)}) %collective-permute-start.13) | collective-permute-done | bytes 524320 | tf_op jit(solution)/shard_map/ppermute | solution.py:47
  253.9 20.0 %collective-permute-done.14 = bf16[256,1024]{1,0:T(8,128)(2,1)S(1)} collective-permute-done((bf16[256,1024]{1,0:T(8,128)(2,1)S(1)}, bf16[256,1024]{1,0:T(8,128)(2,1)S(1)}, u32[]{:S(2)}, u32[]{:S(2)}) %collective-permute-start.14) | collective-permute-done | bytes 524320 | tf_op jit(solution)/shard_map/ppermute | solution.py:47
  275.5 20.9 %collective-permute-done.15 = bf16[256,1024]{1,0:T(8,128)(2,1)S(1)} collective-permute-done((bf16[256,1024]{1,0:T(8,128)(2,1)S(1)}, bf16[256,1024]{1,0:T(8,128)(2,1)S(1)}, u32[]{:S(2)}, u32[]{:S(2)}) %collective-permute-start.15) | collective-permute-done | bytes 524320 | tf_op jit(solution)/shard_map/ppermute | solution.py:47
  297.1 1.5 fusion.173
  298.6 20.2 %collective-permute-done.16 = bf16[256,1024]{1,0:T(8,128)(2,1)S(1)} collective-permute-done((bf16[256,1024]{1,0:T(8,128)(2,1)S(1)}, bf16[256,1024]{1,0:T(8,128)(2,1)S(1)}, u32[]{:S(2)}, u32[]{:S(2)}) %collective-permute-start.16) | collective-permute-done | bytes 524320 | tf_op jit(solution)/shard_map/ppermute | solution.py:47
  319.6 1.5 fusion.174
  321.1 20.2 %collective-permute-done.17 = bf16[256,1024]{1,0:T(8,128)(2,1)S(1)} collective-permute-done((bf16[256,1024]{1,0:T(8,128)(2,1)S(1)}, bf16[256,1024]{1,0:T(8,128)(2,1)S(1)}, u32[]{:S(2)}, u32[]{:S(2)}) %collective-permute-start.17) | collective-permute-done | bytes 524320 | tf_op jit(solution)/shard_map/ppermute | solution.py:47
  342.0 1.5 fusion.175
  344.3 2.5 copy.10
  346.8 7.6 %copy.11 = bf16[2,4,128,4,512]{2,1,0,4,3:T(4,128)(2,1)} copy(bf16[2,4,128,4,512]{4,2,0,3,1:T(8,128)(2,1)} %bitcast.452) | data formatting | bytes 8388608 | tf_op jit(solution)/shard_map/transpose | solution.py:54
  354.4 7.7 %reshape.129 = bf16[1024,2,1024]{0,2,1:T(8,128)(2,1)} reshape(bf16[2,4,128,4,512]{2,1,0,4,3:T(4,128)(2,1)} %copy.11) | data formatting | bytes 8388608 | tf_op jit(solution)/shard_map/reshape | solution.py:54
  362.1 2.4 fusion.64
  364.5 3.5 fusion.67
  368.1 1.7 fusion.70
  369.8 1.7 fusion.73
  371.5 1.7 fusion.76
  373.2 1.7 fusion.79
  381.9 3.1 fusion.272
  385.0 1.1 pad_bitcast_fusion
  386.1 3.5 fusion.278
  389.7 3.2 fusion.284
  392.9 2.2 fusion.290
  395.1 2.2 fusion.296
  397.3 2.1 fusion.302
  399.4 2.3 fusion.308
  401.8 2.1 fusion.314
  403.9 2.1 fusion.320
  406.0 2.1 fusion.326
  408.1 2.1 fusion.332
  410.2 2.0 fusion.338
  412.2 2.0 fusion.103
  414.2 2.0 fusion.344
  416.3 3.1 fusion.350
  419.4 1.9 fusion.106
  421.3 1.9 fusion.109
  423.3 3.1 fusion.356
  426.4 3.4 copy-done.5
  429.8 2.8 fusion.362
  (166 shorter events, 29.2 us)
Async XLA Ops:
  1.0 6.6 %copy-start = (bf16[1024,1024]{1,0:T(8,128)(2,1)S(1)}, bf16[1024,1024]{1,0:T(8,128)(2,1)}, u32[]{:S(2)}) copy-start(bf16[1024,1024]{1,0:T(8,128)(2,1)} %param.7) | copy-start | bytes 6291460
  1.0 20.6 %collective-permute-start = (bf16[128,512]{1,0:T(8,128)(2,1)S(1)}, bf16[128,512]{1,0:T(8,128)(2,1)S(1)}, u32[]{:S(2)}, u32[]{:S(2)}) collective-permute-start(bf16[128,512]{1,0:T(8,128)(2,1)S(1)} %get-tuple-element.64), channel_id=1, source_target_pairs={{0,4},{4,0},{1,5},{5,1},{2,6},{6,2},{3,7},{7,3},{8,12},{12,8},{9,1... | collective-permute-start | bytes 393224 | tf_op jit(solution)/shard_map/ppermute | solution.py:26
  9.4 79.0 %collective-permute-start.5 = (bf16[256,1024]{1,0:T(8,128)(2,1)S(1)}, bf16[256,1024]{1,0:T(8,128)(2,1)}, u32[]{:S(2)}, u32[]{:S(2)}) collective-permute-start(bf16[256,1024]{1,0:T(8,128)(2,1)S(1)} %fusion.161), channel_id=1, source_target_pairs={{0,4},{4,0},{1,5},{5,1},{2,6},{6,2},{3,7},{7,3},{8,12},{12,8},{9,1... | collective-permute-start | bytes 1572872 | tf_op jit(solution)/shard_map/ppermute | solution.py:47
  13.7 77.7 %collective-permute-start.7 = (bf16[256,1024]{1,0:T(8,128)(2,1)S(1)}, bf16[256,1024]{1,0:T(8,128)(2,1)}, u32[]{:S(2)}, u32[]{:S(2)}) collective-permute-start(bf16[256,1024]{1,0:T(8,128)(2,1)S(1)} %fusion.160), channel_id=1, source_target_pairs={{0,4},{4,0},{1,5},{5,1},{2,6},{6,2},{3,7},{7,3},{8,12},{12,8},{9,1... | collective-permute-start | bytes 1572872 | tf_op jit(solution)/shard_map/ppermute | solution.py:47
  21.5 74.0 %collective-permute-start.8 = (bf16[256,1024]{1,0:T(8,128)(2,1)}, bf16[256,1024]{1,0:T(8,128)(2,1)}, u32[]{:S(2)}, u32[]{:S(2)}) collective-permute-start(bf16[256,1024]{1,0:T(8,128)(2,1)} %fusion.163), channel_id=1, source_target_pairs={{0,4},{4,0},{1,5},{5,1},{2,6},{6,2},{3,7},{7,3},{8,12},{12,8},{9,1... | collective-permute-start | bytes 1572872 | tf_op jit(solution)/shard_map/ppermute | solution.py:47
  23.3 30.6 %copy-start.50 = (f32[2]{0:T(128)S(1)}, f32[2]{0:T(128)}, u32[]{:S(2)}) copy-start(f32[2]{0:T(128)} %param.9) | copy-start | bytes 28
  23.3 31.2 %copy-start.28 = (f32[16]{0:T(128)S(1)}, f32[16]{0:T(128)}, u32[]{:S(2)}) copy-start(f32[16]{0:T(128)} %param.10) | copy-start | bytes 196
  23.3 31.8 %copy-start.29 = (f32[1024]{0:T(1024)S(1)}, f32[1024]{0:T(1024)}, u32[]{:S(2)}) copy-start(f32[1024]{0:T(1024)} %param.11) | copy-start | bytes 12292
  23.3 62.3 %collective-permute-start.1 = (bf16[1,2,128,512]{3,2,1,0:T(8,128)(2,1)S(1)}, bf16[1,2,128,512]{3,2,1,0:T(8,128)(2,1)}, u32[]{:S(2)}, u32[]{:S(2)}) collective-permute-start(bf16[1,2,128,512]{3,2,1,0:T(8,128)(2,1)S(1)} %maximum_select_fusion.4), channel_id=1, source_target_pairs={{0,2},{1,3},{2,0},{3,1},{4,6},{5,7},{6,4},{7,5},{8,10},{9,11},{10,... | collective-permute-start | bytes 786440 | tf_op jit(solution)/shard_map/ppermute | solution.py:31
  86.8 3.4 copy-start.3
  86.8 13.9 %collective-permute-start.2 = (bf16[2,2,128,512]{3,2,1,0:T(8,128)(2,1)S(1)}, bf16[2,2,128,512]{3,2,1,0:T(8,128)(2,1)S(1)}, u32[]{:S(2)}, u32[]{:S(2)}) collective-permute-start(bf16[2,2,128,512]{3,2,1,0:T(8,128)(2,1)S(1)} %maximum_select_fusion.3), channel_id=1, source_target_pairs={{0,1},{1,0},{2,3},{3,2},{4,5},{5,4},{6,7},{7,6},{8,9},{9,8},{10,11... | collective-permute-start | bytes 1572872 | tf_op jit(solution)/shard_map/ppermute | solution.py:31
  90.2 1.6 copy-start.4
  90.9 2.3 copy-start.7
  90.9 84.3 %collective-permute-start.6 = (bf16[256,1024]{1,0:T(8,128)(2,1)S(1)}, bf16[256,1024]{1,0:T(8,128)(2,1)S(1)}, u32[]{:S(2)}, u32[]{:S(2)}) collective-permute-start(bf16[256,1024]{1,0:T(8,128)(2,1)S(1)} %fusion.162), channel_id=1, source_target_pairs={{0,4},{4,0},{1,5},{5,1},{2,6},{6,2},{3,7},{7,3},{8,12},{12,8},{9,1... | collective-permute-start | bytes 1572872 | tf_op jit(solution)/shard_map/ppermute | solution.py:47
  93.2 3.7 copy-start.9
  93.3 57.0 %collective-permute-start.9 = (bf16[256,1024]{1,0:T(8,128)(2,1)S(1)}, bf16[256,1024]{1,0:T(8,128)(2,1)S(1)}, u32[]{:S(2)}, u32[]{:S(2)}) collective-permute-start(bf16[256,1024]{1,0:T(8,128)(2,1)S(1)} %fusion.164), channel_id=1, source_target_pairs={{0,4},{4,0},{1,5},{5,1},{2,6},{6,2},{3,7},{7,3},{8,12},{12,8},{9,1... | collective-permute-start | bytes 1572872 | tf_op jit(solution)/shard_map/ppermute | solution.py:47
  97.0 54.1 %copy-start.11 = (bf16[256,1024]{1,0:T(8,128)(2,1)}, bf16[256,1024]{1,0:T(8,128)(2,1)S(1)}, u32[]{:S(2)}) copy-start(bf16[256,1024]{1,0:T(8,128)(2,1)S(1)} %fusion.165) | copy-start | bytes 1572868
  97.0 75.8 %collective-permute-start.10 = (bf16[256,1024]{1,0:T(8,128)(2,1)S(1)}, bf16[256,1024]{1,0:T(8,128)(2,1)S(1)}, u32[]{:S(2)}, u32[]{:S(2)}) collective-permute-start(bf16[256,1024]{1,0:T(8,128)(2,1)S(1)} %fusion.165), channel_id=1, source_target_pairs={{0,4},{4,0},{1,5},{5,1},{2,6},{6,2},{3,7},{7,3},{8,12},{12,8},{9,1... | collective-permute-start | bytes 1572872 | tf_op jit(solution)/shard_map/ppermute | solution.py:47
  100.9 152.1 %collective-permute-start.3 = (bf16[4,2,128,512]{3,2,1,0:T(8,128)(2,1)S(1)}, bf16[4,2,128,512]{3,2,1,0:T(8,128)(2,1)S(1)}, u32[]{:S(2)}, u32[]{:S(2)}) collective-permute-start(bf16[4,2,128,512]{3,2,1,0:T(8,128)(2,1)S(1)} %maximum_select_fusion.2), channel_id=1, source_target_pairs={{0,16},{8,24},{16,0},{24,8},{1,17},{9,25},{17,1},{25,9},{2,18},{10... | collective-permute-start | bytes 3145736 | tf_op jit(solution)/shard_map/ppermute | solution.py:31
  151.8 23.3 %copy-start.13 = (bf16[256,1024]{1,0:T(8,128)(2,1)}, bf16[256,1024]{1,0:T(8,128)(2,1)S(1)}, u32[]{:S(2)}) copy-start(bf16[256,1024]{1,0:T(8,128)(2,1)S(1)} %fusion.166) | copy-start | bytes 1572868
  151.8 54.7 %collective-permute-start.11 = (bf16[256,1024]{1,0:T(8,128)(2,1)S(1)}, bf16[256,1024]{1,0:T(8,128)(2,1)S(1)}, u32[]{:S(2)}, u32[]{:S(2)}) collective-permute-start(bf16[256,1024]{1,0:T(8,128)(2,1)S(1)} %fusion.166), channel_id=1, source_target_pairs={{0,4},{4,0},{1,5},{5,1},{2,6},{6,2},{3,7},{7,3},{8,12},{12,8},{9,1... | collective-permute-start | bytes 1572872 | tf_op jit(solution)/shard_map/ppermute | solution.py:47
  174.3 1.6 copy-start.2
  175.1 2.3 copy-start.15
  175.1 53.8 %collective-permute-start.12 = (bf16[256,1024]{1,0:T(8,128)(2,1)S(1)}, bf16[256,1024]{1,0:T(8,128)(2,1)S(1)}, u32[]{:S(2)}, u32[]{:S(2)}) collective-permute-start(bf16[256,1024]{1,0:T(8,128)(2,1)S(1)} %fusion.167), channel_id=1, source_target_pairs={{0,4},{4,0},{1,5},{5,1},{2,6},{6,2},{3,7},{7,3},{8,12},{12,8},{9,1... | collective-permute-start | bytes 1572872 | tf_op jit(solution)/shard_map/ppermute | solution.py:47
  175.2 2.2 copy-start.30
  177.4 30.5 %copy-start.17 = (bf16[256,1024]{1,0:T(8,128)(2,1)}, bf16[256,1024]{1,0:T(8,128)(2,1)S(1)}, u32[]{:S(2)}) copy-start(bf16[256,1024]{1,0:T(8,128)(2,1)S(1)} %fusion.168) | copy-start | bytes 1572868
  177.4 74.0 %collective-permute-start.13 = (bf16[256,1024]{1,0:T(8,128)(2,1)S(1)}, bf16[256,1024]{1,0:T(8,128)(2,1)S(1)}, u32[]{:S(2)}, u32[]{:S(2)}) collective-permute-start(bf16[256,1024]{1,0:T(8,128)(2,1)S(1)} %fusion.168), channel_id=1, source_target_pairs={{0,4},{4,0},{1,5},{5,1},{2,6},{6,2},{3,7},{7,3},{8,12},{12,8},{9,1... | collective-permute-start | bytes 1572872 | tf_op jit(solution)/shard_map/ppermute | solution.py:47
  206.5 1.5 copy-start.36
  208.0 22.5 %copy-start.19 = (bf16[256,1024]{1,0:T(8,128)(2,1)}, bf16[256,1024]{1,0:T(8,128)(2,1)S(1)}, u32[]{:S(2)}) copy-start(bf16[256,1024]{1,0:T(8,128)(2,1)S(1)} %fusion.169) | copy-start | bytes 1572868
  208.0 65.9 %collective-permute-start.14 = (bf16[256,1024]{1,0:T(8,128)(2,1)S(1)}, bf16[256,1024]{1,0:T(8,128)(2,1)S(1)}, u32[]{:S(2)}, u32[]{:S(2)}) collective-permute-start(bf16[256,1024]{1,0:T(8,128)(2,1)S(1)} %fusion.169), channel_id=1, source_target_pairs={{0,4},{4,0},{1,5},{5,1},{2,6},{6,2},{3,7},{7,3},{8,12},{12,8},{9,1... | collective-permute-start | bytes 1572872 | tf_op jit(solution)/shard_map/ppermute | solution.py:47
  230.4 22.5 %copy-start.21 = (bf16[256,1024]{1,0:T(8,128)(2,1)}, bf16[256,1024]{1,0:T(8,128)(2,1)S(1)}, u32[]{:S(2)}) copy-start(bf16[256,1024]{1,0:T(8,128)(2,1)S(1)} %fusion.170) | copy-start | bytes 1572868
  230.4 65.9 %collective-permute-start.15 = (bf16[256,1024]{1,0:T(8,128)(2,1)S(1)}, bf16[256,1024]{1,0:T(8,128)(2,1)S(1)}, u32[]{:S(2)}, u32[]{:S(2)}) collective-permute-start(bf16[256,1024]{1,0:T(8,128)(2,1)S(1)} %fusion.170), channel_id=1, source_target_pairs={{0,4},{4,0},{1,5},{5,1},{2,6},{6,2},{3,7},{7,3},{8,12},{12,8},{9,1... | collective-permute-start | bytes 1572872 | tf_op jit(solution)/shard_map/ppermute | solution.py:47
  251.4 1.5 copy-start.40
  252.9 21.0 %copy-start.1 = (bf16[1024,1024]{1,0:T(8,128)(2,1)S(1)}, bf16[1024,1024]{1,0:T(8,128)(2,1)}, u32[]{:S(2)}) copy-start(bf16[1024,1024]{1,0:T(8,128)(2,1)} %get-tuple-element.58) | copy-start | bytes 6291460
  252.9 65.9 %collective-permute-start.16 = (bf16[256,1024]{1,0:T(8,128)(2,1)S(1)}, bf16[256,1024]{1,0:T(8,128)(2,1)S(1)}, u32[]{:S(2)}, u32[]{:S(2)}) collective-permute-start(bf16[256,1024]{1,0:T(8,128)(2,1)S(1)} %fusion.171), channel_id=1, source_target_pairs={{0,4},{4,0},{1,5},{5,1},{2,6},{6,2},{3,7},{7,3},{8,12},{12,8},{9,1... | collective-permute-start | bytes 1572872 | tf_op jit(solution)/shard_map/ppermute | solution.py:47
  253.8 89.8 %collective-permute-start.4 = (bf16[8,2,128,512]{3,2,1,0:T(8,128)(2,1)S(1)}, bf16[8,2,128,512]{3,2,1,0:T(8,128)(2,1)S(1)}, u32[]{:S(2)}, u32[]{:S(2)}) collective-permute-start(bf16[8,2,128,512]{3,2,1,0:T(8,128)(2,1)S(1)} %maximum_select_fusion.1), channel_id=1, source_target_pairs={{0,8},{8,0},{16,24},{24,16},{1,9},{9,1},{17,25},{25,17},{2,10},{10... | collective-permute-start | bytes 6291464 | tf_op jit(solution)/shard_map/ppermute | solution.py:31
  275.4 23.3 %copy-start.25 = (bf16[256,1024]{1,0:T(8,128)(2,1)}, bf16[256,1024]{1,0:T(8,128)(2,1)S(1)}, u32[]{:S(2)}) copy-start(bf16[256,1024]{1,0:T(8,128)(2,1)S(1)} %fusion.172) | copy-start | bytes 1572868
  275.4 65.9 %collective-permute-start.17 = (bf16[256,1024]{1,0:T(8,128)(2,1)S(1)}, bf16[256,1024]{1,0:T(8,128)(2,1)S(1)}, u32[]{:S(2)}, u32[]{:S(2)}) collective-permute-start(bf16[256,1024]{1,0:T(8,128)(2,1)S(1)} %fusion.172), channel_id=1, source_target_pairs={{0,4},{4,0},{1,5},{5,1},{2,6},{6,2},{3,7},{7,3},{8,12},{12,8},{9,1... | collective-permute-start | bytes 1572872 | tf_op jit(solution)/shard_map/ppermute | solution.py:47
  296.3 2.3 copy-start.44
  298.6 117.6 %collective-permute-start.18 = (bf16[256,1024]{1,0:T(8,128)(2,1)}, bf16[256,1024]{1,0:T(8,128)(2,1)}, u32[]{:S(2)}, u32[]{:S(2)}) collective-permute-start(bf16[256,1024]{1,0:T(8,128)(2,1)} %fusion.173), channel_id=1, source_target_pairs={{0,4},{4,0},{1,5},{5,1},{2,6},{6,2},{3,7},{7,3},{8,12},{12,8},{9,1... | collective-permute-start | bytes 1572872 | tf_op jit(solution)/shard_map/ppermute | solution.py:47
  318.8 2.3 copy-start.46
  321.1 102.2 %collective-permute-start.19 = (bf16[256,1024]{1,0:T(8,128)(2,1)}, bf16[256,1024]{1,0:T(8,128)(2,1)}, u32[]{:S(2)}, u32[]{:S(2)}) collective-permute-start(bf16[256,1024]{1,0:T(8,128)(2,1)} %fusion.174), channel_id=1, source_target_pairs={{0,4},{4,0},{1,5},{5,1},{2,6},{6,2},{3,7},{7,3},{8,12},{12,8},{9,1... | collective-permute-start | bytes 1572872 | tf_op jit(solution)/shard_map/ppermute | solution.py:47
  341.3 2.3 copy-start.48
  343.6 82.8 %collective-permute-start.20 = (bf16[256,1024]{1,0:T(8,128)(2,1)}, bf16[256,1024]{1,0:T(8,128)(2,1)S(1)}, u32[]{:S(2)}, u32[]{:S(2)}) collective-permute-start(bf16[256,1024]{1,0:T(8,128)(2,1)} %fusion.175), channel_id=1, source_target_pairs={{0,4},{4,0},{1,5},{5,1},{2,6},{6,2},{3,7},{7,3},{8,12},{12,8},{9,1... | collective-permute-start | bytes 1572872 | tf_op jit(solution)/shard_map/ppermute | solution.py:47
  362.1 6.0 %copy-start.6 = (bf16[1024,2,1024]{0,2,1:T(8,128)(2,1)S(1)}, bf16[1024,2,1024]{0,2,1:T(8,128)(2,1)}, u32[]{:S(2)}) copy-start(bf16[1024,2,1024]{0,2,1:T(8,128)(2,1)} %reshape.129) | copy-start | bytes 12582916
  368.1 1.7 copy-start.10
  369.8 1.7 copy-start.12
  371.5 1.7 copy-start.8
  373.2 1.7 copy-start.14
  386.1 3.5 copy-start.54
  389.7 3.2 copy-start.33
  389.7 3.2 copy-start.53
  392.9 2.2 copy-start.35
  392.9 2.2 copy-start.52
  395.1 2.2 copy-start.31
  395.1 2.2 copy-start.51
  397.3 2.1 copy-start.37
  399.4 2.3 copy-start.39
  401.8 2.1 copy-start.41
  403.9 2.1 copy-start.43
  406.0 2.1 copy-start.45
  408.1 2.1 copy-start.47
  412.2 2.0 copy-start.49
  426.4 3.4 copy-start.5
  (12 other events, 13.1 us)

commit v3 on v1

v3 whole, which is shorter than its diff:
```python
import jax
import jax.numpy as jnp
from jax import lax
from jax.experimental import pallas as pl
from jax.experimental.pallas import tpu as pltpu
from jax.sharding import Mesh, PartitionSpec as P

ROWS = 256
COLS = 256
DEPTH = 3
VMEM = 48 * 1024 * 1024
PANEL_STEPS = [0, 0, 1, 0, 1, 1, 1, 1, 2, 2, 1]
SWAP = [(0, 1), (1, 0)]
NT = (((1,), (1,)), ((), ()))


def dot_nt(x, y):
    return lax.dot_general(x, y, NT, preferred_element_type=jnp.float32)


def dress_kernel(f_rows, t_cols, t_rows, f_cols, *rest):
    out = rest[-1]
    total = jnp.dot(f_rows[...], t_cols[...], preferred_element_type=jnp.float32)
    out[...] = (total + dot_nt(t_rows[...], f_cols[...])).astype(out.dtype)


def dress(amplitudes, fock, pair, first_row, rows, events):
    virt = fock.shape[0]
    cols = min(COLS, virt)
    block = first_row // rows
    return pl.pallas_call(
        dress_kernel,
        out_shape=jax.ShapeDtypeStruct((rows, virt), jnp.bfloat16),
        grid=(virt // cols,),
        in_specs=[
            pl.BlockSpec((rows, virt), lambda j: (block, 0)),
            pl.BlockSpec((None, None, virt, cols), lambda j: (0, pair, 0, j)),
            pl.BlockSpec((None, None, rows, virt), lambda j: (0, pair, block, 0)),
            pl.BlockSpec((cols, virt), lambda j: (j, 0)),
        ]
        + [pl.BlockSpec(memory_space=pltpu.HBM)] * len(events),
        out_specs=pl.BlockSpec((rows, cols), lambda j: (0, j)),
        compiler_params=pltpu.CompilerParams(vmem_limit_bytes=VMEM),
        cost_estimate=pl.CostEstimate(
            flops=4 * rows * virt * virt, bytes_accessed=4 * virt * virt + 6 * rows * virt, transcendentals=0
        ),
    )(fock, amplitudes, amplitudes, fock, *events)


def finish_kernel(energies, mine, own_cols, theirs, panel_own, panel_other, a_energy, b_energy, *rest):
    out = rest[-1]
    total = dot_nt(mine[...], panel_own[...]) + dot_nt(theirs[...], panel_other[...])
    total = total + own_cols[...].astype(jnp.float32)
    divisor = ((a_energy[...] + b_energy[...]) - energies[0]) - energies[1]
    out[...] = (total / divisor).astype(out.dtype)


def finish(out, shape, pair, first_row, energies, mine, theirs, panel, a_energy, b_energy, events):
    rows, virt = mine.shape
    cols = min(COLS, virt)
    block = first_row // rows
    behind = list(events) + ([] if out is None else [out])
    return pl.pallas_call(
        finish_kernel,
        out_shape=jax.ShapeDtypeStruct(shape, jnp.bfloat16),
        grid=(virt // cols,),
        in_specs=[
            pl.BlockSpec(memory_space=pltpu.SMEM),
            pl.BlockSpec((rows, virt), lambda j: (0, 0)),
            pl.BlockSpec((rows, cols), lambda j: (0, j)),
            pl.BlockSpec((rows, virt), lambda j: (0, 0)),
            pl.BlockSpec((None, cols, virt), lambda j: (0, j, 0)),
            pl.BlockSpec((None, cols, virt), lambda j: (1, j, 0)),
            pl.BlockSpec((rows, 1), lambda j: (block, 0)),
            pl.BlockSpec((1, cols), lambda j: (0, j)),
        ]
        + [pl.BlockSpec(memory_space=pltpu.HBM)] * len(behind),
        out_specs=pl.BlockSpec((None, None, rows, cols), lambda j: (0, pair, block, j)),
        input_output_aliases={} if out is None else {7 + len(behind): 0},
        compiler_params=pltpu.CompilerParams(vmem_limit_bytes=VMEM),
        cost_estimate=pl.CostEstimate(
            flops=4 * rows * virt * virt, bytes_accessed=4 * virt * virt + 6 * rows * virt, transcendentals=0
        ),
    )(energies, mine, mine, theirs, panel, panel, a_energy, b_energy, *behind)


def join_kernel(first, block, swapped, *rest):
    out = rest[-1]
    out[first[0]] = block[...]
    out[1 - first[0]] = swapped[...]


def join_columns_kernel(first, block, swapped, *rest):
    out = rest[-1]
    cols = block.shape[2]

    @pl.when(first[0] == 0)
    def _():
        out[:, :, :cols] = block[...]
        out[:, :, cols:] = swapped[...]

    @pl.when(first[0] == 1)
    def _():
        out[:, :, :cols] = swapped[...]
        out[:, :, cols:] = block[...]


def join_kernel(place, block, swapped, *rest):
    out = rest[-1]
    out[:, place[0]] = block[...]
    out[:, 1 - place[0]] = swapped[...]


def join(block, swapped, place, events):
    lead, rows, cols = block.shape
    joined = pl.pallas_call(
        join_kernel,
        out_shape=jax.ShapeDtypeStruct((lead, 2, rows, cols), block.dtype),
        in_specs=[pl.BlockSpec(memory_space=pltpu.SMEM)]
        + [pl.BlockSpec(memory_space=pltpu.VMEM)] * 2
        + [pl.BlockSpec(memory_space=pltpu.HBM)] * len(events),
        out_specs=pl.BlockSpec(memory_space=pltpu.VMEM),
        compiler_params=pltpu.CompilerParams(vmem_limit_bytes=VMEM),
    )(place[None], block, swapped, *events)
    return joined.reshape(2 * lead, rows, cols)


def place_kernel(where, block, *rest):
    rest[-1][...] = block[...]


def place(panel, block, where, col_blocks, events):
    lead, rows, cols = block.shape
    behind = list(events) + ([] if panel is None else [panel])
    return pl.pallas_call(
        place_kernel,
        out_shape=jax.ShapeDtypeStruct((2, lead, 2, rows, col_blocks * cols), block.dtype),
        grid_spec=pltpu.PrefetchScalarGridSpec(
            num_scalar_prefetch=1,
            grid=(1,),
            in_specs=[pl.BlockSpec((lead, rows, cols), lambda i, w: (0, 0, 0))]
            + [pl.BlockSpec(memory_space=pltpu.HBM)] * len(behind),
            out_specs=pl.BlockSpec((None, lead, None, rows, cols), lambda i, w: (w[0], 0, w[1], 0, w[2])),
        ),
        input_output_aliases={} if panel is None else {1 + len(behind): 0},
        compiler_params=pltpu.CompilerParams(vmem_limit_bytes=VMEM),
    )(where, block, *behind)


def shards(amplitudes, vv_fock, cycle_panels, row_energy, col_energy, virt_energy):
    per_dev, virt_count = amplitudes.shape[1:3]
    group_j = col_energy.shape[0]
    half, rest = lax.axis_index("half"), lax.axis_index("rest")
    n_rest, n_grp = lax.axis_size("rest"), lax.axis_size("grp")
    rows = min(ROWS, virt_count)
    chunks = [(p, a) for p in range(per_dev) for a in range(0, virt_count, rows)]

    row = lax.dynamic_index_in_dim(row_energy, half, 0, keepdims=False)
    cols = lax.dynamic_slice_in_dim(col_energy, (rest * per_dev) % group_j, per_dev)
    energies = [jnp.stack([row, cols[p]]) for p in range(per_dev)]
    a_energy, b_energy = virt_energy[:, None], virt_energy[None, :]

    own, other = [], []

    def send(n, events):
        piece = dress(amplitudes, vv_fock, *chunks[n], rows, events)
        own.append(piece)
        other.append(lax.ppermute(piece, "half", SWAP))

    given = lax.dynamic_index_in_dim(cycle_panels, 1 - half, 0, keepdims=False)
    kept = lax.dynamic_index_in_dim(cycle_panels, half, 0, keepdims=False)
    got = lax.ppermute(given, "half", SWAP)
    send(0, [])
    grp, col_blocks = lax.axis_index("grp"), n_grp // 2
    steps = [1 << bit for bit in range(n_rest.bit_length() - 2, 0, -1)]
    others = [(g, r) for g in range(n_grp - 1, -1, -1) for r in (1, 0)]
    block, panel, swapped = None, None, None

    def start_swap():
        return lax.ppermute(block, "rest", [(i, i ^ steps[0]) for i in range(n_rest)]) if steps else None

    def next_panel_step(last_piece):
        nonlocal block, panel, swapped
        if block is None:
            block = join(kept[None], got[None], half, [last_piece])
            swapped = start_swap()
        elif steps:
            step = steps.pop(0)
            block = join(block, swapped, (rest & step) // step, [last_piece])
            swapped = start_swap()
        else:
            g, r = others.pop()
            part = block
            if g or r:
                pairs = [(i * n_rest + j, (i ^ g) * n_rest + (j ^ r)) for i in range(n_grp) for j in range(n_rest)]
                part = lax.ppermute(block, ("grp", "rest"), pairs)
            from_grp = grp ^ g
            where = jnp.stack([(from_grp // col_blocks) ^ half, (rest ^ r) & 1, from_grp % col_blocks])
            panel = place(panel, part, where, col_blocks, [last_piece])

    out, finished = None, 0

    def end(n, events):
        whole = panel.reshape(2, virt_count, virt_count)
        return finish(
            out, amplitudes.shape, *chunks[n], energies[chunks[n][0]], own[n], other[n], whole, a_energy, b_energy, events
        )

    for n in range(1, len(chunks)):
        events = [own[n - 1]] + [x for x in (out, panel, block) if x is not None][:1]
        if n >= DEPTH:
            events.append(other[n - DEPTH])
        send(n, events)
        for _ in range(PANEL_STEPS[n] if n < len(PANEL_STEPS) else 0):
            if others:
                next_panel_step(own[n])
        while not others and finished <= min(2 * (n - 10) + 1, n - DEPTH):
            out = end(finished, [own[n]])
            finished += 1
    while others:
        next_panel_step(own[-1])
    for n in range(finished, len(chunks)):
        out = end(n, [own[-1]])
    return out


def solution(mesh):
    n_grp, n_pair = mesh.shape["grp"], mesh.shape["pair"]
    split = Mesh(mesh.devices.reshape(n_grp, 2, n_pair // 2), ("grp", "half", "rest"))
    pair = ("half", "rest")
    in_specs = (P("grp", pair, None, None), P(), P(None, pair, "grp"), P(), P("grp"), P())
    out_specs = P("grp", pair, None, None)
    return jax.shard_map(shards, mesh=split, in_specs=in_specs, out_specs=out_specs, check_vma=False)
```

time: 446 us -> 379 us (0.85)
  Pallas kernels: 0 us -> 149 us
  matrix products: 110 us -> 0 us
  waiting for transfers between devices: 275 us -> 173 us
  between operations: 14.3 us -> 0.68 us
  other arithmetic: 0.76 us -> 5.94 us
  starting transfers between devices: 16.3 us -> 21 us
    pallas_call x0 -> x42, Pallas kernels: none -> 149 us  [the longest x16 77.3 us: finish(): pl.pallas_call(finish_kernel, out_shape=jax.ShapeDtypeStruct(shape, jnp.b...]
    dot_general x64 -> x0, matrix products: 110 us -> none  [the longest x16 38.1 us: shards(): lax.dot_general(theirs, other_panel, nt, preferred_element_type=jnp.float32)]
    all_gather x2 -> x0, waiting for transfers between devices: 82.1 us -> none  [the longest x1 79.8 us: shards(): panel = lax.all_gather(panel, 'rest', axis=1, tiled=True)]
    unnamed x42 -> x86, local copies, waits for them, and re-layouts: 2.51 us -> 24.2 us
    ppermute x16 -> x24, waiting for transfers between devices: 193 us -> 173 us  [the longest x16 173 us: send(): other.append(lax.ppermute(piece, 'half', SWAP))]
    dynamic_slice x2 -> x1, local copies, waits for them, and re-layouts: 11 us -> 0.07 us  [shards(): lax.dynamic_slice_in_dim(col_energy, rest * per_dev % group_j, per_dev)]
    reshape x1 -> x0, local copies, waits for them, and re-layouts: 7.78 us -> none  [shards(): panel = panel.reshape(virt_count, 2, virt_count)]
    another operation x2 -> x12, other arithmetic: 0.75 us -> 5.94 us  [the longest x4 5.33 us: shards(): energies = [jnp.stack([row, cols[p]]) for p in range(per_dev)]]
  transfers between devices with their start and end apart: 19 -> 25, of which waited for: 13 -> 16; matrix products, arithmetic and copies ran while one was open for 30% -> 2% of each run, Pallas kernels for 0% -> 39%
where the time goes in v3:
time: 379 us; the launch traced here: 376 us
  waiting for transfers between devices  173 us (46%)
  Pallas kernels  149 us (39%)
  local copies, waits for them, and re-layouts  26.8 us (7%)
  starting transfers between devices  21 us (6%)
  other arithmetic  5.94 us (2%)
    ppermute x16, waiting for transfers between devices, send(): other.append(lax.ppermute(piece, 'half', SWAP))  173 us
    pallas_call x16, Pallas kernels, finish(): pl.pallas_call(finish_kernel, out_shape=jax.ShapeDtypeStruct(shape, jnp.b...  77.3 us
    pallas_call x16, Pallas kernels, dress(): pl.pallas_call(dress_kernel, out_shape=jax.ShapeDtypeStruct((rows, virt),...  62.1 us
    unnamed x86, local copies, waits for them, and re-layouts  24.2 us
    pallas_call x8, Pallas kernels, place(): pl.pallas_call(place_kernel, out_shape=jax.ShapeDtypeStruct((2, lead, 2,...  8.8 us
    ppermute x7, starting transfers between devices, next_panel_step(): part = lax.ppermute(block, ('grp', 'rest'), pairs)  8.11 us
  transfers between devices with their start and end apart: 25, of which 16 were waited for; matrix products, arithmetic and copies ran while one was open for 2% of the time, Pallas kernels for 39%

profile of v3, /device:TPU:0, one launch (start us, length us, event | category | flops | bytes accessed | tf_op | source)
XLA Modules:
  0.0 376.5 jit_solution(15439772974726651843)
XLA Ops:
  1.0 4.1 %collective-permute-start = (bf16[128,512]{1,0:T(8,128)(2,1)S(1)}, bf16[128,512]{1,0:T(8,128)(2,1)S(1)}, u32[]{:S(2)}, u32[]{:S(2)}) collective-permute-start(bf16[128,512]{1,0:T(8,128)(2,1)S(1)} %get-tuple-element.5), channel_id=1, source_target_pairs={{0,4},{4,0},{1,5},{5,1},{2,6},{6,2},{3,7},{7,3},{8,12},{12,8},{9,1... | collective-permute-start | bytes 393224 | tf_op jit(solution)/shard_map/ppermute | solution.py:172
  6.7 3.8 shard_map.64.rest_0_.mine.own_cols
  10.5 4.7 %shard_map.65.rest_0_.mine.own_cols = bf16[256,1024]{1,0:T(8,128)(2,1)} custom-call(bf16[1024,1024]{1,0:T(8,128)(2,1)S(1)} %copy-done.12, bf16[1,4,1024,1024]{3,2,1,0:T(8,128)(2,1)} %t_rows.31, bf16[1,4,1024,1024]{3,2,1,0:T(8,128)(2,1)} %t_rows.31, bf16[1024,1024]{1,0:T(8,128)(2,1)S(1)} %copy-done.12, bf16[256,1024]{1,0:T(8,128)(2,1)S(1)} %shard_map.64.rest_0_.mine.own_cols), custom_call_target="tpu_custom_call" | custom-call | flops 1073741824 | bytes 5767168 | tf_op jit(solution)/shard_map/pallas_call | solution.py:31
  15.2 2.9 collective-permute-start.2
  18.1 3.8 shard_map.66.rest_0_.mine.own_cols
  23.2 2.0 collective-permute-start.3
  25.2 34.6 %collective-permute-done.1.rest_2_.theirs = bf16[256,1024]{1,0:T(8,128)(2,1)} collective-permute-done((bf16[256,1024]{1,0:T(8,128)(2,1)S(1)}, bf16[256,1024]{1,0:T(8,128)(2,1)}, u32[]{:S(2)}, u32[]{:S(2)}) %collective-permute-start.1) | collective-permute-done | bytes 524320 | tf_op jit(solution)/shard_map/ppermute | solution.py:168
  59.8 3.8 shard_map.68.rest_0_.mine.own_cols
  63.6 18.6 %collective-permute-done.2.rest_2_.theirs = bf16[256,1024]{1,0:T(8,128)(2,1)} collective-permute-done((bf16[256,1024]{1,0:T(8,128)(2,1)}, bf16[256,1024]{1,0:T(8,128)(2,1)}, u32[]{:S(2)}, u32[]{:S(2)}) %collective-permute-start.2) | collective-permute-done | bytes 524320 | tf_op jit(solution)/shard_map/ppermute | solution.py:168
  82.2 3.8 shard_map.69.rest_0_.mine.own_cols
  88.7 16.0 %collective-permute-done.4.rest_2_.theirs = bf16[256,1024]{1,0:T(8,128)(2,1)} collective-permute-done((bf16[256,1024]{1,0:T(8,128)(2,1)S(1)}, bf16[256,1024]{1,0:T(8,128)(2,1)}, u32[]{:S(2)}, u32[]{:S(2)}) %collective-permute-start.4) | collective-permute-done | bytes 524320 | tf_op jit(solution)/shard_map/ppermute | solution.py:168
  104.7 3.8 shard_map.71.rest_0_.mine.own_cols
  108.5 7.3 %collective-permute-done.5.rest_2_.theirs = bf16[256,1024]{1,0:T(8,128)(2,1)S(1)} collective-permute-done((bf16[256,1024]{1,0:T(8,128)(2,1)S(1)}, bf16[256,1024]{1,0:T(8,128)(2,1)S(1)}, u32[]{:S(2)}, u32[]{:S(2)}) %collective-permute-start.5) | collective-permute-done | bytes 524320 | tf_op jit(solution)/shard_map/ppermute | solution.py:168
  117.6 2.0 copy-done
  121.9 3.8 %shard_map.73.rest_0_.mine.own_cols = bf16[256,1024]{1,0:T(8,128)(2,1)S(1)} custom-call(bf16[1024,1024]{1,0:T(8,128)(2,1)S(1)} %copy-done.13, bf16[1,4,1024,1024]{3,2,1,0:T(8,128)(2,1)} %t_rows.31, bf16[1,4,1024,1024]{3,2,1,0:T(8,128)(2,1)} %t_rows.31, bf16[1024,1024]{1,0:T(8,128)(2,1)S(1)} %copy-done.13, ...), custom_call_target="tpu_custom_call" | custom-call | flops 1073741824 | bytes 5767168 | tf_op jit(solution)/shard_map/pallas_call | solution.py:31
  125.7 12.6 %collective-permute-done.7.rest_2_.theirs = bf16[256,1024]{1,0:T(8,128)(2,1)S(1)} collective-permute-done((bf16[256,1024]{1,0:T(8,128)(2,1)S(1)}, bf16[256,1024]{1,0:T(8,128)(2,1)S(1)}, u32[]{:S(2)}, u32[]{:S(2)}) %collective-permute-start.7) | collective-permute-done | bytes 524320 | tf_op jit(solution)/shard_map/ppermute | solution.py:168
  139.7 2.0 copy-done.2
  141.7 4.6 %shard_map.75.rest_0_.mine.own_cols = bf16[256,1024]{1,0:T(8,128)(2,1)} custom-call(bf16[1024,1024]{1,0:T(8,128)(2,1)S(1)} %copy-done.13, bf16[1,4,1024,1024]{3,2,1,0:T(8,128)(2,1)} %t_rows.31, bf16[1,4,1024,1024]{3,2,1,0:T(8,128)(2,1)} %t_rows.31, bf16[1024,1024]{1,0:T(8,128)(2,1)S(1)} %copy-done.13, bf16[256,1024]{1,0:T(8,128)(2,1)S(1)} %shard_map.73.rest_0_.mine.own_cols, ...), custom_call_target="tpu_custom_call" | custom-call | flops 1073741824 | bytes 5767168 | tf_op jit(solution)/shard_map/pallas_call | solution.py:31
  146.3 2.5 collective-permute-start.14
  148.8 12.0 %collective-permute-done.9.rest_2_.theirs = bf16[256,1024]{1,0:T(8,128)(2,1)S(1)} collective-permute-done((bf16[256,1024]{1,0:T(8,128)(2,1)S(1)}, bf16[256,1024]{1,0:T(8,128)(2,1)S(1)}, u32[]{:S(2)}, u32[]{:S(2)}) %collective-permute-start.9) | collective-permute-done | bytes 524320 | tf_op jit(solution)/shard_map/ppermute | solution.py:168
  162.3 2.2 copy-done.3
  165.1 2.0 copy-done.4
  167.9 2.6 collective-permute-start.16
  170.5 3.8 shard_map.77.rest_0_.mine.own_cols
  174.2 9.0 %collective-permute-done.12.rest_2_.theirs = bf16[256,1024]{1,0:T(8,128)(2,1)S(1)} collective-permute-done((bf16[256,1024]{1,0:T(8,128)(2,1)S(1)}, bf16[256,1024]{1,0:T(8,128)(2,1)S(1)}, u32[]{:S(2)}, u32[]{:S(2)}) %collective-permute-start.12) | collective-permute-done | bytes 524320 | tf_op jit(solution)/shard_map/ppermute | solution.py:168
  187.0 2.2 copy-done.5
  191.9 2.0 copy-done.6
  193.9 3.8 shard_map.80.rest_0_.mine.own_cols
  197.6 3.0 collective-permute-start.18
  200.6 2.2 copy-done.7
  204.5 1.6 shard_map.82.rest_1_
  206.1 2.0 copy-done.8
  208.1 9.0 %collective-permute-done.15.rest_2_.theirs = bf16[256,1024]{1,0:T(8,128)(2,1)} collective-permute-done((bf16[256,1024]{1,0:T(8,128)(2,1)}, bf16[256,1024]{1,0:T(8,128)(2,1)}, u32[]{:S(2)}, u32[]{:S(2)}) %collective-permute-start.15) | collective-permute-done | bytes 524320 | tf_op jit(solution)/shard_map/ppermute | solution.py:168
  217.1 3.9 %shard_map.83.rest_0_.mine.own_cols = bf16[256,1024]{1,0:T(8,128)(2,1)S(1)} custom-call(bf16[1024,1024]{1,0:T(8,128)(2,1)S(1)} %copy-done.13, bf16[1,4,1024,1024]{3,2,1,0:T(8,128)(2,1)} %t_rows.31, bf16[1,4,1024,1024]{3,2,1,0:T(8,128)(2,1)} %t_rows.31, bf16[1024,1024]{1,0:T(8,128)(2,1)S(1)} %copy-done.13, ...), custom_call_target="tpu_custom_call" | custom-call | flops 1073741824 | bytes 5767168 | tf_op jit(solution)/shard_map/pallas_call | solution.py:31
  222.7 2.0 copy-done.10
  224.7 5.0 %shard_map.85.rest_1_ = bf16[1,4,1024,1024]{3,2,1,0:T(8,128)(2,1)} custom-call(f32[2]{0:T(128)S(1)} %pad_maximum_fusion.1.energies, bf16[256,1024]{1,0:T(8,128)(2,1)S(1)} %copy-done.23, bf16[256,1024]{1,0:T(8,128)(2,1)S(1)} %copy-done.23, bf16[256,1024]{1,0:T(8,128)(2,1)} %collective-permute-done.1.rest_2_.theirs, bf16[2,1024,1024]{2,1,0:T(8,128)(2,1)} %bitcast.20, ...), custom_call_target="tpu_custom_call" | custom-call | flops 1073741824 | bytes 5767168 | tf_op jit(solution)/shard_map/pallas_call | solution.py:63
  229.7 5.3 %shard_map.86.rest_1_ = bf16[1,4,1024,1024]{3,2,1,0:T(8,128)(2,1)} custom-call(f32[2]{0:T(128)S(1)} %pad_maximum_fusion.1.energies, bf16[256,1024]{1,0:T(8,128)(2,1)} %shard_map.65.rest_0_.mine.own_cols, bf16[256,1024]{1,0:T(8,128)(2,1)} %shard_map.65.rest_0_.mine.own_cols, ...), custom_call_target="tpu_custom_call", output_to_operand_aliasing={{}: (9, {})} | custom-call | flops 1073741824 | bytes 5767168 | tf_op jit(solution)/shard_map/pallas_call | solution.py:63
  235.0 4.5 %collective-permute-done.17.rest_2_.theirs = bf16[256,1024]{1,0:T(8,128)(2,1)} collective-permute-done((bf16[256,1024]{1,0:T(8,128)(2,1)S(1)}, bf16[256,1024]{1,0:T(8,128)(2,1)}, u32[]{:S(2)}, u32[]{:S(2)}) %collective-permute-start.17) | collective-permute-done | bytes 524320 | tf_op jit(solution)/shard_map/ppermute | solution.py:168
  239.5 3.8 shard_map.87.rest_0_.mine.own_cols
  243.4 5.1 %shard_map.88.rest_1_ = bf16[1,4,1024,1024]{3,2,1,0:T(8,128)(2,1)} custom-call(f32[2]{0:T(128)S(1)} %pad_maximum_fusion.1.energies, bf16[256,1024]{1,0:T(8,128)(2,1)S(1)} %copy-done.19, bf16[256,1024]{1,0:T(8,128)(2,1)S(1)} %copy-done.19, bf16[256,1024]{1,0:T(8,128)(2,1)} %collective-permute-done.4.rest_2_.theirs, ...), custom_call_target="tpu_custom_call", output_to_operand_aliasing={{}: (9, {})} | custom-call | flops 1073741824 | bytes 5767168 | tf_op jit(solution)/shard_map/pallas_call | solution.py:63
  248.5 4.8 %shard_map.89.rest_1_ = bf16[1,4,1024,1024]{3,2,1,0:T(8,128)(2,1)} custom-call(f32[2]{0:T(128)S(1)} %pad_maximum_fusion.1.energies, bf16[256,1024]{1,0:T(8,128)(2,1)S(1)} %copy-done.25, bf16[256,1024]{1,0:T(8,128)(2,1)S(1)} %copy-done.25, bf16[256,1024]{1,0:T(8,128)(2,1)S(1)} %copy-done.27, ...), custom_call_target="tpu_custom_call", output_to_operand_aliasing={{}: (9, {})} | custom-call | flops 1073741824 | bytes 5767168 | tf_op jit(solution)/shard_map/pallas_call | solution.py:63
  253.3 8.6 %collective-permute-done.18.rest_2_.theirs = bf16[256,1024]{1,0:T(8,128)(2,1)S(1)} collective-permute-done((bf16[256,1024]{1,0:T(8,128)(2,1)S(1)}, bf16[256,1024]{1,0:T(8,128)(2,1)S(1)}, u32[]{:S(2)}, u32[]{:S(2)}) %collective-permute-start.18) | collective-permute-done | bytes 524320 | tf_op jit(solution)/shard_map/ppermute | solution.py:168
  261.9 3.8 %shard_map.90.rest_0_.mine.own_cols = bf16[256,1024]{1,0:T(8,128)(2,1)S(1)} custom-call(bf16[1024,1024]{1,0:T(8,128)(2,1)S(1)} %copy-done.13, bf16[1,4,1024,1024]{3,2,1,0:T(8,128)(2,1)} %t_rows.31, bf16[1,4,1024,1024]{3,2,1,0:T(8,128)(2,1)} %t_rows.31, bf16[1024,1024]{1,0:T(8,128)(2,1)S(1)} %copy-done.13, ...), custom_call_target="tpu_custom_call" | custom-call | flops 1073741824 | bytes 5767168 | tf_op jit(solution)/shard_map/pallas_call | solution.py:31
  265.8 4.9 %shard_map.91.rest_1_ = bf16[1,4,1024,1024]{3,2,1,0:T(8,128)(2,1)} custom-call(f32[2]{0:T(128)S(1)} %pad_maximum_fusion.2.energies, bf16[256,1024]{1,0:T(8,128)(2,1)S(1)} %copy-done.15, bf16[256,1024]{1,0:T(8,128)(2,1)S(1)} %copy-done.15, bf16[256,1024]{1,0:T(8,128)(2,1)S(1)} %copy-done.29, ...), custom_call_target="tpu_custom_call", output_to_operand_aliasing={{}: (9, {})} | custom-call | flops 1073741824 | bytes 5767168 | tf_op jit(solution)/shard_map/pallas_call | solution.py:63
  270.7 4.8 %shard_map.92.rest_1_ = bf16[1,4,1024,1024]{3,2,1,0:T(8,128)(2,1)} custom-call(f32[2]{0:T(128)S(1)} %pad_maximum_fusion.2.energies, bf16[256,1024]{1,0:T(8,128)(2,1)S(1)} %copy-done.21, bf16[256,1024]{1,0:T(8,128)(2,1)S(1)} %copy-done.21, bf16[256,1024]{1,0:T(8,128)(2,1)S(1)} %copy-done.31, ...), custom_call_target="tpu_custom_call", output_to_operand_aliasing={{}: (9, {})} | custom-call | flops 1073741824 | bytes 5767168 | tf_op jit(solution)/shard_map/pallas_call | solution.py:63
  275.5 8.8 %collective-permute-done.19.rest_2_.theirs = bf16[256,1024]{1,0:T(8,128)(2,1)S(1)} collective-permute-done((bf16[256,1024]{1,0:T(8,128)(2,1)S(1)}, bf16[256,1024]{1,0:T(8,128)(2,1)S(1)}, u32[]{:S(2)}, u32[]{:S(2)}) %collective-permute-start.19) | collective-permute-done | bytes 524320 | tf_op jit(solution)/shard_map/ppermute | solution.py:168
  284.4 3.8 shard_map.93.rest_0_.mine.own_cols
  288.2 4.8 %shard_map.94.rest_1_ = bf16[1,4,1024,1024]{3,2,1,0:T(8,128)(2,1)} custom-call(f32[2]{0:T(128)S(1)} %pad_maximum_fusion.2.energies, bf16[256,1024]{1,0:T(8,128)(2,1)S(1)} %copy-done.17, bf16[256,1024]{1,0:T(8,128)(2,1)S(1)} %copy-done.17, bf16[256,1024]{1,0:T(8,128)(2,1)S(1)} %copy-done.33, ...), custom_call_target="tpu_custom_call", output_to_operand_aliasing={{}: (9, {})} | custom-call | flops 1073741824 | bytes 5767168 | tf_op jit(solution)/shard_map/pallas_call | solution.py:63
  293.0 5.3 %shard_map.95.rest_1_ = bf16[1,4,1024,1024]{3,2,1,0:T(8,128)(2,1)} custom-call(f32[2]{0:T(128)S(1)} %pad_maximum_fusion.2.energies, bf16[256,1024]{1,0:T(8,128)(2,1)} %shard_map.75.rest_0_.mine.own_cols, bf16[256,1024]{1,0:T(8,128)(2,1)} %shard_map.75.rest_0_.mine.own_cols, ...), custom_call_target="tpu_custom_call", output_to_operand_aliasing={{}: (9, {})} | custom-call | flops 1073741824 | bytes 5767168 | tf_op jit(solution)/shard_map/pallas_call | solution.py:63
  298.4 8.5 %collective-permute-done.20.rest_2_.theirs = bf16[256,1024]{1,0:T(8,128)(2,1)S(1)} collective-permute-done((bf16[256,1024]{1,0:T(8,128)(2,1)S(1)}, bf16[256,1024]{1,0:T(8,128)(2,1)S(1)}, u32[]{:S(2)}, u32[]{:S(2)}) %collective-permute-start.20) | collective-permute-done | bytes 524320 | tf_op jit(solution)/shard_map/ppermute | solution.py:168
  306.8 3.8 shard_map.96.rest_0_.mine.own_cols
  310.7 5.2 %shard_map.97.rest_1_ = bf16[1,4,1024,1024]{3,2,1,0:T(8,128)(2,1)} custom-call(f32[2]{0:T(128)S(1)} %pad_maximum_fusion.3.energies, bf16[256,1024]{1,0:T(8,128)(2,1)S(1)} %shard_map.77.rest_0_.mine.own_cols, bf16[256,1024]{1,0:T(8,128)(2,1)S(1)} %shard_map.77.rest_0_.mine.own_cols, ...), custom_call_target="tpu_custom_call", output_to_operand_aliasing={{}: (9, {})} | custom-call | flops 1073741824 | bytes 5767168 | tf_op jit(solution)/shard_map/pallas_call | solution.py:63
  315.9 4.8 %shard_map.98.rest_1_ = bf16[1,4,1024,1024]{3,2,1,0:T(8,128)(2,1)} custom-call(f32[2]{0:T(128)S(1)} %pad_maximum_fusion.3.energies, bf16[256,1024]{1,0:T(8,128)(2,1)S(1)} %shard_map.80.rest_0_.mine.own_cols, bf16[256,1024]{1,0:T(8,128)(2,1)S(1)} %shard_map.80.rest_0_.mine.own_cols, ...), custom_call_target="tpu_custom_call", output_to_operand_aliasing={{}: (9, {})} | custom-call | flops 1073741824 | bytes 5767168 | tf_op jit(solution)/shard_map/pallas_call | solution.py:63
  320.7 8.7 %collective-permute-done.21.rest_2_.theirs = bf16[256,1024]{1,0:T(8,128)(2,1)S(1)} collective-permute-done((bf16[256,1024]{1,0:T(8,128)(2,1)S(1)}, bf16[256,1024]{1,0:T(8,128)(2,1)S(1)}, u32[]{:S(2)}, u32[]{:S(2)}) %collective-permute-start.21) | collective-permute-done | bytes 524320 | tf_op jit(solution)/shard_map/ppermute | solution.py:168
  329.3 3.8 shard_map.99.rest_0_.mine.own_cols
  334.4 4.8 %shard_map.100.rest_1_ = bf16[1,4,1024,1024]{3,2,1,0:T(8,128)(2,1)} custom-call(f32[2]{0:T(128)S(1)} %pad_maximum_fusion.3.energies, bf16[256,1024]{1,0:T(8,128)(2,1)S(1)} %shard_map.83.rest_0_.mine.own_cols, bf16[256,1024]{1,0:T(8,128)(2,1)S(1)} %shard_map.83.rest_0_.mine.own_cols, ...), custom_call_target="tpu_custom_call", output_to_operand_aliasing={{}: (9, {})} | custom-call | flops 1073741824 | bytes 5767168 | tf_op jit(solution)/shard_map/pallas_call | solution.py:63
  339.2 4.8 %shard_map.101.rest_1_ = bf16[1,4,1024,1024]{3,2,1,0:T(8,128)(2,1)} custom-call(f32[2]{0:T(128)S(1)} %pad_maximum_fusion.3.energies, bf16[256,1024]{1,0:T(8,128)(2,1)S(1)} %shard_map.87.rest_0_.mine.own_cols, bf16[256,1024]{1,0:T(8,128)(2,1)S(1)} %shard_map.87.rest_0_.mine.own_cols, ...), custom_call_target="tpu_custom_call", output_to_operand_aliasing={{}: (9, {})} | custom-call | flops 1073741824 | bytes 5767168 | tf_op jit(solution)/shard_map/pallas_call | solution.py:63
  344.0 4.8 %shard_map.102.rest_1_ = bf16[1,4,1024,1024]{3,2,1,0:T(8,128)(2,1)} custom-call(f32[2]{0:T(128)S(1)} %pad_maximum_fusion.energies, bf16[256,1024]{1,0:T(8,128)(2,1)S(1)} %shard_map.90.rest_0_.mine.own_cols, bf16[256,1024]{1,0:T(8,128)(2,1)S(1)} %shard_map.90.rest_0_.mine.own_cols, ...), custom_call_target="tpu_custom_call", output_to_operand_aliasing={{}: (9, {})} | custom-call | flops 1073741824 | bytes 5767168 | tf_op jit(solution)/shard_map/pallas_call | solution.py:63
  348.8 3.0 collective-permute-done.24.theirs
  351.8 4.8 %shard_map.103.rest_1_ = bf16[1,4,1024,1024]{3,2,1,0:T(8,128)(2,1)} custom-call(f32[2]{0:T(128)S(1)} %pad_maximum_fusion.energies, bf16[256,1024]{1,0:T(8,128)(2,1)S(1)} %shard_map.93.rest_0_.mine.own_cols, bf16[256,1024]{1,0:T(8,128)(2,1)S(1)} %shard_map.93.rest_0_.mine.own_cols, ...), custom_call_target="tpu_custom_call", output_to_operand_aliasing={{}: (9, {})} | custom-call | flops 1073741824 | bytes 5767168 | tf_op jit(solution)/shard_map/pallas_call | solution.py:63
  356.6 6.4 %collective-permute-done.23.theirs = bf16[256,1024]{1,0:T(8,128)(2,1)S(1)} collective-permute-done((bf16[256,1024]{1,0:T(8,128)(2,1)S(1)}, bf16[256,1024]{1,0:T(8,128)(2,1)S(1)}, u32[]{:S(2)}, u32[]{:S(2)}) %collective-permute-start.23) | collective-permute-done | bytes 524320 | tf_op jit(solution)/shard_map/ppermute | solution.py:168
  363.0 4.8 %shard_map.104.rest_1_ = bf16[1,4,1024,1024]{3,2,1,0:T(8,128)(2,1)} custom-call(f32[2]{0:T(128)S(1)} %pad_maximum_fusion.energies, bf16[256,1024]{1,0:T(8,128)(2,1)S(1)} %shard_map.96.rest_0_.mine.own_cols, bf16[256,1024]{1,0:T(8,128)(2,1)S(1)} %shard_map.96.rest_0_.mine.own_cols, ...), custom_call_target="tpu_custom_call", output_to_operand_aliasing={{}: (9, {})} | custom-call | flops 1073741824 | bytes 5767168 | tf_op jit(solution)/shard_map/pallas_call | solution.py:63
  367.8 5.3 %collective-permute-done.22.theirs = bf16[256,1024]{1,0:T(8,128)(2,1)S(1)} collective-permute-done((bf16[256,1024]{1,0:T(8,128)(2,1)S(1)}, bf16[256,1024]{1,0:T(8,128)(2,1)S(1)}, u32[]{:S(2)}, u32[]{:S(2)}) %collective-permute-start.22) | collective-permute-done | bytes 524320 | tf_op jit(solution)/shard_map/ppermute | solution.py:168
  373.1 3.4 shard_map.105
  (131 shorter events, 26.4 us)
Async XLA Ops:
  1.0 22.1 %collective-permute-start = (bf16[128,512]{1,0:T(8,128)(2,1)S(1)}, bf16[128,512]{1,0:T(8,128)(2,1)S(1)}, u32[]{:S(2)}, u32[]{:S(2)}) collective-permute-start(bf16[128,512]{1,0:T(8,128)(2,1)S(1)} %get-tuple-element.5), channel_id=1, source_target_pairs={{0,4},{4,0},{1,5},{5,1},{2,6},{6,2},{3,7},{7,3},{8,12},{12,8},{9,1... | collective-permute-start | bytes 393224 | tf_op jit(solution)/shard_map/ppermute | solution.py:172
  5.1 1.6 copy-start.12
  10.4 4.8 %copy-start.22 = (bf16[256,1024]{1,0:T(8,128)(2,1)}, bf16[256,1024]{1,0:T(8,128)(2,1)S(1)}, u32[]{:S(2)}) copy-start(bf16[256,1024]{1,0:T(8,128)(2,1)S(1)} %shard_map.64.rest_0_.mine.own_cols) | copy-start | bytes 1572868
  10.5 49.3 %collective-permute-start.1 = (bf16[256,1024]{1,0:T(8,128)(2,1)S(1)}, bf16[256,1024]{1,0:T(8,128)(2,1)}, u32[]{:S(2)}, u32[]{:S(2)}) collective-permute-start(bf16[256,1024]{1,0:T(8,128)(2,1)S(1)} %shard_map.64.rest_0_.mine.own_cols), channel_id=1, source_target_pairs={{0,4},{4,0},{1,5},{5,1},{2,6},{6,2},{3,7},{7,3},{8,12},{12,8},{9,1... | collective-permute-start | bytes 1572872 | tf_op jit(solution)/shard_map/ppermute | solution.py:168
  15.2 7.1 %copy-start.41 = (f32[2]{0:T(128)S(1)}, f32[2]{0:T(128)}, u32[]{:S(2)}) copy-start(f32[2]{0:T(128)} %param.9) | copy-start | bytes 28
  15.2 7.8 %copy-start.42 = (f32[16]{0:T(128)S(1)}, f32[16]{0:T(128)}, u32[]{:S(2)}) copy-start(f32[16]{0:T(128)} %param.10) | copy-start | bytes 196
  15.2 44.6 %copy-start.13 = (bf16[1024,1024]{1,0:T(8,128)(2,1)S(1)}, bf16[1024,1024]{1,0:T(8,128)(2,1)}, u32[]{:S(2)}) copy-start(bf16[1024,1024]{1,0:T(8,128)(2,1)} %f_cols.31) | copy-start | bytes 6291460
  15.2 67.0 %collective-permute-start.2 = (bf16[256,1024]{1,0:T(8,128)(2,1)}, bf16[256,1024]{1,0:T(8,128)(2,1)}, u32[]{:S(2)}, u32[]{:S(2)}) collective-permute-start(bf16[256,1024]{1,0:T(8,128)(2,1)} %shard_map.65.rest_0_.mine.own_cols), channel_id=1, source_target_pairs={{0,4},{4,0},{1,5},{5,1},{2,6},{6,2},{3,7},{7,3},{8,12},{12,8},{9,1... | collective-permute-start | bytes 1572872 | tf_op jit(solution)/shard_map/ppermute | solution.py:168
  21.9 41.7 %copy-start.18 = (bf16[256,1024]{1,0:T(8,128)(2,1)}, bf16[256,1024]{1,0:T(8,128)(2,1)S(1)}, u32[]{:S(2)}) copy-start(bf16[256,1024]{1,0:T(8,128)(2,1)S(1)} %shard_map.66.rest_0_.mine.own_cols) | copy-start | bytes 1572868
  21.9 82.9 %collective-permute-start.4 = (bf16[256,1024]{1,0:T(8,128)(2,1)S(1)}, bf16[256,1024]{1,0:T(8,128)(2,1)}, u32[]{:S(2)}, u32[]{:S(2)}) collective-permute-start(bf16[256,1024]{1,0:T(8,128)(2,1)S(1)} %shard_map.66.rest_0_.mine.own_cols), channel_id=1, source_target_pairs={{0,4},{4,0},{1,5},{5,1},{2,6},{6,2},{3,7},{7,3},{8,12},{12,8},{9,1... | collective-permute-start | bytes 1572872 | tf_op jit(solution)/shard_map/ppermute | solution.py:168
  23.2 62.9 %collective-permute-start.3 = (bf16[2,128,512]{2,1,0:T(8,128)(2,1)S(1)}, bf16[2,128,512]{2,1,0:T(8,128)(2,1)S(1)}, u32[]{:S(2)}, u32[]{:S(2)}) collective-permute-start(bf16[2,128,512]{2,1,0:T(8,128)(2,1)S(1)} %bitcast.52), channel_id=1, source_target_pairs={{0,2},{1,3},{2,0},{3,1},{4,6},{5,7},{6,4},{7,5},{8,10},{9,11},{10,... | collective-permute-start | bytes 786440 | tf_op jit(solution)/shard_map/ppermute | solution.py:180
  63.6 22.5 %copy-start.24 = (bf16[256,1024]{1,0:T(8,128)(2,1)}, bf16[256,1024]{1,0:T(8,128)(2,1)S(1)}, u32[]{:S(2)}) copy-start(bf16[256,1024]{1,0:T(8,128)(2,1)S(1)} %shard_map.68.rest_0_.mine.own_cols) | copy-start | bytes 1572868
  63.6 52.3 %collective-permute-start.5 = (bf16[256,1024]{1,0:T(8,128)(2,1)S(1)}, bf16[256,1024]{1,0:T(8,128)(2,1)S(1)}, u32[]{:S(2)}, u32[]{:S(2)}) collective-permute-start(bf16[256,1024]{1,0:T(8,128)(2,1)S(1)} %shard_map.68.rest_0_.mine.own_cols), channel_id=1, source_target_pairs={{0,4},{4,0},{1,5},{5,1},{2,6},{6,2},{3,7},{7,3},{8,12},{12,8},{9,1... | collective-permute-start | bytes 1572872 | tf_op jit(solution)/shard_map/ppermute | solution.py:168
  86.0 22.5 %copy-start.14 = (bf16[256,1024]{1,0:T(8,128)(2,1)}, bf16[256,1024]{1,0:T(8,128)(2,1)S(1)}, u32[]{:S(2)}) copy-start(bf16[256,1024]{1,0:T(8,128)(2,1)S(1)} %shard_map.69.rest_0_.mine.own_cols) | copy-start | bytes 1572868
  87.0 32.6 %collective-permute-start.6 = (bf16[4,128,512]{2,1,0:T(8,128)(2,1)}, bf16[4,128,512]{2,1,0:T(8,128)(2,1)S(1)}, u32[]{:S(2)}, u32[]{:S(2)}) collective-permute-start(bf16[4,128,512]{2,1,0:T(8,128)(2,1)} %bitcast.5.rest_1_.block), channel_id=1, source_target_pairs={{0,1},{1,0},{2,3},{3,2},{8,9},{9,8},{10,11},{11,10},{16,17},{17,16... | collective-permute-start | bytes 1572872 | tf_op jit(solution)/shard_map/ppermute | solution.py:196
  88.5 49.8 %collective-permute-start.7 = (bf16[256,1024]{1,0:T(8,128)(2,1)S(1)}, bf16[256,1024]{1,0:T(8,128)(2,1)S(1)}, u32[]{:S(2)}, u32[]{:S(2)}) collective-permute-start(bf16[256,1024]{1,0:T(8,128)(2,1)S(1)} %shard_map.69.rest_0_.mine.own_cols), channel_id=1, source_target_pairs={{0,4},{4,0},{1,5},{5,1},{2,6},{6,2},{3,7},{7,3},{8,12},{12,8},{9,1... | collective-permute-start | bytes 1572872 | tf_op jit(solution)/shard_map/ppermute | solution.py:168
  88.7 57.6 %collective-permute-start.8 = (bf16[4,128,512]{2,1,0:T(8,128)(2,1)}, bf16[4,128,512]{2,1,0:T(8,128)(2,1)S(1)}, u32[]{:S(2)}, u32[]{:S(2)}) collective-permute-start(bf16[4,128,512]{2,1,0:T(8,128)(2,1)} %bitcast.5.rest_1_.block), channel_id=1, source_target_pairs={{0,8},{1,9},{2,10},{3,11},{8,0},{9,1},{10,2},{11,3},{16,24},{17,25... | collective-permute-start | bytes 1572872 | tf_op jit(solution)/shard_map/ppermute | solution.py:196
  104.7 56.1 %collective-permute-start.11 = (bf16[4,128,512]{2,1,0:T(8,128)(2,1)}, bf16[4,128,512]{2,1,0:T(8,128)(2,1)S(1)}, u32[]{:S(2)}, u32[]{:S(2)}) collective-permute-start(bf16[4,128,512]{2,1,0:T(8,128)(2,1)} %bitcast.5.rest_1_.block), channel_id=1, source_target_pairs={{0,9},{1,8},{2,11},{3,10},{8,1},{9,0},{10,3},{11,2},{16,25},{17,24... | collective-permute-start | bytes 1572872 | tf_op jit(solution)/shard_map/ppermute | solution.py:196
  108.5 17.2 %copy-start.20 = (bf16[256,1024]{1,0:T(8,128)(2,1)}, bf16[256,1024]{1,0:T(8,128)(2,1)S(1)}, u32[]{:S(2)}) copy-start(bf16[256,1024]{1,0:T(8,128)(2,1)S(1)} %shard_map.71.rest_0_.mine.own_cols) | copy-start | bytes 1572868
  115.8 9.9 %copy-start.26 = (bf16[256,1024]{1,0:T(8,128)(2,1)}, bf16[256,1024]{1,0:T(8,128)(2,1)S(1)}, u32[]{:S(2)}) copy-start(bf16[256,1024]{1,0:T(8,128)(2,1)S(1)} %collective-permute-done.5.rest_2_.theirs) | copy-start | bytes 1572868
  115.8 44.9 %collective-permute-start.9 = (bf16[256,1024]{1,0:T(8,128)(2,1)S(1)}, bf16[256,1024]{1,0:T(8,128)(2,1)S(1)}, u32[]{:S(2)}, u32[]{:S(2)}) collective-permute-start(bf16[256,1024]{1,0:T(8,128)(2,1)S(1)} %shard_map.71.rest_0_.mine.own_cols), channel_id=1, source_target_pairs={{0,4},{4,0},{1,5},{5,1},{2,6},{6,2},{3,7},{7,3},{8,12},{12,8},{9,1... | collective-permute-start | bytes 1572872 | tf_op jit(solution)/shard_map/ppermute | solution.py:168
  117.6 2.0 copy-start
  120.4 18.7 %copy-start.1 = (bf16[2,4,2,128,1024]{4,3,2,1,0:T(8,128)(2,1)S(1)}, bf16[2,4,2,128,1024]{4,3,2,1,0:T(8,128)(2,1)}, u32[]{:S(2)}) copy-start(bf16[2,4,2,128,1024]{4,3,2,1,0:T(8,128)(2,1)} %copy-done) | copy-start | bytes 12582916
  120.4 46.7 %collective-permute-start.10 = (bf16[4,128,512]{2,1,0:T(8,128)(2,1)}, bf16[4,128,512]{2,1,0:T(8,128)(2,1)S(1)}, u32[]{:S(2)}, u32[]{:S(2)}) collective-permute-start(bf16[4,128,512]{2,1,0:T(8,128)(2,1)} %bitcast.5.rest_1_.block), channel_id=1, source_target_pairs={{0,16},{1,17},{2,18},{3,19},{8,24},{9,25},{10,26},{11,27},{16,0},{... | collective-permute-start | bytes 1572872 | tf_op jit(solution)/shard_map/ppermute | solution.py:196
  121.9 17.2 %copy-start.40 = (bf16[4,128,512]{2,1,0:T(8,128)(2,1)S(1)}, bf16[4,128,512]{2,1,0:T(8,128)(2,1)}, u32[]{:S(2)}) copy-start(bf16[4,128,512]{2,1,0:T(8,128)(2,1)} %copy-done.39) | copy-start | bytes 1572868
  125.7 20.6 %copy-start.16 = (bf16[256,1024]{1,0:T(8,128)(2,1)}, bf16[256,1024]{1,0:T(8,128)(2,1)S(1)}, u32[]{:S(2)}) copy-start(bf16[256,1024]{1,0:T(8,128)(2,1)S(1)} %shard_map.73.rest_0_.mine.own_cols) | copy-start | bytes 1572868
  138.3 8.0 %copy-start.28 = (bf16[256,1024]{1,0:T(8,128)(2,1)}, bf16[256,1024]{1,0:T(8,128)(2,1)S(1)}, u32[]{:S(2)}) copy-start(bf16[256,1024]{1,0:T(8,128)(2,1)S(1)} %collective-permute-done.7.rest_2_.theirs) | copy-start | bytes 1572868
  138.3 44.9 %collective-permute-start.12 = (bf16[256,1024]{1,0:T(8,128)(2,1)S(1)}, bf16[256,1024]{1,0:T(8,128)(2,1)S(1)}, u32[]{:S(2)}, u32[]{:S(2)}) collective-permute-start(bf16[256,1024]{1,0:T(8,128)(2,1)S(1)} %shard_map.73.rest_0_.mine.own_cols), channel_id=1, source_target_pairs={{0,4},{4,0},{1,5},{5,1},{2,6},{6,2},{3,7},{7,3},{8,12},{12,8},{9,1... | collective-permute-start | bytes 1572872 | tf_op jit(solution)/shard_map/ppermute | solution.py:168
  139.7 2.0 copy-start.2
  146.3 51.3 %collective-permute-start.14 = (bf16[4,128,512]{2,1,0:T(8,128)(2,1)}, bf16[4,128,512]{2,1,0:T(8,128)(2,1)}, u32[]{:S(2)}, u32[]{:S(2)}) collective-permute-start(bf16[4,128,512]{2,1,0:T(8,128)(2,1)} %bitcast.5.rest_1_.block), channel_id=1, source_target_pairs={{0,17},{1,16},{2,19},{3,18},{8,25},{9,24},{10,27},{11,26},{16,1},{... | collective-permute-start | bytes 1572872 | tf_op jit(solution)/shard_map/ppermute | solution.py:196
  160.8 13.4 %copy-start.30 = (bf16[256,1024]{1,0:T(8,128)(2,1)}, bf16[256,1024]{1,0:T(8,128)(2,1)S(1)}, u32[]{:S(2)}) copy-start(bf16[256,1024]{1,0:T(8,128)(2,1)S(1)} %collective-permute-done.9.rest_2_.theirs) | copy-start | bytes 1572868
  160.8 43.7 %collective-permute-start.13 = (bf16[4,128,512]{2,1,0:T(8,128)(2,1)}, bf16[4,128,512]{2,1,0:T(8,128)(2,1)}, u32[]{:S(2)}, u32[]{:S(2)}) collective-permute-start(bf16[4,128,512]{2,1,0:T(8,128)(2,1)} %bitcast.5.rest_1_.block), channel_id=1, source_target_pairs={{0,24},{1,25},{2,26},{3,27},{8,16},{9,17},{10,18},{11,19},{16,8},{... | collective-permute-start | bytes 1572872 | tf_op jit(solution)/shard_map/ppermute | solution.py:196
  160.8 13.4 %copy-start.35 = (bf16[4,128,512]{2,1,0:T(8,128)(2,1)}, bf16[4,128,512]{2,1,0:T(8,128)(2,1)S(1)}, u32[]{:S(2)}) copy-start(bf16[4,128,512]{2,1,0:T(8,128)(2,1)S(1)} %collective-permute-done.11.block) | copy-start | bytes 1572868
  160.8 56.3 %collective-permute-start.15 = (bf16[256,1024]{1,0:T(8,128)(2,1)}, bf16[256,1024]{1,0:T(8,128)(2,1)}, u32[]{:S(2)}, u32[]{:S(2)}) collective-permute-start(bf16[256,1024]{1,0:T(8,128)(2,1)} %shard_map.75.rest_0_.mine.own_cols), channel_id=1, source_target_pairs={{0,4},{4,0},{1,5},{5,1},{2,6},{6,2},{3,7},{7,3},{8,12},{12,8},{9,1... | collective-permute-start | bytes 1572872 | tf_op jit(solution)/shard_map/ppermute | solution.py:168
  162.3 2.2 copy-start.3
  165.1 2.0 copy-start.4
  167.1 18.3 %copy-start.34 = (f32[1024]{0:T(1024)S(1)}, f32[1024]{0:T(1024)}, u32[]{:S(2)}) copy-start(f32[1024]{0:T(1024)} %param.11) | copy-start | bytes 12292
  167.9 53.2 %collective-permute-start.16 = (bf16[4,128,512]{2,1,0:T(8,128)(2,1)}, bf16[4,128,512]{2,1,0:T(8,128)(2,1)}, u32[]{:S(2)}, u32[]{:S(2)}) collective-permute-start(bf16[4,128,512]{2,1,0:T(8,128)(2,1)} %bitcast.5.rest_1_.block), channel_id=1, source_target_pairs={{0,25},{1,24},{2,27},{3,26},{8,17},{9,16},{10,19},{11,18},{16,9},{... | collective-permute-start | bytes 1572872 | tf_op jit(solution)/shard_map/ppermute | solution.py:196
  184.1 55.5 %collective-permute-start.17 = (bf16[256,1024]{1,0:T(8,128)(2,1)S(1)}, bf16[256,1024]{1,0:T(8,128)(2,1)}, u32[]{:S(2)}, u32[]{:S(2)}) collective-permute-start(bf16[256,1024]{1,0:T(8,128)(2,1)S(1)} %shard_map.77.rest_0_.mine.own_cols), channel_id=1, source_target_pairs={{0,4},{4,0},{1,5},{5,1},{2,6},{6,2},{3,7},{7,3},{8,12},{12,8},{9,1... | collective-permute-start | bytes 1572872 | tf_op jit(solution)/shard_map/ppermute | solution.py:168
  187.0 2.2 copy-start.5
  189.2 1.0 copy-start.36
  190.2 3.6 copy-start.33
  191.8 2.0 copy-start.6
  197.6 64.3 %collective-permute-start.18 = (bf16[256,1024]{1,0:T(8,128)(2,1)S(1)}, bf16[256,1024]{1,0:T(8,128)(2,1)S(1)}, u32[]{:S(2)}, u32[]{:S(2)}) collective-permute-start(bf16[256,1024]{1,0:T(8,128)(2,1)S(1)} %shard_map.80.rest_0_.mine.own_cols), channel_id=1, source_target_pairs={{0,4},{4,0},{1,5},{5,1},{2,6},{6,2},{3,7},{7,3},{8,12},{12,8},{9,1... | collective-permute-start | bytes 1572872 | tf_op jit(solution)/shard_map/ppermute | solution.py:168
  200.6 2.2 copy-start.7
  206.1 2.0 copy-start.8
  217.1 4.0 %copy-start.9 = (bf16[2,4,2,128,1024]{4,3,2,1,0:T(8,128)(2,1)S(1)}, bf16[2,4,2,128,1024]{4,3,2,1,0:T(8,128)(2,1)}, u32[]{:S(2)}) copy-start(bf16[2,4,2,128,1024]{4,3,2,1,0:T(8,128)(2,1)} %copy-done.8) | copy-start | bytes 12582916
  221.0 3.7 copy-start.23
  221.0 63.4 %collective-permute-start.19 = (bf16[256,1024]{1,0:T(8,128)(2,1)S(1)}, bf16[256,1024]{1,0:T(8,128)(2,1)S(1)}, u32[]{:S(2)}, u32[]{:S(2)}) collective-permute-start(bf16[256,1024]{1,0:T(8,128)(2,1)S(1)} %shard_map.83.rest_0_.mine.own_cols), channel_id=1, source_target_pairs={{0,4},{4,0},{1,5},{5,1},{2,6},{6,2},{3,7},{7,3},{8,12},{12,8},{9,1... | collective-permute-start | bytes 1572872 | tf_op jit(solution)/shard_map/ppermute | solution.py:168
  222.7 2.0 copy-start.10
  235.0 8.4 %copy-start.19 = (bf16[256,1024]{1,0:T(8,128)(2,1)S(1)}, bf16[256,1024]{1,0:T(8,128)(2,1)}, u32[]{:S(2)}) copy-start(bf16[256,1024]{1,0:T(8,128)(2,1)} %copy-done.18) | copy-start | bytes 1572868
  243.3 5.2 %copy-start.25 = (bf16[256,1024]{1,0:T(8,128)(2,1)S(1)}, bf16[256,1024]{1,0:T(8,128)(2,1)}, u32[]{:S(2)}) copy-start(bf16[256,1024]{1,0:T(8,128)(2,1)} %copy-done.24) | copy-start | bytes 1572868
  243.3 5.2 %copy-start.27 = (bf16[256,1024]{1,0:T(8,128)(2,1)S(1)}, bf16[256,1024]{1,0:T(8,128)(2,1)}, u32[]{:S(2)}) copy-start(bf16[256,1024]{1,0:T(8,128)(2,1)} %copy-done.26) | copy-start | bytes 1572868
  243.3 63.5 %collective-permute-start.20 = (bf16[256,1024]{1,0:T(8,128)(2,1)S(1)}, bf16[256,1024]{1,0:T(8,128)(2,1)S(1)}, u32[]{:S(2)}, u32[]{:S(2)}) collective-permute-start(bf16[256,1024]{1,0:T(8,128)(2,1)S(1)} %shard_map.87.rest_0_.mine.own_cols), channel_id=1, source_target_pairs={{0,4},{4,0},{1,5},{5,1},{2,6},{6,2},{3,7},{7,3},{8,12},{12,8},{9,1... | collective-permute-start | bytes 1572872 | tf_op jit(solution)/shard_map/ppermute | solution.py:168
  253.3 12.5 %copy-start.15 = (bf16[256,1024]{1,0:T(8,128)(2,1)S(1)}, bf16[256,1024]{1,0:T(8,128)(2,1)}, u32[]{:S(2)}) copy-start(bf16[256,1024]{1,0:T(8,128)(2,1)} %copy-done.14) | copy-start | bytes 1572868
  253.3 12.5 %copy-start.29 = (bf16[256,1024]{1,0:T(8,128)(2,1)S(1)}, bf16[256,1024]{1,0:T(8,128)(2,1)}, u32[]{:S(2)}) copy-start(bf16[256,1024]{1,0:T(8,128)(2,1)} %copy-done.28) | copy-start | bytes 1572868
  265.7 5.0 %copy-start.21 = (bf16[256,1024]{1,0:T(8,128)(2,1)S(1)}, bf16[256,1024]{1,0:T(8,128)(2,1)}, u32[]{:S(2)}) copy-start(bf16[256,1024]{1,0:T(8,128)(2,1)} %copy-done.20) | copy-start | bytes 1572868
  265.7 5.0 %copy-start.31 = (bf16[256,1024]{1,0:T(8,128)(2,1)S(1)}, bf16[256,1024]{1,0:T(8,128)(2,1)}, u32[]{:S(2)}) copy-start(bf16[256,1024]{1,0:T(8,128)(2,1)} %copy-done.30) | copy-start | bytes 1572868
  265.7 63.6 %collective-permute-start.21 = (bf16[256,1024]{1,0:T(8,128)(2,1)S(1)}, bf16[256,1024]{1,0:T(8,128)(2,1)S(1)}, u32[]{:S(2)}, u32[]{:S(2)}) collective-permute-start(bf16[256,1024]{1,0:T(8,128)(2,1)S(1)} %shard_map.90.rest_0_.mine.own_cols), channel_id=1, source_target_pairs={{0,4},{4,0},{1,5},{5,1},{2,6},{6,2},{3,7},{7,3},{8,12},{12,8},{9,1... | collective-permute-start | bytes 1572872 | tf_op jit(solution)/shard_map/ppermute | solution.py:168
  275.5 12.7 %copy-start.17 = (bf16[256,1024]{1,0:T(8,128)(2,1)S(1)}, bf16[256,1024]{1,0:T(8,128)(2,1)}, u32[]{:S(2)}) copy-start(bf16[256,1024]{1,0:T(8,128)(2,1)} %copy-done.16) | copy-start | bytes 1572868
  288.1 63.6 %collective-permute-start.24 = (bf16[256,1024]{1,0:T(8,128)(2,1)S(1)}, bf16[256,1024]{1,0:T(8,128)(2,1)S(1)}, u32[]{:S(2)}, u32[]{:S(2)}) collective-permute-start(bf16[256,1024]{1,0:T(8,128)(2,1)S(1)} %shard_map.93.rest_0_.mine.own_cols), channel_id=1, source_target_pairs={{0,4},{4,0},{1,5},{5,1},{2,6},{6,2},{3,7},{7,3},{8,12},{12,8},{9,1... | collective-permute-start | bytes 1572872 | tf_op jit(solution)/shard_map/ppermute | solution.py:168
  310.6 52.4 %collective-permute-start.23 = (bf16[256,1024]{1,0:T(8,128)(2,1)S(1)}, bf16[256,1024]{1,0:T(8,128)(2,1)S(1)}, u32[]{:S(2)}, u32[]{:S(2)}) collective-permute-start(bf16[256,1024]{1,0:T(8,128)(2,1)S(1)} %shard_map.96.rest_0_.mine.own_cols), channel_id=1, source_target_pairs={{0,4},{4,0},{1,5},{5,1},{2,6},{6,2},{3,7},{7,3},{8,12},{12,8},{9,1... | collective-permute-start | bytes 1572872 | tf_op jit(solution)/shard_map/ppermute | solution.py:168
  333.1 40.0 %collective-permute-start.22 = (bf16[256,1024]{1,0:T(8,128)(2,1)S(1)}, bf16[256,1024]{1,0:T(8,128)(2,1)S(1)}, u32[]{:S(2)}, u32[]{:S(2)}) collective-permute-start(bf16[256,1024]{1,0:T(8,128)(2,1)S(1)} %shard_map.99.rest_0_.mine.own_cols), channel_id=1, source_target_pairs={{0,4},{4,0},{1,5},{5,1},{2,6},{6,2},{3,7},{7,3},{8,12},{12,8},{9,1... | collective-permute-start | bytes 1572872 | tf_op jit(solution)/shard_map/ppermute | solution.py:168
  356.6 16.5 %copy-start.11 = (bf16[2,4,2,128,1024]{4,3,2,1,0:T(8,128)(2,1)S(1)}, bf16[2,4,2,128,1024]{4,3,2,1,0:T(8,128)(2,1)}, u32[]{:S(2)}) copy-start(bf16[2,4,2,128,1024]{4,3,2,1,0:T(8,128)(2,1)} %copy-done.10) | copy-start | bytes 12582916
  (4 other events, 3.4 us)

commit v4 on v3

--- a/solution.py
+++ b/solution.py
@@ -9,6 +9,7 @@
 COLS = 256
 DEPTH = 3
 VMEM = 48 * 1024 * 1024
+LAST_VMEM = 24 * 1024 * 1024
 PANEL_STEPS = [0, 0, 1, 0, 1, 1, 1, 1, 2, 2, 1]
 SWAP = [(0, 1), (1, 0)]
 NT = (((1,), (1,)), ((), ()))
@@ -84,6 +85,58 @@
     )(energies, mine, mine, theirs, panel, panel, a_energy, b_energy, *behind)
 
 
+def half_finish_kernel(mine, panel_own, panel_other, out, other_out):
+    out[...] = mine[...].astype(jnp.float32) + dot_nt(mine[...], panel_own[...])
+    other_out[...] = panel_other[...]
+
+
+def half_finish(mine, panel):
+    rows, virt = mine.shape
+    return pl.pallas_call(
+        half_finish_kernel,
+        out_shape=(jax.ShapeDtypeStruct((rows, virt), jnp.float32), jax.ShapeDtypeStruct((virt, virt), panel.dtype)),
+        grid_spec=pl.GridSpec(
+            grid=(1,),
+            in_specs=[
+                pl.BlockSpec((rows, virt), lambda i: (0, 0)),
+                pl.BlockSpec((None, virt, virt), lambda i: (0, 0, 0)),
+                pl.BlockSpec((None, virt, virt), lambda i: (1, 0, 0)),
+            ],
+            out_specs=(pl.BlockSpec((rows, virt), lambda i: (0, 0)), pl.BlockSpec((virt, virt), lambda i: (0, 0))),
+        ),
+        compiler_params=pltpu.CompilerParams(vmem_limit_bytes=LAST_VMEM),
+    )(mine, panel, panel)
+
+
+def last_finish_kernel(energies, part, theirs, panel_other, a_energy, b_energy, _, out):
+    total = part[...] + dot_nt(theirs[...], panel_other[...])
+    divisor = ((a_energy[...] + b_energy[...]) - energies[0]) - energies[1]
+    out[...] = (total / divisor).astype(out.dtype)
+
+
+def last_finish(out, pair, first_row, energies, part, theirs, panel_other, a_energy, b_energy):
+    rows, virt = theirs.shape
+    block = first_row // rows
+    whole = pl.BlockSpec(memory_space=pltpu.VMEM)
+    return pl.pallas_call(
+        last_finish_kernel,
+        out_shape=jax.ShapeDtypeStruct(out.shape, out.dtype),
+        grid=(1,),
+        in_specs=[
+            pl.BlockSpec(memory_space=pltpu.SMEM),
+            whole,
+            whole,
+            whole,
+            pl.BlockSpec((rows, 1), lambda i: (block, 0)),
+            whole,
+            pl.BlockSpec(memory_space=pltpu.HBM),
+        ],
+        out_specs=pl.BlockSpec((None, None, rows, virt), lambda i: (0, pair, block, 0)),
+        input_output_aliases={6: 0},
+        compiler_params=pltpu.CompilerParams(vmem_limit_bytes=LAST_VMEM),
+    )(energies, part, theirs, panel_other, a_energy, b_energy, out)
+
+
 def join_kernel(first, block, swapped, *rest):
     out = rest[-1]
     out[first[0]] = block[...]
@@ -153,7 +206,7 @@
     half, rest = lax.axis_index("half"), lax.axis_index("rest")
     n_rest, n_grp = lax.axis_size("rest"), lax.axis_size("grp")
     rows = min(ROWS, virt_count)
-    chunks = [(p, a) for p in range(per_dev) for a in range(0, virt_count, rows)]
+    chunks = [(p, a, rows) for p in range(per_dev) for a in range(0, virt_count, rows)]
 
     row = lax.dynamic_index_in_dim(row_energy, half, 0, keepdims=False)
     cols = lax.dynamic_slice_in_dim(col_energy, (rest * per_dev) % group_j, per_dev)
@@ -163,7 +216,7 @@
     own, other = [], []
 
     def send(n, events):
-        piece = dress(amplitudes, vv_fock, *chunks[n], rows, events)
+        piece = dress(amplitudes, vv_fock, *chunks[n], events)
         own.append(piece)
         other.append(lax.ppermute(piece, "half", SWAP))
 
@@ -203,7 +256,7 @@
     def end(n, events):
         whole = panel.reshape(2, virt_count, virt_count)
         return finish(
-            out, amplitudes.shape, *chunks[n], energies[chunks[n][0]], own[n], other[n], whole, a_energy, b_energy, events
+            out, amplitudes.shape, *chunks[n][:2], energies[chunks[n][0]], own[n], other[n], whole, a_energy, b_energy, events
         )
 
     for n in range(1, len(chunks)):
@@ -219,8 +272,11 @@
             finished += 1
     while others:
         next_panel_step(own[-1])
-    for n in range(finished, len(chunks)):
+    part, panel_other = half_finish(own[-1], panel.reshape(2, virt_count, virt_count))
+    for n in range(finished, len(chunks) - 1):
         out = end(n, [own[-1]])
+    p, a, _ = chunks[-1]
+    out = last_finish(out, p, a, energies[p], part, other[-1], panel_other, a_energy, b_energy)
     return out
 
 

time: 379 us -> 378 us (level)
    pallas_call x16 -> x15, Pallas kernels: 77.3 us -> 74.2 us  [finish(): pl.pallas_call(finish_kernel, out_shape=jax.ShapeDtypeStruct(shape, jnp.b...]
    unnamed x86 -> x90, local copies, waits for them, and re-layouts: 24.2 us -> 24.2 us
where the time goes in v4:
time: 378 us; the launch traced here: 375 us
  waiting for transfers between devices  172 us (46%)
  Pallas kernels  149 us (39%)
  local copies, waits for them, and re-layouts  26.7 us (7%)
  starting transfers between devices  21 us (6%)
  other arithmetic  5.78 us (2%)
    ppermute x16, waiting for transfers between devices, send(): other.append(lax.ppermute(piece, 'half', SWAP))  172 us
    pallas_call x15, Pallas kernels, finish(): pl.pallas_call(finish_kernel, out_shape=jax.ShapeDtypeStruct(shape, jnp.b...  74.2 us
    pallas_call x16, Pallas kernels, dress(): pl.pallas_call(dress_kernel, out_shape=jax.ShapeDtypeStruct((rows, virt),...  62.2 us
    unnamed x90, local copies, waits for them, and re-layouts  24.2 us
    pallas_call x8, Pallas kernels, place(): pl.pallas_call(place_kernel, out_shape=jax.ShapeDtypeStruct((2, lead, 2,...  8.81 us
    ppermute x7, starting transfers between devices, next_panel_step(): part = lax.ppermute(block, ('grp', 'rest'), pairs)  8.11 us
  transfers between devices with their start and end apart: 25, of which 16 were waited for; matrix products, arithmetic and copies ran while one was open for 2% of the time, Pallas kernels for 39%

profile of v4, /device:TPU:0, one launch (start us, length us, event | category | flops | bytes accessed | tf_op | source)
XLA Modules:
  0.0 375.2 jit_solution(10930127488914643131)
XLA Ops:
  1.0 4.1 %collective-permute-start = (bf16[128,512]{1,0:T(8,128)(2,1)S(1)}, bf16[128,512]{1,0:T(8,128)(2,1)S(1)}, u32[]{:S(2)}, u32[]{:S(2)}) collective-permute-start(bf16[128,512]{1,0:T(8,128)(2,1)S(1)} %get-tuple-element.9), channel_id=1, source_target_pairs={{0,4},{4,0},{1,5},{5,1},{2,6},{6,2},{3,7},{7,3},{8,12},{12,8},{9,1... | collective-permute-start | bytes 393224 | tf_op jit(solution)/shard_map/ppermute | solution.py:225
  6.7 3.8 %shard_map.64.rest_0_.mine.own_cols = bf16[256,1024]{1,0:T(8,128)(2,1)S(1)} custom-call(bf16[1024,1024]{1,0:T(8,128)(2,1)S(1)} %copy-done.12, bf16[1,4,1024,1024]{3,2,1,0:T(8,128)(2,1)} %t_rows.31, bf16[1,4,1024,1024]{3,2,1,0:T(8,128)(2,1)} %t_rows.31, bf16[1024,1024]{1,0:T(8,128)(2,1)S(1)} %copy-done.12), custom_call_target="tpu_custom_call" | custom-call | flops 1073741824 | bytes 5767168 | tf_op jit(solution)/shard_map/pallas_call | solution.py:32
  10.5 4.7 %shard_map.65.rest_0_.mine.own_cols = bf16[256,1024]{1,0:T(8,128)(2,1)} custom-call(bf16[1024,1024]{1,0:T(8,128)(2,1)S(1)} %copy-done.12, bf16[1,4,1024,1024]{3,2,1,0:T(8,128)(2,1)} %t_rows.31, bf16[1,4,1024,1024]{3,2,1,0:T(8,128)(2,1)} %t_rows.31, bf16[1024,1024]{1,0:T(8,128)(2,1)S(1)} %copy-done.12, bf16[256,1024]{1,0:T(8,128)(2,1)S(1)} %shard_map.64.rest_0_.mine.own_cols), custom_call_target="tpu_custom_call" | custom-call | flops 1073741824 | bytes 5767168 | tf_op jit(solution)/shard_map/pallas_call | solution.py:32
  15.2 2.9 collective-permute-start.2
  18.1 3.8 %shard_map.66.rest_0_.mine.own_cols = bf16[256,1024]{1,0:T(8,128)(2,1)S(1)} custom-call(bf16[1024,1024]{1,0:T(8,128)(2,1)S(1)} %copy-done.12, bf16[1,4,1024,1024]{3,2,1,0:T(8,128)(2,1)} %t_rows.31, bf16[1,4,1024,1024]{3,2,1,0:T(8,128)(2,1)} %t_rows.31, bf16[1024,1024]{1,0:T(8,128)(2,1)S(1)} %copy-done.12, bf16[256,1024]{1,0:T(8,128)(2,1)} %shard_map.65.rest_0_.mine.own_cols), custom_call_target="tpu_custom_call" | custom-call | flops 1073741824 | bytes 5767168 | tf_op jit(solution)/shard_map/pallas_call | solution.py:32
  23.1 2.0 collective-permute-start.3
  25.1 34.6 %collective-permute-done.1.rest_2_.theirs = bf16[256,1024]{1,0:T(8,128)(2,1)} collective-permute-done((bf16[256,1024]{1,0:T(8,128)(2,1)S(1)}, bf16[256,1024]{1,0:T(8,128)(2,1)}, u32[]{:S(2)}, u32[]{:S(2)}) %collective-permute-start.1) | collective-permute-done | bytes 524320 | tf_op jit(solution)/shard_map/ppermute | solution.py:221
  59.8 3.8 %shard_map.68.rest_0_.mine.own_cols = bf16[256,1024]{1,0:T(8,128)(2,1)S(1)} custom-call(bf16[1024,1024]{1,0:T(8,128)(2,1)S(1)} %copy-done.13, bf16[1,4,1024,1024]{3,2,1,0:T(8,128)(2,1)} %t_rows.31, bf16[1,4,1024,1024]{3,2,1,0:T(8,128)(2,1)} %t_rows.31, bf16[1024,1024]{1,0:T(8,128)(2,1)S(1)} %copy-done.13, ...), custom_call_target="tpu_custom_call" | custom-call | flops 1073741824 | bytes 5767168 | tf_op jit(solution)/shard_map/pallas_call | solution.py:32
  63.6 18.6 %collective-permute-done.2.rest_2_.theirs = bf16[256,1024]{1,0:T(8,128)(2,1)} collective-permute-done((bf16[256,1024]{1,0:T(8,128)(2,1)}, bf16[256,1024]{1,0:T(8,128)(2,1)}, u32[]{:S(2)}, u32[]{:S(2)}) %collective-permute-start.2) | collective-permute-done | bytes 524320 | tf_op jit(solution)/shard_map/ppermute | solution.py:221
  82.2 3.8 %shard_map.69.rest_0_.mine.own_cols = bf16[256,1024]{1,0:T(8,128)(2,1)S(1)} custom-call(bf16[1024,1024]{1,0:T(8,128)(2,1)S(1)} %copy-done.13, bf16[1,4,1024,1024]{3,2,1,0:T(8,128)(2,1)} %t_rows.31, bf16[1,4,1024,1024]{3,2,1,0:T(8,128)(2,1)} %t_rows.31, bf16[1024,1024]{1,0:T(8,128)(2,1)S(1)} %copy-done.13, ...), custom_call_target="tpu_custom_call" | custom-call | flops 1073741824 | bytes 5767168 | tf_op jit(solution)/shard_map/pallas_call | solution.py:32
  88.7 16.0 %collective-permute-done.4.rest_2_.theirs = bf16[256,1024]{1,0:T(8,128)(2,1)} collective-permute-done((bf16[256,1024]{1,0:T(8,128)(2,1)S(1)}, bf16[256,1024]{1,0:T(8,128)(2,1)}, u32[]{:S(2)}, u32[]{:S(2)}) %collective-permute-start.4) | collective-permute-done | bytes 524320 | tf_op jit(solution)/shard_map/ppermute | solution.py:221
  104.7 3.8 %shard_map.71.rest_0_.mine.own_cols = bf16[256,1024]{1,0:T(8,128)(2,1)S(1)} custom-call(bf16[1024,1024]{1,0:T(8,128)(2,1)S(1)} %copy-done.13, bf16[1,4,1024,1024]{3,2,1,0:T(8,128)(2,1)} %t_rows.31, bf16[1,4,1024,1024]{3,2,1,0:T(8,128)(2,1)} %t_rows.31, bf16[1024,1024]{1,0:T(8,128)(2,1)S(1)} %copy-done.13, ...), custom_call_target="tpu_custom_call" | custom-call | flops 1073741824 | bytes 5767168 | tf_op jit(solution)/shard_map/pallas_call | solution.py:32
  108.5 7.3 %collective-permute-done.5.rest_2_.theirs = bf16[256,1024]{1,0:T(8,128)(2,1)S(1)} collective-permute-done((bf16[256,1024]{1,0:T(8,128)(2,1)S(1)}, bf16[256,1024]{1,0:T(8,128)(2,1)S(1)}, u32[]{:S(2)}, u32[]{:S(2)}) %collective-permute-start.5) | collective-permute-done | bytes 524320 | tf_op jit(solution)/shard_map/ppermute | solution.py:221
  117.6 2.0 copy-done
  121.9 3.8 %shard_map.73.rest_0_.mine.own_cols = bf16[256,1024]{1,0:T(8,128)(2,1)S(1)} custom-call(bf16[1024,1024]{1,0:T(8,128)(2,1)S(1)} %copy-done.13, bf16[1,4,1024,1024]{3,2,1,0:T(8,128)(2,1)} %t_rows.31, bf16[1,4,1024,1024]{3,2,1,0:T(8,128)(2,1)} %t_rows.31, bf16[1024,1024]{1,0:T(8,128)(2,1)S(1)} %copy-done.13, ...), custom_call_target="tpu_custom_call" | custom-call | flops 1073741824 | bytes 5767168 | tf_op jit(solution)/shard_map/pallas_call | solution.py:32
  125.7 12.6 %collective-permute-done.7.rest_2_.theirs = bf16[256,1024]{1,0:T(8,128)(2,1)S(1)} collective-permute-done((bf16[256,1024]{1,0:T(8,128)(2,1)S(1)}, bf16[256,1024]{1,0:T(8,128)(2,1)S(1)}, u32[]{:S(2)}, u32[]{:S(2)}) %collective-permute-start.7) | collective-permute-done | bytes 524320 | tf_op jit(solution)/shard_map/ppermute | solution.py:221
  139.7 2.0 copy-done.2
  141.7 4.5 %shard_map.75.rest_0_.mine.own_cols = bf16[256,1024]{1,0:T(8,128)(2,1)} custom-call(bf16[1024,1024]{1,0:T(8,128)(2,1)S(1)} %copy-done.13, bf16[1,4,1024,1024]{3,2,1,0:T(8,128)(2,1)} %t_rows.31, bf16[1,4,1024,1024]{3,2,1,0:T(8,128)(2,1)} %t_rows.31, bf16[1024,1024]{1,0:T(8,128)(2,1)S(1)} %copy-done.13, bf16[256,1024]{1,0:T(8,128)(2,1)S(1)} %shard_map.73.rest_0_.mine.own_cols, ...), custom_call_target="tpu_custom_call" | custom-call | flops 1073741824 | bytes 5767168 | tf_op jit(solution)/shard_map/pallas_call | solution.py:32
  146.3 2.5 collective-permute-start.14
  148.8 12.0 %collective-permute-done.9.rest_2_.theirs = bf16[256,1024]{1,0:T(8,128)(2,1)S(1)} collective-permute-done((bf16[256,1024]{1,0:T(8,128)(2,1)S(1)}, bf16[256,1024]{1,0:T(8,128)(2,1)S(1)}, u32[]{:S(2)}, u32[]{:S(2)}) %collective-permute-start.9) | collective-permute-done | bytes 524320 | tf_op jit(solution)/shard_map/ppermute | solution.py:221
  162.2 2.2 copy-done.3
  165.0 2.0 copy-done.4
  167.8 2.6 collective-permute-start.16
  170.4 3.8 %shard_map.77.rest_0_.mine.own_cols = bf16[256,1024]{1,0:T(8,128)(2,1)S(1)} custom-call(bf16[1024,1024]{1,0:T(8,128)(2,1)S(1)} %copy-done.13, bf16[1,4,1024,1024]{3,2,1,0:T(8,128)(2,1)} %t_rows.31, bf16[1,4,1024,1024]{3,2,1,0:T(8,128)(2,1)} %t_rows.31, bf16[1024,1024]{1,0:T(8,128)(2,1)S(1)} %copy-done.13, bf16[256,1024]{1,0:T(8,128)(2,1)} %shard_map.75.rest_0_.mine.own_cols, ...), custom_call_target="tpu_custom_call" | custom-call | flops 1073741824 | bytes 5767168 | tf_op jit(solution)/shard_map/pallas_call | solution.py:32
  174.2 9.1 %collective-permute-done.12.rest_2_.theirs = bf16[256,1024]{1,0:T(8,128)(2,1)S(1)} collective-permute-done((bf16[256,1024]{1,0:T(8,128)(2,1)S(1)}, bf16[256,1024]{1,0:T(8,128)(2,1)S(1)}, u32[]{:S(2)}, u32[]{:S(2)}) %collective-permute-start.12) | collective-permute-done | bytes 524320 | tf_op jit(solution)/shard_map/ppermute | solution.py:221
  186.8 2.2 copy-done.5
  191.7 2.0 copy-done.6
  193.7 3.8 %shard_map.80.rest_0_.mine.own_cols = bf16[256,1024]{1,0:T(8,128)(2,1)S(1)} custom-call(bf16[1024,1024]{1,0:T(8,128)(2,1)S(1)} %copy-done.13, bf16[1,4,1024,1024]{3,2,1,0:T(8,128)(2,1)} %t_rows.31, bf16[1,4,1024,1024]{3,2,1,0:T(8,128)(2,1)} %t_rows.31, bf16[1024,1024]{1,0:T(8,128)(2,1)S(1)} %copy-done.13, ...), custom_call_target="tpu_custom_call" | custom-call | flops 1073741824 | bytes 5767168 | tf_op jit(solution)/shard_map/pallas_call | solution.py:32
  197.5 3.0 collective-permute-start.18
  200.5 2.2 copy-done.7
  204.3 1.6 shard_map.82.rest_1_
  205.9 2.0 copy-done.8
  208.0 9.1 %collective-permute-done.15.rest_2_.theirs = bf16[256,1024]{1,0:T(8,128)(2,1)} collective-permute-done((bf16[256,1024]{1,0:T(8,128)(2,1)}, bf16[256,1024]{1,0:T(8,128)(2,1)}, u32[]{:S(2)}, u32[]{:S(2)}) %collective-permute-start.15) | collective-permute-done | bytes 524320 | tf_op jit(solution)/shard_map/ppermute | solution.py:221
  217.1 3.9 %shard_map.83.rest_0_.mine.own_cols = bf16[256,1024]{1,0:T(8,128)(2,1)S(1)} custom-call(bf16[1024,1024]{1,0:T(8,128)(2,1)S(1)} %copy-done.13, bf16[1,4,1024,1024]{3,2,1,0:T(8,128)(2,1)} %t_rows.31, bf16[1,4,1024,1024]{3,2,1,0:T(8,128)(2,1)} %t_rows.31, bf16[1024,1024]{1,0:T(8,128)(2,1)S(1)} %copy-done.13, ...), custom_call_target="tpu_custom_call" | custom-call | flops 1073741824 | bytes 5767168 | tf_op jit(solution)/shard_map/pallas_call | solution.py:32
  222.7 2.0 copy-done.10
  224.7 5.0 %shard_map.85.rest_1_ = bf16[1,4,1024,1024]{3,2,1,0:T(8,128)(2,1)} custom-call(f32[2]{0:T(128)S(1)} %pad_maximum_fusion.1.energies, bf16[256,1024]{1,0:T(8,128)(2,1)S(1)} %copy-done.23, bf16[256,1024]{1,0:T(8,128)(2,1)S(1)} %copy-done.23, bf16[256,1024]{1,0:T(8,128)(2,1)} %collective-permute-done.1.rest_2_.theirs, bf16[2,1024,1024]{2,1,0:T(8,128)(2,1)} %bitcast.20, ...), custom_call_target="tpu_custom_call" | custom-call | flops 1073741824 | bytes 5767168 | tf_op jit(solution)/shard_map/pallas_call | solution.py:64
  229.7 5.3 %shard_map.86.rest_1_ = bf16[1,4,1024,1024]{3,2,1,0:T(8,128)(2,1)} custom-call(f32[2]{0:T(128)S(1)} %pad_maximum_fusion.1.energies, bf16[256,1024]{1,0:T(8,128)(2,1)} %shard_map.65.rest_0_.mine.own_cols, bf16[256,1024]{1,0:T(8,128)(2,1)} %shard_map.65.rest_0_.mine.own_cols, ...), custom_call_target="tpu_custom_call", output_to_operand_aliasing={{}: (9, {})} | custom-call | flops 1073741824 | bytes 5767168 | tf_op jit(solution)/shard_map/pallas_call | solution.py:64
  235.0 4.5 %collective-permute-done.17.rest_2_.theirs = bf16[256,1024]{1,0:T(8,128)(2,1)} collective-permute-done((bf16[256,1024]{1,0:T(8,128)(2,1)S(1)}, bf16[256,1024]{1,0:T(8,128)(2,1)}, u32[]{:S(2)}, u32[]{:S(2)}) %collective-permute-start.17) | collective-permute-done | bytes 524320 | tf_op jit(solution)/shard_map/ppermute | solution.py:221
  239.5 3.8 %shard_map.87.rest_0_.mine.own_cols = bf16[256,1024]{1,0:T(8,128)(2,1)S(1)} custom-call(bf16[1024,1024]{1,0:T(8,128)(2,1)S(1)} %copy-done.13, bf16[1,4,1024,1024]{3,2,1,0:T(8,128)(2,1)} %t_rows.31, bf16[1,4,1024,1024]{3,2,1,0:T(8,128)(2,1)} %t_rows.31, bf16[1024,1024]{1,0:T(8,128)(2,1)S(1)} %copy-done.13, ...), custom_call_target="tpu_custom_call" | custom-call | flops 1073741824 | bytes 5767168 | tf_op jit(solution)/shard_map/pallas_call | solution.py:32
  243.4 5.1 %shard_map.88.rest_1_ = bf16[1,4,1024,1024]{3,2,1,0:T(8,128)(2,1)} custom-call(f32[2]{0:T(128)S(1)} %pad_maximum_fusion.1.energies, bf16[256,1024]{1,0:T(8,128)(2,1)S(1)} %copy-done.19, bf16[256,1024]{1,0:T(8,128)(2,1)S(1)} %copy-done.19, bf16[256,1024]{1,0:T(8,128)(2,1)} %collective-permute-done.4.rest_2_.theirs, ...), custom_call_target="tpu_custom_call", output_to_operand_aliasing={{}: (9, {})} | custom-call | flops 1073741824 | bytes 5767168 | tf_op jit(solution)/shard_map/pallas_call | solution.py:64
  248.5 4.8 %shard_map.89.rest_1_ = bf16[1,4,1024,1024]{3,2,1,0:T(8,128)(2,1)} custom-call(f32[2]{0:T(128)S(1)} %pad_maximum_fusion.1.energies, bf16[256,1024]{1,0:T(8,128)(2,1)S(1)} %copy-done.25, bf16[256,1024]{1,0:T(8,128)(2,1)S(1)} %copy-done.25, bf16[256,1024]{1,0:T(8,128)(2,1)S(1)} %copy-done.29, ...), custom_call_target="tpu_custom_call", output_to_operand_aliasing={{}: (9, {})} | custom-call | flops 1073741824 | bytes 5767168 | tf_op jit(solution)/shard_map/pallas_call | solution.py:64
  253.3 8.6 %collective-permute-done.18.rest_2_.theirs = bf16[256,1024]{1,0:T(8,128)(2,1)S(1)} collective-permute-done((bf16[256,1024]{1,0:T(8,128)(2,1)S(1)}, bf16[256,1024]{1,0:T(8,128)(2,1)S(1)}, u32[]{:S(2)}, u32[]{:S(2)}) %collective-permute-start.18) | collective-permute-done | bytes 524320 | tf_op jit(solution)/shard_map/ppermute | solution.py:221
  261.9 3.8 %shard_map.90.rest_0_.mine.own_cols = bf16[256,1024]{1,0:T(8,128)(2,1)S(1)} custom-call(bf16[1024,1024]{1,0:T(8,128)(2,1)S(1)} %copy-done.13, bf16[1,4,1024,1024]{3,2,1,0:T(8,128)(2,1)} %t_rows.31, bf16[1,4,1024,1024]{3,2,1,0:T(8,128)(2,1)} %t_rows.31, bf16[1024,1024]{1,0:T(8,128)(2,1)S(1)} %copy-done.13, ...), custom_call_target="tpu_custom_call" | custom-call | flops 1073741824 | bytes 5767168 | tf_op jit(solution)/shard_map/pallas_call | solution.py:32
  265.8 4.9 %shard_map.91.rest_1_ = bf16[1,4,1024,1024]{3,2,1,0:T(8,128)(2,1)} custom-call(f32[2]{0:T(128)S(1)} %pad_maximum_fusion.2.energies, bf16[256,1024]{1,0:T(8,128)(2,1)S(1)} %copy-done.15, bf16[256,1024]{1,0:T(8,128)(2,1)S(1)} %copy-done.15, bf16[256,1024]{1,0:T(8,128)(2,1)S(1)} %copy-done.31, ...), custom_call_target="tpu_custom_call", output_to_operand_aliasing={{}: (9, {})} | custom-call | flops 1073741824 | bytes 5767168 | tf_op jit(solution)/shard_map/pallas_call | solution.py:64
  270.7 4.8 %shard_map.92.rest_1_ = bf16[1,4,1024,1024]{3,2,1,0:T(8,128)(2,1)} custom-call(f32[2]{0:T(128)S(1)} %pad_maximum_fusion.2.energies, bf16[256,1024]{1,0:T(8,128)(2,1)S(1)} %copy-done.21, bf16[256,1024]{1,0:T(8,128)(2,1)S(1)} %copy-done.21, bf16[256,1024]{1,0:T(8,128)(2,1)S(1)} %copy-done.33, ...), custom_call_target="tpu_custom_call", output_to_operand_aliasing={{}: (9, {})} | custom-call | flops 1073741824 | bytes 5767168 | tf_op jit(solution)/shard_map/pallas_call | solution.py:64
  275.5 8.8 %collective-permute-done.19.rest_2_.theirs = bf16[256,1024]{1,0:T(8,128)(2,1)S(1)} collective-permute-done((bf16[256,1024]{1,0:T(8,128)(2,1)S(1)}, bf16[256,1024]{1,0:T(8,128)(2,1)S(1)}, u32[]{:S(2)}, u32[]{:S(2)}) %collective-permute-start.19) | collective-permute-done | bytes 524320 | tf_op jit(solution)/shard_map/ppermute | solution.py:221
  284.4 3.8 %shard_map.93.rest_0_.mine.own_cols = bf16[256,1024]{1,0:T(8,128)(2,1)S(1)} custom-call(bf16[1024,1024]{1,0:T(8,128)(2,1)S(1)} %copy-done.13, bf16[1,4,1024,1024]{3,2,1,0:T(8,128)(2,1)} %t_rows.31, bf16[1,4,1024,1024]{3,2,1,0:T(8,128)(2,1)} %t_rows.31, bf16[1024,1024]{1,0:T(8,128)(2,1)S(1)} %copy-done.13, ...), custom_call_target="tpu_custom_call" | custom-call | flops 1073741824 | bytes 5767168 | tf_op jit(solution)/shard_map/pallas_call | solution.py:32
  288.2 4.8 %shard_map.94.rest_1_ = bf16[1,4,1024,1024]{3,2,1,0:T(8,128)(2,1)} custom-call(f32[2]{0:T(128)S(1)} %pad_maximum_fusion.2.energies, bf16[256,1024]{1,0:T(8,128)(2,1)S(1)} %copy-done.17, bf16[256,1024]{1,0:T(8,128)(2,1)S(1)} %copy-done.17, bf16[256,1024]{1,0:T(8,128)(2,1)S(1)} %copy-done.35, ...), custom_call_target="tpu_custom_call", output_to_operand_aliasing={{}: (9, {})} | custom-call | flops 1073741824 | bytes 5767168 | tf_op jit(solution)/shard_map/pallas_call | solution.py:64
  293.0 5.3 %shard_map.95.rest_1_ = bf16[1,4,1024,1024]{3,2,1,0:T(8,128)(2,1)} custom-call(f32[2]{0:T(128)S(1)} %pad_maximum_fusion.2.energies, bf16[256,1024]{1,0:T(8,128)(2,1)} %shard_map.75.rest_0_.mine.own_cols, bf16[256,1024]{1,0:T(8,128)(2,1)} %shard_map.75.rest_0_.mine.own_cols, ...), custom_call_target="tpu_custom_call", output_to_operand_aliasing={{}: (9, {})} | custom-call | flops 1073741824 | bytes 5767168 | tf_op jit(solution)/shard_map/pallas_call | solution.py:64
  298.4 8.5 %collective-permute-done.20.rest_2_.theirs = bf16[256,1024]{1,0:T(8,128)(2,1)S(1)} collective-permute-done((bf16[256,1024]{1,0:T(8,128)(2,1)S(1)}, bf16[256,1024]{1,0:T(8,128)(2,1)S(1)}, u32[]{:S(2)}, u32[]{:S(2)}) %collective-permute-start.20) | collective-permute-done | bytes 524320 | tf_op jit(solution)/shard_map/ppermute | solution.py:221
  306.8 3.8 %shard_map.96.rest_0_.mine.own_cols = bf16[256,1024]{1,0:T(8,128)(2,1)S(1)} custom-call(bf16[1024,1024]{1,0:T(8,128)(2,1)S(1)} %copy-done.13, bf16[1,4,1024,1024]{3,2,1,0:T(8,128)(2,1)} %t_rows.31, bf16[1,4,1024,1024]{3,2,1,0:T(8,128)(2,1)} %t_rows.31, bf16[1024,1024]{1,0:T(8,128)(2,1)S(1)} %copy-done.13, ...), custom_call_target="tpu_custom_call" | custom-call | flops 1073741824 | bytes 5767168 | tf_op jit(solution)/shard_map/pallas_call | solution.py:32
  310.7 5.2 %shard_map.97.rest_1_ = bf16[1,4,1024,1024]{3,2,1,0:T(8,128)(2,1)} custom-call(f32[2]{0:T(128)S(1)} %pad_maximum_fusion.3.energies, bf16[256,1024]{1,0:T(8,128)(2,1)S(1)} %shard_map.77.rest_0_.mine.own_cols, bf16[256,1024]{1,0:T(8,128)(2,1)S(1)} %shard_map.77.rest_0_.mine.own_cols, ...), custom_call_target="tpu_custom_call", output_to_operand_aliasing={{}: (9, {})} | custom-call | flops 1073741824 | bytes 5767168 | tf_op jit(solution)/shard_map/pallas_call | solution.py:64
  315.9 4.8 %shard_map.98.rest_1_ = bf16[1,4,1024,1024]{3,2,1,0:T(8,128)(2,1)} custom-call(f32[2]{0:T(128)S(1)} %pad_maximum_fusion.3.energies, bf16[256,1024]{1,0:T(8,128)(2,1)S(1)} %shard_map.80.rest_0_.mine.own_cols, bf16[256,1024]{1,0:T(8,128)(2,1)S(1)} %shard_map.80.rest_0_.mine.own_cols, ...), custom_call_target="tpu_custom_call", output_to_operand_aliasing={{}: (9, {})} | custom-call | flops 1073741824 | bytes 5767168 | tf_op jit(solution)/shard_map/pallas_call | solution.py:64
  320.7 8.7 %collective-permute-done.21.rest_2_.theirs = bf16[256,1024]{1,0:T(8,128)(2,1)S(1)} collective-permute-done((bf16[256,1024]{1,0:T(8,128)(2,1)S(1)}, bf16[256,1024]{1,0:T(8,128)(2,1)S(1)}, u32[]{:S(2)}, u32[]{:S(2)}) %collective-permute-start.21) | collective-permute-done | bytes 524320 | tf_op jit(solution)/shard_map/ppermute | solution.py:221
  329.3 3.9 %shard_map.99.mine.rest_0_ = bf16[256,1024]{1,0:T(8,128)(2,1)S(1)} custom-call(bf16[1024,1024]{1,0:T(8,128)(2,1)S(1)} %copy-done.13, bf16[1,4,1024,1024]{3,2,1,0:T(8,128)(2,1)} %t_rows.31, bf16[1,4,1024,1024]{3,2,1,0:T(8,128)(2,1)} %t_rows.31, bf16[1024,1024]{1,0:T(8,128)(2,1)S(1)} %copy-done.13, bf16[256,1024]{1,0:T(8,128)(2,1)S(1)} %shard_map.96.rest_0_.mine.own_cols, ...), custom_call_target="tpu_custom_call" | custom-call | flops 1073741824 | bytes 5767168 | tf_op jit(solution)/shard_map/pallas_call | solution.py:32
  335.5 4.8 %shard_map.101.rest_1_ = bf16[1,4,1024,1024]{3,2,1,0:T(8,128)(2,1)} custom-call(f32[2]{0:T(128)S(1)} %pad_maximum_fusion.3.energies, bf16[256,1024]{1,0:T(8,128)(2,1)S(1)} %shard_map.83.rest_0_.mine.own_cols, bf16[256,1024]{1,0:T(8,128)(2,1)S(1)} %shard_map.83.rest_0_.mine.own_cols, ...), custom_call_target="tpu_custom_call", output_to_operand_aliasing={{}: (9, {})} | custom-call | flops 1073741824 | bytes 5767168 | tf_op jit(solution)/shard_map/pallas_call | solution.py:64
  340.4 4.9 %shard_map.102.rest_1_ = bf16[1,4,1024,1024]{3,2,1,0:T(8,128)(2,1)} custom-call(f32[2]{0:T(128)S(1)} %pad_maximum_fusion.3.energies, bf16[256,1024]{1,0:T(8,128)(2,1)S(1)} %shard_map.87.rest_0_.mine.own_cols, bf16[256,1024]{1,0:T(8,128)(2,1)S(1)} %shard_map.87.rest_0_.mine.own_cols, ...), custom_call_target="tpu_custom_call", output_to_operand_aliasing={{}: (9, {})} | custom-call | flops 1073741824 | bytes 5767168 | tf_op jit(solution)/shard_map/pallas_call | solution.py:64
  345.2 4.8 %shard_map.103.rest_1_ = bf16[1,4,1024,1024]{3,2,1,0:T(8,128)(2,1)} custom-call(f32[2]{0:T(128)S(1)} %pad_maximum_fusion.energies, bf16[256,1024]{1,0:T(8,128)(2,1)S(1)} %shard_map.90.rest_0_.mine.own_cols, bf16[256,1024]{1,0:T(8,128)(2,1)S(1)} %shard_map.90.rest_0_.mine.own_cols, bf16[256,1024]{1,0:T(8,128)(2,1)S(1)} %copy-done.27, ...), custom_call_target="tpu_custom_call", output_to_operand_aliasing={{}: (9, {})} | custom-call | flops 1073741824 | bytes 5767168 | tf_op jit(solution)/shard_map/pallas_call | solution.py:64
  350.0 1.8 collective-permute-done.24.theirs
  351.8 4.8 %shard_map.104.rest_1_ = bf16[1,4,1024,1024]{3,2,1,0:T(8,128)(2,1)} custom-call(f32[2]{0:T(128)S(1)} %pad_maximum_fusion.energies, bf16[256,1024]{1,0:T(8,128)(2,1)S(1)} %shard_map.93.rest_0_.mine.own_cols, bf16[256,1024]{1,0:T(8,128)(2,1)S(1)} %shard_map.93.rest_0_.mine.own_cols, ...), custom_call_target="tpu_custom_call", output_to_operand_aliasing={{}: (9, {})} | custom-call | flops 1073741824 | bytes 5767168 | tf_op jit(solution)/shard_map/pallas_call | solution.py:64
  356.6 6.6 %collective-permute-done.23.theirs = bf16[256,1024]{1,0:T(8,128)(2,1)} collective-permute-done((bf16[256,1024]{1,0:T(8,128)(2,1)S(1)}, bf16[256,1024]{1,0:T(8,128)(2,1)}, u32[]{:S(2)}, u32[]{:S(2)}) %collective-permute-start.23) | collective-permute-done | bytes 524320 | tf_op jit(solution)/shard_map/ppermute | solution.py:221
  363.1 5.0 %shard_map.105._ = bf16[1,4,1024,1024]{3,2,1,0:T(8,128)(2,1)} custom-call(f32[2]{0:T(128)S(1)} %pad_maximum_fusion.energies, bf16[256,1024]{1,0:T(8,128)(2,1)S(1)} %shard_map.96.rest_0_.mine.own_cols, bf16[256,1024]{1,0:T(8,128)(2,1)S(1)} %shard_map.96.rest_0_.mine.own_cols, ...), custom_call_target="tpu_custom_call", output_to_operand_aliasing={{}: (9, {})} | custom-call | flops 1073741824 | bytes 5767168 | tf_op jit(solution)/shard_map/pallas_call | solution.py:64
  368.1 5.0 %collective-permute-done.22.theirs = bf16[256,1024]{1,0:T(8,128)(2,1)S(1)} collective-permute-done((bf16[256,1024]{1,0:T(8,128)(2,1)S(1)}, bf16[256,1024]{1,0:T(8,128)(2,1)S(1)}, u32[]{:S(2)}, u32[]{:S(2)}) %collective-permute-start.22) | collective-permute-done | bytes 524320 | tf_op jit(solution)/shard_map/ppermute | solution.py:221
  373.1 2.1 shard_map.106
  (136 shorter events, 27.0 us)
Async XLA Ops:
  1.0 22.1 %collective-permute-start = (bf16[128,512]{1,0:T(8,128)(2,1)S(1)}, bf16[128,512]{1,0:T(8,128)(2,1)S(1)}, u32[]{:S(2)}, u32[]{:S(2)}) collective-permute-start(bf16[128,512]{1,0:T(8,128)(2,1)S(1)} %get-tuple-element.9), channel_id=1, source_target_pairs={{0,4},{4,0},{1,5},{5,1},{2,6},{6,2},{3,7},{7,3},{8,12},{12,8},{9,1... | collective-permute-start | bytes 393224 | tf_op jit(solution)/shard_map/ppermute | solution.py:225
  10.4 4.8 %copy-start.22 = (bf16[256,1024]{1,0:T(8,128)(2,1)}, bf16[256,1024]{1,0:T(8,128)(2,1)S(1)}, u32[]{:S(2)}) copy-start(bf16[256,1024]{1,0:T(8,128)(2,1)S(1)} %shard_map.64.rest_0_.mine.own_cols) | copy-start | bytes 1572868
  10.5 49.3 %collective-permute-start.1 = (bf16[256,1024]{1,0:T(8,128)(2,1)S(1)}, bf16[256,1024]{1,0:T(8,128)(2,1)}, u32[]{:S(2)}, u32[]{:S(2)}) collective-permute-start(bf16[256,1024]{1,0:T(8,128)(2,1)S(1)} %shard_map.64.rest_0_.mine.own_cols), channel_id=1, source_target_pairs={{0,4},{4,0},{1,5},{5,1},{2,6},{6,2},{3,7},{7,3},{8,12},{12,8},{9,1... | collective-permute-start | bytes 1572872 | tf_op jit(solution)/shard_map/ppermute | solution.py:221
  15.2 7.1 %copy-start.43 = (f32[2]{0:T(128)S(1)}, f32[2]{0:T(128)}, u32[]{:S(2)}) copy-start(f32[2]{0:T(128)} %param.9) | copy-start | bytes 28
  15.2 7.7 %copy-start.44 = (f32[16]{0:T(128)S(1)}, f32[16]{0:T(128)}, u32[]{:S(2)}) copy-start(f32[16]{0:T(128)} %param.10) | copy-start | bytes 196
  15.2 44.6 %copy-start.13 = (bf16[1024,1024]{1,0:T(8,128)(2,1)S(1)}, bf16[1024,1024]{1,0:T(8,128)(2,1)}, u32[]{:S(2)}) copy-start(bf16[1024,1024]{1,0:T(8,128)(2,1)} %f_cols.31) | copy-start | bytes 6291460
  15.2 67.0 %collective-permute-start.2 = (bf16[256,1024]{1,0:T(8,128)(2,1)}, bf16[256,1024]{1,0:T(8,128)(2,1)}, u32[]{:S(2)}, u32[]{:S(2)}) collective-permute-start(bf16[256,1024]{1,0:T(8,128)(2,1)} %shard_map.65.rest_0_.mine.own_cols), channel_id=1, source_target_pairs={{0,4},{4,0},{1,5},{5,1},{2,6},{6,2},{3,7},{7,3},{8,12},{12,8},{9,1... | collective-permute-start | bytes 1572872 | tf_op jit(solution)/shard_map/ppermute | solution.py:221
  21.9 41.7 %copy-start.18 = (bf16[256,1024]{1,0:T(8,128)(2,1)}, bf16[256,1024]{1,0:T(8,128)(2,1)S(1)}, u32[]{:S(2)}) copy-start(bf16[256,1024]{1,0:T(8,128)(2,1)S(1)} %shard_map.66.rest_0_.mine.own_cols) | copy-start | bytes 1572868
  21.9 82.9 %collective-permute-start.4 = (bf16[256,1024]{1,0:T(8,128)(2,1)S(1)}, bf16[256,1024]{1,0:T(8,128)(2,1)}, u32[]{:S(2)}, u32[]{:S(2)}) collective-permute-start(bf16[256,1024]{1,0:T(8,128)(2,1)S(1)} %shard_map.66.rest_0_.mine.own_cols), channel_id=1, source_target_pairs={{0,4},{4,0},{1,5},{5,1},{2,6},{6,2},{3,7},{7,3},{8,12},{12,8},{9,1... | collective-permute-start | bytes 1572872 | tf_op jit(solution)/shard_map/ppermute | solution.py:221
  23.1 62.9 %collective-permute-start.3 = (bf16[2,128,512]{2,1,0:T(8,128)(2,1)S(1)}, bf16[2,128,512]{2,1,0:T(8,128)(2,1)S(1)}, u32[]{:S(2)}, u32[]{:S(2)}) collective-permute-start(bf16[2,128,512]{2,1,0:T(8,128)(2,1)S(1)} %bitcast.52), channel_id=1, source_target_pairs={{0,2},{1,3},{2,0},{3,1},{4,6},{5,7},{6,4},{7,5},{8,10},{9,11},{10,... | collective-permute-start | bytes 786440 | tf_op jit(solution)/shard_map/ppermute | solution.py:233
  63.6 22.5 %copy-start.24 = (bf16[256,1024]{1,0:T(8,128)(2,1)}, bf16[256,1024]{1,0:T(8,128)(2,1)S(1)}, u32[]{:S(2)}) copy-start(bf16[256,1024]{1,0:T(8,128)(2,1)S(1)} %shard_map.68.rest_0_.mine.own_cols) | copy-start | bytes 1572868
  63.6 52.3 %collective-permute-start.5 = (bf16[256,1024]{1,0:T(8,128)(2,1)S(1)}, bf16[256,1024]{1,0:T(8,128)(2,1)S(1)}, u32[]{:S(2)}, u32[]{:S(2)}) collective-permute-start(bf16[256,1024]{1,0:T(8,128)(2,1)S(1)} %shard_map.68.rest_0_.mine.own_cols), channel_id=1, source_target_pairs={{0,4},{4,0},{1,5},{5,1},{2,6},{6,2},{3,7},{7,3},{8,12},{12,8},{9,1... | collective-permute-start | bytes 1572872 | tf_op jit(solution)/shard_map/ppermute | solution.py:221
  86.0 22.5 %copy-start.14 = (bf16[256,1024]{1,0:T(8,128)(2,1)}, bf16[256,1024]{1,0:T(8,128)(2,1)S(1)}, u32[]{:S(2)}) copy-start(bf16[256,1024]{1,0:T(8,128)(2,1)S(1)} %shard_map.69.rest_0_.mine.own_cols) | copy-start | bytes 1572868
  87.0 32.6 %collective-permute-start.6 = (bf16[4,128,512]{2,1,0:T(8,128)(2,1)}, bf16[4,128,512]{2,1,0:T(8,128)(2,1)S(1)}, u32[]{:S(2)}, u32[]{:S(2)}) collective-permute-start(bf16[4,128,512]{2,1,0:T(8,128)(2,1)} %bitcast.5.rest_1_.block), channel_id=1, source_target_pairs={{0,1},{1,0},{2,3},{3,2},{8,9},{9,8},{10,11},{11,10},{16,17},{17,16... | collective-permute-start | bytes 1572872 | tf_op jit(solution)/shard_map/ppermute | solution.py:249
  88.5 49.8 %collective-permute-start.7 = (bf16[256,1024]{1,0:T(8,128)(2,1)S(1)}, bf16[256,1024]{1,0:T(8,128)(2,1)S(1)}, u32[]{:S(2)}, u32[]{:S(2)}) collective-permute-start(bf16[256,1024]{1,0:T(8,128)(2,1)S(1)} %shard_map.69.rest_0_.mine.own_cols), channel_id=1, source_target_pairs={{0,4},{4,0},{1,5},{5,1},{2,6},{6,2},{3,7},{7,3},{8,12},{12,8},{9,1... | collective-permute-start | bytes 1572872 | tf_op jit(solution)/shard_map/ppermute | solution.py:221
  88.7 57.5 %collective-permute-start.8 = (bf16[4,128,512]{2,1,0:T(8,128)(2,1)}, bf16[4,128,512]{2,1,0:T(8,128)(2,1)S(1)}, u32[]{:S(2)}, u32[]{:S(2)}) collective-permute-start(bf16[4,128,512]{2,1,0:T(8,128)(2,1)} %bitcast.5.rest_1_.block), channel_id=1, source_target_pairs={{0,8},{1,9},{2,10},{3,11},{8,0},{9,1},{10,2},{11,3},{16,24},{17,25... | collective-permute-start | bytes 1572872 | tf_op jit(solution)/shard_map/ppermute | solution.py:249
  104.7 56.1 %collective-permute-start.11 = (bf16[4,128,512]{2,1,0:T(8,128)(2,1)}, bf16[4,128,512]{2,1,0:T(8,128)(2,1)S(1)}, u32[]{:S(2)}, u32[]{:S(2)}) collective-permute-start(bf16[4,128,512]{2,1,0:T(8,128)(2,1)} %bitcast.5.rest_1_.block), channel_id=1, source_target_pairs={{0,9},{1,8},{2,11},{3,10},{8,1},{9,0},{10,3},{11,2},{16,25},{17,24... | collective-permute-start | bytes 1572872 | tf_op jit(solution)/shard_map/ppermute | solution.py:249
  108.5 17.2 %copy-start.20 = (bf16[256,1024]{1,0:T(8,128)(2,1)}, bf16[256,1024]{1,0:T(8,128)(2,1)S(1)}, u32[]{:S(2)}) copy-start(bf16[256,1024]{1,0:T(8,128)(2,1)S(1)} %shard_map.71.rest_0_.mine.own_cols) | copy-start | bytes 1572868
  115.8 9.9 %copy-start.28 = (bf16[256,1024]{1,0:T(8,128)(2,1)}, bf16[256,1024]{1,0:T(8,128)(2,1)S(1)}, u32[]{:S(2)}) copy-start(bf16[256,1024]{1,0:T(8,128)(2,1)S(1)} %collective-permute-done.5.rest_2_.theirs) | copy-start | bytes 1572868
  115.8 44.9 %collective-permute-start.9 = (bf16[256,1024]{1,0:T(8,128)(2,1)S(1)}, bf16[256,1024]{1,0:T(8,128)(2,1)S(1)}, u32[]{:S(2)}, u32[]{:S(2)}) collective-permute-start(bf16[256,1024]{1,0:T(8,128)(2,1)S(1)} %shard_map.71.rest_0_.mine.own_cols), channel_id=1, source_target_pairs={{0,4},{4,0},{1,5},{5,1},{2,6},{6,2},{3,7},{7,3},{8,12},{12,8},{9,1... | collective-permute-start | bytes 1572872 | tf_op jit(solution)/shard_map/ppermute | solution.py:221
  117.6 2.0 copy-start
  120.4 18.7 %copy-start.1 = (bf16[2,4,2,128,1024]{4,3,2,1,0:T(8,128)(2,1)S(1)}, bf16[2,4,2,128,1024]{4,3,2,1,0:T(8,128)(2,1)}, u32[]{:S(2)}) copy-start(bf16[2,4,2,128,1024]{4,3,2,1,0:T(8,128)(2,1)} %copy-done) | copy-start | bytes 12582916
  120.4 46.6 %collective-permute-start.10 = (bf16[4,128,512]{2,1,0:T(8,128)(2,1)}, bf16[4,128,512]{2,1,0:T(8,128)(2,1)S(1)}, u32[]{:S(2)}, u32[]{:S(2)}) collective-permute-start(bf16[4,128,512]{2,1,0:T(8,128)(2,1)} %bitcast.5.rest_1_.block), channel_id=1, source_target_pairs={{0,16},{1,17},{2,18},{3,19},{8,24},{9,25},{10,26},{11,27},{16,0},{... | collective-permute-start | bytes 1572872 | tf_op jit(solution)/shard_map/ppermute | solution.py:249
  121.9 17.2 %copy-start.42 = (bf16[4,128,512]{2,1,0:T(8,128)(2,1)S(1)}, bf16[4,128,512]{2,1,0:T(8,128)(2,1)}, u32[]{:S(2)}) copy-start(bf16[4,128,512]{2,1,0:T(8,128)(2,1)} %copy-done.41) | copy-start | bytes 1572868
  125.7 20.5 %copy-start.16 = (bf16[256,1024]{1,0:T(8,128)(2,1)}, bf16[256,1024]{1,0:T(8,128)(2,1)S(1)}, u32[]{:S(2)}) copy-start(bf16[256,1024]{1,0:T(8,128)(2,1)S(1)} %shard_map.73.rest_0_.mine.own_cols) | copy-start | bytes 1572868
  138.3 7.9 %copy-start.30 = (bf16[256,1024]{1,0:T(8,128)(2,1)}, bf16[256,1024]{1,0:T(8,128)(2,1)S(1)}, u32[]{:S(2)}) copy-start(bf16[256,1024]{1,0:T(8,128)(2,1)S(1)} %collective-permute-done.7.rest_2_.theirs) | copy-start | bytes 1572868
  138.3 44.9 %collective-permute-start.12 = (bf16[256,1024]{1,0:T(8,128)(2,1)S(1)}, bf16[256,1024]{1,0:T(8,128)(2,1)S(1)}, u32[]{:S(2)}, u32[]{:S(2)}) collective-permute-start(bf16[256,1024]{1,0:T(8,128)(2,1)S(1)} %shard_map.73.rest_0_.mine.own_cols), channel_id=1, source_target_pairs={{0,4},{4,0},{1,5},{5,1},{2,6},{6,2},{3,7},{7,3},{8,12},{12,8},{9,1... | collective-permute-start | bytes 1572872 | tf_op jit(solution)/shard_map/ppermute | solution.py:221
  139.7 2.0 copy-start.2
  146.3 51.2 %collective-permute-start.14 = (bf16[4,128,512]{2,1,0:T(8,128)(2,1)}, bf16[4,128,512]{2,1,0:T(8,128)(2,1)}, u32[]{:S(2)}, u32[]{:S(2)}) collective-permute-start(bf16[4,128,512]{2,1,0:T(8,128)(2,1)} %bitcast.5.rest_1_.block), channel_id=1, source_target_pairs={{0,17},{1,16},{2,19},{3,18},{8,25},{9,24},{10,27},{11,26},{16,1},{... | collective-permute-start | bytes 1572872 | tf_op jit(solution)/shard_map/ppermute | solution.py:249
  160.8 13.4 %copy-start.32 = (bf16[256,1024]{1,0:T(8,128)(2,1)}, bf16[256,1024]{1,0:T(8,128)(2,1)S(1)}, u32[]{:S(2)}) copy-start(bf16[256,1024]{1,0:T(8,128)(2,1)S(1)} %collective-permute-done.9.rest_2_.theirs) | copy-start | bytes 1572868
  160.8 43.5 %collective-permute-start.13 = (bf16[4,128,512]{2,1,0:T(8,128)(2,1)}, bf16[4,128,512]{2,1,0:T(8,128)(2,1)}, u32[]{:S(2)}, u32[]{:S(2)}) collective-permute-start(bf16[4,128,512]{2,1,0:T(8,128)(2,1)} %bitcast.5.rest_1_.block), channel_id=1, source_target_pairs={{0,24},{1,25},{2,26},{3,27},{8,16},{9,17},{10,18},{11,19},{16,8},{... | collective-permute-start | bytes 1572872 | tf_op jit(solution)/shard_map/ppermute | solution.py:249
  160.8 13.4 %copy-start.37 = (bf16[4,128,512]{2,1,0:T(8,128)(2,1)}, bf16[4,128,512]{2,1,0:T(8,128)(2,1)S(1)}, u32[]{:S(2)}) copy-start(bf16[4,128,512]{2,1,0:T(8,128)(2,1)S(1)} %collective-permute-done.11.block) | copy-start | bytes 1572868
  160.8 56.3 %collective-permute-start.15 = (bf16[256,1024]{1,0:T(8,128)(2,1)}, bf16[256,1024]{1,0:T(8,128)(2,1)}, u32[]{:S(2)}, u32[]{:S(2)}) collective-permute-start(bf16[256,1024]{1,0:T(8,128)(2,1)} %shard_map.75.rest_0_.mine.own_cols), channel_id=1, source_target_pairs={{0,4},{4,0},{1,5},{5,1},{2,6},{6,2},{3,7},{7,3},{8,12},{12,8},{9,1... | collective-permute-start | bytes 1572872 | tf_op jit(solution)/shard_map/ppermute | solution.py:221
  162.2 2.2 copy-start.3
  165.0 2.0 copy-start.4
  167.0 18.3 %copy-start.36 = (f32[1024]{0:T(1024)S(1)}, f32[1024]{0:T(1024)}, u32[]{:S(2)}) copy-start(f32[1024]{0:T(1024)} %param.11) | copy-start | bytes 12292
  167.8 53.3 %collective-permute-start.16 = (bf16[4,128,512]{2,1,0:T(8,128)(2,1)}, bf16[4,128,512]{2,1,0:T(8,128)(2,1)}, u32[]{:S(2)}, u32[]{:S(2)}) collective-permute-start(bf16[4,128,512]{2,1,0:T(8,128)(2,1)} %bitcast.5.rest_1_.block), channel_id=1, source_target_pairs={{0,25},{1,24},{2,27},{3,26},{8,17},{9,16},{10,19},{11,18},{16,9},{... | collective-permute-start | bytes 1572872 | tf_op jit(solution)/shard_map/ppermute | solution.py:249
  184.1 55.5 %collective-permute-start.17 = (bf16[256,1024]{1,0:T(8,128)(2,1)S(1)}, bf16[256,1024]{1,0:T(8,128)(2,1)}, u32[]{:S(2)}, u32[]{:S(2)}) collective-permute-start(bf16[256,1024]{1,0:T(8,128)(2,1)S(1)} %shard_map.77.rest_0_.mine.own_cols), channel_id=1, source_target_pairs={{0,4},{4,0},{1,5},{5,1},{2,6},{6,2},{3,7},{7,3},{8,12},{12,8},{9,1... | collective-permute-start | bytes 1572872 | tf_op jit(solution)/shard_map/ppermute | solution.py:221
  186.8 2.2 copy-start.5
  190.1 3.6 copy-start.35
  191.7 2.0 copy-start.6
  197.5 64.4 %collective-permute-start.18 = (bf16[256,1024]{1,0:T(8,128)(2,1)S(1)}, bf16[256,1024]{1,0:T(8,128)(2,1)S(1)}, u32[]{:S(2)}, u32[]{:S(2)}) collective-permute-start(bf16[256,1024]{1,0:T(8,128)(2,1)S(1)} %shard_map.80.rest_0_.mine.own_cols), channel_id=1, source_target_pairs={{0,4},{4,0},{1,5},{5,1},{2,6},{6,2},{3,7},{7,3},{8,12},{12,8},{9,1... | collective-permute-start | bytes 1572872 | tf_op jit(solution)/shard_map/ppermute | solution.py:221
  200.5 2.2 copy-start.7
  205.9 2.0 copy-start.8
  217.1 4.0 %copy-start.9 = (bf16[2,4,2,128,1024]{4,3,2,1,0:T(8,128)(2,1)S(1)}, bf16[2,4,2,128,1024]{4,3,2,1,0:T(8,128)(2,1)}, u32[]{:S(2)}) copy-start(bf16[2,4,2,128,1024]{4,3,2,1,0:T(8,128)(2,1)} %copy-done.8) | copy-start | bytes 12582916
  221.0 3.7 copy-start.23
  221.0 63.4 %collective-permute-start.19 = (bf16[256,1024]{1,0:T(8,128)(2,1)S(1)}, bf16[256,1024]{1,0:T(8,128)(2,1)S(1)}, u32[]{:S(2)}, u32[]{:S(2)}) collective-permute-start(bf16[256,1024]{1,0:T(8,128)(2,1)S(1)} %shard_map.83.rest_0_.mine.own_cols), channel_id=1, source_target_pairs={{0,4},{4,0},{1,5},{5,1},{2,6},{6,2},{3,7},{7,3},{8,12},{12,8},{9,1... | collective-permute-start | bytes 1572872 | tf_op jit(solution)/shard_map/ppermute | solution.py:221
  222.7 2.0 copy-start.10
  235.0 8.4 %copy-start.19 = (bf16[256,1024]{1,0:T(8,128)(2,1)S(1)}, bf16[256,1024]{1,0:T(8,128)(2,1)}, u32[]{:S(2)}) copy-start(bf16[256,1024]{1,0:T(8,128)(2,1)} %copy-done.18) | copy-start | bytes 1572868
  243.3 5.2 %copy-start.25 = (bf16[256,1024]{1,0:T(8,128)(2,1)S(1)}, bf16[256,1024]{1,0:T(8,128)(2,1)}, u32[]{:S(2)}) copy-start(bf16[256,1024]{1,0:T(8,128)(2,1)} %copy-done.24) | copy-start | bytes 1572868
  243.3 5.2 %copy-start.29 = (bf16[256,1024]{1,0:T(8,128)(2,1)S(1)}, bf16[256,1024]{1,0:T(8,128)(2,1)}, u32[]{:S(2)}) copy-start(bf16[256,1024]{1,0:T(8,128)(2,1)} %copy-done.28) | copy-start | bytes 1572868
  243.3 63.5 %collective-permute-start.20 = (bf16[256,1024]{1,0:T(8,128)(2,1)S(1)}, bf16[256,1024]{1,0:T(8,128)(2,1)S(1)}, u32[]{:S(2)}, u32[]{:S(2)}) collective-permute-start(bf16[256,1024]{1,0:T(8,128)(2,1)S(1)} %shard_map.87.rest_0_.mine.own_cols), channel_id=1, source_target_pairs={{0,4},{4,0},{1,5},{5,1},{2,6},{6,2},{3,7},{7,3},{8,12},{12,8},{9,1... | collective-permute-start | bytes 1572872 | tf_op jit(solution)/shard_map/ppermute | solution.py:221
  253.3 12.5 %copy-start.15 = (bf16[256,1024]{1,0:T(8,128)(2,1)S(1)}, bf16[256,1024]{1,0:T(8,128)(2,1)}, u32[]{:S(2)}) copy-start(bf16[256,1024]{1,0:T(8,128)(2,1)} %copy-done.14) | copy-start | bytes 1572868
  253.3 12.5 %copy-start.31 = (bf16[256,1024]{1,0:T(8,128)(2,1)S(1)}, bf16[256,1024]{1,0:T(8,128)(2,1)}, u32[]{:S(2)}) copy-start(bf16[256,1024]{1,0:T(8,128)(2,1)} %copy-done.30) | copy-start | bytes 1572868
  265.7 5.0 %copy-start.21 = (bf16[256,1024]{1,0:T(8,128)(2,1)S(1)}, bf16[256,1024]{1,0:T(8,128)(2,1)}, u32[]{:S(2)}) copy-start(bf16[256,1024]{1,0:T(8,128)(2,1)} %copy-done.20) | copy-start | bytes 1572868
  265.7 5.0 %copy-start.33 = (bf16[256,1024]{1,0:T(8,128)(2,1)S(1)}, bf16[256,1024]{1,0:T(8,128)(2,1)}, u32[]{:S(2)}) copy-start(bf16[256,1024]{1,0:T(8,128)(2,1)} %copy-done.32) | copy-start | bytes 1572868
  265.7 63.6 %collective-permute-start.21 = (bf16[256,1024]{1,0:T(8,128)(2,1)S(1)}, bf16[256,1024]{1,0:T(8,128)(2,1)S(1)}, u32[]{:S(2)}, u32[]{:S(2)}) collective-permute-start(bf16[256,1024]{1,0:T(8,128)(2,1)S(1)} %shard_map.90.rest_0_.mine.own_cols), channel_id=1, source_target_pairs={{0,4},{4,0},{1,5},{5,1},{2,6},{6,2},{3,7},{7,3},{8,12},{12,8},{9,1... | collective-permute-start | bytes 1572872 | tf_op jit(solution)/shard_map/ppermute | solution.py:221
  275.5 12.7 %copy-start.17 = (bf16[256,1024]{1,0:T(8,128)(2,1)S(1)}, bf16[256,1024]{1,0:T(8,128)(2,1)}, u32[]{:S(2)}) copy-start(bf16[256,1024]{1,0:T(8,128)(2,1)} %copy-done.16) | copy-start | bytes 1572868
  288.1 63.6 %collective-permute-start.24 = (bf16[256,1024]{1,0:T(8,128)(2,1)S(1)}, bf16[256,1024]{1,0:T(8,128)(2,1)S(1)}, u32[]{:S(2)}, u32[]{:S(2)}) collective-permute-start(bf16[256,1024]{1,0:T(8,128)(2,1)S(1)} %shard_map.93.rest_0_.mine.own_cols), channel_id=1, source_target_pairs={{0,4},{4,0},{1,5},{5,1},{2,6},{6,2},{3,7},{7,3},{8,12},{12,8},{9,1... | collective-permute-start | bytes 1572872 | tf_op jit(solution)/shard_map/ppermute | solution.py:221
  310.6 52.5 %collective-permute-start.23 = (bf16[256,1024]{1,0:T(8,128)(2,1)S(1)}, bf16[256,1024]{1,0:T(8,128)(2,1)}, u32[]{:S(2)}, u32[]{:S(2)}) collective-permute-start(bf16[256,1024]{1,0:T(8,128)(2,1)S(1)} %shard_map.96.rest_0_.mine.own_cols), channel_id=1, source_target_pairs={{0,4},{4,0},{1,5},{5,1},{2,6},{6,2},{3,7},{7,3},{8,12},{12,8},{9,1... | collective-permute-start | bytes 1572872 | tf_op jit(solution)/shard_map/ppermute | solution.py:221
  320.7 14.0 %copy-start.11 = (bf16[2,4,2,128,1024]{4,3,2,1,0:T(8,128)(2,1)S(1)}, bf16[2,4,2,128,1024]{4,3,2,1,0:T(8,128)(2,1)}, u32[]{:S(2)}) copy-start(bf16[2,4,2,128,1024]{4,3,2,1,0:T(8,128)(2,1)} %copy-done.10) | copy-start | bytes 12582916
  329.3 4.0 %copy-start.26 = (bf16[256,1024]{1,0:T(8,128)(2,1)}, bf16[256,1024]{1,0:T(8,128)(2,1)S(1)}, u32[]{:S(2)}) copy-start(bf16[256,1024]{1,0:T(8,128)(2,1)S(1)} %collective-permute-done.21.rest_2_.theirs) | copy-start | bytes 1572868
  333.3 39.8 %collective-permute-start.22 = (bf16[256,1024]{1,0:T(8,128)(2,1)S(1)}, bf16[256,1024]{1,0:T(8,128)(2,1)S(1)}, u32[]{:S(2)}, u32[]{:S(2)}) collective-permute-start(bf16[256,1024]{1,0:T(8,128)(2,1)S(1)} %shard_map.99.mine.rest_0_), channel_id=1, source_target_pairs={{0,4},{4,0},{1,5},{5,1},{2,6},{6,2},{3,7},{7,3},{8,12},{12,8},{9,1... | collective-permute-start | bytes 1572872 | tf_op jit(solution)/shard_map/ppermute | solution.py:221
  340.4 4.9 %copy-start.27 = (bf16[256,1024]{1,0:T(8,128)(2,1)S(1)}, bf16[256,1024]{1,0:T(8,128)(2,1)}, u32[]{:S(2)}) copy-start(bf16[256,1024]{1,0:T(8,128)(2,1)} %copy-done.26) | copy-start | bytes 1572868
  (6 other events, 6.1 us)

commit v5 on v4

--- a/solution.py
+++ b/solution.py
@@ -27,7 +27,7 @@
 
 def dress(amplitudes, fock, pair, first_row, rows, events):
     virt = fock.shape[0]
-    cols = min(COLS, virt)
+    cols = min(COLS, virt) if events else virt
     block = first_row // rows
     return pl.pallas_call(
         dress_kernel,

time: 378 us -> 377 us (level)
  waiting for transfers between devices: 172 us -> 150 us
  starting transfers between devices: 21 us -> 42.8 us
    ppermute x1, starting transfers between devices: 1.95 us -> 23.7 us  [start_swap(): lax.ppermute(block, 'rest', [(i, i ^ steps[0]) for i in range(n_rest)])]
    ppermute x16, waiting for transfers between devices: 172 us -> 150 us  [send(): other.append(lax.ppermute(piece, 'half', SWAP))]
where the time goes in v5:
time: 377 us; the launch traced here: 374 us
  waiting for transfers between devices  150 us (40%)
  Pallas kernels  148 us (39%)
  starting transfers between devices  42.8 us (11%)
  local copies, waits for them, and re-layouts  26.7 us (7%)
  other arithmetic  5.78 us (2%)
    ppermute x16, waiting for transfers between devices, send(): other.append(lax.ppermute(piece, 'half', SWAP))  150 us
    pallas_call x15, Pallas kernels, finish(): pl.pallas_call(finish_kernel, out_shape=jax.ShapeDtypeStruct(shape, jnp.b...  74 us
    pallas_call x16, Pallas kernels, dress(): pl.pallas_call(dress_kernel, out_shape=jax.ShapeDtypeStruct((rows, virt),...  61.4 us
    unnamed x90, local copies, waits for them, and re-layouts  24.2 us
    ppermute x1, starting transfers between devices, start_swap(): lax.ppermute(block, 'rest', [(i, i ^ steps[0]) for i in range(n_rest)])  23.7 us
    pallas_call x8, Pallas kernels, place(): pl.pallas_call(place_kernel, out_shape=jax.ShapeDtypeStruct((2, lead, 2,...  8.81 us
    ppermute x7, starting transfers between devices, next_panel_step(): part = lax.ppermute(block, ('grp', 'rest'), pairs)  8.1 us
  transfers between devices with their start and end apart: 25, of which 16 were waited for; matrix products, arithmetic and copies ran while one was open for 2% of the time, Pallas kernels for 39%

profile of v5, /device:TPU:0, one launch (start us, length us, event | category | flops | bytes accessed | tf_op | source)
XLA Modules:
  0.0 374.4 jit_solution(6287336208287760528)
XLA Ops:
  1.0 4.1 %collective-permute-start = (bf16[128,512]{1,0:T(8,128)(2,1)S(1)}, bf16[128,512]{1,0:T(8,128)(2,1)S(1)}, u32[]{:S(2)}, u32[]{:S(2)}) collective-permute-start(bf16[128,512]{1,0:T(8,128)(2,1)S(1)} %get-tuple-element.9), channel_id=1, source_target_pairs={{0,4},{4,0},{1,5},{5,1},{2,6},{6,2},{3,7},{7,3},{8,12},{12,8},{9,1... | collective-permute-start | bytes 393224 | tf_op jit(solution)/shard_map/ppermute | solution.py:225
  6.7 2.9 shard_map.64.rest_0_.mine.own_cols
  9.7 4.7 %shard_map.65.rest_0_.mine.own_cols = bf16[256,1024]{1,0:T(8,128)(2,1)} custom-call(bf16[1024,1024]{1,0:T(8,128)(2,1)S(1)} %copy-done.12, bf16[1,4,1024,1024]{3,2,1,0:T(8,128)(2,1)} %t_rows.31, bf16[1,4,1024,1024]{3,2,1,0:T(8,128)(2,1)} %t_rows.31, bf16[1024,1024]{1,0:T(8,128)(2,1)S(1)} %copy-done.12, bf16[256,1024]{1,0:T(8,128)(2,1)S(1)} %shard_map.64.rest_0_.mine.own_cols), custom_call_target="tpu_custom_call" | custom-call | flops 1073741824 | bytes 5767168 | tf_op jit(solution)/shard_map/pallas_call | solution.py:32
  14.4 2.9 collective-permute-start.2
  17.3 3.8 %shard_map.66.rest_0_.mine.own_cols = bf16[256,1024]{1,0:T(8,128)(2,1)S(1)} custom-call(bf16[1024,1024]{1,0:T(8,128)(2,1)S(1)} %copy-done.12, bf16[1,4,1024,1024]{3,2,1,0:T(8,128)(2,1)} %t_rows.31, bf16[1,4,1024,1024]{3,2,1,0:T(8,128)(2,1)} %t_rows.31, bf16[1024,1024]{1,0:T(8,128)(2,1)S(1)} %copy-done.12, bf16[256,1024]{1,0:T(8,128)(2,1)} %shard_map.65.rest_0_.mine.own_cols), custom_call_target="tpu_custom_call" | custom-call | flops 1073741824 | bytes 5767168 | tf_op jit(solution)/shard_map/pallas_call | solution.py:32
  22.3 23.7 %collective-permute-start.3 = (bf16[2,128,512]{2,1,0:T(8,128)(2,1)S(1)}, bf16[2,128,512]{2,1,0:T(8,128)(2,1)S(1)}, u32[]{:S(2)}, u32[]{:S(2)}) collective-permute-start(bf16[2,128,512]{2,1,0:T(8,128)(2,1)S(1)} %bitcast.52), channel_id=1, source_target_pairs={{0,2},{1,3},{2,0},{3,1},{4,6},{5,7},{6,4},{7,5},{8,10},{9,11},{10,... | collective-permute-start | bytes 786440 | tf_op jit(solution)/shard_map/ppermute | solution.py:233
  46.1 13.0 %collective-permute-done.1.rest_2_.theirs = bf16[256,1024]{1,0:T(8,128)(2,1)} collective-permute-done((bf16[256,1024]{1,0:T(8,128)(2,1)S(1)}, bf16[256,1024]{1,0:T(8,128)(2,1)}, u32[]{:S(2)}, u32[]{:S(2)}) %collective-permute-start.1) | collective-permute-done | bytes 524320 | tf_op jit(solution)/shard_map/ppermute | solution.py:221
  59.1 3.8 %shard_map.68.rest_0_.mine.own_cols = bf16[256,1024]{1,0:T(8,128)(2,1)S(1)} custom-call(bf16[1024,1024]{1,0:T(8,128)(2,1)S(1)} %copy-done.13, bf16[1,4,1024,1024]{3,2,1,0:T(8,128)(2,1)} %t_rows.31, bf16[1,4,1024,1024]{3,2,1,0:T(8,128)(2,1)} %t_rows.31, bf16[1024,1024]{1,0:T(8,128)(2,1)S(1)} %copy-done.13, ...), custom_call_target="tpu_custom_call" | custom-call | flops 1073741824 | bytes 5767168 | tf_op jit(solution)/shard_map/pallas_call | solution.py:32
  62.9 18.5 %collective-permute-done.2.rest_2_.theirs = bf16[256,1024]{1,0:T(8,128)(2,1)} collective-permute-done((bf16[256,1024]{1,0:T(8,128)(2,1)}, bf16[256,1024]{1,0:T(8,128)(2,1)}, u32[]{:S(2)}, u32[]{:S(2)}) %collective-permute-start.2) | collective-permute-done | bytes 524320 | tf_op jit(solution)/shard_map/ppermute | solution.py:221
  81.5 3.8 %shard_map.69.rest_0_.mine.own_cols = bf16[256,1024]{1,0:T(8,128)(2,1)S(1)} custom-call(bf16[1024,1024]{1,0:T(8,128)(2,1)S(1)} %copy-done.13, bf16[1,4,1024,1024]{3,2,1,0:T(8,128)(2,1)} %t_rows.31, bf16[1,4,1024,1024]{3,2,1,0:T(8,128)(2,1)} %t_rows.31, bf16[1024,1024]{1,0:T(8,128)(2,1)S(1)} %copy-done.13, ...), custom_call_target="tpu_custom_call" | custom-call | flops 1073741824 | bytes 5767168 | tf_op jit(solution)/shard_map/pallas_call | solution.py:32
  88.0 16.0 %collective-permute-done.4.rest_2_.theirs = bf16[256,1024]{1,0:T(8,128)(2,1)} collective-permute-done((bf16[256,1024]{1,0:T(8,128)(2,1)S(1)}, bf16[256,1024]{1,0:T(8,128)(2,1)}, u32[]{:S(2)}, u32[]{:S(2)}) %collective-permute-start.4) | collective-permute-done | bytes 524320 | tf_op jit(solution)/shard_map/ppermute | solution.py:221
  104.0 3.8 %shard_map.71.rest_0_.mine.own_cols = bf16[256,1024]{1,0:T(8,128)(2,1)S(1)} custom-call(bf16[1024,1024]{1,0:T(8,128)(2,1)S(1)} %copy-done.13, bf16[1,4,1024,1024]{3,2,1,0:T(8,128)(2,1)} %t_rows.31, bf16[1,4,1024,1024]{3,2,1,0:T(8,128)(2,1)} %t_rows.31, bf16[1024,1024]{1,0:T(8,128)(2,1)S(1)} %copy-done.13, ...), custom_call_target="tpu_custom_call" | custom-call | flops 1073741824 | bytes 5767168 | tf_op jit(solution)/shard_map/pallas_call | solution.py:32
  107.8 7.3 %collective-permute-done.5.rest_2_.theirs = bf16[256,1024]{1,0:T(8,128)(2,1)S(1)} collective-permute-done((bf16[256,1024]{1,0:T(8,128)(2,1)S(1)}, bf16[256,1024]{1,0:T(8,128)(2,1)S(1)}, u32[]{:S(2)}, u32[]{:S(2)}) %collective-permute-start.5) | collective-permute-done | bytes 524320 | tf_op jit(solution)/shard_map/ppermute | solution.py:221
  116.8 2.0 copy-done
  121.1 3.8 %shard_map.73.rest_0_.mine.own_cols = bf16[256,1024]{1,0:T(8,128)(2,1)S(1)} custom-call(bf16[1024,1024]{1,0:T(8,128)(2,1)S(1)} %copy-done.13, bf16[1,4,1024,1024]{3,2,1,0:T(8,128)(2,1)} %t_rows.31, bf16[1,4,1024,1024]{3,2,1,0:T(8,128)(2,1)} %t_rows.31, bf16[1024,1024]{1,0:T(8,128)(2,1)S(1)} %copy-done.13, ...), custom_call_target="tpu_custom_call" | custom-call | flops 1073741824 | bytes 5767168 | tf_op jit(solution)/shard_map/pallas_call | solution.py:32
  125.0 12.6 %collective-permute-done.7.rest_2_.theirs = bf16[256,1024]{1,0:T(8,128)(2,1)S(1)} collective-permute-done((bf16[256,1024]{1,0:T(8,128)(2,1)S(1)}, bf16[256,1024]{1,0:T(8,128)(2,1)S(1)}, u32[]{:S(2)}, u32[]{:S(2)}) %collective-permute-start.7) | collective-permute-done | bytes 524320 | tf_op jit(solution)/shard_map/ppermute | solution.py:221
  138.9 2.0 copy-done.2
  140.9 4.5 %shard_map.75.rest_0_.mine.own_cols = bf16[256,1024]{1,0:T(8,128)(2,1)} custom-call(bf16[1024,1024]{1,0:T(8,128)(2,1)S(1)} %copy-done.13, bf16[1,4,1024,1024]{3,2,1,0:T(8,128)(2,1)} %t_rows.31, bf16[1,4,1024,1024]{3,2,1,0:T(8,128)(2,1)} %t_rows.31, bf16[1024,1024]{1,0:T(8,128)(2,1)S(1)} %copy-done.13, bf16[256,1024]{1,0:T(8,128)(2,1)S(1)} %shard_map.73.rest_0_.mine.own_cols, ...), custom_call_target="tpu_custom_call" | custom-call | flops 1073741824 | bytes 5767168 | tf_op jit(solution)/shard_map/pallas_call | solution.py:32
  145.5 2.5 collective-permute-start.14
  148.0 12.0 %collective-permute-done.9.rest_2_.theirs = bf16[256,1024]{1,0:T(8,128)(2,1)S(1)} collective-permute-done((bf16[256,1024]{1,0:T(8,128)(2,1)S(1)}, bf16[256,1024]{1,0:T(8,128)(2,1)S(1)}, u32[]{:S(2)}, u32[]{:S(2)}) %collective-permute-start.9) | collective-permute-done | bytes 524320 | tf_op jit(solution)/shard_map/ppermute | solution.py:221
  161.5 2.2 copy-done.3
  164.2 2.0 copy-done.4
  167.0 2.6 collective-permute-start.16
  169.6 3.8 %shard_map.77.rest_0_.mine.own_cols = bf16[256,1024]{1,0:T(8,128)(2,1)S(1)} custom-call(bf16[1024,1024]{1,0:T(8,128)(2,1)S(1)} %copy-done.13, bf16[1,4,1024,1024]{3,2,1,0:T(8,128)(2,1)} %t_rows.31, bf16[1,4,1024,1024]{3,2,1,0:T(8,128)(2,1)} %t_rows.31, bf16[1024,1024]{1,0:T(8,128)(2,1)S(1)} %copy-done.13, bf16[256,1024]{1,0:T(8,128)(2,1)} %shard_map.75.rest_0_.mine.own_cols, ...), custom_call_target="tpu_custom_call" | custom-call | flops 1073741824 | bytes 5767168 | tf_op jit(solution)/shard_map/pallas_call | solution.py:32
  173.4 9.1 %collective-permute-done.12.rest_2_.theirs = bf16[256,1024]{1,0:T(8,128)(2,1)S(1)} collective-permute-done((bf16[256,1024]{1,0:T(8,128)(2,1)S(1)}, bf16[256,1024]{1,0:T(8,128)(2,1)S(1)}, u32[]{:S(2)}, u32[]{:S(2)}) %collective-permute-start.12) | collective-permute-done | bytes 524320 | tf_op jit(solution)/shard_map/ppermute | solution.py:221
  186.1 2.2 copy-done.5
  191.0 2.0 copy-done.6
  193.0 3.8 %shard_map.80.rest_0_.mine.own_cols = bf16[256,1024]{1,0:T(8,128)(2,1)S(1)} custom-call(bf16[1024,1024]{1,0:T(8,128)(2,1)S(1)} %copy-done.13, bf16[1,4,1024,1024]{3,2,1,0:T(8,128)(2,1)} %t_rows.31, bf16[1,4,1024,1024]{3,2,1,0:T(8,128)(2,1)} %t_rows.31, bf16[1024,1024]{1,0:T(8,128)(2,1)S(1)} %copy-done.13, ...), custom_call_target="tpu_custom_call" | custom-call | flops 1073741824 | bytes 5767168 | tf_op jit(solution)/shard_map/pallas_call | solution.py:32
  196.7 3.0 collective-permute-start.18
  199.7 2.2 copy-done.7
  203.6 1.6 shard_map.82.rest_1_
  205.2 2.0 copy-done.8
  207.2 9.1 %collective-permute-done.15.rest_2_.theirs = bf16[256,1024]{1,0:T(8,128)(2,1)} collective-permute-done((bf16[256,1024]{1,0:T(8,128)(2,1)}, bf16[256,1024]{1,0:T(8,128)(2,1)}, u32[]{:S(2)}, u32[]{:S(2)}) %collective-permute-start.15) | collective-permute-done | bytes 524320 | tf_op jit(solution)/shard_map/ppermute | solution.py:221
  216.3 3.9 %shard_map.83.rest_0_.mine.own_cols = bf16[256,1024]{1,0:T(8,128)(2,1)S(1)} custom-call(bf16[1024,1024]{1,0:T(8,128)(2,1)S(1)} %copy-done.13, bf16[1,4,1024,1024]{3,2,1,0:T(8,128)(2,1)} %t_rows.31, bf16[1,4,1024,1024]{3,2,1,0:T(8,128)(2,1)} %t_rows.31, bf16[1024,1024]{1,0:T(8,128)(2,1)S(1)} %copy-done.13, ...), custom_call_target="tpu_custom_call" | custom-call | flops 1073741824 | bytes 5767168 | tf_op jit(solution)/shard_map/pallas_call | solution.py:32
  222.0 2.0 copy-done.10
  224.0 5.0 %shard_map.85.rest_1_ = bf16[1,4,1024,1024]{3,2,1,0:T(8,128)(2,1)} custom-call(f32[2]{0:T(128)S(1)} %pad_maximum_fusion.1.energies, bf16[256,1024]{1,0:T(8,128)(2,1)S(1)} %copy-done.23, bf16[256,1024]{1,0:T(8,128)(2,1)S(1)} %copy-done.23, bf16[256,1024]{1,0:T(8,128)(2,1)} %collective-permute-done.1.rest_2_.theirs, bf16[2,1024,1024]{2,1,0:T(8,128)(2,1)} %bitcast.20, ...), custom_call_target="tpu_custom_call" | custom-call | flops 1073741824 | bytes 5767168 | tf_op jit(solution)/shard_map/pallas_call | solution.py:64
  228.9 5.3 %shard_map.86.rest_1_ = bf16[1,4,1024,1024]{3,2,1,0:T(8,128)(2,1)} custom-call(f32[2]{0:T(128)S(1)} %pad_maximum_fusion.1.energies, bf16[256,1024]{1,0:T(8,128)(2,1)} %shard_map.65.rest_0_.mine.own_cols, bf16[256,1024]{1,0:T(8,128)(2,1)} %shard_map.65.rest_0_.mine.own_cols, ...), custom_call_target="tpu_custom_call", output_to_operand_aliasing={{}: (9, {})} | custom-call | flops 1073741824 | bytes 5767168 | tf_op jit(solution)/shard_map/pallas_call | solution.py:64
  234.3 4.5 %collective-permute-done.17.rest_2_.theirs = bf16[256,1024]{1,0:T(8,128)(2,1)} collective-permute-done((bf16[256,1024]{1,0:T(8,128)(2,1)S(1)}, bf16[256,1024]{1,0:T(8,128)(2,1)}, u32[]{:S(2)}, u32[]{:S(2)}) %collective-permute-start.17) | collective-permute-done | bytes 524320 | tf_op jit(solution)/shard_map/ppermute | solution.py:221
  238.8 3.8 %shard_map.87.rest_0_.mine.own_cols = bf16[256,1024]{1,0:T(8,128)(2,1)S(1)} custom-call(bf16[1024,1024]{1,0:T(8,128)(2,1)S(1)} %copy-done.13, bf16[1,4,1024,1024]{3,2,1,0:T(8,128)(2,1)} %t_rows.31, bf16[1,4,1024,1024]{3,2,1,0:T(8,128)(2,1)} %t_rows.31, bf16[1024,1024]{1,0:T(8,128)(2,1)S(1)} %copy-done.13, ...), custom_call_target="tpu_custom_call" | custom-call | flops 1073741824 | bytes 5767168 | tf_op jit(solution)/shard_map/pallas_call | solution.py:32
  242.7 5.1 %shard_map.88.rest_1_ = bf16[1,4,1024,1024]{3,2,1,0:T(8,128)(2,1)} custom-call(f32[2]{0:T(128)S(1)} %pad_maximum_fusion.1.energies, bf16[256,1024]{1,0:T(8,128)(2,1)S(1)} %copy-done.19, bf16[256,1024]{1,0:T(8,128)(2,1)S(1)} %copy-done.19, bf16[256,1024]{1,0:T(8,128)(2,1)} %collective-permute-done.4.rest_2_.theirs, ...), custom_call_target="tpu_custom_call", output_to_operand_aliasing={{}: (9, {})} | custom-call | flops 1073741824 | bytes 5767168 | tf_op jit(solution)/shard_map/pallas_call | solution.py:64
  247.7 4.8 %shard_map.89.rest_1_ = bf16[1,4,1024,1024]{3,2,1,0:T(8,128)(2,1)} custom-call(f32[2]{0:T(128)S(1)} %pad_maximum_fusion.1.energies, bf16[256,1024]{1,0:T(8,128)(2,1)S(1)} %copy-done.25, bf16[256,1024]{1,0:T(8,128)(2,1)S(1)} %copy-done.25, bf16[256,1024]{1,0:T(8,128)(2,1)S(1)} %copy-done.29, ...), custom_call_target="tpu_custom_call", output_to_operand_aliasing={{}: (9, {})} | custom-call | flops 1073741824 | bytes 5767168 | tf_op jit(solution)/shard_map/pallas_call | solution.py:64
  252.6 8.6 %collective-permute-done.18.rest_2_.theirs = bf16[256,1024]{1,0:T(8,128)(2,1)S(1)} collective-permute-done((bf16[256,1024]{1,0:T(8,128)(2,1)S(1)}, bf16[256,1024]{1,0:T(8,128)(2,1)S(1)}, u32[]{:S(2)}, u32[]{:S(2)}) %collective-permute-start.18) | collective-permute-done | bytes 524320 | tf_op jit(solution)/shard_map/ppermute | solution.py:221
  261.2 3.8 %shard_map.90.rest_0_.mine.own_cols = bf16[256,1024]{1,0:T(8,128)(2,1)S(1)} custom-call(bf16[1024,1024]{1,0:T(8,128)(2,1)S(1)} %copy-done.13, bf16[1,4,1024,1024]{3,2,1,0:T(8,128)(2,1)} %t_rows.31, bf16[1,4,1024,1024]{3,2,1,0:T(8,128)(2,1)} %t_rows.31, bf16[1024,1024]{1,0:T(8,128)(2,1)S(1)} %copy-done.13, ...), custom_call_target="tpu_custom_call" | custom-call | flops 1073741824 | bytes 5767168 | tf_op jit(solution)/shard_map/pallas_call | solution.py:32
  265.1 4.9 %shard_map.91.rest_1_ = bf16[1,4,1024,1024]{3,2,1,0:T(8,128)(2,1)} custom-call(f32[2]{0:T(128)S(1)} %pad_maximum_fusion.2.energies, bf16[256,1024]{1,0:T(8,128)(2,1)S(1)} %copy-done.15, bf16[256,1024]{1,0:T(8,128)(2,1)S(1)} %copy-done.15, bf16[256,1024]{1,0:T(8,128)(2,1)S(1)} %copy-done.31, ...), custom_call_target="tpu_custom_call", output_to_operand_aliasing={{}: (9, {})} | custom-call | flops 1073741824 | bytes 5767168 | tf_op jit(solution)/shard_map/pallas_call | solution.py:64
  270.0 4.8 %shard_map.92.rest_1_ = bf16[1,4,1024,1024]{3,2,1,0:T(8,128)(2,1)} custom-call(f32[2]{0:T(128)S(1)} %pad_maximum_fusion.2.energies, bf16[256,1024]{1,0:T(8,128)(2,1)S(1)} %copy-done.21, bf16[256,1024]{1,0:T(8,128)(2,1)S(1)} %copy-done.21, bf16[256,1024]{1,0:T(8,128)(2,1)S(1)} %copy-done.33, ...), custom_call_target="tpu_custom_call", output_to_operand_aliasing={{}: (9, {})} | custom-call | flops 1073741824 | bytes 5767168 | tf_op jit(solution)/shard_map/pallas_call | solution.py:64
  274.8 8.8 %collective-permute-done.19.rest_2_.theirs = bf16[256,1024]{1,0:T(8,128)(2,1)S(1)} collective-permute-done((bf16[256,1024]{1,0:T(8,128)(2,1)S(1)}, bf16[256,1024]{1,0:T(8,128)(2,1)S(1)}, u32[]{:S(2)}, u32[]{:S(2)}) %collective-permute-start.19) | collective-permute-done | bytes 524320 | tf_op jit(solution)/shard_map/ppermute | solution.py:221
  283.6 3.8 %shard_map.93.rest_0_.mine.own_cols = bf16[256,1024]{1,0:T(8,128)(2,1)S(1)} custom-call(bf16[1024,1024]{1,0:T(8,128)(2,1)S(1)} %copy-done.13, bf16[1,4,1024,1024]{3,2,1,0:T(8,128)(2,1)} %t_rows.31, bf16[1,4,1024,1024]{3,2,1,0:T(8,128)(2,1)} %t_rows.31, bf16[1024,1024]{1,0:T(8,128)(2,1)S(1)} %copy-done.13, ...), custom_call_target="tpu_custom_call" | custom-call | flops 1073741824 | bytes 5767168 | tf_op jit(solution)/shard_map/pallas_call | solution.py:32
  287.5 4.8 %shard_map.94.rest_1_ = bf16[1,4,1024,1024]{3,2,1,0:T(8,128)(2,1)} custom-call(f32[2]{0:T(128)S(1)} %pad_maximum_fusion.2.energies, bf16[256,1024]{1,0:T(8,128)(2,1)S(1)} %copy-done.17, bf16[256,1024]{1,0:T(8,128)(2,1)S(1)} %copy-done.17, bf16[256,1024]{1,0:T(8,128)(2,1)S(1)} %copy-done.35, ...), custom_call_target="tpu_custom_call", output_to_operand_aliasing={{}: (9, {})} | custom-call | flops 1073741824 | bytes 5767168 | tf_op jit(solution)/shard_map/pallas_call | solution.py:64
  292.3 5.3 %shard_map.95.rest_1_ = bf16[1,4,1024,1024]{3,2,1,0:T(8,128)(2,1)} custom-call(f32[2]{0:T(128)S(1)} %pad_maximum_fusion.2.energies, bf16[256,1024]{1,0:T(8,128)(2,1)} %shard_map.75.rest_0_.mine.own_cols, bf16[256,1024]{1,0:T(8,128)(2,1)} %shard_map.75.rest_0_.mine.own_cols, ...), custom_call_target="tpu_custom_call", output_to_operand_aliasing={{}: (9, {})} | custom-call | flops 1073741824 | bytes 5767168 | tf_op jit(solution)/shard_map/pallas_call | solution.py:64
  297.6 8.5 %collective-permute-done.20.rest_2_.theirs = bf16[256,1024]{1,0:T(8,128)(2,1)S(1)} collective-permute-done((bf16[256,1024]{1,0:T(8,128)(2,1)S(1)}, bf16[256,1024]{1,0:T(8,128)(2,1)S(1)}, u32[]{:S(2)}, u32[]{:S(2)}) %collective-permute-start.20) | collective-permute-done | bytes 524320 | tf_op jit(solution)/shard_map/ppermute | solution.py:221
  306.1 3.8 %shard_map.96.rest_0_.mine.own_cols = bf16[256,1024]{1,0:T(8,128)(2,1)S(1)} custom-call(bf16[1024,1024]{1,0:T(8,128)(2,1)S(1)} %copy-done.13, bf16[1,4,1024,1024]{3,2,1,0:T(8,128)(2,1)} %t_rows.31, bf16[1,4,1024,1024]{3,2,1,0:T(8,128)(2,1)} %t_rows.31, bf16[1024,1024]{1,0:T(8,128)(2,1)S(1)} %copy-done.13, ...), custom_call_target="tpu_custom_call" | custom-call | flops 1073741824 | bytes 5767168 | tf_op jit(solution)/shard_map/pallas_call | solution.py:32
  309.9 5.0 %shard_map.97.rest_1_ = bf16[1,4,1024,1024]{3,2,1,0:T(8,128)(2,1)} custom-call(f32[2]{0:T(128)S(1)} %pad_maximum_fusion.3.energies, bf16[256,1024]{1,0:T(8,128)(2,1)S(1)} %shard_map.77.rest_0_.mine.own_cols, bf16[256,1024]{1,0:T(8,128)(2,1)S(1)} %shard_map.77.rest_0_.mine.own_cols, ...), custom_call_target="tpu_custom_call", output_to_operand_aliasing={{}: (9, {})} | custom-call | flops 1073741824 | bytes 5767168 | tf_op jit(solution)/shard_map/pallas_call | solution.py:64
  314.9 4.8 %shard_map.98.rest_1_ = bf16[1,4,1024,1024]{3,2,1,0:T(8,128)(2,1)} custom-call(f32[2]{0:T(128)S(1)} %pad_maximum_fusion.3.energies, bf16[256,1024]{1,0:T(8,128)(2,1)S(1)} %shard_map.80.rest_0_.mine.own_cols, bf16[256,1024]{1,0:T(8,128)(2,1)S(1)} %shard_map.80.rest_0_.mine.own_cols, ...), custom_call_target="tpu_custom_call", output_to_operand_aliasing={{}: (9, {})} | custom-call | flops 1073741824 | bytes 5767168 | tf_op jit(solution)/shard_map/pallas_call | solution.py:64
  319.7 8.8 %collective-permute-done.21.rest_2_.theirs = bf16[256,1024]{1,0:T(8,128)(2,1)S(1)} collective-permute-done((bf16[256,1024]{1,0:T(8,128)(2,1)S(1)}, bf16[256,1024]{1,0:T(8,128)(2,1)S(1)}, u32[]{:S(2)}, u32[]{:S(2)}) %collective-permute-start.21) | collective-permute-done | bytes 524320 | tf_op jit(solution)/shard_map/ppermute | solution.py:221
  328.6 3.9 %shard_map.99.mine.rest_0_ = bf16[256,1024]{1,0:T(8,128)(2,1)S(1)} custom-call(bf16[1024,1024]{1,0:T(8,128)(2,1)S(1)} %copy-done.13, bf16[1,4,1024,1024]{3,2,1,0:T(8,128)(2,1)} %t_rows.31, bf16[1,4,1024,1024]{3,2,1,0:T(8,128)(2,1)} %t_rows.31, bf16[1024,1024]{1,0:T(8,128)(2,1)S(1)} %copy-done.13, bf16[256,1024]{1,0:T(8,128)(2,1)S(1)} %shard_map.96.rest_0_.mine.own_cols, ...), custom_call_target="tpu_custom_call" | custom-call | flops 1073741824 | bytes 5767168 | tf_op jit(solution)/shard_map/pallas_call | solution.py:32
  334.8 4.8 %shard_map.101.rest_1_ = bf16[1,4,1024,1024]{3,2,1,0:T(8,128)(2,1)} custom-call(f32[2]{0:T(128)S(1)} %pad_maximum_fusion.3.energies, bf16[256,1024]{1,0:T(8,128)(2,1)S(1)} %shard_map.83.rest_0_.mine.own_cols, bf16[256,1024]{1,0:T(8,128)(2,1)S(1)} %shard_map.83.rest_0_.mine.own_cols, ...), custom_call_target="tpu_custom_call", output_to_operand_aliasing={{}: (9, {})} | custom-call | flops 1073741824 | bytes 5767168 | tf_op jit(solution)/shard_map/pallas_call | solution.py:64
  339.6 4.9 %shard_map.102.rest_1_ = bf16[1,4,1024,1024]{3,2,1,0:T(8,128)(2,1)} custom-call(f32[2]{0:T(128)S(1)} %pad_maximum_fusion.3.energies, bf16[256,1024]{1,0:T(8,128)(2,1)S(1)} %shard_map.87.rest_0_.mine.own_cols, bf16[256,1024]{1,0:T(8,128)(2,1)S(1)} %shard_map.87.rest_0_.mine.own_cols, ...), custom_call_target="tpu_custom_call", output_to_operand_aliasing={{}: (9, {})} | custom-call | flops 1073741824 | bytes 5767168 | tf_op jit(solution)/shard_map/pallas_call | solution.py:64
  344.5 4.8 %shard_map.103.rest_1_ = bf16[1,4,1024,1024]{3,2,1,0:T(8,128)(2,1)} custom-call(f32[2]{0:T(128)S(1)} %pad_maximum_fusion.energies, bf16[256,1024]{1,0:T(8,128)(2,1)S(1)} %shard_map.90.rest_0_.mine.own_cols, bf16[256,1024]{1,0:T(8,128)(2,1)S(1)} %shard_map.90.rest_0_.mine.own_cols, bf16[256,1024]{1,0:T(8,128)(2,1)S(1)} %copy-done.27, ...), custom_call_target="tpu_custom_call", output_to_operand_aliasing={{}: (9, {})} | custom-call | flops 1073741824 | bytes 5767168 | tf_op jit(solution)/shard_map/pallas_call | solution.py:64
  349.3 1.8 collective-permute-done.24.theirs
  351.0 4.8 %shard_map.104.rest_1_ = bf16[1,4,1024,1024]{3,2,1,0:T(8,128)(2,1)} custom-call(f32[2]{0:T(128)S(1)} %pad_maximum_fusion.energies, bf16[256,1024]{1,0:T(8,128)(2,1)S(1)} %shard_map.93.rest_0_.mine.own_cols, bf16[256,1024]{1,0:T(8,128)(2,1)S(1)} %shard_map.93.rest_0_.mine.own_cols, ...), custom_call_target="tpu_custom_call", output_to_operand_aliasing={{}: (9, {})} | custom-call | flops 1073741824 | bytes 5767168 | tf_op jit(solution)/shard_map/pallas_call | solution.py:64
  355.8 6.6 %collective-permute-done.23.theirs = bf16[256,1024]{1,0:T(8,128)(2,1)} collective-permute-done((bf16[256,1024]{1,0:T(8,128)(2,1)S(1)}, bf16[256,1024]{1,0:T(8,128)(2,1)}, u32[]{:S(2)}, u32[]{:S(2)}) %collective-permute-start.23) | collective-permute-done | bytes 524320 | tf_op jit(solution)/shard_map/ppermute | solution.py:221
  362.4 5.0 %shard_map.105._ = bf16[1,4,1024,1024]{3,2,1,0:T(8,128)(2,1)} custom-call(f32[2]{0:T(128)S(1)} %pad_maximum_fusion.energies, bf16[256,1024]{1,0:T(8,128)(2,1)S(1)} %shard_map.96.rest_0_.mine.own_cols, bf16[256,1024]{1,0:T(8,128)(2,1)S(1)} %shard_map.96.rest_0_.mine.own_cols, ...), custom_call_target="tpu_custom_call", output_to_operand_aliasing={{}: (9, {})} | custom-call | flops 1073741824 | bytes 5767168 | tf_op jit(solution)/shard_map/pallas_call | solution.py:64
  367.3 5.0 %collective-permute-done.22.theirs = bf16[256,1024]{1,0:T(8,128)(2,1)S(1)} collective-permute-done((bf16[256,1024]{1,0:T(8,128)(2,1)S(1)}, bf16[256,1024]{1,0:T(8,128)(2,1)S(1)}, u32[]{:S(2)}, u32[]{:S(2)}) %collective-permute-start.22) | collective-permute-done | bytes 524320 | tf_op jit(solution)/shard_map/ppermute | solution.py:221
  372.3 2.1 shard_map.106
  (136 shorter events, 26.9 us)
Async XLA Ops:
  1.0 21.3 %collective-permute-start = (bf16[128,512]{1,0:T(8,128)(2,1)S(1)}, bf16[128,512]{1,0:T(8,128)(2,1)S(1)}, u32[]{:S(2)}, u32[]{:S(2)}) collective-permute-start(bf16[128,512]{1,0:T(8,128)(2,1)S(1)} %get-tuple-element.9), channel_id=1, source_target_pairs={{0,4},{4,0},{1,5},{5,1},{2,6},{6,2},{3,7},{7,3},{8,12},{12,8},{9,1... | collective-permute-start | bytes 393224 | tf_op jit(solution)/shard_map/ppermute | solution.py:225
  9.6 4.8 %copy-start.22 = (bf16[256,1024]{1,0:T(8,128)(2,1)}, bf16[256,1024]{1,0:T(8,128)(2,1)S(1)}, u32[]{:S(2)}) copy-start(bf16[256,1024]{1,0:T(8,128)(2,1)S(1)} %shard_map.64.rest_0_.mine.own_cols) | copy-start | bytes 1572868
  9.6 49.4 %collective-permute-start.1 = (bf16[256,1024]{1,0:T(8,128)(2,1)S(1)}, bf16[256,1024]{1,0:T(8,128)(2,1)}, u32[]{:S(2)}, u32[]{:S(2)}) collective-permute-start(bf16[256,1024]{1,0:T(8,128)(2,1)S(1)} %shard_map.64.rest_0_.mine.own_cols), channel_id=1, source_target_pairs={{0,4},{4,0},{1,5},{5,1},{2,6},{6,2},{3,7},{7,3},{8,12},{12,8},{9,1... | collective-permute-start | bytes 1572872 | tf_op jit(solution)/shard_map/ppermute | solution.py:221
  14.4 7.1 %copy-start.43 = (f32[2]{0:T(128)S(1)}, f32[2]{0:T(128)}, u32[]{:S(2)}) copy-start(f32[2]{0:T(128)} %param.9) | copy-start | bytes 28
  14.4 7.7 %copy-start.44 = (f32[16]{0:T(128)S(1)}, f32[16]{0:T(128)}, u32[]{:S(2)}) copy-start(f32[16]{0:T(128)} %param.10) | copy-start | bytes 196
  14.4 44.7 %copy-start.13 = (bf16[1024,1024]{1,0:T(8,128)(2,1)S(1)}, bf16[1024,1024]{1,0:T(8,128)(2,1)}, u32[]{:S(2)}) copy-start(bf16[1024,1024]{1,0:T(8,128)(2,1)} %f_cols.31) | copy-start | bytes 6291460
  14.4 67.1 %collective-permute-start.2 = (bf16[256,1024]{1,0:T(8,128)(2,1)}, bf16[256,1024]{1,0:T(8,128)(2,1)}, u32[]{:S(2)}, u32[]{:S(2)}) collective-permute-start(bf16[256,1024]{1,0:T(8,128)(2,1)} %shard_map.65.rest_0_.mine.own_cols), channel_id=1, source_target_pairs={{0,4},{4,0},{1,5},{5,1},{2,6},{6,2},{3,7},{7,3},{8,12},{12,8},{9,1... | collective-permute-start | bytes 1572872 | tf_op jit(solution)/shard_map/ppermute | solution.py:221
  21.0 41.8 %copy-start.18 = (bf16[256,1024]{1,0:T(8,128)(2,1)}, bf16[256,1024]{1,0:T(8,128)(2,1)S(1)}, u32[]{:S(2)}) copy-start(bf16[256,1024]{1,0:T(8,128)(2,1)S(1)} %shard_map.66.rest_0_.mine.own_cols) | copy-start | bytes 1572868
  21.1 82.9 %collective-permute-start.4 = (bf16[256,1024]{1,0:T(8,128)(2,1)S(1)}, bf16[256,1024]{1,0:T(8,128)(2,1)}, u32[]{:S(2)}, u32[]{:S(2)}) collective-permute-start(bf16[256,1024]{1,0:T(8,128)(2,1)S(1)} %shard_map.66.rest_0_.mine.own_cols), channel_id=1, source_target_pairs={{0,4},{4,0},{1,5},{5,1},{2,6},{6,2},{3,7},{7,3},{8,12},{12,8},{9,1... | collective-permute-start | bytes 1572872 | tf_op jit(solution)/shard_map/ppermute | solution.py:221
  22.3 63.0 %collective-permute-start.3 = (bf16[2,128,512]{2,1,0:T(8,128)(2,1)S(1)}, bf16[2,128,512]{2,1,0:T(8,128)(2,1)S(1)}, u32[]{:S(2)}, u32[]{:S(2)}) collective-permute-start(bf16[2,128,512]{2,1,0:T(8,128)(2,1)S(1)} %bitcast.52), channel_id=1, source_target_pairs={{0,2},{1,3},{2,0},{3,1},{4,6},{5,7},{6,4},{7,5},{8,10},{9,11},{10,... | collective-permute-start | bytes 786440 | tf_op jit(solution)/shard_map/ppermute | solution.py:233
  62.9 22.4 %copy-start.24 = (bf16[256,1024]{1,0:T(8,128)(2,1)}, bf16[256,1024]{1,0:T(8,128)(2,1)S(1)}, u32[]{:S(2)}) copy-start(bf16[256,1024]{1,0:T(8,128)(2,1)S(1)} %shard_map.68.rest_0_.mine.own_cols) | copy-start | bytes 1572868
  62.9 52.2 %collective-permute-start.5 = (bf16[256,1024]{1,0:T(8,128)(2,1)S(1)}, bf16[256,1024]{1,0:T(8,128)(2,1)S(1)}, u32[]{:S(2)}, u32[]{:S(2)}) collective-permute-start(bf16[256,1024]{1,0:T(8,128)(2,1)S(1)} %shard_map.68.rest_0_.mine.own_cols), channel_id=1, source_target_pairs={{0,4},{4,0},{1,5},{5,1},{2,6},{6,2},{3,7},{7,3},{8,12},{12,8},{9,1... | collective-permute-start | bytes 1572872 | tf_op jit(solution)/shard_map/ppermute | solution.py:221
  85.3 22.5 %copy-start.14 = (bf16[256,1024]{1,0:T(8,128)(2,1)}, bf16[256,1024]{1,0:T(8,128)(2,1)S(1)}, u32[]{:S(2)}) copy-start(bf16[256,1024]{1,0:T(8,128)(2,1)S(1)} %shard_map.69.rest_0_.mine.own_cols) | copy-start | bytes 1572868
  86.2 32.6 %collective-permute-start.6 = (bf16[4,128,512]{2,1,0:T(8,128)(2,1)}, bf16[4,128,512]{2,1,0:T(8,128)(2,1)S(1)}, u32[]{:S(2)}, u32[]{:S(2)}) collective-permute-start(bf16[4,128,512]{2,1,0:T(8,128)(2,1)} %bitcast.5.rest_1_.block), channel_id=1, source_target_pairs={{0,1},{1,0},{2,3},{3,2},{8,9},{9,8},{10,11},{11,10},{16,17},{17,16... | collective-permute-start | bytes 1572872 | tf_op jit(solution)/shard_map/ppermute | solution.py:249
  87.8 49.8 %collective-permute-start.7 = (bf16[256,1024]{1,0:T(8,128)(2,1)S(1)}, bf16[256,1024]{1,0:T(8,128)(2,1)S(1)}, u32[]{:S(2)}, u32[]{:S(2)}) collective-permute-start(bf16[256,1024]{1,0:T(8,128)(2,1)S(1)} %shard_map.69.rest_0_.mine.own_cols), channel_id=1, source_target_pairs={{0,4},{4,0},{1,5},{5,1},{2,6},{6,2},{3,7},{7,3},{8,12},{12,8},{9,1... | collective-permute-start | bytes 1572872 | tf_op jit(solution)/shard_map/ppermute | solution.py:221
  87.9 57.5 %collective-permute-start.8 = (bf16[4,128,512]{2,1,0:T(8,128)(2,1)}, bf16[4,128,512]{2,1,0:T(8,128)(2,1)S(1)}, u32[]{:S(2)}, u32[]{:S(2)}) collective-permute-start(bf16[4,128,512]{2,1,0:T(8,128)(2,1)} %bitcast.5.rest_1_.block), channel_id=1, source_target_pairs={{0,8},{1,9},{2,10},{3,11},{8,0},{9,1},{10,2},{11,3},{16,24},{17,25... | collective-permute-start | bytes 1572872 | tf_op jit(solution)/shard_map/ppermute | solution.py:249
  104.0 56.1 %collective-permute-start.11 = (bf16[4,128,512]{2,1,0:T(8,128)(2,1)}, bf16[4,128,512]{2,1,0:T(8,128)(2,1)S(1)}, u32[]{:S(2)}, u32[]{:S(2)}) collective-permute-start(bf16[4,128,512]{2,1,0:T(8,128)(2,1)} %bitcast.5.rest_1_.block), channel_id=1, source_target_pairs={{0,9},{1,8},{2,11},{3,10},{8,1},{9,0},{10,3},{11,2},{16,25},{17,24... | collective-permute-start | bytes 1572872 | tf_op jit(solution)/shard_map/ppermute | solution.py:249
  107.7 17.2 %copy-start.20 = (bf16[256,1024]{1,0:T(8,128)(2,1)}, bf16[256,1024]{1,0:T(8,128)(2,1)S(1)}, u32[]{:S(2)}) copy-start(bf16[256,1024]{1,0:T(8,128)(2,1)S(1)} %shard_map.71.rest_0_.mine.own_cols) | copy-start | bytes 1572868
  115.1 9.9 %copy-start.28 = (bf16[256,1024]{1,0:T(8,128)(2,1)}, bf16[256,1024]{1,0:T(8,128)(2,1)S(1)}, u32[]{:S(2)}) copy-start(bf16[256,1024]{1,0:T(8,128)(2,1)S(1)} %collective-permute-done.5.rest_2_.theirs) | copy-start | bytes 1572868
  115.1 44.9 %collective-permute-start.9 = (bf16[256,1024]{1,0:T(8,128)(2,1)S(1)}, bf16[256,1024]{1,0:T(8,128)(2,1)S(1)}, u32[]{:S(2)}, u32[]{:S(2)}) collective-permute-start(bf16[256,1024]{1,0:T(8,128)(2,1)S(1)} %shard_map.71.rest_0_.mine.own_cols), channel_id=1, source_target_pairs={{0,4},{4,0},{1,5},{5,1},{2,6},{6,2},{3,7},{7,3},{8,12},{12,8},{9,1... | collective-permute-start | bytes 1572872 | tf_op jit(solution)/shard_map/ppermute | solution.py:221
  116.8 2.0 copy-start
  119.6 18.7 %copy-start.1 = (bf16[2,4,2,128,1024]{4,3,2,1,0:T(8,128)(2,1)S(1)}, bf16[2,4,2,128,1024]{4,3,2,1,0:T(8,128)(2,1)}, u32[]{:S(2)}) copy-start(bf16[2,4,2,128,1024]{4,3,2,1,0:T(8,128)(2,1)} %copy-done) | copy-start | bytes 12582916
  119.6 46.6 %collective-permute-start.10 = (bf16[4,128,512]{2,1,0:T(8,128)(2,1)}, bf16[4,128,512]{2,1,0:T(8,128)(2,1)S(1)}, u32[]{:S(2)}, u32[]{:S(2)}) collective-permute-start(bf16[4,128,512]{2,1,0:T(8,128)(2,1)} %bitcast.5.rest_1_.block), channel_id=1, source_target_pairs={{0,16},{1,17},{2,18},{3,19},{8,24},{9,25},{10,26},{11,27},{16,0},{... | collective-permute-start | bytes 1572872 | tf_op jit(solution)/shard_map/ppermute | solution.py:249
  121.1 17.2 %copy-start.42 = (bf16[4,128,512]{2,1,0:T(8,128)(2,1)S(1)}, bf16[4,128,512]{2,1,0:T(8,128)(2,1)}, u32[]{:S(2)}) copy-start(bf16[4,128,512]{2,1,0:T(8,128)(2,1)} %copy-done.41) | copy-start | bytes 1572868
  125.0 20.5 %copy-start.16 = (bf16[256,1024]{1,0:T(8,128)(2,1)}, bf16[256,1024]{1,0:T(8,128)(2,1)S(1)}, u32[]{:S(2)}) copy-start(bf16[256,1024]{1,0:T(8,128)(2,1)S(1)} %shard_map.73.rest_0_.mine.own_cols) | copy-start | bytes 1572868
  137.6 7.9 %copy-start.30 = (bf16[256,1024]{1,0:T(8,128)(2,1)}, bf16[256,1024]{1,0:T(8,128)(2,1)S(1)}, u32[]{:S(2)}) copy-start(bf16[256,1024]{1,0:T(8,128)(2,1)S(1)} %collective-permute-done.7.rest_2_.theirs) | copy-start | bytes 1572868
  137.6 44.9 %collective-permute-start.12 = (bf16[256,1024]{1,0:T(8,128)(2,1)S(1)}, bf16[256,1024]{1,0:T(8,128)(2,1)S(1)}, u32[]{:S(2)}, u32[]{:S(2)}) collective-permute-start(bf16[256,1024]{1,0:T(8,128)(2,1)S(1)} %shard_map.73.rest_0_.mine.own_cols), channel_id=1, source_target_pairs={{0,4},{4,0},{1,5},{5,1},{2,6},{6,2},{3,7},{7,3},{8,12},{12,8},{9,1... | collective-permute-start | bytes 1572872 | tf_op jit(solution)/shard_map/ppermute | solution.py:221
  138.9 2.0 copy-start.2
  145.5 51.2 %collective-permute-start.14 = (bf16[4,128,512]{2,1,0:T(8,128)(2,1)}, bf16[4,128,512]{2,1,0:T(8,128)(2,1)}, u32[]{:S(2)}, u32[]{:S(2)}) collective-permute-start(bf16[4,128,512]{2,1,0:T(8,128)(2,1)} %bitcast.5.rest_1_.block), channel_id=1, source_target_pairs={{0,17},{1,16},{2,19},{3,18},{8,25},{9,24},{10,27},{11,26},{16,1},{... | collective-permute-start | bytes 1572872 | tf_op jit(solution)/shard_map/ppermute | solution.py:249
  160.0 13.3 %copy-start.32 = (bf16[256,1024]{1,0:T(8,128)(2,1)}, bf16[256,1024]{1,0:T(8,128)(2,1)S(1)}, u32[]{:S(2)}) copy-start(bf16[256,1024]{1,0:T(8,128)(2,1)S(1)} %collective-permute-done.9.rest_2_.theirs) | copy-start | bytes 1572868
  160.0 43.5 %collective-permute-start.13 = (bf16[4,128,512]{2,1,0:T(8,128)(2,1)}, bf16[4,128,512]{2,1,0:T(8,128)(2,1)}, u32[]{:S(2)}, u32[]{:S(2)}) collective-permute-start(bf16[4,128,512]{2,1,0:T(8,128)(2,1)} %bitcast.5.rest_1_.block), channel_id=1, source_target_pairs={{0,24},{1,25},{2,26},{3,27},{8,16},{9,17},{10,18},{11,19},{16,8},{... | collective-permute-start | bytes 1572872 | tf_op jit(solution)/shard_map/ppermute | solution.py:249
  160.0 13.3 %copy-start.37 = (bf16[4,128,512]{2,1,0:T(8,128)(2,1)}, bf16[4,128,512]{2,1,0:T(8,128)(2,1)S(1)}, u32[]{:S(2)}) copy-start(bf16[4,128,512]{2,1,0:T(8,128)(2,1)S(1)} %collective-permute-done.11.block) | copy-start | bytes 1572868
  160.1 56.3 %collective-permute-start.15 = (bf16[256,1024]{1,0:T(8,128)(2,1)}, bf16[256,1024]{1,0:T(8,128)(2,1)}, u32[]{:S(2)}, u32[]{:S(2)}) collective-permute-start(bf16[256,1024]{1,0:T(8,128)(2,1)} %shard_map.75.rest_0_.mine.own_cols), channel_id=1, source_target_pairs={{0,4},{4,0},{1,5},{5,1},{2,6},{6,2},{3,7},{7,3},{8,12},{12,8},{9,1... | collective-permute-start | bytes 1572872 | tf_op jit(solution)/shard_map/ppermute | solution.py:221
  161.5 2.2 copy-start.3
  164.2 2.0 copy-start.4
  166.2 18.3 %copy-start.36 = (f32[1024]{0:T(1024)S(1)}, f32[1024]{0:T(1024)}, u32[]{:S(2)}) copy-start(f32[1024]{0:T(1024)} %param.11) | copy-start | bytes 12292
  167.0 53.3 %collective-permute-start.16 = (bf16[4,128,512]{2,1,0:T(8,128)(2,1)}, bf16[4,128,512]{2,1,0:T(8,128)(2,1)}, u32[]{:S(2)}, u32[]{:S(2)}) collective-permute-start(bf16[4,128,512]{2,1,0:T(8,128)(2,1)} %bitcast.5.rest_1_.block), channel_id=1, source_target_pairs={{0,25},{1,24},{2,27},{3,26},{8,17},{9,16},{10,19},{11,18},{16,9},{... | collective-permute-start | bytes 1572872 | tf_op jit(solution)/shard_map/ppermute | solution.py:249
  183.3 55.5 %collective-permute-start.17 = (bf16[256,1024]{1,0:T(8,128)(2,1)S(1)}, bf16[256,1024]{1,0:T(8,128)(2,1)}, u32[]{:S(2)}, u32[]{:S(2)}) collective-permute-start(bf16[256,1024]{1,0:T(8,128)(2,1)S(1)} %shard_map.77.rest_0_.mine.own_cols), channel_id=1, source_target_pairs={{0,4},{4,0},{1,5},{5,1},{2,6},{6,2},{3,7},{7,3},{8,12},{12,8},{9,1... | collective-permute-start | bytes 1572872 | tf_op jit(solution)/shard_map/ppermute | solution.py:221
  186.1 2.2 copy-start.5
  189.3 3.6 copy-start.35
  190.9 2.0 copy-start.6
  196.7 64.4 %collective-permute-start.18 = (bf16[256,1024]{1,0:T(8,128)(2,1)S(1)}, bf16[256,1024]{1,0:T(8,128)(2,1)S(1)}, u32[]{:S(2)}, u32[]{:S(2)}) collective-permute-start(bf16[256,1024]{1,0:T(8,128)(2,1)S(1)} %shard_map.80.rest_0_.mine.own_cols), channel_id=1, source_target_pairs={{0,4},{4,0},{1,5},{5,1},{2,6},{6,2},{3,7},{7,3},{8,12},{12,8},{9,1... | collective-permute-start | bytes 1572872 | tf_op jit(solution)/shard_map/ppermute | solution.py:221
  199.7 2.2 copy-start.7
  205.2 2.0 copy-start.8
  216.3 4.0 %copy-start.9 = (bf16[2,4,2,128,1024]{4,3,2,1,0:T(8,128)(2,1)S(1)}, bf16[2,4,2,128,1024]{4,3,2,1,0:T(8,128)(2,1)}, u32[]{:S(2)}) copy-start(bf16[2,4,2,128,1024]{4,3,2,1,0:T(8,128)(2,1)} %copy-done.8) | copy-start | bytes 12582916
  220.2 3.7 copy-start.23
  220.2 63.4 %collective-permute-start.19 = (bf16[256,1024]{1,0:T(8,128)(2,1)S(1)}, bf16[256,1024]{1,0:T(8,128)(2,1)S(1)}, u32[]{:S(2)}, u32[]{:S(2)}) collective-permute-start(bf16[256,1024]{1,0:T(8,128)(2,1)S(1)} %shard_map.83.rest_0_.mine.own_cols), channel_id=1, source_target_pairs={{0,4},{4,0},{1,5},{5,1},{2,6},{6,2},{3,7},{7,3},{8,12},{12,8},{9,1... | collective-permute-start | bytes 1572872 | tf_op jit(solution)/shard_map/ppermute | solution.py:221
  222.0 2.0 copy-start.10
  234.3 8.4 %copy-start.19 = (bf16[256,1024]{1,0:T(8,128)(2,1)S(1)}, bf16[256,1024]{1,0:T(8,128)(2,1)}, u32[]{:S(2)}) copy-start(bf16[256,1024]{1,0:T(8,128)(2,1)} %copy-done.18) | copy-start | bytes 1572868
  242.6 5.2 %copy-start.25 = (bf16[256,1024]{1,0:T(8,128)(2,1)S(1)}, bf16[256,1024]{1,0:T(8,128)(2,1)}, u32[]{:S(2)}) copy-start(bf16[256,1024]{1,0:T(8,128)(2,1)} %copy-done.24) | copy-start | bytes 1572868
  242.6 5.2 %copy-start.29 = (bf16[256,1024]{1,0:T(8,128)(2,1)S(1)}, bf16[256,1024]{1,0:T(8,128)(2,1)}, u32[]{:S(2)}) copy-start(bf16[256,1024]{1,0:T(8,128)(2,1)} %copy-done.28) | copy-start | bytes 1572868
  242.6 63.5 %collective-permute-start.20 = (bf16[256,1024]{1,0:T(8,128)(2,1)S(1)}, bf16[256,1024]{1,0:T(8,128)(2,1)S(1)}, u32[]{:S(2)}, u32[]{:S(2)}) collective-permute-start(bf16[256,1024]{1,0:T(8,128)(2,1)S(1)} %shard_map.87.rest_0_.mine.own_cols), channel_id=1, source_target_pairs={{0,4},{4,0},{1,5},{5,1},{2,6},{6,2},{3,7},{7,3},{8,12},{12,8},{9,1... | collective-permute-start | bytes 1572872 | tf_op jit(solution)/shard_map/ppermute | solution.py:221
  252.5 12.5 %copy-start.15 = (bf16[256,1024]{1,0:T(8,128)(2,1)S(1)}, bf16[256,1024]{1,0:T(8,128)(2,1)}, u32[]{:S(2)}) copy-start(bf16[256,1024]{1,0:T(8,128)(2,1)} %copy-done.14) | copy-start | bytes 1572868
  252.6 12.5 %copy-start.31 = (bf16[256,1024]{1,0:T(8,128)(2,1)S(1)}, bf16[256,1024]{1,0:T(8,128)(2,1)}, u32[]{:S(2)}) copy-start(bf16[256,1024]{1,0:T(8,128)(2,1)} %copy-done.30) | copy-start | bytes 1572868
  264.9 5.0 %copy-start.21 = (bf16[256,1024]{1,0:T(8,128)(2,1)S(1)}, bf16[256,1024]{1,0:T(8,128)(2,1)}, u32[]{:S(2)}) copy-start(bf16[256,1024]{1,0:T(8,128)(2,1)} %copy-done.20) | copy-start | bytes 1572868
  265.0 5.0 %copy-start.33 = (bf16[256,1024]{1,0:T(8,128)(2,1)S(1)}, bf16[256,1024]{1,0:T(8,128)(2,1)}, u32[]{:S(2)}) copy-start(bf16[256,1024]{1,0:T(8,128)(2,1)} %copy-done.32) | copy-start | bytes 1572868
  265.0 63.6 %collective-permute-start.21 = (bf16[256,1024]{1,0:T(8,128)(2,1)S(1)}, bf16[256,1024]{1,0:T(8,128)(2,1)S(1)}, u32[]{:S(2)}, u32[]{:S(2)}) collective-permute-start(bf16[256,1024]{1,0:T(8,128)(2,1)S(1)} %shard_map.90.rest_0_.mine.own_cols), channel_id=1, source_target_pairs={{0,4},{4,0},{1,5},{5,1},{2,6},{6,2},{3,7},{7,3},{8,12},{12,8},{9,1... | collective-permute-start | bytes 1572872 | tf_op jit(solution)/shard_map/ppermute | solution.py:221
  274.8 12.7 %copy-start.17 = (bf16[256,1024]{1,0:T(8,128)(2,1)S(1)}, bf16[256,1024]{1,0:T(8,128)(2,1)}, u32[]{:S(2)}) copy-start(bf16[256,1024]{1,0:T(8,128)(2,1)} %copy-done.16) | copy-start | bytes 1572868
  287.4 63.6 %collective-permute-start.24 = (bf16[256,1024]{1,0:T(8,128)(2,1)S(1)}, bf16[256,1024]{1,0:T(8,128)(2,1)S(1)}, u32[]{:S(2)}, u32[]{:S(2)}) collective-permute-start(bf16[256,1024]{1,0:T(8,128)(2,1)S(1)} %shard_map.93.rest_0_.mine.own_cols), channel_id=1, source_target_pairs={{0,4},{4,0},{1,5},{5,1},{2,6},{6,2},{3,7},{7,3},{8,12},{12,8},{9,1... | collective-permute-start | bytes 1572872 | tf_op jit(solution)/shard_map/ppermute | solution.py:221
  309.9 52.5 %collective-permute-start.23 = (bf16[256,1024]{1,0:T(8,128)(2,1)S(1)}, bf16[256,1024]{1,0:T(8,128)(2,1)}, u32[]{:S(2)}, u32[]{:S(2)}) collective-permute-start(bf16[256,1024]{1,0:T(8,128)(2,1)S(1)} %shard_map.96.rest_0_.mine.own_cols), channel_id=1, source_target_pairs={{0,4},{4,0},{1,5},{5,1},{2,6},{6,2},{3,7},{7,3},{8,12},{12,8},{9,1... | collective-permute-start | bytes 1572872 | tf_op jit(solution)/shard_map/ppermute | solution.py:221
  319.7 14.2 %copy-start.11 = (bf16[2,4,2,128,1024]{4,3,2,1,0:T(8,128)(2,1)S(1)}, bf16[2,4,2,128,1024]{4,3,2,1,0:T(8,128)(2,1)}, u32[]{:S(2)}) copy-start(bf16[2,4,2,128,1024]{4,3,2,1,0:T(8,128)(2,1)} %copy-done.10) | copy-start | bytes 12582916
  328.6 4.0 %copy-start.26 = (bf16[256,1024]{1,0:T(8,128)(2,1)}, bf16[256,1024]{1,0:T(8,128)(2,1)S(1)}, u32[]{:S(2)}) copy-start(bf16[256,1024]{1,0:T(8,128)(2,1)S(1)} %collective-permute-done.21.rest_2_.theirs) | copy-start | bytes 1572868
  332.5 39.8 %collective-permute-start.22 = (bf16[256,1024]{1,0:T(8,128)(2,1)S(1)}, bf16[256,1024]{1,0:T(8,128)(2,1)S(1)}, u32[]{:S(2)}, u32[]{:S(2)}) collective-permute-start(bf16[256,1024]{1,0:T(8,128)(2,1)S(1)} %shard_map.99.mine.rest_0_), channel_id=1, source_target_pairs={{0,4},{4,0},{1,5},{5,1},{2,6},{6,2},{3,7},{7,3},{8,12},{12,8},{9,1... | collective-permute-start | bytes 1572872 | tf_op jit(solution)/shard_map/ppermute | solution.py:221
  339.6 4.9 %copy-start.27 = (bf16[256,1024]{1,0:T(8,128)(2,1)S(1)}, bf16[256,1024]{1,0:T(8,128)(2,1)}, u32[]{:S(2)}) copy-start(bf16[256,1024]{1,0:T(8,128)(2,1)} %copy-done.26) | copy-start | bytes 1572868
  (6 other events, 6.1 us)

commit v6 on v3

--- a/solution.py
+++ b/solution.py
@@ -9,6 +9,7 @@
 COLS = 256
 DEPTH = 3
 VMEM = 48 * 1024 * 1024
+LAST_VMEM = 24 * 1024 * 1024
 PANEL_STEPS = [0, 0, 1, 0, 1, 1, 1, 1, 2, 2, 1]
 SWAP = [(0, 1), (1, 0)]
 NT = (((1,), (1,)), ((), ()))
@@ -26,7 +27,7 @@
 
 def dress(amplitudes, fock, pair, first_row, rows, events):
     virt = fock.shape[0]
-    cols = min(COLS, virt)
+    cols = min(COLS, virt) if events else virt
     block = first_row // rows
     return pl.pallas_call(
         dress_kernel,
@@ -84,6 +85,58 @@
     )(energies, mine, mine, theirs, panel, panel, a_energy, b_energy, *behind)
 
 
+def half_finish_kernel(energies, mine, panel_own, panel_other, a_energy, b_energy, part, divisor, other_out):
+    part[...] = mine[...].astype(jnp.float32) + dot_nt(mine[...], panel_own[...])
+    divisor[...] = ((a_energy[...] + b_energy[...]) - energies[0]) - energies[1]
+    other_out[...] = panel_other[...]
+
+
+def half_finish(energies, first_row, mine, panel, a_energy, b_energy):
+    rows, virt = mine.shape
+    block = first_row // rows
+    full = pl.BlockSpec((rows, virt), lambda i: (0, 0))
+    square = pl.BlockSpec((virt, virt), lambda i: (0, 0))
+    shape = jax.ShapeDtypeStruct((rows, virt), jnp.float32)
+    return pl.pallas_call(
+        half_finish_kernel,
+        out_shape=(shape, shape, jax.ShapeDtypeStruct((virt, virt), panel.dtype)),
+        grid_spec=pl.GridSpec(
+            grid=(1,),
+            in_specs=[
+                pl.BlockSpec(memory_space=pltpu.SMEM),
+                full,
+                pl.BlockSpec((None, virt, virt), lambda i: (0, 0, 0)),
+                pl.BlockSpec((None, virt, virt), lambda i: (1, 0, 0)),
+                pl.BlockSpec((rows, 1), lambda i: (block, 0)),
+                pl.BlockSpec((1, virt), lambda i: (0, 0)),
+            ],
+            out_specs=(full, full, square),
+        ),
+        compiler_params=pltpu.CompilerParams(vmem_limit_bytes=LAST_VMEM),
+    )(energies, mine, panel, panel, a_energy, b_energy)
+
+
+def last_finish_kernel(part, divisor, theirs, panel_other, _, out):
+    cols = out.shape[-1]
+    here = pl.ds(pl.multiple_of(pl.program_id(0) * cols, cols), cols)
+    total = part[:, here] + dot_nt(theirs[...], panel_other[here, :])
+    out[...] = (total / divisor[:, here]).astype(out.dtype)
+
+
+def last_finish(out, pair, first_row, part, divisor, theirs, panel_other):
+    rows, virt = theirs.shape
+    block, cols = first_row // rows, min(2 * COLS, virt)
+    return pl.pallas_call(
+        last_finish_kernel,
+        out_shape=jax.ShapeDtypeStruct(out.shape, out.dtype),
+        grid=(virt // cols,),
+        in_specs=[pl.BlockSpec(memory_space=pltpu.VMEM)] * 4 + [pl.BlockSpec(memory_space=pltpu.HBM)],
+        out_specs=pl.BlockSpec((None, None, rows, cols), lambda j: (0, pair, block, j)),
+        input_output_aliases={4: 0},
+        compiler_params=pltpu.CompilerParams(vmem_limit_bytes=LAST_VMEM),
+    )(part, divisor, theirs, panel_other, out)
+
+
 def join_kernel(first, block, swapped, *rest):
     out = rest[-1]
     out[first[0]] = block[...]
@@ -153,7 +206,9 @@
     half, rest = lax.axis_index("half"), lax.axis_index("rest")
     n_rest, n_grp = lax.axis_size("rest"), lax.axis_size("grp")
     rows = min(ROWS, virt_count)
-    chunks = [(p, a) for p in range(per_dev) for a in range(0, virt_count, rows)]
+    chunks = [(p, a, rows) for p in range(per_dev) for a in range(0, virt_count, rows)]
+    p, a, size = chunks.pop()
+    chunks += [(p, a, size // 2), (p, a + size // 2, size // 2)]
 
     row = lax.dynamic_index_in_dim(row_energy, half, 0, keepdims=False)
     cols = lax.dynamic_slice_in_dim(col_energy, (rest * per_dev) % group_j, per_dev)
@@ -163,7 +218,7 @@
     own, other = [], []
 
     def send(n, events):
-        piece = dress(amplitudes, vv_fock, *chunks[n], rows, events)
+        piece = dress(amplitudes, vv_fock, *chunks[n], events)
         own.append(piece)
         other.append(lax.ppermute(piece, "half", SWAP))
 
@@ -203,7 +258,7 @@
     def end(n, events):
         whole = panel.reshape(2, virt_count, virt_count)
         return finish(
-            out, amplitudes.shape, *chunks[n], energies[chunks[n][0]], own[n], other[n], whole, a_energy, b_energy, events
+            out, amplitudes.shape, *chunks[n][:2], energies[chunks[n][0]], own[n], other[n], whole, a_energy, b_energy, events
         )
 
     for n in range(1, len(chunks)):
@@ -219,8 +274,12 @@
             finished += 1
     while others:
         next_panel_step(own[-1])
-    for n in range(finished, len(chunks)):
+    p, a, _ = chunks[-1]
+    whole = panel.reshape(2, virt_count, virt_count)
+    part, divisor, panel_other = half_finish(energies[p], a, own[-1], whole, a_energy, b_energy)
+    for n in range(finished, len(chunks) - 1):
         out = end(n, [own[-1]])
+    out = last_finish(out, p, a, part, divisor, other[-1], panel_other)
     return out
 
 

time: 379 us -> 376 us (level)
  waiting for transfers between devices: 173 us -> 150 us
  starting transfers between devices: 21 us -> 42.7 us
    ppermute x16 -> x17, waiting for transfers between devices: 173 us -> 150 us  [send(): other.append(lax.ppermute(piece, 'half', SWAP))]
    ppermute x1, starting transfers between devices: 1.96 us -> 23.6 us  [start_swap(): lax.ppermute(block, 'rest', [(i, i ^ steps[0]) for i in range(n_rest)])]
    pallas_call x16, Pallas kernels: 77.3 us -> 70.5 us  [finish(): pl.pallas_call(finish_kernel, out_shape=jax.ShapeDtypeStruct(shape, jnp.b...]
    pallas_call x16 -> x17, Pallas kernels: 62.1 us -> 64.5 us  [dress(): pl.pallas_call(dress_kernel, out_shape=jax.ShapeDtypeStruct((rows, virt),...]
    unnamed x86 -> x92, local copies, waits for them, and re-layouts: 24.2 us -> 24.2 us
  transfers between devices with their start and end apart: 25 -> 26, of which waited for: 16 -> 17; matrix products, arithmetic and copies ran while one was open for 2% -> 2% of each run, Pallas kernels for 39% -> 39%
where the time goes in v6:
time: 376 us; the launch traced here: 374 us
  waiting for transfers between devices  150 us (40%)
  Pallas kernels  148 us (39%)
  starting transfers between devices  42.7 us (11%)
  local copies, waits for them, and re-layouts  26.8 us (7%)
  other arithmetic  6.11 us (2%)
    ppermute x17, waiting for transfers between devices, send(): other.append(lax.ppermute(piece, 'half', SWAP))  150 us
    pallas_call x16, Pallas kernels, finish(): pl.pallas_call(finish_kernel, out_shape=jax.ShapeDtypeStruct(shape, jnp.b...  70.5 us
    pallas_call x17, Pallas kernels, dress(): pl.pallas_call(dress_kernel, out_shape=jax.ShapeDtypeStruct((rows, virt),...  64.5 us
    unnamed x92, local copies, waits for them, and re-layouts  24.2 us
    ppermute x1, starting transfers between devices, start_swap(): lax.ppermute(block, 'rest', [(i, i ^ steps[0]) for i in range(n_rest)])  23.6 us
    pallas_call x8, Pallas kernels, place(): pl.pallas_call(place_kernel, out_shape=jax.ShapeDtypeStruct((2, lead, 2,...  8.8 us
    ppermute x7, starting transfers between devices, next_panel_step(): part = lax.ppermute(block, ('grp', 'rest'), pairs)  8.09 us
  transfers between devices with their start and end apart: 26, of which 17 were waited for; matrix products, arithmetic and copies ran while one was open for 2% of the time, Pallas kernels for 39%

profile of v6, /device:TPU:0, one launch (start us, length us, event | category | flops | bytes accessed | tf_op | source)
XLA Modules:
  0.0 374.0 jit_solution(1901322336474052650)
XLA Ops:
  1.0 4.1 %collective-permute-start = (bf16[128,512]{1,0:T(8,128)(2,1)S(1)}, bf16[128,512]{1,0:T(8,128)(2,1)S(1)}, u32[]{:S(2)}, u32[]{:S(2)}) collective-permute-start(bf16[128,512]{1,0:T(8,128)(2,1)S(1)} %get-tuple-element.11), channel_id=1, source_target_pairs={{0,4},{4,0},{1,5},{5,1},{2,6},{6,2},{3,7},{7,3},{8,12},{12,8},{9,1... | collective-permute-start | bytes 393224 | tf_op jit(solution)/shard_map/ppermute | solution.py:227
  6.7 2.9 shard_map.64.rest_0_.mine.own_cols
  9.7 4.6 %shard_map.65.rest_0_.mine.own_cols = bf16[256,1024]{1,0:T(8,128)(2,1)} custom-call(bf16[1024,1024]{1,0:T(8,128)(2,1)S(1)} %copy-done.12, bf16[1,4,1024,1024]{3,2,1,0:T(8,128)(2,1)} %t_rows.33, bf16[1,4,1024,1024]{3,2,1,0:T(8,128)(2,1)} %t_rows.33, bf16[1024,1024]{1,0:T(8,128)(2,1)S(1)} %copy-done.12, bf16[256,1024]{1,0:T(8,128)(2,1)S(1)} %shard_map.64.rest_0_.mine.own_cols), custom_call_target="tpu_custom_call" | custom-call | flops 1073741824 | bytes 5767168 | tf_op jit(solution)/shard_map/pallas_call | solution.py:32
  14.4 2.9 collective-permute-start.2
  17.3 3.8 %shard_map.66.rest_0_.mine.own_cols = bf16[256,1024]{1,0:T(8,128)(2,1)S(1)} custom-call(bf16[1024,1024]{1,0:T(8,128)(2,1)S(1)} %copy-done.12, bf16[1,4,1024,1024]{3,2,1,0:T(8,128)(2,1)} %t_rows.33, bf16[1,4,1024,1024]{3,2,1,0:T(8,128)(2,1)} %t_rows.33, bf16[1024,1024]{1,0:T(8,128)(2,1)S(1)} %copy-done.12, bf16[256,1024]{1,0:T(8,128)(2,1)} %shard_map.65.rest_0_.mine.own_cols), custom_call_target="tpu_custom_call" | custom-call | flops 1073741824 | bytes 5767168 | tf_op jit(solution)/shard_map/pallas_call | solution.py:32
  22.4 23.6 %collective-permute-start.3 = (bf16[2,128,512]{2,1,0:T(8,128)(2,1)S(1)}, bf16[2,128,512]{2,1,0:T(8,128)(2,1)S(1)}, u32[]{:S(2)}, u32[]{:S(2)}) collective-permute-start(bf16[2,128,512]{2,1,0:T(8,128)(2,1)S(1)} %bitcast.54), channel_id=1, source_target_pairs={{0,2},{1,3},{2,0},{3,1},{4,6},{5,7},{6,4},{7,5},{8,10},{9,11},{10,... | collective-permute-start | bytes 786440 | tf_op jit(solution)/shard_map/ppermute | solution.py:235
  46.1 13.0 %collective-permute-done.1.rest_2_.theirs = bf16[256,1024]{1,0:T(8,128)(2,1)} collective-permute-done((bf16[256,1024]{1,0:T(8,128)(2,1)S(1)}, bf16[256,1024]{1,0:T(8,128)(2,1)}, u32[]{:S(2)}, u32[]{:S(2)}) %collective-permute-start.1) | collective-permute-done | bytes 524320 | tf_op jit(solution)/shard_map/ppermute | solution.py:223
  59.1 3.8 %shard_map.68.rest_0_.mine.own_cols = bf16[256,1024]{1,0:T(8,128)(2,1)S(1)} custom-call(bf16[1024,1024]{1,0:T(8,128)(2,1)S(1)} %copy-done.13, bf16[1,4,1024,1024]{3,2,1,0:T(8,128)(2,1)} %t_rows.33, bf16[1,4,1024,1024]{3,2,1,0:T(8,128)(2,1)} %t_rows.33, bf16[1024,1024]{1,0:T(8,128)(2,1)S(1)} %copy-done.13, ...), custom_call_target="tpu_custom_call" | custom-call | flops 1073741824 | bytes 5767168 | tf_op jit(solution)/shard_map/pallas_call | solution.py:32
  62.9 18.5 %collective-permute-done.2.rest_2_.theirs = bf16[256,1024]{1,0:T(8,128)(2,1)} collective-permute-done((bf16[256,1024]{1,0:T(8,128)(2,1)}, bf16[256,1024]{1,0:T(8,128)(2,1)}, u32[]{:S(2)}, u32[]{:S(2)}) %collective-permute-start.2) | collective-permute-done | bytes 524320 | tf_op jit(solution)/shard_map/ppermute | solution.py:223
  81.5 3.8 %shard_map.69.rest_0_.mine.own_cols = bf16[256,1024]{1,0:T(8,128)(2,1)S(1)} custom-call(bf16[1024,1024]{1,0:T(8,128)(2,1)S(1)} %copy-done.13, bf16[1,4,1024,1024]{3,2,1,0:T(8,128)(2,1)} %t_rows.33, bf16[1,4,1024,1024]{3,2,1,0:T(8,128)(2,1)} %t_rows.33, bf16[1024,1024]{1,0:T(8,128)(2,1)S(1)} %copy-done.13, ...), custom_call_target="tpu_custom_call" | custom-call | flops 1073741824 | bytes 5767168 | tf_op jit(solution)/shard_map/pallas_call | solution.py:32
  88.6 15.4 %collective-permute-done.4.rest_2_.theirs = bf16[256,1024]{1,0:T(8,128)(2,1)} collective-permute-done((bf16[256,1024]{1,0:T(8,128)(2,1)S(1)}, bf16[256,1024]{1,0:T(8,128)(2,1)}, u32[]{:S(2)}, u32[]{:S(2)}) %collective-permute-start.4) | collective-permute-done | bytes 524320 | tf_op jit(solution)/shard_map/ppermute | solution.py:223
  104.0 3.8 %shard_map.71.rest_0_.mine.own_cols = bf16[256,1024]{1,0:T(8,128)(2,1)S(1)} custom-call(bf16[1024,1024]{1,0:T(8,128)(2,1)S(1)} %copy-done.13, bf16[1,4,1024,1024]{3,2,1,0:T(8,128)(2,1)} %t_rows.33, bf16[1,4,1024,1024]{3,2,1,0:T(8,128)(2,1)} %t_rows.33, bf16[1024,1024]{1,0:T(8,128)(2,1)S(1)} %copy-done.13, ...), custom_call_target="tpu_custom_call" | custom-call | flops 1073741824 | bytes 5767168 | tf_op jit(solution)/shard_map/pallas_call | solution.py:32
  107.8 7.3 %collective-permute-done.5.rest_2_.theirs = bf16[256,1024]{1,0:T(8,128)(2,1)S(1)} collective-permute-done((bf16[256,1024]{1,0:T(8,128)(2,1)S(1)}, bf16[256,1024]{1,0:T(8,128)(2,1)S(1)}, u32[]{:S(2)}, u32[]{:S(2)}) %collective-permute-start.5) | collective-permute-done | bytes 524320 | tf_op jit(solution)/shard_map/ppermute | solution.py:223
  116.8 2.0 copy-done
  121.1 3.8 %shard_map.73.rest_0_.mine.own_cols = bf16[256,1024]{1,0:T(8,128)(2,1)S(1)} custom-call(bf16[1024,1024]{1,0:T(8,128)(2,1)S(1)} %copy-done.13, bf16[1,4,1024,1024]{3,2,1,0:T(8,128)(2,1)} %t_rows.33, bf16[1,4,1024,1024]{3,2,1,0:T(8,128)(2,1)} %t_rows.33, bf16[1024,1024]{1,0:T(8,128)(2,1)S(1)} %copy-done.13, ...), custom_call_target="tpu_custom_call" | custom-call | flops 1073741824 | bytes 5767168 | tf_op jit(solution)/shard_map/pallas_call | solution.py:32
  125.0 12.6 %collective-permute-done.7.rest_2_.theirs = bf16[256,1024]{1,0:T(8,128)(2,1)S(1)} collective-permute-done((bf16[256,1024]{1,0:T(8,128)(2,1)S(1)}, bf16[256,1024]{1,0:T(8,128)(2,1)S(1)}, u32[]{:S(2)}, u32[]{:S(2)}) %collective-permute-start.7) | collective-permute-done | bytes 524320 | tf_op jit(solution)/shard_map/ppermute | solution.py:223
  139.7 2.0 copy-done.2
  141.7 4.6 %shard_map.75.rest_0_.mine.own_cols = bf16[256,1024]{1,0:T(8,128)(2,1)} custom-call(bf16[1024,1024]{1,0:T(8,128)(2,1)S(1)} %copy-done.13, bf16[1,4,1024,1024]{3,2,1,0:T(8,128)(2,1)} %t_rows.33, bf16[1,4,1024,1024]{3,2,1,0:T(8,128)(2,1)} %t_rows.33, bf16[1024,1024]{1,0:T(8,128)(2,1)S(1)} %copy-done.13, bf16[256,1024]{1,0:T(8,128)(2,1)S(1)} %shard_map.73.rest_0_.mine.own_cols, ...), custom_call_target="tpu_custom_call" | custom-call | flops 1073741824 | bytes 5767168 | tf_op jit(solution)/shard_map/pallas_call | solution.py:32
  146.3 2.5 collective-permute-start.14
  148.8 11.3 %collective-permute-done.9.rest_2_.theirs = bf16[256,1024]{1,0:T(8,128)(2,1)S(1)} collective-permute-done((bf16[256,1024]{1,0:T(8,128)(2,1)S(1)}, bf16[256,1024]{1,0:T(8,128)(2,1)S(1)}, u32[]{:S(2)}, u32[]{:S(2)}) %collective-permute-start.9) | collective-permute-done | bytes 524320 | tf_op jit(solution)/shard_map/ppermute | solution.py:223
  161.5 2.2 copy-done.3
  164.3 2.0 copy-done.4
  167.0 2.6 collective-permute-start.16
  169.6 3.8 %shard_map.77.rest_0_.mine.own_cols = bf16[256,1024]{1,0:T(8,128)(2,1)S(1)} custom-call(bf16[1024,1024]{1,0:T(8,128)(2,1)S(1)} %copy-done.13, bf16[1,4,1024,1024]{3,2,1,0:T(8,128)(2,1)} %t_rows.33, bf16[1,4,1024,1024]{3,2,1,0:T(8,128)(2,1)} %t_rows.33, bf16[1024,1024]{1,0:T(8,128)(2,1)S(1)} %copy-done.13, bf16[256,1024]{1,0:T(8,128)(2,1)} %shard_map.75.rest_0_.mine.own_cols, ...), custom_call_target="tpu_custom_call" | custom-call | flops 1073741824 | bytes 5767168 | tf_op jit(solution)/shard_map/pallas_call | solution.py:32
  173.4 9.1 %collective-permute-done.12.rest_2_.theirs = bf16[256,1024]{1,0:T(8,128)(2,1)S(1)} collective-permute-done((bf16[256,1024]{1,0:T(8,128)(2,1)S(1)}, bf16[256,1024]{1,0:T(8,128)(2,1)S(1)}, u32[]{:S(2)}, u32[]{:S(2)}) %collective-permute-start.12) | collective-permute-done | bytes 524320 | tf_op jit(solution)/shard_map/ppermute | solution.py:223
  186.3 2.2 copy-done.5
  191.2 2.0 copy-done.6
  193.2 3.8 %shard_map.80.rest_0_.mine.own_cols = bf16[256,1024]{1,0:T(8,128)(2,1)S(1)} custom-call(bf16[1024,1024]{1,0:T(8,128)(2,1)S(1)} %copy-done.13, bf16[1,4,1024,1024]{3,2,1,0:T(8,128)(2,1)} %t_rows.33, bf16[1,4,1024,1024]{3,2,1,0:T(8,128)(2,1)} %t_rows.33, bf16[1024,1024]{1,0:T(8,128)(2,1)S(1)} %copy-done.13, ...), custom_call_target="tpu_custom_call" | custom-call | flops 1073741824 | bytes 5767168 | tf_op jit(solution)/shard_map/pallas_call | solution.py:32
  196.9 3.0 collective-permute-start.18
  199.9 2.2 copy-done.7
  205.4 2.0 copy-done.8
  207.4 8.9 %collective-permute-done.15.rest_2_.theirs = bf16[256,1024]{1,0:T(8,128)(2,1)} collective-permute-done((bf16[256,1024]{1,0:T(8,128)(2,1)}, bf16[256,1024]{1,0:T(8,128)(2,1)}, u32[]{:S(2)}, u32[]{:S(2)}) %collective-permute-start.15) | collective-permute-done | bytes 524320 | tf_op jit(solution)/shard_map/ppermute | solution.py:223
  216.3 3.9 %shard_map.83.rest_0_.mine.own_cols = bf16[256,1024]{1,0:T(8,128)(2,1)S(1)} custom-call(bf16[1024,1024]{1,0:T(8,128)(2,1)S(1)} %copy-done.13, bf16[1,4,1024,1024]{3,2,1,0:T(8,128)(2,1)} %t_rows.33, bf16[1,4,1024,1024]{3,2,1,0:T(8,128)(2,1)} %t_rows.33, bf16[1024,1024]{1,0:T(8,128)(2,1)S(1)} %copy-done.13, ...), custom_call_target="tpu_custom_call" | custom-call | flops 1073741824 | bytes 5767168 | tf_op jit(solution)/shard_map/pallas_call | solution.py:32
  222.0 2.0 copy-done.10
  224.0 5.0 %shard_map.85.rest_1_ = bf16[1,4,1024,1024]{3,2,1,0:T(8,128)(2,1)} custom-call(f32[2]{0:T(128)S(1)} %pad_maximum_fusion.1.energies, bf16[256,1024]{1,0:T(8,128)(2,1)S(1)} %copy-done.23, bf16[256,1024]{1,0:T(8,128)(2,1)S(1)} %copy-done.23, bf16[256,1024]{1,0:T(8,128)(2,1)} %collective-permute-done.1.rest_2_.theirs, bf16[2,1024,1024]{2,1,0:T(8,128)(2,1)} %bitcast.20, ...), custom_call_target="tpu_custom_call" | custom-call | flops 1073741824 | bytes 5767168 | tf_op jit(solution)/shard_map/pallas_call | solution.py:64
  228.9 5.3 %shard_map.86.rest_1_ = bf16[1,4,1024,1024]{3,2,1,0:T(8,128)(2,1)} custom-call(f32[2]{0:T(128)S(1)} %pad_maximum_fusion.1.energies, bf16[256,1024]{1,0:T(8,128)(2,1)} %shard_map.65.rest_0_.mine.own_cols, bf16[256,1024]{1,0:T(8,128)(2,1)} %shard_map.65.rest_0_.mine.own_cols, ...), custom_call_target="tpu_custom_call", output_to_operand_aliasing={{}: (9, {})} | custom-call | flops 1073741824 | bytes 5767168 | tf_op jit(solution)/shard_map/pallas_call | solution.py:64
  234.2 4.5 %collective-permute-done.17.rest_2_.theirs = bf16[256,1024]{1,0:T(8,128)(2,1)} collective-permute-done((bf16[256,1024]{1,0:T(8,128)(2,1)S(1)}, bf16[256,1024]{1,0:T(8,128)(2,1)}, u32[]{:S(2)}, u32[]{:S(2)}) %collective-permute-start.17) | collective-permute-done | bytes 524320 | tf_op jit(solution)/shard_map/ppermute | solution.py:223
  238.8 3.8 %shard_map.87.rest_0_.mine.own_cols = bf16[256,1024]{1,0:T(8,128)(2,1)S(1)} custom-call(bf16[1024,1024]{1,0:T(8,128)(2,1)S(1)} %copy-done.13, bf16[1,4,1024,1024]{3,2,1,0:T(8,128)(2,1)} %t_rows.33, bf16[1,4,1024,1024]{3,2,1,0:T(8,128)(2,1)} %t_rows.33, bf16[1024,1024]{1,0:T(8,128)(2,1)S(1)} %copy-done.13, ...), custom_call_target="tpu_custom_call" | custom-call | flops 1073741824 | bytes 5767168 | tf_op jit(solution)/shard_map/pallas_call | solution.py:32
  242.7 5.1 %shard_map.88.rest_1_ = bf16[1,4,1024,1024]{3,2,1,0:T(8,128)(2,1)} custom-call(f32[2]{0:T(128)S(1)} %pad_maximum_fusion.1.energies, bf16[256,1024]{1,0:T(8,128)(2,1)S(1)} %copy-done.19, bf16[256,1024]{1,0:T(8,128)(2,1)S(1)} %copy-done.19, bf16[256,1024]{1,0:T(8,128)(2,1)} %collective-permute-done.4.rest_2_.theirs, ...), custom_call_target="tpu_custom_call", output_to_operand_aliasing={{}: (9, {})} | custom-call | flops 1073741824 | bytes 5767168 | tf_op jit(solution)/shard_map/pallas_call | solution.py:64
  247.7 4.8 %shard_map.89.rest_1_ = bf16[1,4,1024,1024]{3,2,1,0:T(8,128)(2,1)} custom-call(f32[2]{0:T(128)S(1)} %pad_maximum_fusion.1.energies, bf16[256,1024]{1,0:T(8,128)(2,1)S(1)} %copy-done.25, bf16[256,1024]{1,0:T(8,128)(2,1)S(1)} %copy-done.25, bf16[256,1024]{1,0:T(8,128)(2,1)S(1)} %copy-done.27, ...), custom_call_target="tpu_custom_call", output_to_operand_aliasing={{}: (9, {})} | custom-call | flops 1073741824 | bytes 5767168 | tf_op jit(solution)/shard_map/pallas_call | solution.py:64
  252.6 8.6 %collective-permute-done.18.rest_2_.theirs = bf16[256,1024]{1,0:T(8,128)(2,1)S(1)} collective-permute-done((bf16[256,1024]{1,0:T(8,128)(2,1)S(1)}, bf16[256,1024]{1,0:T(8,128)(2,1)S(1)}, u32[]{:S(2)}, u32[]{:S(2)}) %collective-permute-start.18) | collective-permute-done | bytes 524320 | tf_op jit(solution)/shard_map/ppermute | solution.py:223
  261.2 3.8 %shard_map.90.rest_0_.mine.own_cols = bf16[256,1024]{1,0:T(8,128)(2,1)S(1)} custom-call(bf16[1024,1024]{1,0:T(8,128)(2,1)S(1)} %copy-done.13, bf16[1,4,1024,1024]{3,2,1,0:T(8,128)(2,1)} %t_rows.33, bf16[1,4,1024,1024]{3,2,1,0:T(8,128)(2,1)} %t_rows.33, bf16[1024,1024]{1,0:T(8,128)(2,1)S(1)} %copy-done.13, ...), custom_call_target="tpu_custom_call" | custom-call | flops 1073741824 | bytes 5767168 | tf_op jit(solution)/shard_map/pallas_call | solution.py:32
  265.1 4.9 %shard_map.91.rest_1_ = bf16[1,4,1024,1024]{3,2,1,0:T(8,128)(2,1)} custom-call(f32[2]{0:T(128)S(1)} %pad_maximum_fusion.2.energies, bf16[256,1024]{1,0:T(8,128)(2,1)S(1)} %copy-done.15, bf16[256,1024]{1,0:T(8,128)(2,1)S(1)} %copy-done.15, bf16[256,1024]{1,0:T(8,128)(2,1)S(1)} %copy-done.29, ...), custom_call_target="tpu_custom_call", output_to_operand_aliasing={{}: (9, {})} | custom-call | flops 1073741824 | bytes 5767168 | tf_op jit(solution)/shard_map/pallas_call | solution.py:64
  270.0 4.8 %shard_map.92.rest_1_ = bf16[1,4,1024,1024]{3,2,1,0:T(8,128)(2,1)} custom-call(f32[2]{0:T(128)S(1)} %pad_maximum_fusion.2.energies, bf16[256,1024]{1,0:T(8,128)(2,1)S(1)} %copy-done.21, bf16[256,1024]{1,0:T(8,128)(2,1)S(1)} %copy-done.21, bf16[256,1024]{1,0:T(8,128)(2,1)S(1)} %copy-done.31, ...), custom_call_target="tpu_custom_call", output_to_operand_aliasing={{}: (9, {})} | custom-call | flops 1073741824 | bytes 5767168 | tf_op jit(solution)/shard_map/pallas_call | solution.py:64
  274.8 8.8 %collective-permute-done.19.rest_2_.theirs = bf16[256,1024]{1,0:T(8,128)(2,1)S(1)} collective-permute-done((bf16[256,1024]{1,0:T(8,128)(2,1)S(1)}, bf16[256,1024]{1,0:T(8,128)(2,1)S(1)}, u32[]{:S(2)}, u32[]{:S(2)}) %collective-permute-start.19) | collective-permute-done | bytes 524320 | tf_op jit(solution)/shard_map/ppermute | solution.py:223
  283.6 3.8 %shard_map.93.rest_0_.mine.own_cols = bf16[256,1024]{1,0:T(8,128)(2,1)S(1)} custom-call(bf16[1024,1024]{1,0:T(8,128)(2,1)S(1)} %copy-done.13, bf16[1,4,1024,1024]{3,2,1,0:T(8,128)(2,1)} %t_rows.33, bf16[1,4,1024,1024]{3,2,1,0:T(8,128)(2,1)} %t_rows.33, bf16[1024,1024]{1,0:T(8,128)(2,1)S(1)} %copy-done.13, ...), custom_call_target="tpu_custom_call" | custom-call | flops 1073741824 | bytes 5767168 | tf_op jit(solution)/shard_map/pallas_call | solution.py:32
  287.5 4.8 %shard_map.94.rest_1_ = bf16[1,4,1024,1024]{3,2,1,0:T(8,128)(2,1)} custom-call(f32[2]{0:T(128)S(1)} %pad_maximum_fusion.2.energies, bf16[256,1024]{1,0:T(8,128)(2,1)S(1)} %copy-done.17, bf16[256,1024]{1,0:T(8,128)(2,1)S(1)} %copy-done.17, bf16[256,1024]{1,0:T(8,128)(2,1)S(1)} %copy-done.34, ...), custom_call_target="tpu_custom_call", output_to_operand_aliasing={{}: (9, {})} | custom-call | flops 1073741824 | bytes 5767168 | tf_op jit(solution)/shard_map/pallas_call | solution.py:64
  292.3 5.3 %shard_map.95.rest_1_ = bf16[1,4,1024,1024]{3,2,1,0:T(8,128)(2,1)} custom-call(f32[2]{0:T(128)S(1)} %pad_maximum_fusion.2.energies, bf16[256,1024]{1,0:T(8,128)(2,1)} %shard_map.75.rest_0_.mine.own_cols, bf16[256,1024]{1,0:T(8,128)(2,1)} %shard_map.75.rest_0_.mine.own_cols, ...), custom_call_target="tpu_custom_call", output_to_operand_aliasing={{}: (9, {})} | custom-call | flops 1073741824 | bytes 5767168 | tf_op jit(solution)/shard_map/pallas_call | solution.py:64
  297.6 8.5 %collective-permute-done.20.rest_2_.theirs = bf16[256,1024]{1,0:T(8,128)(2,1)S(1)} collective-permute-done((bf16[256,1024]{1,0:T(8,128)(2,1)S(1)}, bf16[256,1024]{1,0:T(8,128)(2,1)S(1)}, u32[]{:S(2)}, u32[]{:S(2)}) %collective-permute-start.20) | collective-permute-done | bytes 524320 | tf_op jit(solution)/shard_map/ppermute | solution.py:223
  306.1 3.8 %shard_map.96.rest_0_.mine.own_cols = bf16[256,1024]{1,0:T(8,128)(2,1)S(1)} custom-call(bf16[1024,1024]{1,0:T(8,128)(2,1)S(1)} %copy-done.13, bf16[1,4,1024,1024]{3,2,1,0:T(8,128)(2,1)} %t_rows.33, bf16[1,4,1024,1024]{3,2,1,0:T(8,128)(2,1)} %t_rows.33, bf16[1024,1024]{1,0:T(8,128)(2,1)S(1)} %copy-done.13, ...), custom_call_target="tpu_custom_call" | custom-call | flops 1073741824 | bytes 5767168 | tf_op jit(solution)/shard_map/pallas_call | solution.py:32
  309.9 5.0 %shard_map.97.rest_1_ = bf16[1,4,1024,1024]{3,2,1,0:T(8,128)(2,1)} custom-call(f32[2]{0:T(128)S(1)} %pad_maximum_fusion.3.energies, bf16[256,1024]{1,0:T(8,128)(2,1)S(1)} %shard_map.77.rest_0_.mine.own_cols, bf16[256,1024]{1,0:T(8,128)(2,1)S(1)} %shard_map.77.rest_0_.mine.own_cols, ...), custom_call_target="tpu_custom_call", output_to_operand_aliasing={{}: (9, {})} | custom-call | flops 1073741824 | bytes 5767168 | tf_op jit(solution)/shard_map/pallas_call | solution.py:64
  314.9 4.8 %shard_map.98.rest_1_ = bf16[1,4,1024,1024]{3,2,1,0:T(8,128)(2,1)} custom-call(f32[2]{0:T(128)S(1)} %pad_maximum_fusion.3.energies, bf16[256,1024]{1,0:T(8,128)(2,1)S(1)} %shard_map.80.rest_0_.mine.own_cols, bf16[256,1024]{1,0:T(8,128)(2,1)S(1)} %shard_map.80.rest_0_.mine.own_cols, ...), custom_call_target="tpu_custom_call", output_to_operand_aliasing={{}: (9, {})} | custom-call | flops 1073741824 | bytes 5767168 | tf_op jit(solution)/shard_map/pallas_call | solution.py:64
  319.7 8.8 %collective-permute-done.21.rest_2_.theirs = bf16[256,1024]{1,0:T(8,128)(2,1)S(1)} collective-permute-done((bf16[256,1024]{1,0:T(8,128)(2,1)S(1)}, bf16[256,1024]{1,0:T(8,128)(2,1)S(1)}, u32[]{:S(2)}, u32[]{:S(2)}) %collective-permute-start.21) | collective-permute-done | bytes 524320 | tf_op jit(solution)/shard_map/ppermute | solution.py:223
  328.6 3.6 shard_map.99.rest_0_.mine.own_cols
  332.3 3.4 shard_map.100.rest_1_
  335.6 3.4 shard_map.101.rest_1_
  339.0 6.5 %collective-permute-done.22.rest_2_.theirs = bf16[256,1024]{1,0:T(8,128)(2,1)} collective-permute-done((bf16[256,1024]{1,0:T(8,128)(2,1)S(1)}, bf16[256,1024]{1,0:T(8,128)(2,1)}, u32[]{:S(2)}, u32[]{:S(2)}) %collective-permute-start.22) | collective-permute-done | bytes 524320 | tf_op jit(solution)/shard_map/ppermute | solution.py:223
  345.5 3.4 shard_map.102.mine.rest_0_
  349.0 3.4 shard_map.104.rest_1_
  353.9 3.9 %shard_map.105.rest_1_ = bf16[1,4,1024,1024]{3,2,1,0:T(8,128)(2,1)} custom-call(f32[2]{0:T(128)S(1)} %pad_maximum_fusion.energies, bf16[256,1024]{1,0:T(8,128)(2,1)S(1)} %shard_map.93.rest_0_.mine.own_cols, bf16[256,1024]{1,0:T(8,128)(2,1)S(1)} %shard_map.93.rest_0_.mine.own_cols, ...), custom_call_target="tpu_custom_call", output_to_operand_aliasing={{}: (9, {})} | custom-call | flops 1073741824 | bytes 5767168 | tf_op jit(solution)/shard_map/pallas_call | solution.py:64
  357.8 4.5 %collective-permute-done.25.theirs = bf16[256,1024]{1,0:T(8,128)(2,1)S(1)} collective-permute-done((bf16[256,1024]{1,0:T(8,128)(2,1)S(1)}, bf16[256,1024]{1,0:T(8,128)(2,1)S(1)}, u32[]{:S(2)}, u32[]{:S(2)}) %collective-permute-start.25) | collective-permute-done | bytes 524320 | tf_op jit(solution)/shard_map/ppermute | solution.py:223
  362.3 3.4 shard_map.106.rest_1_
  365.6 2.3 collective-permute-done.24.theirs
  367.9 3.3 shard_map.107._
  (142 shorter events, 32.4 us)
Async XLA Ops:
  1.0 21.4 %collective-permute-start = (bf16[128,512]{1,0:T(8,128)(2,1)S(1)}, bf16[128,512]{1,0:T(8,128)(2,1)S(1)}, u32[]{:S(2)}, u32[]{:S(2)}) collective-permute-start(bf16[128,512]{1,0:T(8,128)(2,1)S(1)} %get-tuple-element.11), channel_id=1, source_target_pairs={{0,4},{4,0},{1,5},{5,1},{2,6},{6,2},{3,7},{7,3},{8,12},{12,8},{9,1... | collective-permute-start | bytes 393224 | tf_op jit(solution)/shard_map/ppermute | solution.py:227
  9.6 4.7 %copy-start.22 = (bf16[256,1024]{1,0:T(8,128)(2,1)}, bf16[256,1024]{1,0:T(8,128)(2,1)S(1)}, u32[]{:S(2)}) copy-start(bf16[256,1024]{1,0:T(8,128)(2,1)S(1)} %shard_map.64.rest_0_.mine.own_cols) | copy-start | bytes 1572868
  9.6 49.4 %collective-permute-start.1 = (bf16[256,1024]{1,0:T(8,128)(2,1)S(1)}, bf16[256,1024]{1,0:T(8,128)(2,1)}, u32[]{:S(2)}, u32[]{:S(2)}) collective-permute-start(bf16[256,1024]{1,0:T(8,128)(2,1)S(1)} %shard_map.64.rest_0_.mine.own_cols), channel_id=1, source_target_pairs={{0,4},{4,0},{1,5},{5,1},{2,6},{6,2},{3,7},{7,3},{8,12},{12,8},{9,1... | collective-permute-start | bytes 1572872 | tf_op jit(solution)/shard_map/ppermute | solution.py:223
  14.4 7.2 %copy-start.44 = (f32[2]{0:T(128)S(1)}, f32[2]{0:T(128)}, u32[]{:S(2)}) copy-start(f32[2]{0:T(128)} %param.9) | copy-start | bytes 28
  14.4 7.8 %copy-start.45 = (f32[16]{0:T(128)S(1)}, f32[16]{0:T(128)}, u32[]{:S(2)}) copy-start(f32[16]{0:T(128)} %param.10) | copy-start | bytes 196
  14.4 44.7 %copy-start.13 = (bf16[1024,1024]{1,0:T(8,128)(2,1)S(1)}, bf16[1024,1024]{1,0:T(8,128)(2,1)}, u32[]{:S(2)}) copy-start(bf16[1024,1024]{1,0:T(8,128)(2,1)} %f_cols.33) | copy-start | bytes 6291460
  14.4 67.1 %collective-permute-start.2 = (bf16[256,1024]{1,0:T(8,128)(2,1)}, bf16[256,1024]{1,0:T(8,128)(2,1)}, u32[]{:S(2)}, u32[]{:S(2)}) collective-permute-start(bf16[256,1024]{1,0:T(8,128)(2,1)} %shard_map.65.rest_0_.mine.own_cols), channel_id=1, source_target_pairs={{0,4},{4,0},{1,5},{5,1},{2,6},{6,2},{3,7},{7,3},{8,12},{12,8},{9,1... | collective-permute-start | bytes 1572872 | tf_op jit(solution)/shard_map/ppermute | solution.py:223
  21.0 41.8 %copy-start.18 = (bf16[256,1024]{1,0:T(8,128)(2,1)}, bf16[256,1024]{1,0:T(8,128)(2,1)S(1)}, u32[]{:S(2)}) copy-start(bf16[256,1024]{1,0:T(8,128)(2,1)S(1)} %shard_map.66.rest_0_.mine.own_cols) | copy-start | bytes 1572868
  21.0 82.9 %collective-permute-start.4 = (bf16[256,1024]{1,0:T(8,128)(2,1)S(1)}, bf16[256,1024]{1,0:T(8,128)(2,1)}, u32[]{:S(2)}, u32[]{:S(2)}) collective-permute-start(bf16[256,1024]{1,0:T(8,128)(2,1)S(1)} %shard_map.66.rest_0_.mine.own_cols), channel_id=1, source_target_pairs={{0,4},{4,0},{1,5},{5,1},{2,6},{6,2},{3,7},{7,3},{8,12},{12,8},{9,1... | collective-permute-start | bytes 1572872 | tf_op jit(solution)/shard_map/ppermute | solution.py:223
  22.4 62.9 %collective-permute-start.3 = (bf16[2,128,512]{2,1,0:T(8,128)(2,1)S(1)}, bf16[2,128,512]{2,1,0:T(8,128)(2,1)S(1)}, u32[]{:S(2)}, u32[]{:S(2)}) collective-permute-start(bf16[2,128,512]{2,1,0:T(8,128)(2,1)S(1)} %bitcast.54), channel_id=1, source_target_pairs={{0,2},{1,3},{2,0},{3,1},{4,6},{5,7},{6,4},{7,5},{8,10},{9,11},{10,... | collective-permute-start | bytes 786440 | tf_op jit(solution)/shard_map/ppermute | solution.py:235
  62.9 22.4 %copy-start.24 = (bf16[256,1024]{1,0:T(8,128)(2,1)}, bf16[256,1024]{1,0:T(8,128)(2,1)S(1)}, u32[]{:S(2)}) copy-start(bf16[256,1024]{1,0:T(8,128)(2,1)S(1)} %shard_map.68.rest_0_.mine.own_cols) | copy-start | bytes 1572868
  62.9 52.2 %collective-permute-start.5 = (bf16[256,1024]{1,0:T(8,128)(2,1)S(1)}, bf16[256,1024]{1,0:T(8,128)(2,1)S(1)}, u32[]{:S(2)}, u32[]{:S(2)}) collective-permute-start(bf16[256,1024]{1,0:T(8,128)(2,1)S(1)} %shard_map.68.rest_0_.mine.own_cols), channel_id=1, source_target_pairs={{0,4},{4,0},{1,5},{5,1},{2,6},{6,2},{3,7},{7,3},{8,12},{12,8},{9,1... | collective-permute-start | bytes 1572872 | tf_op jit(solution)/shard_map/ppermute | solution.py:223
  85.3 22.5 %copy-start.14 = (bf16[256,1024]{1,0:T(8,128)(2,1)}, bf16[256,1024]{1,0:T(8,128)(2,1)S(1)}, u32[]{:S(2)}) copy-start(bf16[256,1024]{1,0:T(8,128)(2,1)S(1)} %shard_map.69.rest_0_.mine.own_cols) | copy-start | bytes 1572868
  86.2 32.6 %collective-permute-start.6 = (bf16[4,128,512]{2,1,0:T(8,128)(2,1)}, bf16[4,128,512]{2,1,0:T(8,128)(2,1)S(1)}, u32[]{:S(2)}, u32[]{:S(2)}) collective-permute-start(bf16[4,128,512]{2,1,0:T(8,128)(2,1)} %bitcast.5.rest_1_.block), channel_id=1, source_target_pairs={{0,1},{1,0},{2,3},{3,2},{8,9},{9,8},{10,11},{11,10},{16,17},{17,16... | collective-permute-start | bytes 1572872 | tf_op jit(solution)/shard_map/ppermute | solution.py:251
  87.8 49.8 %collective-permute-start.7 = (bf16[256,1024]{1,0:T(8,128)(2,1)S(1)}, bf16[256,1024]{1,0:T(8,128)(2,1)S(1)}, u32[]{:S(2)}, u32[]{:S(2)}) collective-permute-start(bf16[256,1024]{1,0:T(8,128)(2,1)S(1)} %shard_map.69.rest_0_.mine.own_cols), channel_id=1, source_target_pairs={{0,4},{4,0},{1,5},{5,1},{2,6},{6,2},{3,7},{7,3},{8,12},{12,8},{9,1... | collective-permute-start | bytes 1572872 | tf_op jit(solution)/shard_map/ppermute | solution.py:223
  88.6 57.7 %collective-permute-start.8 = (bf16[4,128,512]{2,1,0:T(8,128)(2,1)}, bf16[4,128,512]{2,1,0:T(8,128)(2,1)S(1)}, u32[]{:S(2)}, u32[]{:S(2)}) collective-permute-start(bf16[4,128,512]{2,1,0:T(8,128)(2,1)} %bitcast.5.rest_1_.block), channel_id=1, source_target_pairs={{0,8},{1,9},{2,10},{3,11},{8,0},{9,1},{10,2},{11,3},{16,24},{17,25... | collective-permute-start | bytes 1572872 | tf_op jit(solution)/shard_map/ppermute | solution.py:251
  104.0 56.1 %collective-permute-start.11 = (bf16[4,128,512]{2,1,0:T(8,128)(2,1)}, bf16[4,128,512]{2,1,0:T(8,128)(2,1)S(1)}, u32[]{:S(2)}, u32[]{:S(2)}) collective-permute-start(bf16[4,128,512]{2,1,0:T(8,128)(2,1)} %bitcast.5.rest_1_.block), channel_id=1, source_target_pairs={{0,9},{1,8},{2,11},{3,10},{8,1},{9,0},{10,3},{11,2},{16,25},{17,24... | collective-permute-start | bytes 1572872 | tf_op jit(solution)/shard_map/ppermute | solution.py:251
  107.7 17.2 %copy-start.20 = (bf16[256,1024]{1,0:T(8,128)(2,1)}, bf16[256,1024]{1,0:T(8,128)(2,1)S(1)}, u32[]{:S(2)}) copy-start(bf16[256,1024]{1,0:T(8,128)(2,1)S(1)} %shard_map.71.rest_0_.mine.own_cols) | copy-start | bytes 1572868
  115.1 9.9 %copy-start.26 = (bf16[256,1024]{1,0:T(8,128)(2,1)}, bf16[256,1024]{1,0:T(8,128)(2,1)S(1)}, u32[]{:S(2)}) copy-start(bf16[256,1024]{1,0:T(8,128)(2,1)S(1)} %collective-permute-done.5.rest_2_.theirs) | copy-start | bytes 1572868
  115.1 44.9 %collective-permute-start.9 = (bf16[256,1024]{1,0:T(8,128)(2,1)S(1)}, bf16[256,1024]{1,0:T(8,128)(2,1)S(1)}, u32[]{:S(2)}, u32[]{:S(2)}) collective-permute-start(bf16[256,1024]{1,0:T(8,128)(2,1)S(1)} %shard_map.71.rest_0_.mine.own_cols), channel_id=1, source_target_pairs={{0,4},{4,0},{1,5},{5,1},{2,6},{6,2},{3,7},{7,3},{8,12},{12,8},{9,1... | collective-permute-start | bytes 1572872 | tf_op jit(solution)/shard_map/ppermute | solution.py:223
  119.6 19.5 %copy-start.1 = (bf16[2,4,2,128,1024]{4,3,2,1,0:T(8,128)(2,1)S(1)}, bf16[2,4,2,128,1024]{4,3,2,1,0:T(8,128)(2,1)}, u32[]{:S(2)}) copy-start(bf16[2,4,2,128,1024]{4,3,2,1,0:T(8,128)(2,1)} %copy-done) | copy-start | bytes 12582916
  119.6 46.6 %collective-permute-start.10 = (bf16[4,128,512]{2,1,0:T(8,128)(2,1)}, bf16[4,128,512]{2,1,0:T(8,128)(2,1)S(1)}, u32[]{:S(2)}, u32[]{:S(2)}) collective-permute-start(bf16[4,128,512]{2,1,0:T(8,128)(2,1)} %bitcast.5.rest_1_.block), channel_id=1, source_target_pairs={{0,16},{1,17},{2,18},{3,19},{8,24},{9,25},{10,26},{11,27},{16,0},{... | collective-permute-start | bytes 1572872 | tf_op jit(solution)/shard_map/ppermute | solution.py:251
  121.1 18.0 %copy-start.43 = (bf16[4,128,512]{2,1,0:T(8,128)(2,1)S(1)}, bf16[4,128,512]{2,1,0:T(8,128)(2,1)}, u32[]{:S(2)}) copy-start(bf16[4,128,512]{2,1,0:T(8,128)(2,1)} %copy-done.42) | copy-start | bytes 1572868
  125.0 21.3 %copy-start.16 = (bf16[256,1024]{1,0:T(8,128)(2,1)}, bf16[256,1024]{1,0:T(8,128)(2,1)S(1)}, u32[]{:S(2)}) copy-start(bf16[256,1024]{1,0:T(8,128)(2,1)S(1)} %shard_map.73.rest_0_.mine.own_cols) | copy-start | bytes 1572868
  137.6 8.7 %copy-start.28 = (bf16[256,1024]{1,0:T(8,128)(2,1)}, bf16[256,1024]{1,0:T(8,128)(2,1)S(1)}, u32[]{:S(2)}) copy-start(bf16[256,1024]{1,0:T(8,128)(2,1)S(1)} %collective-permute-done.7.rest_2_.theirs) | copy-start | bytes 1572868
  137.6 44.9 %collective-permute-start.12 = (bf16[256,1024]{1,0:T(8,128)(2,1)S(1)}, bf16[256,1024]{1,0:T(8,128)(2,1)S(1)}, u32[]{:S(2)}, u32[]{:S(2)}) collective-permute-start(bf16[256,1024]{1,0:T(8,128)(2,1)S(1)} %shard_map.73.rest_0_.mine.own_cols), channel_id=1, source_target_pairs={{0,4},{4,0},{1,5},{5,1},{2,6},{6,2},{3,7},{7,3},{8,12},{12,8},{9,1... | collective-permute-start | bytes 1572872 | tf_op jit(solution)/shard_map/ppermute | solution.py:223
  139.7 2.0 copy-start.2
  146.3 50.7 %collective-permute-start.14 = (bf16[4,128,512]{2,1,0:T(8,128)(2,1)}, bf16[4,128,512]{2,1,0:T(8,128)(2,1)}, u32[]{:S(2)}, u32[]{:S(2)}) collective-permute-start(bf16[4,128,512]{2,1,0:T(8,128)(2,1)} %bitcast.5.rest_1_.block), channel_id=1, source_target_pairs={{0,17},{1,16},{2,19},{3,18},{8,25},{9,24},{10,27},{11,26},{16,1},{... | collective-permute-start | bytes 1572872 | tf_op jit(solution)/shard_map/ppermute | solution.py:251
  160.0 13.4 %copy-start.30 = (bf16[256,1024]{1,0:T(8,128)(2,1)}, bf16[256,1024]{1,0:T(8,128)(2,1)S(1)}, u32[]{:S(2)}) copy-start(bf16[256,1024]{1,0:T(8,128)(2,1)S(1)} %collective-permute-done.9.rest_2_.theirs) | copy-start | bytes 1572868
  160.0 43.7 %collective-permute-start.13 = (bf16[4,128,512]{2,1,0:T(8,128)(2,1)}, bf16[4,128,512]{2,1,0:T(8,128)(2,1)}, u32[]{:S(2)}, u32[]{:S(2)}) collective-permute-start(bf16[4,128,512]{2,1,0:T(8,128)(2,1)} %bitcast.5.rest_1_.block), channel_id=1, source_target_pairs={{0,24},{1,25},{2,26},{3,27},{8,16},{9,17},{10,18},{11,19},{16,8},{... | collective-permute-start | bytes 1572872 | tf_op jit(solution)/shard_map/ppermute | solution.py:251
  160.0 13.4 %copy-start.38 = (bf16[4,128,512]{2,1,0:T(8,128)(2,1)}, bf16[4,128,512]{2,1,0:T(8,128)(2,1)S(1)}, u32[]{:S(2)}) copy-start(bf16[4,128,512]{2,1,0:T(8,128)(2,1)S(1)} %collective-permute-done.11.block) | copy-start | bytes 1572868
  160.1 56.3 %collective-permute-start.15 = (bf16[256,1024]{1,0:T(8,128)(2,1)}, bf16[256,1024]{1,0:T(8,128)(2,1)}, u32[]{:S(2)}, u32[]{:S(2)}) collective-permute-start(bf16[256,1024]{1,0:T(8,128)(2,1)} %shard_map.75.rest_0_.mine.own_cols), channel_id=1, source_target_pairs={{0,4},{4,0},{1,5},{5,1},{2,6},{6,2},{3,7},{7,3},{8,12},{12,8},{9,1... | collective-permute-start | bytes 1572872 | tf_op jit(solution)/shard_map/ppermute | solution.py:223
  161.5 2.2 copy-start.3
  164.2 2.0 copy-start.4
  166.3 18.4 %copy-start.37 = (f32[1024]{0:T(1024)S(1)}, f32[1024]{0:T(1024)}, u32[]{:S(2)}) copy-start(f32[1024]{0:T(1024)} %param.11) | copy-start | bytes 12292
  167.0 53.3 %collective-permute-start.16 = (bf16[4,128,512]{2,1,0:T(8,128)(2,1)}, bf16[4,128,512]{2,1,0:T(8,128)(2,1)}, u32[]{:S(2)}, u32[]{:S(2)}) collective-permute-start(bf16[4,128,512]{2,1,0:T(8,128)(2,1)} %bitcast.5.rest_1_.block), channel_id=1, source_target_pairs={{0,25},{1,24},{2,27},{3,26},{8,17},{9,16},{10,19},{11,18},{16,9},{... | collective-permute-start | bytes 1572872 | tf_op jit(solution)/shard_map/ppermute | solution.py:251
  183.3 55.5 %collective-permute-start.17 = (bf16[256,1024]{1,0:T(8,128)(2,1)S(1)}, bf16[256,1024]{1,0:T(8,128)(2,1)}, u32[]{:S(2)}, u32[]{:S(2)}) collective-permute-start(bf16[256,1024]{1,0:T(8,128)(2,1)S(1)} %shard_map.77.rest_0_.mine.own_cols), channel_id=1, source_target_pairs={{0,4},{4,0},{1,5},{5,1},{2,6},{6,2},{3,7},{7,3},{8,12},{12,8},{9,1... | collective-permute-start | bytes 1572872 | tf_op jit(solution)/shard_map/ppermute | solution.py:223
  186.3 2.2 copy-start.5
  189.5 3.6 copy-start.33
  191.1 2.0 copy-start.6
  196.9 64.2 %collective-permute-start.18 = (bf16[256,1024]{1,0:T(8,128)(2,1)S(1)}, bf16[256,1024]{1,0:T(8,128)(2,1)S(1)}, u32[]{:S(2)}, u32[]{:S(2)}) collective-permute-start(bf16[256,1024]{1,0:T(8,128)(2,1)S(1)} %shard_map.80.rest_0_.mine.own_cols), channel_id=1, source_target_pairs={{0,4},{4,0},{1,5},{5,1},{2,6},{6,2},{3,7},{7,3},{8,12},{12,8},{9,1... | collective-permute-start | bytes 1572872 | tf_op jit(solution)/shard_map/ppermute | solution.py:223
  199.9 2.2 copy-start.7
  205.4 2.0 copy-start.8
  216.3 4.0 %copy-start.9 = (bf16[2,4,2,128,1024]{4,3,2,1,0:T(8,128)(2,1)S(1)}, bf16[2,4,2,128,1024]{4,3,2,1,0:T(8,128)(2,1)}, u32[]{:S(2)}) copy-start(bf16[2,4,2,128,1024]{4,3,2,1,0:T(8,128)(2,1)} %copy-done.8) | copy-start | bytes 12582916
  220.2 3.7 copy-start.23
  220.2 63.4 %collective-permute-start.19 = (bf16[256,1024]{1,0:T(8,128)(2,1)S(1)}, bf16[256,1024]{1,0:T(8,128)(2,1)S(1)}, u32[]{:S(2)}, u32[]{:S(2)}) collective-permute-start(bf16[256,1024]{1,0:T(8,128)(2,1)S(1)} %shard_map.83.rest_0_.mine.own_cols), channel_id=1, source_target_pairs={{0,4},{4,0},{1,5},{5,1},{2,6},{6,2},{3,7},{7,3},{8,12},{12,8},{9,1... | collective-permute-start | bytes 1572872 | tf_op jit(solution)/shard_map/ppermute | solution.py:223
  234.2 8.4 %copy-start.19 = (bf16[256,1024]{1,0:T(8,128)(2,1)S(1)}, bf16[256,1024]{1,0:T(8,128)(2,1)}, u32[]{:S(2)}) copy-start(bf16[256,1024]{1,0:T(8,128)(2,1)} %copy-done.18) | copy-start | bytes 1572868
  242.6 5.2 %copy-start.25 = (bf16[256,1024]{1,0:T(8,128)(2,1)S(1)}, bf16[256,1024]{1,0:T(8,128)(2,1)}, u32[]{:S(2)}) copy-start(bf16[256,1024]{1,0:T(8,128)(2,1)} %copy-done.24) | copy-start | bytes 1572868
  242.6 5.2 %copy-start.27 = (bf16[256,1024]{1,0:T(8,128)(2,1)S(1)}, bf16[256,1024]{1,0:T(8,128)(2,1)}, u32[]{:S(2)}) copy-start(bf16[256,1024]{1,0:T(8,128)(2,1)} %copy-done.26) | copy-start | bytes 1572868
  242.6 63.5 %collective-permute-start.20 = (bf16[256,1024]{1,0:T(8,128)(2,1)S(1)}, bf16[256,1024]{1,0:T(8,128)(2,1)S(1)}, u32[]{:S(2)}, u32[]{:S(2)}) collective-permute-start(bf16[256,1024]{1,0:T(8,128)(2,1)S(1)} %shard_map.87.rest_0_.mine.own_cols), channel_id=1, source_target_pairs={{0,4},{4,0},{1,5},{5,1},{2,6},{6,2},{3,7},{7,3},{8,12},{12,8},{9,1... | collective-permute-start | bytes 1572872 | tf_op jit(solution)/shard_map/ppermute | solution.py:223
  252.5 12.5 %copy-start.15 = (bf16[256,1024]{1,0:T(8,128)(2,1)S(1)}, bf16[256,1024]{1,0:T(8,128)(2,1)}, u32[]{:S(2)}) copy-start(bf16[256,1024]{1,0:T(8,128)(2,1)} %copy-done.14) | copy-start | bytes 1572868
  252.6 12.5 %copy-start.29 = (bf16[256,1024]{1,0:T(8,128)(2,1)S(1)}, bf16[256,1024]{1,0:T(8,128)(2,1)}, u32[]{:S(2)}) copy-start(bf16[256,1024]{1,0:T(8,128)(2,1)} %copy-done.28) | copy-start | bytes 1572868
  264.9 5.0 %copy-start.21 = (bf16[256,1024]{1,0:T(8,128)(2,1)S(1)}, bf16[256,1024]{1,0:T(8,128)(2,1)}, u32[]{:S(2)}) copy-start(bf16[256,1024]{1,0:T(8,128)(2,1)} %copy-done.20) | copy-start | bytes 1572868
  265.0 5.0 %copy-start.31 = (bf16[256,1024]{1,0:T(8,128)(2,1)S(1)}, bf16[256,1024]{1,0:T(8,128)(2,1)}, u32[]{:S(2)}) copy-start(bf16[256,1024]{1,0:T(8,128)(2,1)} %copy-done.30) | copy-start | bytes 1572868
  265.0 63.6 %collective-permute-start.21 = (bf16[256,1024]{1,0:T(8,128)(2,1)S(1)}, bf16[256,1024]{1,0:T(8,128)(2,1)S(1)}, u32[]{:S(2)}, u32[]{:S(2)}) collective-permute-start(bf16[256,1024]{1,0:T(8,128)(2,1)S(1)} %shard_map.90.rest_0_.mine.own_cols), channel_id=1, source_target_pairs={{0,4},{4,0},{1,5},{5,1},{2,6},{6,2},{3,7},{7,3},{8,12},{12,8},{9,1... | collective-permute-start | bytes 1572872 | tf_op jit(solution)/shard_map/ppermute | solution.py:223
  274.8 12.7 %copy-start.17 = (bf16[256,1024]{1,0:T(8,128)(2,1)S(1)}, bf16[256,1024]{1,0:T(8,128)(2,1)}, u32[]{:S(2)}) copy-start(bf16[256,1024]{1,0:T(8,128)(2,1)} %copy-done.16) | copy-start | bytes 1572868
  274.8 12.7 %copy-start.34 = (bf16[256,1024]{1,0:T(8,128)(2,1)S(1)}, bf16[256,1024]{1,0:T(8,128)(2,1)}, u32[]{:S(2)}) copy-start(bf16[256,1024]{1,0:T(8,128)(2,1)} %copy-done.32) | copy-start | bytes 1572868
  287.4 58.1 %collective-permute-start.22 = (bf16[256,1024]{1,0:T(8,128)(2,1)S(1)}, bf16[256,1024]{1,0:T(8,128)(2,1)}, u32[]{:S(2)}, u32[]{:S(2)}) collective-permute-start(bf16[256,1024]{1,0:T(8,128)(2,1)S(1)} %shard_map.93.rest_0_.mine.own_cols), channel_id=1, source_target_pairs={{0,4},{4,0},{1,5},{5,1},{2,6},{6,2},{3,7},{7,3},{8,12},{12,8},{9,1... | collective-permute-start | bytes 1572872 | tf_op jit(solution)/shard_map/ppermute | solution.py:223
  309.9 52.4 %collective-permute-start.25 = (bf16[256,1024]{1,0:T(8,128)(2,1)S(1)}, bf16[256,1024]{1,0:T(8,128)(2,1)S(1)}, u32[]{:S(2)}, u32[]{:S(2)}) collective-permute-start(bf16[256,1024]{1,0:T(8,128)(2,1)S(1)} %shard_map.96.rest_0_.mine.own_cols), channel_id=1, source_target_pairs={{0,4},{4,0},{1,5},{5,1},{2,6},{6,2},{3,7},{7,3},{8,12},{12,8},{9,1... | collective-permute-start | bytes 1572872 | tf_op jit(solution)/shard_map/ppermute | solution.py:223
  319.7 12.5 %copy-start.11 = (bf16[2,4,2,128,1024]{4,3,2,1,0:T(8,128)(2,1)S(1)}, bf16[2,4,2,128,1024]{4,3,2,1,0:T(8,128)(2,1)}, u32[]{:S(2)}) copy-start(bf16[2,4,2,128,1024]{4,3,2,1,0:T(8,128)(2,1)} %copy-done.10) | copy-start | bytes 12582916
  328.6 3.6 copy-start.35
  332.2 35.7 %collective-permute-start.24 = (bf16[128,1024]{1,0:T(8,128)(2,1)S(1)}, bf16[128,1024]{1,0:T(8,128)(2,1)S(1)}, u32[]{:S(2)}, u32[]{:S(2)}) collective-permute-start(bf16[128,1024]{1,0:T(8,128)(2,1)S(1)} %shard_map.99.rest_0_.mine.own_cols), channel_id=1, source_target_pairs={{0,4},{4,0},{1,5},{5,1},{2,6},{6,2},{3,7},{7,3},{8,12},{12,8},{9,1... | collective-permute-start | bytes 786440 | tf_op jit(solution)/shard_map/ppermute | solution.py:223
  339.0 10.0 %copy-start.36 = (bf16[256,1024]{1,0:T(8,128)(2,1)S(1)}, bf16[256,1024]{1,0:T(8,128)(2,1)}, u32[]{:S(2)}) copy-start(bf16[256,1024]{1,0:T(8,128)(2,1)} %copy-done.35) | copy-start | bytes 1572868
  348.9 23.4 %collective-permute-start.23 = (bf16[128,1024]{1,0:T(8,128)(2,1)S(1)}, bf16[128,1024]{1,0:T(8,128)(2,1)S(1)}, u32[]{:S(2)}, u32[]{:S(2)}) collective-permute-start(bf16[128,1024]{1,0:T(8,128)(2,1)S(1)} %shard_map.102.mine.rest_0_), channel_id=1, source_target_pairs={{0,4},{4,0},{1,5},{5,1},{2,6},{6,2},{3,7},{7,3},{8,12},{12,8},{9,1... | collective-permute-start | bytes 786440 | tf_op jit(solution)/shard_map/ppermute | solution.py:223
  (8 other events, 10.1 us)

commit v7 on v6

--- a/solution.py
+++ b/solution.py
@@ -10,7 +10,7 @@
 DEPTH = 3
 VMEM = 48 * 1024 * 1024
 LAST_VMEM = 24 * 1024 * 1024
-PANEL_STEPS = [0, 0, 1, 0, 1, 1, 1, 1, 2, 2, 1]
+PANEL_STEPS = [0, 0, 1, 0, 1] + [1] * 8
 SWAP = [(0, 1), (1, 0)]
 NT = (((1,), (1,)), ((), ()))
 
@@ -269,7 +269,7 @@
         for _ in range(PANEL_STEPS[n] if n < len(PANEL_STEPS) else 0):
             if others:
                 next_panel_step(own[n])
-        while not others and finished <= min(2 * (n - 10) + 1, n - DEPTH):
+        while not others and finished <= min(3 * (n - 12) + 2, n - DEPTH):
             out = end(finished, [own[n]])
             finished += 1
     while others:

time: 376 us -> 376 us (level)
    ppermute x17, starting transfers between devices: 6.9 us -> 13.7 us  [send(): other.append(lax.ppermute(piece, 'half', SWAP))]
    unnamed x92 -> x94, local copies, waits for them, and re-layouts: 24.2 us -> 21.8 us
  transfers between devices with their start and end apart: 26 -> 26, of which waited for: 17 -> 15; matrix products, arithmetic and copies ran while one was open for 2% -> 2% of each run, Pallas kernels for 39% -> 39%
where the time goes in v7:
time: 376 us; the launch traced here: 374 us
  Pallas kernels  149 us (40%)
  waiting for transfers between devices  148 us (39%)
  starting transfers between devices  46.4 us (12%)
  local copies, waits for them, and re-layouts  24.4 us (6%)
  other arithmetic  5.92 us (2%)
    ppermute x17, waiting for transfers between devices, send(): other.append(lax.ppermute(piece, 'half', SWAP))  148 us
    pallas_call x16, Pallas kernels, finish(): pl.pallas_call(finish_kernel, out_shape=jax.ShapeDtypeStruct(shape, jnp.b...  71 us
    pallas_call x17, Pallas kernels, dress(): pl.pallas_call(dress_kernel, out_shape=jax.ShapeDtypeStruct((rows, virt),...  65.7 us
    ppermute x1, starting transfers between devices, start_swap(): lax.ppermute(block, 'rest', [(i, i ^ steps[0]) for i in range(n_rest)])  23 us
    unnamed x94, local copies, waits for them, and re-layouts  21.8 us
    ppermute x17, starting transfers between devices, send(): other.append(lax.ppermute(piece, 'half', SWAP))  13.7 us
    pallas_call x8, Pallas kernels, place(): pl.pallas_call(place_kernel, out_shape=jax.ShapeDtypeStruct((2, lead, 2,...  7.77 us
  transfers between devices with their start and end apart: 26, of which 15 were waited for; matrix products, arithmetic and copies ran while one was open for 2% of the time, Pallas kernels for 39%

profile of v7, /device:TPU:0, one launch (start us, length us, event | category | flops | bytes accessed | tf_op | source)
XLA Modules:
  0.0 374.0 jit_solution(8235407038902858277)
XLA Ops:
  1.0 4.1 %collective-permute-start = (bf16[128,512]{1,0:T(8,128)(2,1)S(1)}, bf16[128,512]{1,0:T(8,128)(2,1)S(1)}, u32[]{:S(2)}, u32[]{:S(2)}) collective-permute-start(bf16[128,512]{1,0:T(8,128)(2,1)S(1)} %get-tuple-element.11), channel_id=1, source_target_pairs={{0,4},{4,0},{1,5},{5,1},{2,6},{6,2},{3,7},{7,3},{8,12},{12,8},{9,1... | collective-permute-start | bytes 393224 | tf_op jit(solution)/shard_map/ppermute | solution.py:227
  6.7 2.9 shard_map.64.rest_0_.mine.own_cols
  9.7 4.7 %shard_map.65.rest_0_.mine.own_cols = bf16[256,1024]{1,0:T(8,128)(2,1)} custom-call(bf16[1024,1024]{1,0:T(8,128)(2,1)S(1)} %copy-done.16, bf16[1,4,1024,1024]{3,2,1,0:T(8,128)(2,1)} %t_rows.33, bf16[1,4,1024,1024]{3,2,1,0:T(8,128)(2,1)} %t_rows.33, bf16[1024,1024]{1,0:T(8,128)(2,1)S(1)} %copy-done.16, bf16[256,1024]{1,0:T(8,128)(2,1)S(1)} %shard_map.64.rest_0_.mine.own_cols), custom_call_target="tpu_custom_call" | custom-call | flops 1073741824 | bytes 5767168 | tf_op jit(solution)/shard_map/pallas_call | solution.py:32
  14.4 2.9 collective-permute-start.2
  17.3 3.8 %shard_map.66.rest_0_.mine.own_cols = bf16[256,1024]{1,0:T(8,128)(2,1)S(1)} custom-call(bf16[1024,1024]{1,0:T(8,128)(2,1)S(1)} %copy-done.16, bf16[1,4,1024,1024]{3,2,1,0:T(8,128)(2,1)} %t_rows.33, bf16[1,4,1024,1024]{3,2,1,0:T(8,128)(2,1)} %t_rows.33, bf16[1024,1024]{1,0:T(8,128)(2,1)S(1)} %copy-done.16, bf16[256,1024]{1,0:T(8,128)(2,1)} %shard_map.65.rest_0_.mine.own_cols), custom_call_target="tpu_custom_call" | custom-call | flops 1073741824 | bytes 5767168 | tf_op jit(solution)/shard_map/pallas_call | solution.py:32
  23.0 23.0 %collective-permute-start.3 = (bf16[2,128,512]{2,1,0:T(8,128)(2,1)S(1)}, bf16[2,128,512]{2,1,0:T(8,128)(2,1)S(1)}, u32[]{:S(2)}, u32[]{:S(2)}) collective-permute-start(bf16[2,128,512]{2,1,0:T(8,128)(2,1)S(1)} %bitcast.54), channel_id=1, source_target_pairs={{0,2},{1,3},{2,0},{3,1},{4,6},{5,7},{6,4},{7,5},{8,10},{9,11},{10,... | collective-permute-start | bytes 786440 | tf_op jit(solution)/shard_map/ppermute | solution.py:235
  46.1 13.0 %collective-permute-done.1.rest_2_.theirs = bf16[256,1024]{1,0:T(8,128)(2,1)} collective-permute-done((bf16[256,1024]{1,0:T(8,128)(2,1)S(1)}, bf16[256,1024]{1,0:T(8,128)(2,1)}, u32[]{:S(2)}, u32[]{:S(2)}) %collective-permute-start.1) | collective-permute-done | bytes 524320 | tf_op jit(solution)/shard_map/ppermute | solution.py:223
  59.1 3.8 %shard_map.68.rest_0_.mine.own_cols = bf16[256,1024]{1,0:T(8,128)(2,1)S(1)} custom-call(bf16[1024,1024]{1,0:T(8,128)(2,1)S(1)} %copy-done.17, bf16[1,4,1024,1024]{3,2,1,0:T(8,128)(2,1)} %t_rows.33, bf16[1,4,1024,1024]{3,2,1,0:T(8,128)(2,1)} %t_rows.33, bf16[1024,1024]{1,0:T(8,128)(2,1)S(1)} %copy-done.17, ...), custom_call_target="tpu_custom_call" | custom-call | flops 1073741824 | bytes 5767168 | tf_op jit(solution)/shard_map/pallas_call | solution.py:32
  62.9 18.5 %collective-permute-done.2.rest_2_.theirs = bf16[256,1024]{1,0:T(8,128)(2,1)} collective-permute-done((bf16[256,1024]{1,0:T(8,128)(2,1)}, bf16[256,1024]{1,0:T(8,128)(2,1)}, u32[]{:S(2)}, u32[]{:S(2)}) %collective-permute-start.2) | collective-permute-done | bytes 524320 | tf_op jit(solution)/shard_map/ppermute | solution.py:223
  81.5 3.8 %shard_map.69.rest_0_.mine.own_cols = bf16[256,1024]{1,0:T(8,128)(2,1)S(1)} custom-call(bf16[1024,1024]{1,0:T(8,128)(2,1)S(1)} %copy-done.17, bf16[1,4,1024,1024]{3,2,1,0:T(8,128)(2,1)} %t_rows.33, bf16[1,4,1024,1024]{3,2,1,0:T(8,128)(2,1)} %t_rows.33, bf16[1024,1024]{1,0:T(8,128)(2,1)S(1)} %copy-done.17, ...), custom_call_target="tpu_custom_call" | custom-call | flops 1073741824 | bytes 5767168 | tf_op jit(solution)/shard_map/pallas_call | solution.py:32
  88.0 16.0 %collective-permute-done.4.rest_2_.theirs = bf16[256,1024]{1,0:T(8,128)(2,1)} collective-permute-done((bf16[256,1024]{1,0:T(8,128)(2,1)S(1)}, bf16[256,1024]{1,0:T(8,128)(2,1)}, u32[]{:S(2)}, u32[]{:S(2)}) %collective-permute-start.4) | collective-permute-done | bytes 524320 | tf_op jit(solution)/shard_map/ppermute | solution.py:223
  104.0 3.8 %shard_map.71.rest_0_.mine.own_cols = bf16[256,1024]{1,0:T(8,128)(2,1)S(1)} custom-call(bf16[1024,1024]{1,0:T(8,128)(2,1)S(1)} %copy-done.17, bf16[1,4,1024,1024]{3,2,1,0:T(8,128)(2,1)} %t_rows.33, bf16[1,4,1024,1024]{3,2,1,0:T(8,128)(2,1)} %t_rows.33, bf16[1024,1024]{1,0:T(8,128)(2,1)S(1)} %copy-done.17, ...), custom_call_target="tpu_custom_call" | custom-call | flops 1073741824 | bytes 5767168 | tf_op jit(solution)/shard_map/pallas_call | solution.py:32
  107.8 1.6 shard_map.72.rest_1_
  109.5 2.0 copy-done
  111.5 14.9 %collective-permute-done.5.rest_2_.theirs = bf16[256,1024]{1,0:T(8,128)(2,1)S(1)} collective-permute-done((bf16[256,1024]{1,0:T(8,128)(2,1)S(1)}, bf16[256,1024]{1,0:T(8,128)(2,1)S(1)}, u32[]{:S(2)}, u32[]{:S(2)}) %collective-permute-start.5) | collective-permute-done | bytes 524320 | tf_op jit(solution)/shard_map/ppermute | solution.py:223
  126.3 4.0 %shard_map.73.rest_0_.mine.own_cols = bf16[256,1024]{1,0:T(8,128)(2,1)S(1)} custom-call(bf16[1024,1024]{1,0:T(8,128)(2,1)S(1)} %copy-done.17, bf16[1,4,1024,1024]{3,2,1,0:T(8,128)(2,1)} %t_rows.33, bf16[1,4,1024,1024]{3,2,1,0:T(8,128)(2,1)} %t_rows.33, bf16[1024,1024]{1,0:T(8,128)(2,1)S(1)} %copy-done.17, ...), custom_call_target="tpu_custom_call" | custom-call | flops 1073741824 | bytes 5767168 | tf_op jit(solution)/shard_map/pallas_call | solution.py:32
  131.1 2.0 copy-done.2
  133.1 15.7 %collective-permute-done.7.rest_2_.theirs = bf16[256,1024]{1,0:T(8,128)(2,1)S(1)} collective-permute-done((bf16[256,1024]{1,0:T(8,128)(2,1)S(1)}, bf16[256,1024]{1,0:T(8,128)(2,1)S(1)}, u32[]{:S(2)}, u32[]{:S(2)}) %collective-permute-start.7) | collective-permute-done | bytes 524320 | tf_op jit(solution)/shard_map/ppermute | solution.py:223
  150.3 3.8 %shard_map.75.rest_0_.mine.own_cols = bf16[256,1024]{1,0:T(8,128)(2,1)S(1)} custom-call(bf16[1024,1024]{1,0:T(8,128)(2,1)S(1)} %copy-done.17, bf16[1,4,1024,1024]{3,2,1,0:T(8,128)(2,1)} %t_rows.33, bf16[1,4,1024,1024]{3,2,1,0:T(8,128)(2,1)} %t_rows.33, bf16[1024,1024]{1,0:T(8,128)(2,1)S(1)} %copy-done.17, ...), custom_call_target="tpu_custom_call" | custom-call | flops 1073741824 | bytes 5767168 | tf_op jit(solution)/shard_map/pallas_call | solution.py:32
  156.3 2.0 copy-done.4
  158.3 13.0 %collective-permute-done.9.rest_2_.theirs = bf16[256,1024]{1,0:T(8,128)(2,1)S(1)} collective-permute-done((bf16[256,1024]{1,0:T(8,128)(2,1)S(1)}, bf16[256,1024]{1,0:T(8,128)(2,1)S(1)}, u32[]{:S(2)}, u32[]{:S(2)}) %collective-permute-start.9) | collective-permute-done | bytes 524320 | tf_op jit(solution)/shard_map/ppermute | solution.py:223
  171.3 2.4 collective-permute-start.14
  173.7 4.6 %shard_map.77.rest_0_.mine.own_cols = bf16[256,1024]{1,0:T(8,128)(2,1)} custom-call(bf16[1024,1024]{1,0:T(8,128)(2,1)S(1)} %copy-done.17, bf16[1,4,1024,1024]{3,2,1,0:T(8,128)(2,1)} %t_rows.33, bf16[1,4,1024,1024]{3,2,1,0:T(8,128)(2,1)} %t_rows.33, bf16[1024,1024]{1,0:T(8,128)(2,1)S(1)} %copy-done.17, bf16[256,1024]{1,0:T(8,128)(2,1)S(1)} %shard_map.75.rest_0_.mine.own_cols, ...), custom_call_target="tpu_custom_call" | custom-call | flops 1073741824 | bytes 5767168 | tf_op jit(solution)/shard_map/pallas_call | solution.py:32
  179.0 2.0 copy-done.6
  182.5 4.0 %shard_map.79.rest_0_.mine.own_cols = bf16[256,1024]{1,0:T(8,128)(2,1)S(1)} custom-call(bf16[1024,1024]{1,0:T(8,128)(2,1)S(1)} %copy-done.17, bf16[1,4,1024,1024]{3,2,1,0:T(8,128)(2,1)} %t_rows.33, bf16[1,4,1024,1024]{3,2,1,0:T(8,128)(2,1)} %t_rows.33, bf16[1024,1024]{1,0:T(8,128)(2,1)S(1)} %copy-done.17, bf16[256,1024]{1,0:T(8,128)(2,1)} %shard_map.77.rest_0_.mine.own_cols, ...), custom_call_target="tpu_custom_call" | custom-call | flops 1073741824 | bytes 5767168 | tf_op jit(solution)/shard_map/pallas_call | solution.py:32
  186.5 2.7 collective-permute-start.17
  190.5 25.7 %collective-permute-done.13.rest_2_.theirs = bf16[256,1024]{1,0:T(8,128)(2,1)S(1)} collective-permute-done((bf16[256,1024]{1,0:T(8,128)(2,1)S(1)}, bf16[256,1024]{1,0:T(8,128)(2,1)S(1)}, u32[]{:S(2)}, u32[]{:S(2)}) %collective-permute-start.13) | collective-permute-done | bytes 524320 | tf_op jit(solution)/shard_map/ppermute | solution.py:223
  218.2 2.0 copy-done.8
  220.2 4.6 %shard_map.81.rest_0_.mine.own_cols = bf16[256,1024]{1,0:T(8,128)(2,1)} custom-call(bf16[1024,1024]{1,0:T(8,128)(2,1)S(1)} %copy-done.17, bf16[1,4,1024,1024]{3,2,1,0:T(8,128)(2,1)} %t_rows.33, bf16[1,4,1024,1024]{3,2,1,0:T(8,128)(2,1)} %t_rows.33, bf16[1024,1024]{1,0:T(8,128)(2,1)S(1)} %copy-done.17, bf16[256,1024]{1,0:T(8,128)(2,1)S(1)} %shard_map.79.rest_0_.mine.own_cols, ...), custom_call_target="tpu_custom_call" | custom-call | flops 1073741824 | bytes 5767168 | tf_op jit(solution)/shard_map/pallas_call | solution.py:32
  227.1 2.2 copy-done.9
  230.9 2.0 copy-done.10
  232.9 3.9 %shard_map.83.rest_0_.mine.own_cols = bf16[256,1024]{1,0:T(8,128)(2,1)S(1)} custom-call(bf16[1024,1024]{1,0:T(8,128)(2,1)S(1)} %copy-done.17, bf16[1,4,1024,1024]{3,2,1,0:T(8,128)(2,1)} %t_rows.33, bf16[1,4,1024,1024]{3,2,1,0:T(8,128)(2,1)} %t_rows.33, bf16[1024,1024]{1,0:T(8,128)(2,1)S(1)} %copy-done.17, bf16[256,1024]{1,0:T(8,128)(2,1)} %shard_map.81.rest_0_.mine.own_cols, ...), custom_call_target="tpu_custom_call" | custom-call | flops 1073741824 | bytes 5767168 | tf_op jit(solution)/shard_map/pallas_call | solution.py:32
  236.9 3.0 collective-permute-start.20
  241.5 2.0 copy-done.12
  243.5 17.8 %collective-permute-done.17.rest_2_.theirs = bf16[256,1024]{1,0:T(8,128)(2,1)} collective-permute-done((bf16[256,1024]{1,0:T(8,128)(2,1)S(1)}, bf16[256,1024]{1,0:T(8,128)(2,1)}, u32[]{:S(2)}, u32[]{:S(2)}) %collective-permute-start.17) | collective-permute-done | bytes 524320 | tf_op jit(solution)/shard_map/ppermute | solution.py:223
  261.3 3.9 %shard_map.85.rest_0_.mine.own_cols = bf16[256,1024]{1,0:T(8,128)(2,1)S(1)} custom-call(bf16[1024,1024]{1,0:T(8,128)(2,1)S(1)} %copy-done.17, bf16[1,4,1024,1024]{3,2,1,0:T(8,128)(2,1)} %t_rows.33, bf16[1,4,1024,1024]{3,2,1,0:T(8,128)(2,1)} %t_rows.33, bf16[1024,1024]{1,0:T(8,128)(2,1)S(1)} %copy-done.17, ...), custom_call_target="tpu_custom_call" | custom-call | flops 1073741824 | bytes 5767168 | tf_op jit(solution)/shard_map/pallas_call | solution.py:32
  265.3 1.6 shard_map.86
  266.9 2.0 copy-done.14
  268.9 5.0 %shard_map.87.rest_1_ = bf16[1,4,1024,1024]{3,2,1,0:T(8,128)(2,1)} custom-call(f32[2]{0:T(128)S(1)} %pad_maximum_fusion.1.energies, bf16[256,1024]{1,0:T(8,128)(2,1)S(1)} %copy-done.29, bf16[256,1024]{1,0:T(8,128)(2,1)S(1)} %copy-done.29, bf16[256,1024]{1,0:T(8,128)(2,1)} %collective-permute-done.1.rest_2_.theirs, bf16[2,1024,1024]{2,1,0:T(8,128)(2,1)} %bitcast.20, ...), custom_call_target="tpu_custom_call" | custom-call | flops 1073741824 | bytes 5767168 | tf_op jit(solution)/shard_map/pallas_call | solution.py:64
  273.9 5.4 %shard_map.88.rest_1_ = bf16[1,4,1024,1024]{3,2,1,0:T(8,128)(2,1)} custom-call(f32[2]{0:T(128)S(1)} %pad_maximum_fusion.1.energies, bf16[256,1024]{1,0:T(8,128)(2,1)} %shard_map.65.rest_0_.mine.own_cols, bf16[256,1024]{1,0:T(8,128)(2,1)} %shard_map.65.rest_0_.mine.own_cols, ...), custom_call_target="tpu_custom_call", output_to_operand_aliasing={{}: (9, {})} | custom-call | flops 1073741824 | bytes 5767168 | tf_op jit(solution)/shard_map/pallas_call | solution.py:64
  279.2 5.0 %shard_map.89.rest_1_ = bf16[1,4,1024,1024]{3,2,1,0:T(8,128)(2,1)} custom-call(f32[2]{0:T(128)S(1)} %pad_maximum_fusion.1.energies, bf16[256,1024]{1,0:T(8,128)(2,1)S(1)} %copy-done.25, bf16[256,1024]{1,0:T(8,128)(2,1)S(1)} %copy-done.25, bf16[256,1024]{1,0:T(8,128)(2,1)} %collective-permute-done.4.rest_2_.theirs, ...), custom_call_target="tpu_custom_call", output_to_operand_aliasing={{}: (9, {})} | custom-call | flops 1073741824 | bytes 5767168 | tf_op jit(solution)/shard_map/pallas_call | solution.py:64
  284.2 3.9 %shard_map.90.rest_0_.mine.own_cols = bf16[256,1024]{1,0:T(8,128)(2,1)S(1)} custom-call(bf16[1024,1024]{1,0:T(8,128)(2,1)S(1)} %copy-done.17, bf16[1,4,1024,1024]{3,2,1,0:T(8,128)(2,1)} %t_rows.33, bf16[1,4,1024,1024]{3,2,1,0:T(8,128)(2,1)} %t_rows.33, bf16[1024,1024]{1,0:T(8,128)(2,1)S(1)} %copy-done.17, ...), custom_call_target="tpu_custom_call" | custom-call | flops 1073741824 | bytes 5767168 | tf_op jit(solution)/shard_map/pallas_call | solution.py:32
  288.1 3.0 collective-permute-start.22
  291.1 4.8 %shard_map.91.rest_1_ = bf16[1,4,1024,1024]{3,2,1,0:T(8,128)(2,1)} custom-call(f32[2]{0:T(128)S(1)} %pad_maximum_fusion.1.energies, bf16[256,1024]{1,0:T(8,128)(2,1)S(1)} %copy-done.31, bf16[256,1024]{1,0:T(8,128)(2,1)S(1)} %copy-done.31, bf16[256,1024]{1,0:T(8,128)(2,1)S(1)} %copy-done.33, ...), custom_call_target="tpu_custom_call", output_to_operand_aliasing={{}: (9, {})} | custom-call | flops 1073741824 | bytes 5767168 | tf_op jit(solution)/shard_map/pallas_call | solution.py:64
  295.9 4.9 %shard_map.92.rest_1_ = bf16[1,4,1024,1024]{3,2,1,0:T(8,128)(2,1)} custom-call(f32[2]{0:T(128)S(1)} %pad_maximum_fusion.2.energies, bf16[256,1024]{1,0:T(8,128)(2,1)S(1)} %copy-done.19, bf16[256,1024]{1,0:T(8,128)(2,1)S(1)} %copy-done.19, bf16[256,1024]{1,0:T(8,128)(2,1)S(1)} %copy-done.35, ...), custom_call_target="tpu_custom_call", output_to_operand_aliasing={{}: (9, {})} | custom-call | flops 1073741824 | bytes 5767168 | tf_op jit(solution)/shard_map/pallas_call | solution.py:64
  300.8 4.8 %shard_map.93.rest_1_ = bf16[1,4,1024,1024]{3,2,1,0:T(8,128)(2,1)} custom-call(f32[2]{0:T(128)S(1)} %pad_maximum_fusion.2.energies, bf16[256,1024]{1,0:T(8,128)(2,1)S(1)} %copy-done.27, bf16[256,1024]{1,0:T(8,128)(2,1)S(1)} %copy-done.27, bf16[256,1024]{1,0:T(8,128)(2,1)S(1)} %copy-done.37, ...), custom_call_target="tpu_custom_call", output_to_operand_aliasing={{}: (9, {})} | custom-call | flops 1073741824 | bytes 5767168 | tf_op jit(solution)/shard_map/pallas_call | solution.py:64
  306.1 3.8 %shard_map.94.rest_0_.mine.own_cols = bf16[256,1024]{1,0:T(8,128)(2,1)S(1)} custom-call(bf16[1024,1024]{1,0:T(8,128)(2,1)S(1)} %copy-done.17, bf16[1,4,1024,1024]{3,2,1,0:T(8,128)(2,1)} %t_rows.33, bf16[1,4,1024,1024]{3,2,1,0:T(8,128)(2,1)} %t_rows.33, bf16[1024,1024]{1,0:T(8,128)(2,1)S(1)} %copy-done.17, ...), custom_call_target="tpu_custom_call" | custom-call | flops 1073741824 | bytes 5767168 | tf_op jit(solution)/shard_map/pallas_call | solution.py:32
  310.0 4.9 %shard_map.95.rest_1_ = bf16[1,4,1024,1024]{3,2,1,0:T(8,128)(2,1)} custom-call(f32[2]{0:T(128)S(1)} %pad_maximum_fusion.2.energies, bf16[256,1024]{1,0:T(8,128)(2,1)S(1)} %copy-done.21, bf16[256,1024]{1,0:T(8,128)(2,1)S(1)} %copy-done.21, bf16[256,1024]{1,0:T(8,128)(2,1)S(1)} %copy-done.39, ...), custom_call_target="tpu_custom_call", output_to_operand_aliasing={{}: (9, {})} | custom-call | flops 1073741824 | bytes 5767168 | tf_op jit(solution)/shard_map/pallas_call | solution.py:64
  314.9 4.8 %shard_map.96.rest_1_ = bf16[1,4,1024,1024]{3,2,1,0:T(8,128)(2,1)} custom-call(f32[2]{0:T(128)S(1)} %pad_maximum_fusion.2.energies, bf16[256,1024]{1,0:T(8,128)(2,1)S(1)} %copy-done.23, bf16[256,1024]{1,0:T(8,128)(2,1)S(1)} %copy-done.23, bf16[256,1024]{1,0:T(8,128)(2,1)S(1)} %copy-done.41, ...), custom_call_target="tpu_custom_call", output_to_operand_aliasing={{}: (9, {})} | custom-call | flops 1073741824 | bytes 5767168 | tf_op jit(solution)/shard_map/pallas_call | solution.py:64
  319.7 5.3 %shard_map.97.rest_1_ = bf16[1,4,1024,1024]{3,2,1,0:T(8,128)(2,1)} custom-call(f32[2]{0:T(128)S(1)} %pad_maximum_fusion.3.energies, bf16[256,1024]{1,0:T(8,128)(2,1)} %shard_map.77.rest_0_.mine.own_cols, bf16[256,1024]{1,0:T(8,128)(2,1)} %shard_map.77.rest_0_.mine.own_cols, ...), custom_call_target="tpu_custom_call", output_to_operand_aliasing={{}: (9, {})} | custom-call | flops 1073741824 | bytes 5767168 | tf_op jit(solution)/shard_map/pallas_call | solution.py:64
  325.0 3.5 collective-permute-done.21.rest_2_.theirs
  328.6 3.4 shard_map.98.rest_0_.mine.own_cols
  332.1 3.9 %shard_map.99.rest_1_ = bf16[1,4,1024,1024]{3,2,1,0:T(8,128)(2,1)} custom-call(f32[2]{0:T(128)S(1)} %pad_maximum_fusion.3.energies, bf16[256,1024]{1,0:T(8,128)(2,1)S(1)} %shard_map.79.rest_0_.mine.own_cols, bf16[256,1024]{1,0:T(8,128)(2,1)S(1)} %shard_map.79.rest_0_.mine.own_cols, ...), custom_call_target="tpu_custom_call", output_to_operand_aliasing={{}: (9, {})} | custom-call | flops 1073741824 | bytes 5767168 | tf_op jit(solution)/shard_map/pallas_call | solution.py:64
  336.0 4.5 %shard_map.100.rest_1_ = bf16[1,4,1024,1024]{3,2,1,0:T(8,128)(2,1)} custom-call(f32[2]{0:T(128)S(1)} %pad_maximum_fusion.3.energies, bf16[256,1024]{1,0:T(8,128)(2,1)} %shard_map.81.rest_0_.mine.own_cols, bf16[256,1024]{1,0:T(8,128)(2,1)} %shard_map.81.rest_0_.mine.own_cols, ...), custom_call_target="tpu_custom_call", output_to_operand_aliasing={{}: (9, {})} | custom-call | flops 1073741824 | bytes 5767168 | tf_op jit(solution)/shard_map/pallas_call | solution.py:64
  340.4 3.4 shard_map.101.rest_1_
  343.8 1.7 collective-permute-done.22.rest_2_.theirs
  345.5 3.4 shard_map.102.mine.rest_0_
  350.1 3.4 shard_map.104.rest_1_
  355.0 3.9 %shard_map.105.rest_1_ = bf16[1,4,1024,1024]{3,2,1,0:T(8,128)(2,1)} custom-call(f32[2]{0:T(128)S(1)} %pad_maximum_fusion.energies, bf16[256,1024]{1,0:T(8,128)(2,1)S(1)} %shard_map.90.rest_0_.mine.own_cols, bf16[256,1024]{1,0:T(8,128)(2,1)S(1)} %shard_map.90.rest_0_.mine.own_cols, ...), custom_call_target="tpu_custom_call", output_to_operand_aliasing={{}: (9, {})} | custom-call | flops 1073741824 | bytes 5767168 | tf_op jit(solution)/shard_map/pallas_call | solution.py:64
  358.9 3.5 collective-permute-done.25.theirs
  362.4 3.9 %shard_map.106.rest_1_ = bf16[1,4,1024,1024]{3,2,1,0:T(8,128)(2,1)} custom-call(f32[2]{0:T(128)S(1)} %pad_maximum_fusion.energies, bf16[256,1024]{1,0:T(8,128)(2,1)S(1)} %shard_map.94.rest_0_.mine.own_cols, bf16[256,1024]{1,0:T(8,128)(2,1)S(1)} %shard_map.94.rest_0_.mine.own_cols, ...), custom_call_target="tpu_custom_call", output_to_operand_aliasing={{}: (9, {})} | custom-call | flops 1073741824 | bytes 5767168 | tf_op jit(solution)/shard_map/pallas_call | solution.py:64
  366.2 1.6 collective-permute-done.24.theirs
  367.9 3.3 shard_map.107._
  372.3 1.7 shard_map.108
  (144 shorter events, 27.4 us)
Async XLA Ops:
  1.0 22.0 %collective-permute-start = (bf16[128,512]{1,0:T(8,128)(2,1)S(1)}, bf16[128,512]{1,0:T(8,128)(2,1)S(1)}, u32[]{:S(2)}, u32[]{:S(2)}) collective-permute-start(bf16[128,512]{1,0:T(8,128)(2,1)S(1)} %get-tuple-element.11), channel_id=1, source_target_pairs={{0,4},{4,0},{1,5},{5,1},{2,6},{6,2},{3,7},{7,3},{8,12},{12,8},{9,1... | collective-permute-start | bytes 393224 | tf_op jit(solution)/shard_map/ppermute | solution.py:227
  9.6 4.8 %copy-start.28 = (bf16[256,1024]{1,0:T(8,128)(2,1)}, bf16[256,1024]{1,0:T(8,128)(2,1)S(1)}, u32[]{:S(2)}) copy-start(bf16[256,1024]{1,0:T(8,128)(2,1)S(1)} %shard_map.64.rest_0_.mine.own_cols) | copy-start | bytes 1572868
  9.6 49.4 %collective-permute-start.1 = (bf16[256,1024]{1,0:T(8,128)(2,1)S(1)}, bf16[256,1024]{1,0:T(8,128)(2,1)}, u32[]{:S(2)}, u32[]{:S(2)}) collective-permute-start(bf16[256,1024]{1,0:T(8,128)(2,1)S(1)} %shard_map.64.rest_0_.mine.own_cols), channel_id=1, source_target_pairs={{0,4},{4,0},{1,5},{5,1},{2,6},{6,2},{3,7},{7,3},{8,12},{12,8},{9,1... | collective-permute-start | bytes 1572872 | tf_op jit(solution)/shard_map/ppermute | solution.py:223
  14.4 7.2 %copy-start.45 = (f32[2]{0:T(128)S(1)}, f32[2]{0:T(128)}, u32[]{:S(2)}) copy-start(f32[2]{0:T(128)} %param.9) | copy-start | bytes 28
  14.4 7.8 %copy-start.46 = (f32[16]{0:T(128)S(1)}, f32[16]{0:T(128)}, u32[]{:S(2)}) copy-start(f32[16]{0:T(128)} %param.10) | copy-start | bytes 196
  14.4 44.7 %copy-start.17 = (bf16[1024,1024]{1,0:T(8,128)(2,1)S(1)}, bf16[1024,1024]{1,0:T(8,128)(2,1)}, u32[]{:S(2)}) copy-start(bf16[1024,1024]{1,0:T(8,128)(2,1)} %f_cols.33) | copy-start | bytes 6291460
  14.4 67.1 %collective-permute-start.2 = (bf16[256,1024]{1,0:T(8,128)(2,1)}, bf16[256,1024]{1,0:T(8,128)(2,1)}, u32[]{:S(2)}, u32[]{:S(2)}) collective-permute-start(bf16[256,1024]{1,0:T(8,128)(2,1)} %shard_map.65.rest_0_.mine.own_cols), channel_id=1, source_target_pairs={{0,4},{4,0},{1,5},{5,1},{2,6},{6,2},{3,7},{7,3},{8,12},{12,8},{9,1... | collective-permute-start | bytes 1572872 | tf_op jit(solution)/shard_map/ppermute | solution.py:223
  21.0 41.8 %copy-start.24 = (bf16[256,1024]{1,0:T(8,128)(2,1)}, bf16[256,1024]{1,0:T(8,128)(2,1)S(1)}, u32[]{:S(2)}) copy-start(bf16[256,1024]{1,0:T(8,128)(2,1)S(1)} %shard_map.66.rest_0_.mine.own_cols) | copy-start | bytes 1572868
  21.0 82.9 %collective-permute-start.4 = (bf16[256,1024]{1,0:T(8,128)(2,1)S(1)}, bf16[256,1024]{1,0:T(8,128)(2,1)}, u32[]{:S(2)}, u32[]{:S(2)}) collective-permute-start(bf16[256,1024]{1,0:T(8,128)(2,1)S(1)} %shard_map.66.rest_0_.mine.own_cols), channel_id=1, source_target_pairs={{0,4},{4,0},{1,5},{5,1},{2,6},{6,2},{3,7},{7,3},{8,12},{12,8},{9,1... | collective-permute-start | bytes 1572872 | tf_op jit(solution)/shard_map/ppermute | solution.py:223
  23.0 62.3 %collective-permute-start.3 = (bf16[2,128,512]{2,1,0:T(8,128)(2,1)S(1)}, bf16[2,128,512]{2,1,0:T(8,128)(2,1)S(1)}, u32[]{:S(2)}, u32[]{:S(2)}) collective-permute-start(bf16[2,128,512]{2,1,0:T(8,128)(2,1)S(1)} %bitcast.54), channel_id=1, source_target_pairs={{0,2},{1,3},{2,0},{3,1},{4,6},{5,7},{6,4},{7,5},{8,10},{9,11},{10,... | collective-permute-start | bytes 786440 | tf_op jit(solution)/shard_map/ppermute | solution.py:235
  62.9 22.4 %copy-start.30 = (bf16[256,1024]{1,0:T(8,128)(2,1)}, bf16[256,1024]{1,0:T(8,128)(2,1)S(1)}, u32[]{:S(2)}) copy-start(bf16[256,1024]{1,0:T(8,128)(2,1)S(1)} %shard_map.68.rest_0_.mine.own_cols) | copy-start | bytes 1572868
  62.9 63.5 %collective-permute-start.5 = (bf16[256,1024]{1,0:T(8,128)(2,1)S(1)}, bf16[256,1024]{1,0:T(8,128)(2,1)S(1)}, u32[]{:S(2)}, u32[]{:S(2)}) collective-permute-start(bf16[256,1024]{1,0:T(8,128)(2,1)S(1)} %shard_map.68.rest_0_.mine.own_cols), channel_id=1, source_target_pairs={{0,4},{4,0},{1,5},{5,1},{2,6},{6,2},{3,7},{7,3},{8,12},{12,8},{9,1... | collective-permute-start | bytes 1572872 | tf_op jit(solution)/shard_map/ppermute | solution.py:223
  85.3 22.5 %copy-start.18 = (bf16[256,1024]{1,0:T(8,128)(2,1)}, bf16[256,1024]{1,0:T(8,128)(2,1)S(1)}, u32[]{:S(2)}) copy-start(bf16[256,1024]{1,0:T(8,128)(2,1)S(1)} %shard_map.69.rest_0_.mine.own_cols) | copy-start | bytes 1572868
  86.2 44.2 %collective-permute-start.6 = (bf16[4,128,512]{2,1,0:T(8,128)(2,1)}, bf16[4,128,512]{2,1,0:T(8,128)(2,1)S(1)}, u32[]{:S(2)}, u32[]{:S(2)}) collective-permute-start(bf16[4,128,512]{2,1,0:T(8,128)(2,1)} %bitcast.5.rest_1_.block), channel_id=1, source_target_pairs={{0,1},{1,0},{2,3},{3,2},{8,9},{9,8},{10,11},{11,10},{16,17},{17,16... | collective-permute-start | bytes 1572872 | tf_op jit(solution)/shard_map/ppermute | solution.py:251
  87.8 61.0 %collective-permute-start.7 = (bf16[256,1024]{1,0:T(8,128)(2,1)S(1)}, bf16[256,1024]{1,0:T(8,128)(2,1)S(1)}, u32[]{:S(2)}, u32[]{:S(2)}) collective-permute-start(bf16[256,1024]{1,0:T(8,128)(2,1)S(1)} %shard_map.69.rest_0_.mine.own_cols), channel_id=1, source_target_pairs={{0,4},{4,0},{1,5},{5,1},{2,6},{6,2},{3,7},{7,3},{8,12},{12,8},{9,1... | collective-permute-start | bytes 1572872 | tf_op jit(solution)/shard_map/ppermute | solution.py:223
  87.9 66.2 %collective-permute-start.8 = (bf16[4,128,512]{2,1,0:T(8,128)(2,1)}, bf16[4,128,512]{2,1,0:T(8,128)(2,1)S(1)}, u32[]{:S(2)}, u32[]{:S(2)}) collective-permute-start(bf16[4,128,512]{2,1,0:T(8,128)(2,1)} %bitcast.5.rest_1_.block), channel_id=1, source_target_pairs={{0,8},{1,9},{2,10},{3,11},{8,0},{9,1},{10,2},{11,3},{16,24},{17,25... | collective-permute-start | bytes 1572872 | tf_op jit(solution)/shard_map/ppermute | solution.py:251
  107.7 22.6 %copy-start.26 = (bf16[256,1024]{1,0:T(8,128)(2,1)}, bf16[256,1024]{1,0:T(8,128)(2,1)S(1)}, u32[]{:S(2)}) copy-start(bf16[256,1024]{1,0:T(8,128)(2,1)S(1)} %shard_map.71.rest_0_.mine.own_cols) | copy-start | bytes 1572868
  107.7 63.5 %collective-permute-start.9 = (bf16[256,1024]{1,0:T(8,128)(2,1)S(1)}, bf16[256,1024]{1,0:T(8,128)(2,1)S(1)}, u32[]{:S(2)}, u32[]{:S(2)}) collective-permute-start(bf16[256,1024]{1,0:T(8,128)(2,1)S(1)} %shard_map.71.rest_0_.mine.own_cols), channel_id=1, source_target_pairs={{0,4},{4,0},{1,5},{5,1},{2,6},{6,2},{3,7},{7,3},{8,12},{12,8},{9,1... | collective-permute-start | bytes 1572872 | tf_op jit(solution)/shard_map/ppermute | solution.py:223
  126.3 4.0 %copy-start.32 = (bf16[256,1024]{1,0:T(8,128)(2,1)}, bf16[256,1024]{1,0:T(8,128)(2,1)S(1)}, u32[]{:S(2)}) copy-start(bf16[256,1024]{1,0:T(8,128)(2,1)S(1)} %collective-permute-done.5.rest_2_.theirs) | copy-start | bytes 1572868
  126.3 4.2 %copy-start.1 = (bf16[2,4,2,128,1024]{4,3,2,1,0:T(8,128)(2,1)S(1)}, bf16[2,4,2,128,1024]{4,3,2,1,0:T(8,128)(2,1)}, u32[]{:S(2)}) copy-start(bf16[2,4,2,128,1024]{4,3,2,1,0:T(8,128)(2,1)} %copy-done) | copy-start | bytes 12582916
  126.3 51.9 %collective-permute-start.10 = (bf16[4,128,512]{2,1,0:T(8,128)(2,1)}, bf16[4,128,512]{2,1,0:T(8,128)(2,1)S(1)}, u32[]{:S(2)}, u32[]{:S(2)}) collective-permute-start(bf16[4,128,512]{2,1,0:T(8,128)(2,1)} %bitcast.5.rest_1_.block), channel_id=1, source_target_pairs={{0,9},{1,8},{2,11},{3,10},{8,1},{9,0},{10,3},{11,2},{16,25},{17,24... | collective-permute-start | bytes 1572872 | tf_op jit(solution)/shard_map/ppermute | solution.py:251
  130.4 23.7 %copy-start.20 = (bf16[256,1024]{1,0:T(8,128)(2,1)}, bf16[256,1024]{1,0:T(8,128)(2,1)S(1)}, u32[]{:S(2)}) copy-start(bf16[256,1024]{1,0:T(8,128)(2,1)S(1)} %shard_map.73.rest_0_.mine.own_cols) | copy-start | bytes 1572868
  130.4 52.1 %collective-permute-start.11 = (bf16[256,1024]{1,0:T(8,128)(2,1)S(1)}, bf16[256,1024]{1,0:T(8,128)(2,1)S(1)}, u32[]{:S(2)}, u32[]{:S(2)}) collective-permute-start(bf16[256,1024]{1,0:T(8,128)(2,1)S(1)} %shard_map.73.rest_0_.mine.own_cols), channel_id=1, source_target_pairs={{0,4},{4,0},{1,5},{5,1},{2,6},{6,2},{3,7},{7,3},{8,12},{12,8},{9,1... | collective-permute-start | bytes 1572872 | tf_op jit(solution)/shard_map/ppermute | solution.py:223
  131.1 2.0 copy-start.2
  148.8 5.3 %copy-start.34 = (bf16[256,1024]{1,0:T(8,128)(2,1)}, bf16[256,1024]{1,0:T(8,128)(2,1)S(1)}, u32[]{:S(2)}) copy-start(bf16[256,1024]{1,0:T(8,128)(2,1)S(1)} %collective-permute-done.7.rest_2_.theirs) | copy-start | bytes 1572868
  148.8 6.9 %copy-start.3 = (bf16[2,4,2,128,1024]{4,3,2,1,0:T(8,128)(2,1)S(1)}, bf16[2,4,2,128,1024]{4,3,2,1,0:T(8,128)(2,1)}, u32[]{:S(2)}) copy-start(bf16[2,4,2,128,1024]{4,3,2,1,0:T(8,128)(2,1)} %copy-done.2) | copy-start | bytes 12582916
  148.8 37.7 %collective-permute-start.12 = (bf16[4,128,512]{2,1,0:T(8,128)(2,1)}, bf16[4,128,512]{2,1,0:T(8,128)(2,1)S(1)}, u32[]{:S(2)}, u32[]{:S(2)}) collective-permute-start(bf16[4,128,512]{2,1,0:T(8,128)(2,1)} %bitcast.5.rest_1_.block), channel_id=1, source_target_pairs={{0,16},{1,17},{2,18},{3,19},{8,24},{9,25},{10,26},{11,27},{16,0},{... | collective-permute-start | bytes 1572872 | tf_op jit(solution)/shard_map/ppermute | solution.py:251
  154.1 24.2 %copy-start.22 = (bf16[256,1024]{1,0:T(8,128)(2,1)}, bf16[256,1024]{1,0:T(8,128)(2,1)S(1)}, u32[]{:S(2)}) copy-start(bf16[256,1024]{1,0:T(8,128)(2,1)S(1)} %shard_map.75.rest_0_.mine.own_cols) | copy-start | bytes 1572868
  154.1 62.1 %collective-permute-start.13 = (bf16[256,1024]{1,0:T(8,128)(2,1)S(1)}, bf16[256,1024]{1,0:T(8,128)(2,1)S(1)}, u32[]{:S(2)}, u32[]{:S(2)}) collective-permute-start(bf16[256,1024]{1,0:T(8,128)(2,1)S(1)} %shard_map.75.rest_0_.mine.own_cols), channel_id=1, source_target_pairs={{0,4},{4,0},{1,5},{5,1},{2,6},{6,2},{3,7},{7,3},{8,12},{12,8},{9,1... | collective-permute-start | bytes 1572872 | tf_op jit(solution)/shard_map/ppermute | solution.py:223
  156.3 2.0 copy-start.4
  171.3 7.0 %copy-start.36 = (bf16[256,1024]{1,0:T(8,128)(2,1)}, bf16[256,1024]{1,0:T(8,128)(2,1)S(1)}, u32[]{:S(2)}) copy-start(bf16[256,1024]{1,0:T(8,128)(2,1)S(1)} %collective-permute-done.9.rest_2_.theirs) | copy-start | bytes 1572868
  171.3 7.1 %copy-start.5 = (bf16[2,4,2,128,1024]{4,3,2,1,0:T(8,128)(2,1)S(1)}, bf16[2,4,2,128,1024]{4,3,2,1,0:T(8,128)(2,1)}, u32[]{:S(2)}) copy-start(bf16[2,4,2,128,1024]{4,3,2,1,0:T(8,128)(2,1)} %copy-done.4) | copy-start | bytes 12582916
  171.3 53.4 %collective-permute-start.14 = (bf16[4,128,512]{2,1,0:T(8,128)(2,1)}, bf16[4,128,512]{2,1,0:T(8,128)(2,1)S(1)}, u32[]{:S(2)}, u32[]{:S(2)}) collective-permute-start(bf16[4,128,512]{2,1,0:T(8,128)(2,1)} %bitcast.5.rest_1_.block), channel_id=1, source_target_pairs={{0,17},{1,16},{2,19},{3,18},{8,25},{9,24},{10,27},{11,26},{16,1},{... | collective-permute-start | bytes 1572872 | tf_op jit(solution)/shard_map/ppermute | solution.py:251
  178.3 61.6 %collective-permute-start.16 = (bf16[4,128,512]{2,1,0:T(8,128)(2,1)}, bf16[4,128,512]{2,1,0:T(8,128)(2,1)}, u32[]{:S(2)}, u32[]{:S(2)}) collective-permute-start(bf16[4,128,512]{2,1,0:T(8,128)(2,1)} %bitcast.5.rest_1_.block), channel_id=1, source_target_pairs={{0,24},{1,25},{2,26},{3,27},{8,16},{9,17},{10,18},{11,19},{16,8},{... | collective-permute-start | bytes 1572872 | tf_op jit(solution)/shard_map/ppermute | solution.py:251
  182.5 4.0 %copy-start.38 = (bf16[256,1024]{1,0:T(8,128)(2,1)}, bf16[256,1024]{1,0:T(8,128)(2,1)S(1)}, u32[]{:S(2)}) copy-start(bf16[256,1024]{1,0:T(8,128)(2,1)S(1)} %collective-permute-done.11.rest_2_.theirs) | copy-start | bytes 1572868
  182.5 35.0 %copy-start.7 = (bf16[2,4,2,128,1024]{4,3,2,1,0:T(8,128)(2,1)S(1)}, bf16[2,4,2,128,1024]{4,3,2,1,0:T(8,128)(2,1)}, u32[]{:S(2)}) copy-start(bf16[2,4,2,128,1024]{4,3,2,1,0:T(8,128)(2,1)} %copy-done.6) | copy-start | bytes 12582916
  182.5 50.4 %collective-permute-start.15 = (bf16[256,1024]{1,0:T(8,128)(2,1)}, bf16[256,1024]{1,0:T(8,128)(2,1)}, u32[]{:S(2)}, u32[]{:S(2)}) collective-permute-start(bf16[256,1024]{1,0:T(8,128)(2,1)} %shard_map.77.rest_0_.mine.own_cols), channel_id=1, source_target_pairs={{0,4},{4,0},{1,5},{5,1},{2,6},{6,2},{3,7},{7,3},{8,12},{12,8},{9,1... | collective-permute-start | bytes 1572872 | tf_op jit(solution)/shard_map/ppermute | solution.py:223
  186.5 74.7 %collective-permute-start.17 = (bf16[256,1024]{1,0:T(8,128)(2,1)S(1)}, bf16[256,1024]{1,0:T(8,128)(2,1)}, u32[]{:S(2)}, u32[]{:S(2)}) collective-permute-start(bf16[256,1024]{1,0:T(8,128)(2,1)S(1)} %shard_map.79.rest_0_.mine.own_cols), channel_id=1, source_target_pairs={{0,4},{4,0},{1,5},{5,1},{2,6},{6,2},{3,7},{7,3},{8,12},{12,8},{9,1... | collective-permute-start | bytes 1572872 | tf_op jit(solution)/shard_map/ppermute | solution.py:223
  216.2 8.5 %copy-start.40 = (bf16[256,1024]{1,0:T(8,128)(2,1)}, bf16[256,1024]{1,0:T(8,128)(2,1)S(1)}, u32[]{:S(2)}) copy-start(bf16[256,1024]{1,0:T(8,128)(2,1)S(1)} %collective-permute-done.13.rest_2_.theirs) | copy-start | bytes 1572868
  216.2 49.1 %collective-permute-start.18 = (bf16[4,128,512]{2,1,0:T(8,128)(2,1)}, bf16[4,128,512]{2,1,0:T(8,128)(2,1)}, u32[]{:S(2)}, u32[]{:S(2)}) collective-permute-start(bf16[4,128,512]{2,1,0:T(8,128)(2,1)} %bitcast.5.rest_1_.block), channel_id=1, source_target_pairs={{0,25},{1,24},{2,27},{3,26},{8,17},{9,16},{10,19},{11,18},{16,9},{... | collective-permute-start | bytes 1572872 | tf_op jit(solution)/shard_map/ppermute | solution.py:251
  220.2 6.7 %copy-start.42 = (f32[1024]{0:T(1024)S(1)}, f32[1024]{0:T(1024)}, u32[]{:S(2)}) copy-start(f32[1024]{0:T(1024)} %param.11) | copy-start | bytes 12292
  225.5 58.7 %collective-permute-start.19 = (bf16[256,1024]{1,0:T(8,128)(2,1)}, bf16[256,1024]{1,0:T(8,128)(2,1)}, u32[]{:S(2)}, u32[]{:S(2)}) collective-permute-start(bf16[256,1024]{1,0:T(8,128)(2,1)} %shard_map.81.rest_0_.mine.own_cols), channel_id=1, source_target_pairs={{0,4},{4,0},{1,5},{5,1},{2,6},{6,2},{3,7},{7,3},{8,12},{12,8},{9,1... | collective-permute-start | bytes 1572872 | tf_op jit(solution)/shard_map/ppermute | solution.py:223
  227.1 2.2 copy-start.9
  232.9 6.9 %copy-start.11 = (bf16[2,4,2,128,1024]{4,3,2,1,0:T(8,128)(2,1)S(1)}, bf16[2,4,2,128,1024]{4,3,2,1,0:T(8,128)(2,1)}, u32[]{:S(2)}) copy-start(bf16[2,4,2,128,1024]{4,3,2,1,0:T(8,128)(2,1)} %copy-done.10) | copy-start | bytes 12582916
  236.9 69.2 %collective-permute-start.20 = (bf16[256,1024]{1,0:T(8,128)(2,1)S(1)}, bf16[256,1024]{1,0:T(8,128)(2,1)S(1)}, u32[]{:S(2)}, u32[]{:S(2)}) collective-permute-start(bf16[256,1024]{1,0:T(8,128)(2,1)S(1)} %shard_map.83.rest_0_.mine.own_cols), channel_id=1, source_target_pairs={{0,4},{4,0},{1,5},{5,1},{2,6},{6,2},{3,7},{7,3},{8,12},{12,8},{9,1... | collective-permute-start | bytes 1572872 | tf_op jit(solution)/shard_map/ppermute | solution.py:223
  261.3 4.0 %copy-start.13 = (bf16[2,4,2,128,1024]{4,3,2,1,0:T(8,128)(2,1)S(1)}, bf16[2,4,2,128,1024]{4,3,2,1,0:T(8,128)(2,1)}, u32[]{:S(2)}) copy-start(bf16[2,4,2,128,1024]{4,3,2,1,0:T(8,128)(2,1)} %copy-done.12) | copy-start | bytes 12582916
  265.2 3.7 copy-start.29
  265.2 63.4 %collective-permute-start.21 = (bf16[256,1024]{1,0:T(8,128)(2,1)S(1)}, bf16[256,1024]{1,0:T(8,128)(2,1)S(1)}, u32[]{:S(2)}, u32[]{:S(2)}) collective-permute-start(bf16[256,1024]{1,0:T(8,128)(2,1)S(1)} %shard_map.85.rest_0_.mine.own_cols), channel_id=1, source_target_pairs={{0,4},{4,0},{1,5},{5,1},{2,6},{6,2},{3,7},{7,3},{8,12},{12,8},{9,1... | collective-permute-start | bytes 1572872 | tf_op jit(solution)/shard_map/ppermute | solution.py:223
  273.9 5.4 %copy-start.25 = (bf16[256,1024]{1,0:T(8,128)(2,1)S(1)}, bf16[256,1024]{1,0:T(8,128)(2,1)}, u32[]{:S(2)}) copy-start(bf16[256,1024]{1,0:T(8,128)(2,1)} %copy-done.24) | copy-start | bytes 1572868
  284.2 6.9 %copy-start.31 = (bf16[256,1024]{1,0:T(8,128)(2,1)S(1)}, bf16[256,1024]{1,0:T(8,128)(2,1)}, u32[]{:S(2)}) copy-start(bf16[256,1024]{1,0:T(8,128)(2,1)} %copy-done.30) | copy-start | bytes 1572868
  284.2 6.9 %copy-start.33 = (bf16[256,1024]{1,0:T(8,128)(2,1)S(1)}, bf16[256,1024]{1,0:T(8,128)(2,1)}, u32[]{:S(2)}) copy-start(bf16[256,1024]{1,0:T(8,128)(2,1)} %copy-done.32) | copy-start | bytes 1572868
  288.1 7.8 %copy-start.19 = (bf16[256,1024]{1,0:T(8,128)(2,1)S(1)}, bf16[256,1024]{1,0:T(8,128)(2,1)}, u32[]{:S(2)}) copy-start(bf16[256,1024]{1,0:T(8,128)(2,1)} %copy-done.18) | copy-start | bytes 1572868
  288.1 7.8 %copy-start.35 = (bf16[256,1024]{1,0:T(8,128)(2,1)S(1)}, bf16[256,1024]{1,0:T(8,128)(2,1)}, u32[]{:S(2)}) copy-start(bf16[256,1024]{1,0:T(8,128)(2,1)} %copy-done.34) | copy-start | bytes 1572868
  288.1 57.4 %collective-permute-start.22 = (bf16[256,1024]{1,0:T(8,128)(2,1)S(1)}, bf16[256,1024]{1,0:T(8,128)(2,1)}, u32[]{:S(2)}, u32[]{:S(2)}) collective-permute-start(bf16[256,1024]{1,0:T(8,128)(2,1)S(1)} %shard_map.90.rest_0_.mine.own_cols), channel_id=1, source_target_pairs={{0,4},{4,0},{1,5},{5,1},{2,6},{6,2},{3,7},{7,3},{8,12},{12,8},{9,1... | collective-permute-start | bytes 1572872 | tf_op jit(solution)/shard_map/ppermute | solution.py:223
  295.9 4.9 %copy-start.27 = (bf16[256,1024]{1,0:T(8,128)(2,1)S(1)}, bf16[256,1024]{1,0:T(8,128)(2,1)}, u32[]{:S(2)}) copy-start(bf16[256,1024]{1,0:T(8,128)(2,1)} %copy-done.26) | copy-start | bytes 1572868
  295.9 4.9 %copy-start.37 = (bf16[256,1024]{1,0:T(8,128)(2,1)S(1)}, bf16[256,1024]{1,0:T(8,128)(2,1)}, u32[]{:S(2)}) copy-start(bf16[256,1024]{1,0:T(8,128)(2,1)} %copy-done.36) | copy-start | bytes 1572868
  305.6 4.4 %copy-start.21 = (bf16[256,1024]{1,0:T(8,128)(2,1)S(1)}, bf16[256,1024]{1,0:T(8,128)(2,1)}, u32[]{:S(2)}) copy-start(bf16[256,1024]{1,0:T(8,128)(2,1)} %copy-done.20) | copy-start | bytes 1572868
  305.6 4.4 %copy-start.39 = (bf16[256,1024]{1,0:T(8,128)(2,1)S(1)}, bf16[256,1024]{1,0:T(8,128)(2,1)}, u32[]{:S(2)}) copy-start(bf16[256,1024]{1,0:T(8,128)(2,1)} %copy-done.38) | copy-start | bytes 1572868
  309.9 5.0 %copy-start.23 = (bf16[256,1024]{1,0:T(8,128)(2,1)S(1)}, bf16[256,1024]{1,0:T(8,128)(2,1)}, u32[]{:S(2)}) copy-start(bf16[256,1024]{1,0:T(8,128)(2,1)} %copy-done.22) | copy-start | bytes 1572868
  309.9 5.0 %copy-start.41 = (bf16[256,1024]{1,0:T(8,128)(2,1)S(1)}, bf16[256,1024]{1,0:T(8,128)(2,1)}, u32[]{:S(2)}) copy-start(bf16[256,1024]{1,0:T(8,128)(2,1)} %copy-done.40) | copy-start | bytes 1572868
  309.9 52.5 %collective-permute-start.25 = (bf16[256,1024]{1,0:T(8,128)(2,1)S(1)}, bf16[256,1024]{1,0:T(8,128)(2,1)}, u32[]{:S(2)}, u32[]{:S(2)}) collective-permute-start(bf16[256,1024]{1,0:T(8,128)(2,1)S(1)} %shard_map.94.rest_0_.mine.own_cols), channel_id=1, source_target_pairs={{0,4},{4,0},{1,5},{5,1},{2,6},{6,2},{3,7},{7,3},{8,12},{12,8},{9,1... | collective-permute-start | bytes 1572872 | tf_op jit(solution)/shard_map/ppermute | solution.py:223
  325.0 7.0 %copy-start.15 = (bf16[2,4,2,128,1024]{4,3,2,1,0:T(8,128)(2,1)S(1)}, bf16[2,4,2,128,1024]{4,3,2,1,0:T(8,128)(2,1)}, u32[]{:S(2)}) copy-start(bf16[2,4,2,128,1024]{4,3,2,1,0:T(8,128)(2,1)} %copy-done.14) | copy-start | bytes 12582916
  332.0 35.9 %collective-permute-start.24 = (bf16[128,1024]{1,0:T(8,128)(2,1)S(1)}, bf16[128,1024]{1,0:T(8,128)(2,1)S(1)}, u32[]{:S(2)}, u32[]{:S(2)}) collective-permute-start(bf16[128,1024]{1,0:T(8,128)(2,1)S(1)} %shard_map.98.rest_0_.mine.own_cols), channel_id=1, source_target_pairs={{0,4},{4,0},{1,5},{5,1},{2,6},{6,2},{3,7},{7,3},{8,12},{12,8},{9,1... | collective-permute-start | bytes 786440 | tf_op jit(solution)/shard_map/ppermute | solution.py:223
  348.9 23.4 %collective-permute-start.23 = (bf16[128,1024]{1,0:T(8,128)(2,1)S(1)}, bf16[128,1024]{1,0:T(8,128)(2,1)S(1)}, u32[]{:S(2)}, u32[]{:S(2)}) collective-permute-start(bf16[128,1024]{1,0:T(8,128)(2,1)S(1)} %shard_map.102.mine.rest_0_), channel_id=1, source_target_pairs={{0,4},{4,0},{1,5},{5,1},{2,6},{6,2},{3,7},{7,3},{8,12},{12,8},{9,1... | collective-permute-start | bytes 786440 | tf_op jit(solution)/shard_map/ppermute | solution.py:223
  (9 other events, 15.5 us)

commit v8 on v7

--- a/solution.py
+++ b/solution.py
@@ -27,7 +27,7 @@
 
 def dress(amplitudes, fock, pair, first_row, rows, events):
     virt = fock.shape[0]
-    cols = min(COLS, virt) if events else virt
+    cols = virt
     block = first_row // rows
     return pl.pallas_call(
         dress_kernel,
@@ -125,7 +125,7 @@
 
 def last_finish(out, pair, first_row, part, divisor, theirs, panel_other):
     rows, virt = theirs.shape
-    block, cols = first_row // rows, min(2 * COLS, virt)
+    block, cols = first_row // rows, virt
     return pl.pallas_call(
         last_finish_kernel,
         out_shape=jax.ShapeDtypeStruct(out.shape, out.dtype),

time: 376 us -> 376 us (level)
  Pallas kernels: 149 us -> 136 us
  waiting for transfers between devices: 148 us -> 160 us
    pallas_call x17, Pallas kernels: 65.7 us -> 53.2 us  [dress(): pl.pallas_call(dress_kernel, out_shape=jax.ShapeDtypeStruct((rows, virt),...]
    ppermute x17, waiting for transfers between devices: 148 us -> 160 us  [send(): other.append(lax.ppermute(piece, 'half', SWAP))]
  transfers between devices with their start and end apart: 26 -> 26, of which waited for: 15 -> 16; matrix products, arithmetic and copies ran while one was open for 2% -> 2% of each run, Pallas kernels for 39% -> 36%
where the time goes in v8:
time: 376 us; the launch traced here: 374 us
  waiting for transfers between devices  160 us (43%)
  Pallas kernels  136 us (36%)
  starting transfers between devices  47 us (12%)
  local copies, waits for them, and re-layouts  24.4 us (6%)
  other arithmetic  5.92 us (2%)
    ppermute x17, waiting for transfers between devices, send(): other.append(lax.ppermute(piece, 'half', SWAP))  160 us
    pallas_call x16, Pallas kernels, finish(): pl.pallas_call(finish_kernel, out_shape=jax.ShapeDtypeStruct(shape, jnp.b...  71 us
    pallas_call x17, Pallas kernels, dress(): pl.pallas_call(dress_kernel, out_shape=jax.ShapeDtypeStruct((rows, virt),...  53.2 us
    ppermute x1, starting transfers between devices, start_swap(): lax.ppermute(block, 'rest', [(i, i ^ steps[0]) for i in range(n_rest)])  24.6 us
    unnamed x94, local copies, waits for them, and re-layouts  21.8 us
    ppermute x17, starting transfers between devices, send(): other.append(lax.ppermute(piece, 'half', SWAP))  12.8 us
    pallas_call x8, Pallas kernels, place(): pl.pallas_call(place_kernel, out_shape=jax.ShapeDtypeStruct((2, lead, 2,...  7.77 us
  transfers between devices with their start and end apart: 26, of which 16 were waited for; matrix products, arithmetic and copies ran while one was open for 2% of the time, Pallas kernels for 36%

profile of v8, /device:TPU:0, one launch (start us, length us, event | category | flops | bytes accessed | tf_op | source)
XLA Modules:
  0.0 373.9 jit_solution(3846435775789592112)
XLA Ops:
  1.0 4.1 %collective-permute-start = (bf16[128,512]{1,0:T(8,128)(2,1)S(1)}, bf16[128,512]{1,0:T(8,128)(2,1)S(1)}, u32[]{:S(2)}, u32[]{:S(2)}) collective-permute-start(bf16[128,512]{1,0:T(8,128)(2,1)S(1)} %get-tuple-element.11), channel_id=1, source_target_pairs={{0,4},{4,0},{1,5},{5,1},{2,6},{6,2},{3,7},{7,3},{8,12},{12,8},{9,1... | collective-permute-start | bytes 393224 | tf_op jit(solution)/shard_map/ppermute | solution.py:227
  6.7 2.9 shard_map.64.rest_0_.mine.own_cols
  9.7 3.9 %shard_map.65.rest_0_.mine.own_cols = bf16[256,1024]{1,0:T(8,128)(2,1)} custom-call(bf16[1024,1024]{1,0:T(8,128)(2,1)S(1)} %copy-done.16, bf16[1,4,1024,1024]{3,2,1,0:T(8,128)(2,1)} %t_rows.33, bf16[1,4,1024,1024]{3,2,1,0:T(8,128)(2,1)} %t_rows.33, bf16[1024,1024]{1,0:T(8,128)(2,1)S(1)} %copy-done.16, bf16[256,1024]{1,0:T(8,128)(2,1)S(1)} %shard_map.64.rest_0_.mine.own_cols), custom_call_target="tpu_custom_call" | custom-call | flops 1073741824 | bytes 5767168 | tf_op jit(solution)/shard_map/pallas_call | solution.py:32
  13.6 2.9 collective-permute-start.2
  16.5 2.9 shard_map.66.rest_0_.mine.own_cols
  21.4 24.6 %collective-permute-start.3 = (bf16[2,128,512]{2,1,0:T(8,128)(2,1)S(1)}, bf16[2,128,512]{2,1,0:T(8,128)(2,1)S(1)}, u32[]{:S(2)}, u32[]{:S(2)}) collective-permute-start(bf16[2,128,512]{2,1,0:T(8,128)(2,1)S(1)} %bitcast.54), channel_id=1, source_target_pairs={{0,2},{1,3},{2,0},{3,1},{4,6},{5,7},{6,4},{7,5},{8,10},{9,11},{10,... | collective-permute-start | bytes 786440 | tf_op jit(solution)/shard_map/ppermute | solution.py:235
  46.1 13.0 %collective-permute-done.1.rest_2_.theirs = bf16[256,1024]{1,0:T(8,128)(2,1)} collective-permute-done((bf16[256,1024]{1,0:T(8,128)(2,1)S(1)}, bf16[256,1024]{1,0:T(8,128)(2,1)}, u32[]{:S(2)}, u32[]{:S(2)}) %collective-permute-start.1) | collective-permute-done | bytes 524320 | tf_op jit(solution)/shard_map/ppermute | solution.py:223
  59.1 3.0 shard_map.68.rest_0_.mine.own_cols
  62.1 19.4 %collective-permute-done.2.rest_2_.theirs = bf16[256,1024]{1,0:T(8,128)(2,1)} collective-permute-done((bf16[256,1024]{1,0:T(8,128)(2,1)}, bf16[256,1024]{1,0:T(8,128)(2,1)}, u32[]{:S(2)}, u32[]{:S(2)}) %collective-permute-start.2) | collective-permute-done | bytes 524320 | tf_op jit(solution)/shard_map/ppermute | solution.py:223
  81.5 2.9 shard_map.69.rest_0_.mine.own_cols
  87.2 16.8 %collective-permute-done.4.rest_2_.theirs = bf16[256,1024]{1,0:T(8,128)(2,1)} collective-permute-done((bf16[256,1024]{1,0:T(8,128)(2,1)S(1)}, bf16[256,1024]{1,0:T(8,128)(2,1)}, u32[]{:S(2)}, u32[]{:S(2)}) %collective-permute-start.4) | collective-permute-done | bytes 524320 | tf_op jit(solution)/shard_map/ppermute | solution.py:223
  104.0 3.0 shard_map.71.rest_0_.mine.own_cols
  108.7 2.0 copy-done
  110.7 15.7 %collective-permute-done.5.rest_2_.theirs = bf16[256,1024]{1,0:T(8,128)(2,1)S(1)} collective-permute-done((bf16[256,1024]{1,0:T(8,128)(2,1)S(1)}, bf16[256,1024]{1,0:T(8,128)(2,1)S(1)}, u32[]{:S(2)}, u32[]{:S(2)}) %collective-permute-start.5) | collective-permute-done | bytes 524320 | tf_op jit(solution)/shard_map/ppermute | solution.py:223
  126.3 3.2 shard_map.73.rest_0_.mine.own_cols
  130.3 2.0 copy-done.2
  132.3 16.5 %collective-permute-done.7.rest_2_.theirs = bf16[256,1024]{1,0:T(8,128)(2,1)S(1)} collective-permute-done((bf16[256,1024]{1,0:T(8,128)(2,1)S(1)}, bf16[256,1024]{1,0:T(8,128)(2,1)S(1)}, u32[]{:S(2)}, u32[]{:S(2)}) %collective-permute-start.7) | collective-permute-done | bytes 524320 | tf_op jit(solution)/shard_map/ppermute | solution.py:223
  150.3 2.9 shard_map.75.rest_0_.mine.own_cols
  155.5 2.0 copy-done.4
  157.5 13.8 %collective-permute-done.9.rest_2_.theirs = bf16[256,1024]{1,0:T(8,128)(2,1)S(1)} collective-permute-done((bf16[256,1024]{1,0:T(8,128)(2,1)S(1)}, bf16[256,1024]{1,0:T(8,128)(2,1)S(1)}, u32[]{:S(2)}, u32[]{:S(2)}) %collective-permute-start.9) | collective-permute-done | bytes 524320 | tf_op jit(solution)/shard_map/ppermute | solution.py:223
  171.3 2.4 collective-permute-start.14
  173.7 3.7 shard_map.77.rest_0_.mine.own_cols
  178.2 2.0 copy-done.6
  180.2 2.3 collective-permute-done.11.rest_2_.theirs
  182.5 3.4 shard_map.79.rest_0_.mine.own_cols
  185.9 2.8 collective-permute-start.17
  189.9 26.3 %collective-permute-done.13.rest_2_.theirs = bf16[256,1024]{1,0:T(8,128)(2,1)S(1)} collective-permute-done((bf16[256,1024]{1,0:T(8,128)(2,1)S(1)}, bf16[256,1024]{1,0:T(8,128)(2,1)S(1)}, u32[]{:S(2)}, u32[]{:S(2)}) %collective-permute-start.13) | collective-permute-done | bytes 524320 | tf_op jit(solution)/shard_map/ppermute | solution.py:223
  218.2 2.0 copy-done.8
  220.2 3.8 %shard_map.81.rest_0_.mine.own_cols = bf16[256,1024]{1,0:T(8,128)(2,1)} custom-call(bf16[1024,1024]{1,0:T(8,128)(2,1)S(1)} %copy-done.17, bf16[1,4,1024,1024]{3,2,1,0:T(8,128)(2,1)} %t_rows.33, bf16[1,4,1024,1024]{3,2,1,0:T(8,128)(2,1)} %t_rows.33, bf16[1024,1024]{1,0:T(8,128)(2,1)S(1)} %copy-done.17, bf16[256,1024]{1,0:T(8,128)(2,1)S(1)} %shard_map.79.rest_0_.mine.own_cols, ...), custom_call_target="tpu_custom_call" | custom-call | flops 1073741824 | bytes 5767168 | tf_op jit(solution)/shard_map/pallas_call | solution.py:32
  226.3 2.2 copy-done.9
  230.1 2.0 copy-done.10
  232.2 3.1 shard_map.83.rest_0_.mine.own_cols
  235.3 3.0 collective-permute-start.20
  239.9 2.0 copy-done.12
  241.9 19.4 %collective-permute-done.17.rest_2_.theirs = bf16[256,1024]{1,0:T(8,128)(2,1)} collective-permute-done((bf16[256,1024]{1,0:T(8,128)(2,1)S(1)}, bf16[256,1024]{1,0:T(8,128)(2,1)}, u32[]{:S(2)}, u32[]{:S(2)}) %collective-permute-start.17) | collective-permute-done | bytes 524320 | tf_op jit(solution)/shard_map/ppermute | solution.py:223
  261.3 3.1 shard_map.85.rest_0_.mine.own_cols
  264.5 1.6 shard_map.86
  266.1 2.0 copy-done.14
  268.1 5.0 %shard_map.87.rest_1_ = bf16[1,4,1024,1024]{3,2,1,0:T(8,128)(2,1)} custom-call(f32[2]{0:T(128)S(1)} %pad_maximum_fusion.1.energies, bf16[256,1024]{1,0:T(8,128)(2,1)S(1)} %copy-done.29, bf16[256,1024]{1,0:T(8,128)(2,1)S(1)} %copy-done.29, bf16[256,1024]{1,0:T(8,128)(2,1)} %collective-permute-done.1.rest_2_.theirs, bf16[2,1024,1024]{2,1,0:T(8,128)(2,1)} %bitcast.20, ...), custom_call_target="tpu_custom_call" | custom-call | flops 1073741824 | bytes 5767168 | tf_op jit(solution)/shard_map/pallas_call | solution.py:64
  273.0 5.4 %shard_map.88.rest_1_ = bf16[1,4,1024,1024]{3,2,1,0:T(8,128)(2,1)} custom-call(f32[2]{0:T(128)S(1)} %pad_maximum_fusion.1.energies, bf16[256,1024]{1,0:T(8,128)(2,1)} %shard_map.65.rest_0_.mine.own_cols, bf16[256,1024]{1,0:T(8,128)(2,1)} %shard_map.65.rest_0_.mine.own_cols, ...), custom_call_target="tpu_custom_call", output_to_operand_aliasing={{}: (9, {})} | custom-call | flops 1073741824 | bytes 5767168 | tf_op jit(solution)/shard_map/pallas_call | solution.py:64
  278.4 5.0 %shard_map.89.rest_1_ = bf16[1,4,1024,1024]{3,2,1,0:T(8,128)(2,1)} custom-call(f32[2]{0:T(128)S(1)} %pad_maximum_fusion.1.energies, bf16[256,1024]{1,0:T(8,128)(2,1)S(1)} %copy-done.25, bf16[256,1024]{1,0:T(8,128)(2,1)S(1)} %copy-done.25, bf16[256,1024]{1,0:T(8,128)(2,1)} %collective-permute-done.4.rest_2_.theirs, ...), custom_call_target="tpu_custom_call", output_to_operand_aliasing={{}: (9, {})} | custom-call | flops 1073741824 | bytes 5767168 | tf_op jit(solution)/shard_map/pallas_call | solution.py:64
  283.7 2.9 shard_map.90.rest_0_.mine.own_cols
  286.7 2.7 collective-permute-start.22
  289.4 4.8 %shard_map.91.rest_1_ = bf16[1,4,1024,1024]{3,2,1,0:T(8,128)(2,1)} custom-call(f32[2]{0:T(128)S(1)} %pad_maximum_fusion.1.energies, bf16[256,1024]{1,0:T(8,128)(2,1)S(1)} %copy-done.31, bf16[256,1024]{1,0:T(8,128)(2,1)S(1)} %copy-done.31, bf16[256,1024]{1,0:T(8,128)(2,1)S(1)} %copy-done.33, ...), custom_call_target="tpu_custom_call", output_to_operand_aliasing={{}: (9, {})} | custom-call | flops 1073741824 | bytes 5767168 | tf_op jit(solution)/shard_map/pallas_call | solution.py:64
  294.3 4.9 %shard_map.92.rest_1_ = bf16[1,4,1024,1024]{3,2,1,0:T(8,128)(2,1)} custom-call(f32[2]{0:T(128)S(1)} %pad_maximum_fusion.2.energies, bf16[256,1024]{1,0:T(8,128)(2,1)S(1)} %copy-done.19, bf16[256,1024]{1,0:T(8,128)(2,1)S(1)} %copy-done.19, bf16[256,1024]{1,0:T(8,128)(2,1)S(1)} %copy-done.35, ...), custom_call_target="tpu_custom_call", output_to_operand_aliasing={{}: (9, {})} | custom-call | flops 1073741824 | bytes 5767168 | tf_op jit(solution)/shard_map/pallas_call | solution.py:64
  299.2 4.8 %shard_map.93.rest_1_ = bf16[1,4,1024,1024]{3,2,1,0:T(8,128)(2,1)} custom-call(f32[2]{0:T(128)S(1)} %pad_maximum_fusion.2.energies, bf16[256,1024]{1,0:T(8,128)(2,1)S(1)} %copy-done.27, bf16[256,1024]{1,0:T(8,128)(2,1)S(1)} %copy-done.27, bf16[256,1024]{1,0:T(8,128)(2,1)S(1)} %copy-done.37, ...), custom_call_target="tpu_custom_call", output_to_operand_aliasing={{}: (9, {})} | custom-call | flops 1073741824 | bytes 5767168 | tf_op jit(solution)/shard_map/pallas_call | solution.py:64
  304.0 2.1 collective-permute-done.20.rest_2_.theirs
  306.1 3.0 shard_map.94.rest_0_.mine.own_cols
  309.2 4.9 %shard_map.95.rest_1_ = bf16[1,4,1024,1024]{3,2,1,0:T(8,128)(2,1)} custom-call(f32[2]{0:T(128)S(1)} %pad_maximum_fusion.2.energies, bf16[256,1024]{1,0:T(8,128)(2,1)S(1)} %copy-done.21, bf16[256,1024]{1,0:T(8,128)(2,1)S(1)} %copy-done.21, bf16[256,1024]{1,0:T(8,128)(2,1)S(1)} %copy-done.39, ...), custom_call_target="tpu_custom_call", output_to_operand_aliasing={{}: (9, {})} | custom-call | flops 1073741824 | bytes 5767168 | tf_op jit(solution)/shard_map/pallas_call | solution.py:64
  314.1 4.8 %shard_map.96.rest_1_ = bf16[1,4,1024,1024]{3,2,1,0:T(8,128)(2,1)} custom-call(f32[2]{0:T(128)S(1)} %pad_maximum_fusion.2.energies, bf16[256,1024]{1,0:T(8,128)(2,1)S(1)} %copy-done.23, bf16[256,1024]{1,0:T(8,128)(2,1)S(1)} %copy-done.23, bf16[256,1024]{1,0:T(8,128)(2,1)S(1)} %copy-done.41, ...), custom_call_target="tpu_custom_call", output_to_operand_aliasing={{}: (9, {})} | custom-call | flops 1073741824 | bytes 5767168 | tf_op jit(solution)/shard_map/pallas_call | solution.py:64
  318.9 5.3 %shard_map.97.rest_1_ = bf16[1,4,1024,1024]{3,2,1,0:T(8,128)(2,1)} custom-call(f32[2]{0:T(128)S(1)} %pad_maximum_fusion.3.energies, bf16[256,1024]{1,0:T(8,128)(2,1)} %shard_map.77.rest_0_.mine.own_cols, bf16[256,1024]{1,0:T(8,128)(2,1)} %shard_map.77.rest_0_.mine.own_cols, ...), custom_call_target="tpu_custom_call", output_to_operand_aliasing={{}: (9, {})} | custom-call | flops 1073741824 | bytes 5767168 | tf_op jit(solution)/shard_map/pallas_call | solution.py:64
  324.2 4.3 %collective-permute-done.21.rest_2_.theirs = bf16[256,1024]{1,0:T(8,128)(2,1)S(1)} collective-permute-done((bf16[256,1024]{1,0:T(8,128)(2,1)S(1)}, bf16[256,1024]{1,0:T(8,128)(2,1)S(1)}, u32[]{:S(2)}, u32[]{:S(2)}) %collective-permute-start.21) | collective-permute-done | bytes 524320 | tf_op jit(solution)/shard_map/ppermute | solution.py:223
  328.6 2.7 shard_map.98.rest_0_.mine.own_cols
  331.4 3.9 %shard_map.99.rest_1_ = bf16[1,4,1024,1024]{3,2,1,0:T(8,128)(2,1)} custom-call(f32[2]{0:T(128)S(1)} %pad_maximum_fusion.3.energies, bf16[256,1024]{1,0:T(8,128)(2,1)S(1)} %shard_map.79.rest_0_.mine.own_cols, bf16[256,1024]{1,0:T(8,128)(2,1)S(1)} %shard_map.79.rest_0_.mine.own_cols, ...), custom_call_target="tpu_custom_call", output_to_operand_aliasing={{}: (9, {})} | custom-call | flops 1073741824 | bytes 5767168 | tf_op jit(solution)/shard_map/pallas_call | solution.py:64
  335.3 4.5 %shard_map.100.rest_1_ = bf16[1,4,1024,1024]{3,2,1,0:T(8,128)(2,1)} custom-call(f32[2]{0:T(128)S(1)} %pad_maximum_fusion.3.energies, bf16[256,1024]{1,0:T(8,128)(2,1)} %shard_map.81.rest_0_.mine.own_cols, bf16[256,1024]{1,0:T(8,128)(2,1)} %shard_map.81.rest_0_.mine.own_cols, ...), custom_call_target="tpu_custom_call", output_to_operand_aliasing={{}: (9, {})} | custom-call | flops 1073741824 | bytes 5767168 | tf_op jit(solution)/shard_map/pallas_call | solution.py:64
  339.7 3.4 shard_map.101.rest_1_
  343.1 2.4 collective-permute-done.22.rest_2_.theirs
  345.5 2.7 shard_map.102.mine.rest_0_
  348.8 3.4 shard_map.104.rest_1_
  353.6 3.9 %shard_map.105.rest_1_ = bf16[1,4,1024,1024]{3,2,1,0:T(8,128)(2,1)} custom-call(f32[2]{0:T(128)S(1)} %pad_maximum_fusion.energies, bf16[256,1024]{1,0:T(8,128)(2,1)S(1)} %shard_map.90.rest_0_.mine.own_cols, bf16[256,1024]{1,0:T(8,128)(2,1)S(1)} %shard_map.90.rest_0_.mine.own_cols, ...), custom_call_target="tpu_custom_call", output_to_operand_aliasing={{}: (9, {})} | custom-call | flops 1073741824 | bytes 5767168 | tf_op jit(solution)/shard_map/pallas_call | solution.py:64
  357.5 4.9 %collective-permute-done.25.theirs = bf16[256,1024]{1,0:T(8,128)(2,1)} collective-permute-done((bf16[256,1024]{1,0:T(8,128)(2,1)S(1)}, bf16[256,1024]{1,0:T(8,128)(2,1)}, u32[]{:S(2)}, u32[]{:S(2)}) %collective-permute-start.25) | collective-permute-done | bytes 524320 | tf_op jit(solution)/shard_map/ppermute | solution.py:223
  362.4 3.9 %shard_map.106.rest_1_ = bf16[1,4,1024,1024]{3,2,1,0:T(8,128)(2,1)} custom-call(f32[2]{0:T(128)S(1)} %pad_maximum_fusion.energies, bf16[256,1024]{1,0:T(8,128)(2,1)S(1)} %shard_map.94.rest_0_.mine.own_cols, bf16[256,1024]{1,0:T(8,128)(2,1)S(1)} %shard_map.94.rest_0_.mine.own_cols, ...), custom_call_target="tpu_custom_call", output_to_operand_aliasing={{}: (9, {})} | custom-call | flops 1073741824 | bytes 5767168 | tf_op jit(solution)/shard_map/pallas_call | solution.py:64
  366.2 1.6 collective-permute-done.24.theirs
  367.9 3.3 shard_map.107._
  (144 shorter events, 28.2 us)
Async XLA Ops:
  1.0 20.4 %collective-permute-start = (bf16[128,512]{1,0:T(8,128)(2,1)S(1)}, bf16[128,512]{1,0:T(8,128)(2,1)S(1)}, u32[]{:S(2)}, u32[]{:S(2)}) collective-permute-start(bf16[128,512]{1,0:T(8,128)(2,1)S(1)} %get-tuple-element.11), channel_id=1, source_target_pairs={{0,4},{4,0},{1,5},{5,1},{2,6},{6,2},{3,7},{7,3},{8,12},{12,8},{9,1... | collective-permute-start | bytes 393224 | tf_op jit(solution)/shard_map/ppermute | solution.py:227
  9.6 4.0 %copy-start.28 = (bf16[256,1024]{1,0:T(8,128)(2,1)}, bf16[256,1024]{1,0:T(8,128)(2,1)S(1)}, u32[]{:S(2)}) copy-start(bf16[256,1024]{1,0:T(8,128)(2,1)S(1)} %shard_map.64.rest_0_.mine.own_cols) | copy-start | bytes 1572868
  9.6 49.4 %collective-permute-start.1 = (bf16[256,1024]{1,0:T(8,128)(2,1)S(1)}, bf16[256,1024]{1,0:T(8,128)(2,1)}, u32[]{:S(2)}, u32[]{:S(2)}) collective-permute-start(bf16[256,1024]{1,0:T(8,128)(2,1)S(1)} %shard_map.64.rest_0_.mine.own_cols), channel_id=1, source_target_pairs={{0,4},{4,0},{1,5},{5,1},{2,6},{6,2},{3,7},{7,3},{8,12},{12,8},{9,1... | collective-permute-start | bytes 1572872 | tf_op jit(solution)/shard_map/ppermute | solution.py:223
  13.6 6.4 %copy-start.45 = (f32[2]{0:T(128)S(1)}, f32[2]{0:T(128)}, u32[]{:S(2)}) copy-start(f32[2]{0:T(128)} %param.9) | copy-start | bytes 28
  13.6 7.0 %copy-start.46 = (f32[16]{0:T(128)S(1)}, f32[16]{0:T(128)}, u32[]{:S(2)}) copy-start(f32[16]{0:T(128)} %param.10) | copy-start | bytes 196
  13.6 45.5 %copy-start.17 = (bf16[1024,1024]{1,0:T(8,128)(2,1)S(1)}, bf16[1024,1024]{1,0:T(8,128)(2,1)}, u32[]{:S(2)}) copy-start(bf16[1024,1024]{1,0:T(8,128)(2,1)} %f_cols.33) | copy-start | bytes 6291460
  13.6 67.9 %collective-permute-start.2 = (bf16[256,1024]{1,0:T(8,128)(2,1)}, bf16[256,1024]{1,0:T(8,128)(2,1)}, u32[]{:S(2)}, u32[]{:S(2)}) collective-permute-start(bf16[256,1024]{1,0:T(8,128)(2,1)} %shard_map.65.rest_0_.mine.own_cols), channel_id=1, source_target_pairs={{0,4},{4,0},{1,5},{5,1},{2,6},{6,2},{3,7},{7,3},{8,12},{12,8},{9,1... | collective-permute-start | bytes 1572872 | tf_op jit(solution)/shard_map/ppermute | solution.py:223
  19.5 42.6 %copy-start.24 = (bf16[256,1024]{1,0:T(8,128)(2,1)}, bf16[256,1024]{1,0:T(8,128)(2,1)S(1)}, u32[]{:S(2)}) copy-start(bf16[256,1024]{1,0:T(8,128)(2,1)S(1)} %shard_map.66.rest_0_.mine.own_cols) | copy-start | bytes 1572868
  19.5 84.5 %collective-permute-start.4 = (bf16[256,1024]{1,0:T(8,128)(2,1)S(1)}, bf16[256,1024]{1,0:T(8,128)(2,1)}, u32[]{:S(2)}, u32[]{:S(2)}) collective-permute-start(bf16[256,1024]{1,0:T(8,128)(2,1)S(1)} %shard_map.66.rest_0_.mine.own_cols), channel_id=1, source_target_pairs={{0,4},{4,0},{1,5},{5,1},{2,6},{6,2},{3,7},{7,3},{8,12},{12,8},{9,1... | collective-permute-start | bytes 1572872 | tf_op jit(solution)/shard_map/ppermute | solution.py:223
  21.4 63.1 %collective-permute-start.3 = (bf16[2,128,512]{2,1,0:T(8,128)(2,1)S(1)}, bf16[2,128,512]{2,1,0:T(8,128)(2,1)S(1)}, u32[]{:S(2)}, u32[]{:S(2)}) collective-permute-start(bf16[2,128,512]{2,1,0:T(8,128)(2,1)S(1)} %bitcast.54), channel_id=1, source_target_pairs={{0,2},{1,3},{2,0},{3,1},{4,6},{5,7},{6,4},{7,5},{8,10},{9,11},{10,... | collective-permute-start | bytes 786440 | tf_op jit(solution)/shard_map/ppermute | solution.py:235
  62.0 22.4 %copy-start.30 = (bf16[256,1024]{1,0:T(8,128)(2,1)}, bf16[256,1024]{1,0:T(8,128)(2,1)S(1)}, u32[]{:S(2)}) copy-start(bf16[256,1024]{1,0:T(8,128)(2,1)S(1)} %shard_map.68.rest_0_.mine.own_cols) | copy-start | bytes 1572868
  62.1 64.3 %collective-permute-start.5 = (bf16[256,1024]{1,0:T(8,128)(2,1)S(1)}, bf16[256,1024]{1,0:T(8,128)(2,1)S(1)}, u32[]{:S(2)}, u32[]{:S(2)}) collective-permute-start(bf16[256,1024]{1,0:T(8,128)(2,1)S(1)} %shard_map.68.rest_0_.mine.own_cols), channel_id=1, source_target_pairs={{0,4},{4,0},{1,5},{5,1},{2,6},{6,2},{3,7},{7,3},{8,12},{12,8},{9,1... | collective-permute-start | bytes 1572872 | tf_op jit(solution)/shard_map/ppermute | solution.py:223
  84.5 22.5 %copy-start.18 = (bf16[256,1024]{1,0:T(8,128)(2,1)}, bf16[256,1024]{1,0:T(8,128)(2,1)S(1)}, u32[]{:S(2)}) copy-start(bf16[256,1024]{1,0:T(8,128)(2,1)S(1)} %shard_map.69.rest_0_.mine.own_cols) | copy-start | bytes 1572868
  85.4 44.2 %collective-permute-start.6 = (bf16[4,128,512]{2,1,0:T(8,128)(2,1)}, bf16[4,128,512]{2,1,0:T(8,128)(2,1)S(1)}, u32[]{:S(2)}, u32[]{:S(2)}) collective-permute-start(bf16[4,128,512]{2,1,0:T(8,128)(2,1)} %bitcast.5.rest_1_.block), channel_id=1, source_target_pairs={{0,1},{1,0},{2,3},{3,2},{8,9},{9,8},{10,11},{11,10},{16,17},{17,16... | collective-permute-start | bytes 1572872 | tf_op jit(solution)/shard_map/ppermute | solution.py:251
  87.0 61.8 %collective-permute-start.7 = (bf16[256,1024]{1,0:T(8,128)(2,1)S(1)}, bf16[256,1024]{1,0:T(8,128)(2,1)S(1)}, u32[]{:S(2)}, u32[]{:S(2)}) collective-permute-start(bf16[256,1024]{1,0:T(8,128)(2,1)S(1)} %shard_map.69.rest_0_.mine.own_cols), channel_id=1, source_target_pairs={{0,4},{4,0},{1,5},{5,1},{2,6},{6,2},{3,7},{7,3},{8,12},{12,8},{9,1... | collective-permute-start | bytes 1572872 | tf_op jit(solution)/shard_map/ppermute | solution.py:223
  87.1 66.2 %collective-permute-start.8 = (bf16[4,128,512]{2,1,0:T(8,128)(2,1)}, bf16[4,128,512]{2,1,0:T(8,128)(2,1)S(1)}, u32[]{:S(2)}, u32[]{:S(2)}) collective-permute-start(bf16[4,128,512]{2,1,0:T(8,128)(2,1)} %bitcast.5.rest_1_.block), channel_id=1, source_target_pairs={{0,8},{1,9},{2,10},{3,11},{8,0},{9,1},{10,2},{11,3},{16,24},{17,25... | collective-permute-start | bytes 1572872 | tf_op jit(solution)/shard_map/ppermute | solution.py:251
  106.9 22.6 %copy-start.26 = (bf16[256,1024]{1,0:T(8,128)(2,1)}, bf16[256,1024]{1,0:T(8,128)(2,1)S(1)}, u32[]{:S(2)}) copy-start(bf16[256,1024]{1,0:T(8,128)(2,1)S(1)} %shard_map.71.rest_0_.mine.own_cols) | copy-start | bytes 1572868
  106.9 64.3 %collective-permute-start.9 = (bf16[256,1024]{1,0:T(8,128)(2,1)S(1)}, bf16[256,1024]{1,0:T(8,128)(2,1)S(1)}, u32[]{:S(2)}, u32[]{:S(2)}) collective-permute-start(bf16[256,1024]{1,0:T(8,128)(2,1)S(1)} %shard_map.71.rest_0_.mine.own_cols), channel_id=1, source_target_pairs={{0,4},{4,0},{1,5},{5,1},{2,6},{6,2},{3,7},{7,3},{8,12},{12,8},{9,1... | collective-permute-start | bytes 1572872 | tf_op jit(solution)/shard_map/ppermute | solution.py:223
  108.7 2.0 copy-start
  126.3 3.2 copy-start.32
  126.3 3.4 copy-start.1
  126.3 51.1 %collective-permute-start.10 = (bf16[4,128,512]{2,1,0:T(8,128)(2,1)}, bf16[4,128,512]{2,1,0:T(8,128)(2,1)S(1)}, u32[]{:S(2)}, u32[]{:S(2)}) collective-permute-start(bf16[4,128,512]{2,1,0:T(8,128)(2,1)} %bitcast.5.rest_1_.block), channel_id=1, source_target_pairs={{0,9},{1,8},{2,11},{3,10},{8,1},{9,0},{10,3},{11,2},{16,25},{17,24... | collective-permute-start | bytes 1572872 | tf_op jit(solution)/shard_map/ppermute | solution.py:251
  129.6 23.7 %copy-start.20 = (bf16[256,1024]{1,0:T(8,128)(2,1)}, bf16[256,1024]{1,0:T(8,128)(2,1)S(1)}, u32[]{:S(2)}) copy-start(bf16[256,1024]{1,0:T(8,128)(2,1)S(1)} %shard_map.73.rest_0_.mine.own_cols) | copy-start | bytes 1572868
  129.6 52.9 %collective-permute-start.11 = (bf16[256,1024]{1,0:T(8,128)(2,1)S(1)}, bf16[256,1024]{1,0:T(8,128)(2,1)S(1)}, u32[]{:S(2)}, u32[]{:S(2)}) collective-permute-start(bf16[256,1024]{1,0:T(8,128)(2,1)S(1)} %shard_map.73.rest_0_.mine.own_cols), channel_id=1, source_target_pairs={{0,4},{4,0},{1,5},{5,1},{2,6},{6,2},{3,7},{7,3},{8,12},{12,8},{9,1... | collective-permute-start | bytes 1572872 | tf_op jit(solution)/shard_map/ppermute | solution.py:223
  148.8 4.5 %copy-start.34 = (bf16[256,1024]{1,0:T(8,128)(2,1)}, bf16[256,1024]{1,0:T(8,128)(2,1)S(1)}, u32[]{:S(2)}) copy-start(bf16[256,1024]{1,0:T(8,128)(2,1)S(1)} %collective-permute-done.7.rest_2_.theirs) | copy-start | bytes 1572868
  148.8 6.1 %copy-start.3 = (bf16[2,4,2,128,1024]{4,3,2,1,0:T(8,128)(2,1)S(1)}, bf16[2,4,2,128,1024]{4,3,2,1,0:T(8,128)(2,1)}, u32[]{:S(2)}) copy-start(bf16[2,4,2,128,1024]{4,3,2,1,0:T(8,128)(2,1)} %copy-done.2) | copy-start | bytes 12582916
  148.8 37.1 %collective-permute-start.12 = (bf16[4,128,512]{2,1,0:T(8,128)(2,1)}, bf16[4,128,512]{2,1,0:T(8,128)(2,1)S(1)}, u32[]{:S(2)}, u32[]{:S(2)}) collective-permute-start(bf16[4,128,512]{2,1,0:T(8,128)(2,1)} %bitcast.5.rest_1_.block), channel_id=1, source_target_pairs={{0,16},{1,17},{2,18},{3,19},{8,24},{9,25},{10,26},{11,27},{16,0},{... | collective-permute-start | bytes 1572872 | tf_op jit(solution)/shard_map/ppermute | solution.py:251
  153.3 24.2 %copy-start.22 = (bf16[256,1024]{1,0:T(8,128)(2,1)}, bf16[256,1024]{1,0:T(8,128)(2,1)S(1)}, u32[]{:S(2)}) copy-start(bf16[256,1024]{1,0:T(8,128)(2,1)S(1)} %shard_map.75.rest_0_.mine.own_cols) | copy-start | bytes 1572868
  153.3 62.9 %collective-permute-start.13 = (bf16[256,1024]{1,0:T(8,128)(2,1)S(1)}, bf16[256,1024]{1,0:T(8,128)(2,1)S(1)}, u32[]{:S(2)}, u32[]{:S(2)}) collective-permute-start(bf16[256,1024]{1,0:T(8,128)(2,1)S(1)} %shard_map.75.rest_0_.mine.own_cols), channel_id=1, source_target_pairs={{0,4},{4,0},{1,5},{5,1},{2,6},{6,2},{3,7},{7,3},{8,12},{12,8},{9,1... | collective-permute-start | bytes 1572872 | tf_op jit(solution)/shard_map/ppermute | solution.py:223
  171.3 6.2 %copy-start.36 = (bf16[256,1024]{1,0:T(8,128)(2,1)}, bf16[256,1024]{1,0:T(8,128)(2,1)S(1)}, u32[]{:S(2)}) copy-start(bf16[256,1024]{1,0:T(8,128)(2,1)S(1)} %collective-permute-done.9.rest_2_.theirs) | copy-start | bytes 1572868
  171.3 6.3 %copy-start.5 = (bf16[2,4,2,128,1024]{4,3,2,1,0:T(8,128)(2,1)S(1)}, bf16[2,4,2,128,1024]{4,3,2,1,0:T(8,128)(2,1)}, u32[]{:S(2)}) copy-start(bf16[2,4,2,128,1024]{4,3,2,1,0:T(8,128)(2,1)} %copy-done.4) | copy-start | bytes 12582916
  171.3 52.7 %collective-permute-start.14 = (bf16[4,128,512]{2,1,0:T(8,128)(2,1)}, bf16[4,128,512]{2,1,0:T(8,128)(2,1)S(1)}, u32[]{:S(2)}, u32[]{:S(2)}) collective-permute-start(bf16[4,128,512]{2,1,0:T(8,128)(2,1)} %bitcast.5.rest_1_.block), channel_id=1, source_target_pairs={{0,17},{1,16},{2,19},{3,18},{8,25},{9,24},{10,27},{11,26},{16,1},{... | collective-permute-start | bytes 1572872 | tf_op jit(solution)/shard_map/ppermute | solution.py:251
  177.5 60.8 %collective-permute-start.16 = (bf16[4,128,512]{2,1,0:T(8,128)(2,1)}, bf16[4,128,512]{2,1,0:T(8,128)(2,1)}, u32[]{:S(2)}, u32[]{:S(2)}) collective-permute-start(bf16[4,128,512]{2,1,0:T(8,128)(2,1)} %bitcast.5.rest_1_.block), channel_id=1, source_target_pairs={{0,24},{1,25},{2,26},{3,27},{8,16},{9,17},{10,18},{11,19},{16,8},{... | collective-permute-start | bytes 1572872 | tf_op jit(solution)/shard_map/ppermute | solution.py:251
  178.1 2.0 copy-start.6
  182.5 3.4 copy-start.38
  182.5 35.0 %copy-start.7 = (bf16[2,4,2,128,1024]{4,3,2,1,0:T(8,128)(2,1)S(1)}, bf16[2,4,2,128,1024]{4,3,2,1,0:T(8,128)(2,1)}, u32[]{:S(2)}) copy-start(bf16[2,4,2,128,1024]{4,3,2,1,0:T(8,128)(2,1)} %copy-done.6) | copy-start | bytes 12582916
  182.5 49.6 %collective-permute-start.15 = (bf16[256,1024]{1,0:T(8,128)(2,1)}, bf16[256,1024]{1,0:T(8,128)(2,1)}, u32[]{:S(2)}, u32[]{:S(2)}) collective-permute-start(bf16[256,1024]{1,0:T(8,128)(2,1)} %shard_map.77.rest_0_.mine.own_cols), channel_id=1, source_target_pairs={{0,4},{4,0},{1,5},{5,1},{2,6},{6,2},{3,7},{7,3},{8,12},{12,8},{9,1... | collective-permute-start | bytes 1572872 | tf_op jit(solution)/shard_map/ppermute | solution.py:223
  185.9 75.3 %collective-permute-start.17 = (bf16[256,1024]{1,0:T(8,128)(2,1)S(1)}, bf16[256,1024]{1,0:T(8,128)(2,1)}, u32[]{:S(2)}, u32[]{:S(2)}) collective-permute-start(bf16[256,1024]{1,0:T(8,128)(2,1)S(1)} %shard_map.79.rest_0_.mine.own_cols), channel_id=1, source_target_pairs={{0,4},{4,0},{1,5},{5,1},{2,6},{6,2},{3,7},{7,3},{8,12},{12,8},{9,1... | collective-permute-start | bytes 1572872 | tf_op jit(solution)/shard_map/ppermute | solution.py:223
  216.2 7.7 %copy-start.40 = (bf16[256,1024]{1,0:T(8,128)(2,1)}, bf16[256,1024]{1,0:T(8,128)(2,1)S(1)}, u32[]{:S(2)}) copy-start(bf16[256,1024]{1,0:T(8,128)(2,1)S(1)} %collective-permute-done.13.rest_2_.theirs) | copy-start | bytes 1572868
  216.2 48.2 %collective-permute-start.18 = (bf16[4,128,512]{2,1,0:T(8,128)(2,1)}, bf16[4,128,512]{2,1,0:T(8,128)(2,1)}, u32[]{:S(2)}, u32[]{:S(2)}) collective-permute-start(bf16[4,128,512]{2,1,0:T(8,128)(2,1)} %bitcast.5.rest_1_.block), channel_id=1, source_target_pairs={{0,25},{1,24},{2,27},{3,26},{8,17},{9,16},{10,19},{11,18},{16,9},{... | collective-permute-start | bytes 1572872 | tf_op jit(solution)/shard_map/ppermute | solution.py:251
  220.2 5.9 %copy-start.42 = (f32[1024]{0:T(1024)S(1)}, f32[1024]{0:T(1024)}, u32[]{:S(2)}) copy-start(f32[1024]{0:T(1024)} %param.11) | copy-start | bytes 12292
  224.7 59.0 %collective-permute-start.19 = (bf16[256,1024]{1,0:T(8,128)(2,1)}, bf16[256,1024]{1,0:T(8,128)(2,1)}, u32[]{:S(2)}, u32[]{:S(2)}) collective-permute-start(bf16[256,1024]{1,0:T(8,128)(2,1)} %shard_map.81.rest_0_.mine.own_cols), channel_id=1, source_target_pairs={{0,4},{4,0},{1,5},{5,1},{2,6},{6,2},{3,7},{7,3},{8,12},{12,8},{9,1... | collective-permute-start | bytes 1572872 | tf_op jit(solution)/shard_map/ppermute | solution.py:223
  226.3 2.2 copy-start.9
  232.2 6.1 %copy-start.11 = (bf16[2,4,2,128,1024]{4,3,2,1,0:T(8,128)(2,1)S(1)}, bf16[2,4,2,128,1024]{4,3,2,1,0:T(8,128)(2,1)}, u32[]{:S(2)}) copy-start(bf16[2,4,2,128,1024]{4,3,2,1,0:T(8,128)(2,1)} %copy-done.10) | copy-start | bytes 12582916
  235.3 70.8 %collective-permute-start.20 = (bf16[256,1024]{1,0:T(8,128)(2,1)S(1)}, bf16[256,1024]{1,0:T(8,128)(2,1)S(1)}, u32[]{:S(2)}, u32[]{:S(2)}) collective-permute-start(bf16[256,1024]{1,0:T(8,128)(2,1)S(1)} %shard_map.83.rest_0_.mine.own_cols), channel_id=1, source_target_pairs={{0,4},{4,0},{1,5},{5,1},{2,6},{6,2},{3,7},{7,3},{8,12},{12,8},{9,1... | collective-permute-start | bytes 1572872 | tf_op jit(solution)/shard_map/ppermute | solution.py:223
  261.3 3.2 copy-start.13
  264.4 3.7 copy-start.29
  264.4 64.2 %collective-permute-start.21 = (bf16[256,1024]{1,0:T(8,128)(2,1)S(1)}, bf16[256,1024]{1,0:T(8,128)(2,1)S(1)}, u32[]{:S(2)}, u32[]{:S(2)}) collective-permute-start(bf16[256,1024]{1,0:T(8,128)(2,1)S(1)} %shard_map.85.rest_0_.mine.own_cols), channel_id=1, source_target_pairs={{0,4},{4,0},{1,5},{5,1},{2,6},{6,2},{3,7},{7,3},{8,12},{12,8},{9,1... | collective-permute-start | bytes 1572872 | tf_op jit(solution)/shard_map/ppermute | solution.py:223
  273.0 5.4 %copy-start.25 = (bf16[256,1024]{1,0:T(8,128)(2,1)S(1)}, bf16[256,1024]{1,0:T(8,128)(2,1)}, u32[]{:S(2)}) copy-start(bf16[256,1024]{1,0:T(8,128)(2,1)} %copy-done.24) | copy-start | bytes 1572868
  283.4 6.0 %copy-start.31 = (bf16[256,1024]{1,0:T(8,128)(2,1)S(1)}, bf16[256,1024]{1,0:T(8,128)(2,1)}, u32[]{:S(2)}) copy-start(bf16[256,1024]{1,0:T(8,128)(2,1)} %copy-done.30) | copy-start | bytes 1572868
  283.4 6.0 %copy-start.33 = (bf16[256,1024]{1,0:T(8,128)(2,1)S(1)}, bf16[256,1024]{1,0:T(8,128)(2,1)}, u32[]{:S(2)}) copy-start(bf16[256,1024]{1,0:T(8,128)(2,1)} %copy-done.32) | copy-start | bytes 1572868
  286.7 7.5 %copy-start.19 = (bf16[256,1024]{1,0:T(8,128)(2,1)S(1)}, bf16[256,1024]{1,0:T(8,128)(2,1)}, u32[]{:S(2)}) copy-start(bf16[256,1024]{1,0:T(8,128)(2,1)} %copy-done.18) | copy-start | bytes 1572868
  286.7 7.5 %copy-start.35 = (bf16[256,1024]{1,0:T(8,128)(2,1)S(1)}, bf16[256,1024]{1,0:T(8,128)(2,1)}, u32[]{:S(2)}) copy-start(bf16[256,1024]{1,0:T(8,128)(2,1)} %copy-done.34) | copy-start | bytes 1572868
  286.7 58.8 %collective-permute-start.22 = (bf16[256,1024]{1,0:T(8,128)(2,1)S(1)}, bf16[256,1024]{1,0:T(8,128)(2,1)}, u32[]{:S(2)}, u32[]{:S(2)}) collective-permute-start(bf16[256,1024]{1,0:T(8,128)(2,1)S(1)} %shard_map.90.rest_0_.mine.own_cols), channel_id=1, source_target_pairs={{0,4},{4,0},{1,5},{5,1},{2,6},{6,2},{3,7},{7,3},{8,12},{12,8},{9,1... | collective-permute-start | bytes 1572872 | tf_op jit(solution)/shard_map/ppermute | solution.py:223
  294.2 4.9 %copy-start.27 = (bf16[256,1024]{1,0:T(8,128)(2,1)S(1)}, bf16[256,1024]{1,0:T(8,128)(2,1)}, u32[]{:S(2)}) copy-start(bf16[256,1024]{1,0:T(8,128)(2,1)} %copy-done.26) | copy-start | bytes 1572868
  294.3 4.9 %copy-start.37 = (bf16[256,1024]{1,0:T(8,128)(2,1)S(1)}, bf16[256,1024]{1,0:T(8,128)(2,1)}, u32[]{:S(2)}) copy-start(bf16[256,1024]{1,0:T(8,128)(2,1)} %copy-done.36) | copy-start | bytes 1572868
  304.0 5.2 %copy-start.21 = (bf16[256,1024]{1,0:T(8,128)(2,1)S(1)}, bf16[256,1024]{1,0:T(8,128)(2,1)}, u32[]{:S(2)}) copy-start(bf16[256,1024]{1,0:T(8,128)(2,1)} %copy-done.20) | copy-start | bytes 1572868
  304.0 5.2 %copy-start.39 = (bf16[256,1024]{1,0:T(8,128)(2,1)S(1)}, bf16[256,1024]{1,0:T(8,128)(2,1)}, u32[]{:S(2)}) copy-start(bf16[256,1024]{1,0:T(8,128)(2,1)} %copy-done.38) | copy-start | bytes 1572868
  309.1 5.0 %copy-start.23 = (bf16[256,1024]{1,0:T(8,128)(2,1)S(1)}, bf16[256,1024]{1,0:T(8,128)(2,1)}, u32[]{:S(2)}) copy-start(bf16[256,1024]{1,0:T(8,128)(2,1)} %copy-done.22) | copy-start | bytes 1572868
  309.1 5.0 %copy-start.41 = (bf16[256,1024]{1,0:T(8,128)(2,1)S(1)}, bf16[256,1024]{1,0:T(8,128)(2,1)}, u32[]{:S(2)}) copy-start(bf16[256,1024]{1,0:T(8,128)(2,1)} %copy-done.40) | copy-start | bytes 1572868
  309.1 53.3 %collective-permute-start.25 = (bf16[256,1024]{1,0:T(8,128)(2,1)S(1)}, bf16[256,1024]{1,0:T(8,128)(2,1)}, u32[]{:S(2)}, u32[]{:S(2)}) collective-permute-start(bf16[256,1024]{1,0:T(8,128)(2,1)S(1)} %shard_map.94.rest_0_.mine.own_cols), channel_id=1, source_target_pairs={{0,4},{4,0},{1,5},{5,1},{2,6},{6,2},{3,7},{7,3},{8,12},{12,8},{9,1... | collective-permute-start | bytes 1572872 | tf_op jit(solution)/shard_map/ppermute | solution.py:223
  324.2 7.1 %copy-start.15 = (bf16[2,4,2,128,1024]{4,3,2,1,0:T(8,128)(2,1)S(1)}, bf16[2,4,2,128,1024]{4,3,2,1,0:T(8,128)(2,1)}, u32[]{:S(2)}) copy-start(bf16[2,4,2,128,1024]{4,3,2,1,0:T(8,128)(2,1)} %copy-done.14) | copy-start | bytes 12582916
  331.3 36.6 %collective-permute-start.24 = (bf16[128,1024]{1,0:T(8,128)(2,1)S(1)}, bf16[128,1024]{1,0:T(8,128)(2,1)S(1)}, u32[]{:S(2)}, u32[]{:S(2)}) collective-permute-start(bf16[128,1024]{1,0:T(8,128)(2,1)S(1)} %shard_map.98.rest_0_.mine.own_cols), channel_id=1, source_target_pairs={{0,4},{4,0},{1,5},{5,1},{2,6},{6,2},{3,7},{7,3},{8,12},{12,8},{9,1... | collective-permute-start | bytes 786440 | tf_op jit(solution)/shard_map/ppermute | solution.py:223
  348.2 24.1 %collective-permute-start.23 = (bf16[128,1024]{1,0:T(8,128)(2,1)S(1)}, bf16[128,1024]{1,0:T(8,128)(2,1)S(1)}, u32[]{:S(2)}, u32[]{:S(2)}) collective-permute-start(bf16[128,1024]{1,0:T(8,128)(2,1)S(1)} %shard_map.102.mine.rest_0_), channel_id=1, source_target_pairs={{0,4},{4,0},{1,5},{5,1},{2,6},{6,2},{3,7},{7,3},{8,12},{12,8},{9,1... | collective-permute-start | bytes 786440 | tf_op jit(solution)/shard_map/ppermute | solution.py:223
  (9 other events, 15.5 us)

commit v9 on v8

--- a/solution.py
+++ b/solution.py
@@ -6,7 +6,7 @@
 from jax.sharding import Mesh, PartitionSpec as P
 
 ROWS = 256
-COLS = 256
+COLS = 512
 DEPTH = 3
 VMEM = 48 * 1024 * 1024
 LAST_VMEM = 24 * 1024 * 1024

time: 376 us -> 375 us (level)
  waiting for transfers between devices: 160 us -> 176 us
  Pallas kernels: 136 us -> 123 us
    ppermute x17, waiting for transfers between devices: 160 us -> 176 us  [send(): other.append(lax.ppermute(piece, 'half', SWAP))]
    pallas_call x16, Pallas kernels: 71 us -> 58.3 us  [finish(): pl.pallas_call(finish_kernel, out_shape=jax.ShapeDtypeStruct(shape, jnp.b...]
  transfers between devices with their start and end apart: 26 -> 26, of which waited for: 16 -> 16; matrix products, arithmetic and copies ran while one was open for 2% -> 2% of each run, Pallas kernels for 36% -> 33%
where the time goes in v9:
time: 375 us; the launch traced here: 374 us
  waiting for transfers between devices  176 us (47%)
  Pallas kernels  123 us (33%)
  starting transfers between devices  43.9 us (12%)
  local copies, waits for them, and re-layouts  24.4 us (7%)
  other arithmetic  5.92 us (2%)
    ppermute x17, waiting for transfers between devices, send(): other.append(lax.ppermute(piece, 'half', SWAP))  176 us
    pallas_call x16, Pallas kernels, finish(): pl.pallas_call(finish_kernel, out_shape=jax.ShapeDtypeStruct(shape, jnp.b...  58.3 us
    pallas_call x17, Pallas kernels, dress(): pl.pallas_call(dress_kernel, out_shape=jax.ShapeDtypeStruct((rows, virt),...  53.2 us
    ppermute x1, starting transfers between devices, start_swap(): lax.ppermute(block, 'rest', [(i, i ^ steps[0]) for i in range(n_rest)])  24.6 us
    unnamed x94, local copies, waits for them, and re-layouts  21.8 us
    ppermute x17, starting transfers between devices, send(): other.append(lax.ppermute(piece, 'half', SWAP))  9.66 us
    pallas_call x8, Pallas kernels, place(): pl.pallas_call(place_kernel, out_shape=jax.ShapeDtypeStruct((2, lead, 2,...  7.77 us
  transfers between devices with their start and end apart: 26, of which 16 were waited for; matrix products, arithmetic and copies ran while one was open for 2% of the time, Pallas kernels for 33%

profile of v9, /device:TPU:0, one launch (start us, length us, event | category | flops | bytes accessed | tf_op | source)
XLA Modules:
  0.0 373.9 jit_solution(7884266170934366238)
XLA Ops:
  1.0 4.1 %collective-permute-start = (bf16[128,512]{1,0:T(8,128)(2,1)S(1)}, bf16[128,512]{1,0:T(8,128)(2,1)S(1)}, u32[]{:S(2)}, u32[]{:S(2)}) collective-permute-start(bf16[128,512]{1,0:T(8,128)(2,1)S(1)} %get-tuple-element.11), channel_id=1, source_target_pairs={{0,4},{4,0},{1,5},{5,1},{2,6},{6,2},{3,7},{7,3},{8,12},{12,8},{9,1... | collective-permute-start | bytes 393224 | tf_op jit(solution)/shard_map/ppermute | solution.py:227
  6.7 2.9 shard_map.64.rest_0_.mine.own_cols
  9.7 3.9 %shard_map.65.rest_0_.mine.own_cols = bf16[256,1024]{1,0:T(8,128)(2,1)} custom-call(bf16[1024,1024]{1,0:T(8,128)(2,1)S(1)} %copy-done.16, bf16[1,4,1024,1024]{3,2,1,0:T(8,128)(2,1)} %t_rows.33, bf16[1,4,1024,1024]{3,2,1,0:T(8,128)(2,1)} %t_rows.33, bf16[1024,1024]{1,0:T(8,128)(2,1)S(1)} %copy-done.16, bf16[256,1024]{1,0:T(8,128)(2,1)S(1)} %shard_map.64.rest_0_.mine.own_cols), custom_call_target="tpu_custom_call" | custom-call | flops 1073741824 | bytes 5767168 | tf_op jit(solution)/shard_map/pallas_call | solution.py:32
  13.6 2.9 collective-permute-start.2
  16.5 2.9 shard_map.66.rest_0_.mine.own_cols
  21.4 24.6 %collective-permute-start.3 = (bf16[2,128,512]{2,1,0:T(8,128)(2,1)S(1)}, bf16[2,128,512]{2,1,0:T(8,128)(2,1)S(1)}, u32[]{:S(2)}, u32[]{:S(2)}) collective-permute-start(bf16[2,128,512]{2,1,0:T(8,128)(2,1)S(1)} %bitcast.54), channel_id=1, source_target_pairs={{0,2},{1,3},{2,0},{3,1},{4,6},{5,7},{6,4},{7,5},{8,10},{9,11},{10,... | collective-permute-start | bytes 786440 | tf_op jit(solution)/shard_map/ppermute | solution.py:235
  46.1 13.0 %collective-permute-done.1.rest_2_.theirs = bf16[256,1024]{1,0:T(8,128)(2,1)} collective-permute-done((bf16[256,1024]{1,0:T(8,128)(2,1)S(1)}, bf16[256,1024]{1,0:T(8,128)(2,1)}, u32[]{:S(2)}, u32[]{:S(2)}) %collective-permute-start.1) | collective-permute-done | bytes 524320 | tf_op jit(solution)/shard_map/ppermute | solution.py:223
  59.1 3.0 shard_map.68.rest_0_.mine.own_cols
  62.1 19.4 %collective-permute-done.2.rest_2_.theirs = bf16[256,1024]{1,0:T(8,128)(2,1)} collective-permute-done((bf16[256,1024]{1,0:T(8,128)(2,1)}, bf16[256,1024]{1,0:T(8,128)(2,1)}, u32[]{:S(2)}, u32[]{:S(2)}) %collective-permute-start.2) | collective-permute-done | bytes 524320 | tf_op jit(solution)/shard_map/ppermute | solution.py:223
  81.5 2.9 shard_map.69.rest_0_.mine.own_cols
  87.2 16.8 %collective-permute-done.4.rest_2_.theirs = bf16[256,1024]{1,0:T(8,128)(2,1)} collective-permute-done((bf16[256,1024]{1,0:T(8,128)(2,1)S(1)}, bf16[256,1024]{1,0:T(8,128)(2,1)}, u32[]{:S(2)}, u32[]{:S(2)}) %collective-permute-start.4) | collective-permute-done | bytes 524320 | tf_op jit(solution)/shard_map/ppermute | solution.py:223
  104.0 3.0 shard_map.71.rest_0_.mine.own_cols
  108.7 2.0 copy-done
  110.7 15.7 %collective-permute-done.5.rest_2_.theirs = bf16[256,1024]{1,0:T(8,128)(2,1)S(1)} collective-permute-done((bf16[256,1024]{1,0:T(8,128)(2,1)S(1)}, bf16[256,1024]{1,0:T(8,128)(2,1)S(1)}, u32[]{:S(2)}, u32[]{:S(2)}) %collective-permute-start.5) | collective-permute-done | bytes 524320 | tf_op jit(solution)/shard_map/ppermute | solution.py:223
  126.3 3.2 shard_map.73.rest_0_.mine.own_cols
  130.3 2.0 copy-done.2
  132.3 16.5 %collective-permute-done.7.rest_2_.theirs = bf16[256,1024]{1,0:T(8,128)(2,1)S(1)} collective-permute-done((bf16[256,1024]{1,0:T(8,128)(2,1)S(1)}, bf16[256,1024]{1,0:T(8,128)(2,1)S(1)}, u32[]{:S(2)}, u32[]{:S(2)}) %collective-permute-start.7) | collective-permute-done | bytes 524320 | tf_op jit(solution)/shard_map/ppermute | solution.py:223
  150.3 2.9 shard_map.75.rest_0_.mine.own_cols
  155.5 2.0 copy-done.4
  157.5 13.8 %collective-permute-done.9.rest_2_.theirs = bf16[256,1024]{1,0:T(8,128)(2,1)S(1)} collective-permute-done((bf16[256,1024]{1,0:T(8,128)(2,1)S(1)}, bf16[256,1024]{1,0:T(8,128)(2,1)S(1)}, u32[]{:S(2)}, u32[]{:S(2)}) %collective-permute-start.9) | collective-permute-done | bytes 524320 | tf_op jit(solution)/shard_map/ppermute | solution.py:223
  171.3 2.4 collective-permute-start.14
  173.7 3.7 shard_map.77.rest_0_.mine.own_cols
  178.2 2.0 copy-done.6
  180.2 2.3 collective-permute-done.11.rest_2_.theirs
  182.5 3.4 shard_map.79.rest_0_.mine.own_cols
  185.9 2.8 collective-permute-start.17
  189.9 26.3 %collective-permute-done.13.rest_2_.theirs = bf16[256,1024]{1,0:T(8,128)(2,1)S(1)} collective-permute-done((bf16[256,1024]{1,0:T(8,128)(2,1)S(1)}, bf16[256,1024]{1,0:T(8,128)(2,1)S(1)}, u32[]{:S(2)}, u32[]{:S(2)}) %collective-permute-start.13) | collective-permute-done | bytes 524320 | tf_op jit(solution)/shard_map/ppermute | solution.py:223
  218.2 2.0 copy-done.8
  220.2 3.8 %shard_map.81.rest_0_.mine.own_cols = bf16[256,1024]{1,0:T(8,128)(2,1)} custom-call(bf16[1024,1024]{1,0:T(8,128)(2,1)S(1)} %copy-done.17, bf16[1,4,1024,1024]{3,2,1,0:T(8,128)(2,1)} %t_rows.33, bf16[1,4,1024,1024]{3,2,1,0:T(8,128)(2,1)} %t_rows.33, bf16[1024,1024]{1,0:T(8,128)(2,1)S(1)} %copy-done.17, bf16[256,1024]{1,0:T(8,128)(2,1)S(1)} %shard_map.79.rest_0_.mine.own_cols, ...), custom_call_target="tpu_custom_call" | custom-call | flops 1073741824 | bytes 5767168 | tf_op jit(solution)/shard_map/pallas_call | solution.py:32
  226.3 2.2 copy-done.9
  230.1 2.0 copy-done.10
  232.2 3.1 shard_map.83.rest_0_.mine.own_cols
  235.3 3.0 collective-permute-start.20
  239.9 2.0 copy-done.12
  241.9 19.4 %collective-permute-done.17.rest_2_.theirs = bf16[256,1024]{1,0:T(8,128)(2,1)} collective-permute-done((bf16[256,1024]{1,0:T(8,128)(2,1)S(1)}, bf16[256,1024]{1,0:T(8,128)(2,1)}, u32[]{:S(2)}, u32[]{:S(2)}) %collective-permute-start.17) | collective-permute-done | bytes 524320 | tf_op jit(solution)/shard_map/ppermute | solution.py:223
  261.3 3.1 shard_map.85.rest_0_.mine.own_cols
  264.5 1.6 shard_map.86
  266.1 2.0 copy-done.14
  268.1 3.9 %shard_map.87.rest_1_ = bf16[1,4,1024,1024]{3,2,1,0:T(8,128)(2,1)} custom-call(f32[2]{0:T(128)S(1)} %pad_maximum_fusion.1.energies, bf16[256,1024]{1,0:T(8,128)(2,1)S(1)} %copy-done.29, bf16[256,1024]{1,0:T(8,128)(2,1)S(1)} %copy-done.29, bf16[256,1024]{1,0:T(8,128)(2,1)} %collective-permute-done.1.rest_2_.theirs, bf16[2,1024,1024]{2,1,0:T(8,128)(2,1)} %bitcast.20, ...), custom_call_target="tpu_custom_call" | custom-call | flops 1073741824 | bytes 5767168 | tf_op jit(solution)/shard_map/pallas_call | solution.py:64
  272.0 4.5 %shard_map.88.rest_1_ = bf16[1,4,1024,1024]{3,2,1,0:T(8,128)(2,1)} custom-call(f32[2]{0:T(128)S(1)} %pad_maximum_fusion.1.energies, bf16[256,1024]{1,0:T(8,128)(2,1)} %shard_map.65.rest_0_.mine.own_cols, bf16[256,1024]{1,0:T(8,128)(2,1)} %shard_map.65.rest_0_.mine.own_cols, ...), custom_call_target="tpu_custom_call", output_to_operand_aliasing={{}: (9, {})} | custom-call | flops 1073741824 | bytes 5767168 | tf_op jit(solution)/shard_map/pallas_call | solution.py:64
  276.6 4.0 %shard_map.89.rest_1_ = bf16[1,4,1024,1024]{3,2,1,0:T(8,128)(2,1)} custom-call(f32[2]{0:T(128)S(1)} %pad_maximum_fusion.1.energies, bf16[256,1024]{1,0:T(8,128)(2,1)S(1)} %copy-done.25, bf16[256,1024]{1,0:T(8,128)(2,1)S(1)} %copy-done.25, bf16[256,1024]{1,0:T(8,128)(2,1)} %collective-permute-done.4.rest_2_.theirs, ...), custom_call_target="tpu_custom_call", output_to_operand_aliasing={{}: (9, {})} | custom-call | flops 1073741824 | bytes 5767168 | tf_op jit(solution)/shard_map/pallas_call | solution.py:64
  280.5 3.2 collective-permute-done.19.rest_2_.theirs
  283.7 2.9 shard_map.90.rest_0_.mine.own_cols
  286.8 3.9 %shard_map.91.rest_1_ = bf16[1,4,1024,1024]{3,2,1,0:T(8,128)(2,1)} custom-call(f32[2]{0:T(128)S(1)} %pad_maximum_fusion.1.energies, bf16[256,1024]{1,0:T(8,128)(2,1)S(1)} %copy-done.31, bf16[256,1024]{1,0:T(8,128)(2,1)S(1)} %copy-done.31, bf16[256,1024]{1,0:T(8,128)(2,1)S(1)} %copy-done.33, ...), custom_call_target="tpu_custom_call", output_to_operand_aliasing={{}: (9, {})} | custom-call | flops 1073741824 | bytes 5767168 | tf_op jit(solution)/shard_map/pallas_call | solution.py:64
  290.7 3.9 %shard_map.92.rest_1_ = bf16[1,4,1024,1024]{3,2,1,0:T(8,128)(2,1)} custom-call(f32[2]{0:T(128)S(1)} %pad_maximum_fusion.2.energies, bf16[256,1024]{1,0:T(8,128)(2,1)S(1)} %copy-done.19, bf16[256,1024]{1,0:T(8,128)(2,1)S(1)} %copy-done.19, bf16[256,1024]{1,0:T(8,128)(2,1)S(1)} %copy-done.35, ...), custom_call_target="tpu_custom_call", output_to_operand_aliasing={{}: (9, {})} | custom-call | flops 1073741824 | bytes 5767168 | tf_op jit(solution)/shard_map/pallas_call | solution.py:64
  294.6 3.8 %shard_map.93.rest_1_ = bf16[1,4,1024,1024]{3,2,1,0:T(8,128)(2,1)} custom-call(f32[2]{0:T(128)S(1)} %pad_maximum_fusion.2.energies, bf16[256,1024]{1,0:T(8,128)(2,1)S(1)} %copy-done.27, bf16[256,1024]{1,0:T(8,128)(2,1)S(1)} %copy-done.27, bf16[256,1024]{1,0:T(8,128)(2,1)S(1)} %copy-done.37, ...), custom_call_target="tpu_custom_call", output_to_operand_aliasing={{}: (9, {})} | custom-call | flops 1073741824 | bytes 5767168 | tf_op jit(solution)/shard_map/pallas_call | solution.py:64
  298.5 7.6 %collective-permute-done.20.rest_2_.theirs = bf16[256,1024]{1,0:T(8,128)(2,1)S(1)} collective-permute-done((bf16[256,1024]{1,0:T(8,128)(2,1)S(1)}, bf16[256,1024]{1,0:T(8,128)(2,1)S(1)}, u32[]{:S(2)}, u32[]{:S(2)}) %collective-permute-start.20) | collective-permute-done | bytes 524320 | tf_op jit(solution)/shard_map/ppermute | solution.py:223
  306.1 3.0 shard_map.94.rest_0_.mine.own_cols
  309.2 3.9 %shard_map.95.rest_1_ = bf16[1,4,1024,1024]{3,2,1,0:T(8,128)(2,1)} custom-call(f32[2]{0:T(128)S(1)} %pad_maximum_fusion.2.energies, bf16[256,1024]{1,0:T(8,128)(2,1)S(1)} %copy-done.21, bf16[256,1024]{1,0:T(8,128)(2,1)S(1)} %copy-done.21, bf16[256,1024]{1,0:T(8,128)(2,1)S(1)} %copy-done.39, ...), custom_call_target="tpu_custom_call", output_to_operand_aliasing={{}: (9, {})} | custom-call | flops 1073741824 | bytes 5767168 | tf_op jit(solution)/shard_map/pallas_call | solution.py:64
  313.1 3.8 %shard_map.96.rest_1_ = bf16[1,4,1024,1024]{3,2,1,0:T(8,128)(2,1)} custom-call(f32[2]{0:T(128)S(1)} %pad_maximum_fusion.2.energies, bf16[256,1024]{1,0:T(8,128)(2,1)S(1)} %copy-done.23, bf16[256,1024]{1,0:T(8,128)(2,1)S(1)} %copy-done.23, bf16[256,1024]{1,0:T(8,128)(2,1)S(1)} %copy-done.41, ...), custom_call_target="tpu_custom_call", output_to_operand_aliasing={{}: (9, {})} | custom-call | flops 1073741824 | bytes 5767168 | tf_op jit(solution)/shard_map/pallas_call | solution.py:64
  316.9 4.5 %shard_map.97.rest_1_ = bf16[1,4,1024,1024]{3,2,1,0:T(8,128)(2,1)} custom-call(f32[2]{0:T(128)S(1)} %pad_maximum_fusion.3.energies, bf16[256,1024]{1,0:T(8,128)(2,1)} %shard_map.77.rest_0_.mine.own_cols, bf16[256,1024]{1,0:T(8,128)(2,1)} %shard_map.77.rest_0_.mine.own_cols, ...), custom_call_target="tpu_custom_call", output_to_operand_aliasing={{}: (9, {})} | custom-call | flops 1073741824 | bytes 5767168 | tf_op jit(solution)/shard_map/pallas_call | solution.py:64
  321.4 7.2 %collective-permute-done.21.rest_2_.theirs = bf16[256,1024]{1,0:T(8,128)(2,1)S(1)} collective-permute-done((bf16[256,1024]{1,0:T(8,128)(2,1)S(1)}, bf16[256,1024]{1,0:T(8,128)(2,1)S(1)}, u32[]{:S(2)}, u32[]{:S(2)}) %collective-permute-start.21) | collective-permute-done | bytes 524320 | tf_op jit(solution)/shard_map/ppermute | solution.py:223
  328.6 2.7 shard_map.98.rest_0_.mine.own_cols
  331.4 3.3 shard_map.99.rest_1_
  334.7 3.5 shard_map.100.rest_1_
  338.2 2.8 shard_map.101.rest_1_
  341.0 4.5 %collective-permute-done.22.rest_2_.theirs = bf16[256,1024]{1,0:T(8,128)(2,1)} collective-permute-done((bf16[256,1024]{1,0:T(8,128)(2,1)S(1)}, bf16[256,1024]{1,0:T(8,128)(2,1)}, u32[]{:S(2)}, u32[]{:S(2)}) %collective-permute-start.22) | collective-permute-done | bytes 524320 | tf_op jit(solution)/shard_map/ppermute | solution.py:223
  345.5 2.7 shard_map.102.mine.rest_0_
  348.3 2.8 shard_map.104.rest_1_
  352.6 3.3 shard_map.105.rest_1_
  355.9 6.5 %collective-permute-done.25.theirs = bf16[256,1024]{1,0:T(8,128)(2,1)} collective-permute-done((bf16[256,1024]{1,0:T(8,128)(2,1)S(1)}, bf16[256,1024]{1,0:T(8,128)(2,1)}, u32[]{:S(2)}, u32[]{:S(2)}) %collective-permute-start.25) | collective-permute-done | bytes 524320 | tf_op jit(solution)/shard_map/ppermute | solution.py:223
  362.4 3.3 shard_map.106.rest_1_
  365.7 2.2 collective-permute-done.24.theirs
  367.9 2.9 shard_map.107._
  (144 shorter events, 27.9 us)
Async XLA Ops:
  1.0 20.4 %collective-permute-start = (bf16[128,512]{1,0:T(8,128)(2,1)S(1)}, bf16[128,512]{1,0:T(8,128)(2,1)S(1)}, u32[]{:S(2)}, u32[]{:S(2)}) collective-permute-start(bf16[128,512]{1,0:T(8,128)(2,1)S(1)} %get-tuple-element.11), channel_id=1, source_target_pairs={{0,4},{4,0},{1,5},{5,1},{2,6},{6,2},{3,7},{7,3},{8,12},{12,8},{9,1... | collective-permute-start | bytes 393224 | tf_op jit(solution)/shard_map/ppermute | solution.py:227
  9.6 4.0 %copy-start.28 = (bf16[256,1024]{1,0:T(8,128)(2,1)}, bf16[256,1024]{1,0:T(8,128)(2,1)S(1)}, u32[]{:S(2)}) copy-start(bf16[256,1024]{1,0:T(8,128)(2,1)S(1)} %shard_map.64.rest_0_.mine.own_cols) | copy-start | bytes 1572868
  9.6 49.4 %collective-permute-start.1 = (bf16[256,1024]{1,0:T(8,128)(2,1)S(1)}, bf16[256,1024]{1,0:T(8,128)(2,1)}, u32[]{:S(2)}, u32[]{:S(2)}) collective-permute-start(bf16[256,1024]{1,0:T(8,128)(2,1)S(1)} %shard_map.64.rest_0_.mine.own_cols), channel_id=1, source_target_pairs={{0,4},{4,0},{1,5},{5,1},{2,6},{6,2},{3,7},{7,3},{8,12},{12,8},{9,1... | collective-permute-start | bytes 1572872 | tf_op jit(solution)/shard_map/ppermute | solution.py:223
  13.6 6.4 %copy-start.45 = (f32[2]{0:T(128)S(1)}, f32[2]{0:T(128)}, u32[]{:S(2)}) copy-start(f32[2]{0:T(128)} %param.9) | copy-start | bytes 28
  13.6 7.0 %copy-start.46 = (f32[16]{0:T(128)S(1)}, f32[16]{0:T(128)}, u32[]{:S(2)}) copy-start(f32[16]{0:T(128)} %param.10) | copy-start | bytes 196
  13.6 45.5 %copy-start.17 = (bf16[1024,1024]{1,0:T(8,128)(2,1)S(1)}, bf16[1024,1024]{1,0:T(8,128)(2,1)}, u32[]{:S(2)}) copy-start(bf16[1024,1024]{1,0:T(8,128)(2,1)} %f_cols.33) | copy-start | bytes 6291460
  13.6 67.9 %collective-permute-start.2 = (bf16[256,1024]{1,0:T(8,128)(2,1)}, bf16[256,1024]{1,0:T(8,128)(2,1)}, u32[]{:S(2)}, u32[]{:S(2)}) collective-permute-start(bf16[256,1024]{1,0:T(8,128)(2,1)} %shard_map.65.rest_0_.mine.own_cols), channel_id=1, source_target_pairs={{0,4},{4,0},{1,5},{5,1},{2,6},{6,2},{3,7},{7,3},{8,12},{12,8},{9,1... | collective-permute-start | bytes 1572872 | tf_op jit(solution)/shard_map/ppermute | solution.py:223
  19.5 42.6 %copy-start.24 = (bf16[256,1024]{1,0:T(8,128)(2,1)}, bf16[256,1024]{1,0:T(8,128)(2,1)S(1)}, u32[]{:S(2)}) copy-start(bf16[256,1024]{1,0:T(8,128)(2,1)S(1)} %shard_map.66.rest_0_.mine.own_cols) | copy-start | bytes 1572868
  19.5 84.5 %collective-permute-start.4 = (bf16[256,1024]{1,0:T(8,128)(2,1)S(1)}, bf16[256,1024]{1,0:T(8,128)(2,1)}, u32[]{:S(2)}, u32[]{:S(2)}) collective-permute-start(bf16[256,1024]{1,0:T(8,128)(2,1)S(1)} %shard_map.66.rest_0_.mine.own_cols), channel_id=1, source_target_pairs={{0,4},{4,0},{1,5},{5,1},{2,6},{6,2},{3,7},{7,3},{8,12},{12,8},{9,1... | collective-permute-start | bytes 1572872 | tf_op jit(solution)/shard_map/ppermute | solution.py:223
  21.4 63.1 %collective-permute-start.3 = (bf16[2,128,512]{2,1,0:T(8,128)(2,1)S(1)}, bf16[2,128,512]{2,1,0:T(8,128)(2,1)S(1)}, u32[]{:S(2)}, u32[]{:S(2)}) collective-permute-start(bf16[2,128,512]{2,1,0:T(8,128)(2,1)S(1)} %bitcast.54), channel_id=1, source_target_pairs={{0,2},{1,3},{2,0},{3,1},{4,6},{5,7},{6,4},{7,5},{8,10},{9,11},{10,... | collective-permute-start | bytes 786440 | tf_op jit(solution)/shard_map/ppermute | solution.py:235
  62.0 22.4 %copy-start.30 = (bf16[256,1024]{1,0:T(8,128)(2,1)}, bf16[256,1024]{1,0:T(8,128)(2,1)S(1)}, u32[]{:S(2)}) copy-start(bf16[256,1024]{1,0:T(8,128)(2,1)S(1)} %shard_map.68.rest_0_.mine.own_cols) | copy-start | bytes 1572868
  62.1 64.3 %collective-permute-start.5 = (bf16[256,1024]{1,0:T(8,128)(2,1)S(1)}, bf16[256,1024]{1,0:T(8,128)(2,1)S(1)}, u32[]{:S(2)}, u32[]{:S(2)}) collective-permute-start(bf16[256,1024]{1,0:T(8,128)(2,1)S(1)} %shard_map.68.rest_0_.mine.own_cols), channel_id=1, source_target_pairs={{0,4},{4,0},{1,5},{5,1},{2,6},{6,2},{3,7},{7,3},{8,12},{12,8},{9,1... | collective-permute-start | bytes 1572872 | tf_op jit(solution)/shard_map/ppermute | solution.py:223
  84.5 22.5 %copy-start.18 = (bf16[256,1024]{1,0:T(8,128)(2,1)}, bf16[256,1024]{1,0:T(8,128)(2,1)S(1)}, u32[]{:S(2)}) copy-start(bf16[256,1024]{1,0:T(8,128)(2,1)S(1)} %shard_map.69.rest_0_.mine.own_cols) | copy-start | bytes 1572868
  85.4 44.2 %collective-permute-start.6 = (bf16[4,128,512]{2,1,0:T(8,128)(2,1)}, bf16[4,128,512]{2,1,0:T(8,128)(2,1)S(1)}, u32[]{:S(2)}, u32[]{:S(2)}) collective-permute-start(bf16[4,128,512]{2,1,0:T(8,128)(2,1)} %bitcast.5.rest_1_.block), channel_id=1, source_target_pairs={{0,1},{1,0},{2,3},{3,2},{8,9},{9,8},{10,11},{11,10},{16,17},{17,16... | collective-permute-start | bytes 1572872 | tf_op jit(solution)/shard_map/ppermute | solution.py:251
  87.0 61.8 %collective-permute-start.7 = (bf16[256,1024]{1,0:T(8,128)(2,1)S(1)}, bf16[256,1024]{1,0:T(8,128)(2,1)S(1)}, u32[]{:S(2)}, u32[]{:S(2)}) collective-permute-start(bf16[256,1024]{1,0:T(8,128)(2,1)S(1)} %shard_map.69.rest_0_.mine.own_cols), channel_id=1, source_target_pairs={{0,4},{4,0},{1,5},{5,1},{2,6},{6,2},{3,7},{7,3},{8,12},{12,8},{9,1... | collective-permute-start | bytes 1572872 | tf_op jit(solution)/shard_map/ppermute | solution.py:223
  87.1 66.2 %collective-permute-start.8 = (bf16[4,128,512]{2,1,0:T(8,128)(2,1)}, bf16[4,128,512]{2,1,0:T(8,128)(2,1)S(1)}, u32[]{:S(2)}, u32[]{:S(2)}) collective-permute-start(bf16[4,128,512]{2,1,0:T(8,128)(2,1)} %bitcast.5.rest_1_.block), channel_id=1, source_target_pairs={{0,8},{1,9},{2,10},{3,11},{8,0},{9,1},{10,2},{11,3},{16,24},{17,25... | collective-permute-start | bytes 1572872 | tf_op jit(solution)/shard_map/ppermute | solution.py:251
  106.9 22.6 %copy-start.26 = (bf16[256,1024]{1,0:T(8,128)(2,1)}, bf16[256,1024]{1,0:T(8,128)(2,1)S(1)}, u32[]{:S(2)}) copy-start(bf16[256,1024]{1,0:T(8,128)(2,1)S(1)} %shard_map.71.rest_0_.mine.own_cols) | copy-start | bytes 1572868
  106.9 64.3 %collective-permute-start.9 = (bf16[256,1024]{1,0:T(8,128)(2,1)S(1)}, bf16[256,1024]{1,0:T(8,128)(2,1)S(1)}, u32[]{:S(2)}, u32[]{:S(2)}) collective-permute-start(bf16[256,1024]{1,0:T(8,128)(2,1)S(1)} %shard_map.71.rest_0_.mine.own_cols), channel_id=1, source_target_pairs={{0,4},{4,0},{1,5},{5,1},{2,6},{6,2},{3,7},{7,3},{8,12},{12,8},{9,1... | collective-permute-start | bytes 1572872 | tf_op jit(solution)/shard_map/ppermute | solution.py:223
  108.7 2.0 copy-start
  126.3 3.2 copy-start.32
  126.3 3.4 copy-start.1
  126.3 51.1 %collective-permute-start.10 = (bf16[4,128,512]{2,1,0:T(8,128)(2,1)}, bf16[4,128,512]{2,1,0:T(8,128)(2,1)S(1)}, u32[]{:S(2)}, u32[]{:S(2)}) collective-permute-start(bf16[4,128,512]{2,1,0:T(8,128)(2,1)} %bitcast.5.rest_1_.block), channel_id=1, source_target_pairs={{0,9},{1,8},{2,11},{3,10},{8,1},{9,0},{10,3},{11,2},{16,25},{17,24... | collective-permute-start | bytes 1572872 | tf_op jit(solution)/shard_map/ppermute | solution.py:251
  129.6 23.7 %copy-start.20 = (bf16[256,1024]{1,0:T(8,128)(2,1)}, bf16[256,1024]{1,0:T(8,128)(2,1)S(1)}, u32[]{:S(2)}) copy-start(bf16[256,1024]{1,0:T(8,128)(2,1)S(1)} %shard_map.73.rest_0_.mine.own_cols) | copy-start | bytes 1572868
  129.6 52.9 %collective-permute-start.11 = (bf16[256,1024]{1,0:T(8,128)(2,1)S(1)}, bf16[256,1024]{1,0:T(8,128)(2,1)S(1)}, u32[]{:S(2)}, u32[]{:S(2)}) collective-permute-start(bf16[256,1024]{1,0:T(8,128)(2,1)S(1)} %shard_map.73.rest_0_.mine.own_cols), channel_id=1, source_target_pairs={{0,4},{4,0},{1,5},{5,1},{2,6},{6,2},{3,7},{7,3},{8,12},{12,8},{9,1... | collective-permute-start | bytes 1572872 | tf_op jit(solution)/shard_map/ppermute | solution.py:223
  148.8 4.5 %copy-start.34 = (bf16[256,1024]{1,0:T(8,128)(2,1)}, bf16[256,1024]{1,0:T(8,128)(2,1)S(1)}, u32[]{:S(2)}) copy-start(bf16[256,1024]{1,0:T(8,128)(2,1)S(1)} %collective-permute-done.7.rest_2_.theirs) | copy-start | bytes 1572868
  148.8 6.1 %copy-start.3 = (bf16[2,4,2,128,1024]{4,3,2,1,0:T(8,128)(2,1)S(1)}, bf16[2,4,2,128,1024]{4,3,2,1,0:T(8,128)(2,1)}, u32[]{:S(2)}) copy-start(bf16[2,4,2,128,1024]{4,3,2,1,0:T(8,128)(2,1)} %copy-done.2) | copy-start | bytes 12582916
  148.8 37.1 %collective-permute-start.12 = (bf16[4,128,512]{2,1,0:T(8,128)(2,1)}, bf16[4,128,512]{2,1,0:T(8,128)(2,1)S(1)}, u32[]{:S(2)}, u32[]{:S(2)}) collective-permute-start(bf16[4,128,512]{2,1,0:T(8,128)(2,1)} %bitcast.5.rest_1_.block), channel_id=1, source_target_pairs={{0,16},{1,17},{2,18},{3,19},{8,24},{9,25},{10,26},{11,27},{16,0},{... | collective-permute-start | bytes 1572872 | tf_op jit(solution)/shard_map/ppermute | solution.py:251
  153.3 24.2 %copy-start.22 = (bf16[256,1024]{1,0:T(8,128)(2,1)}, bf16[256,1024]{1,0:T(8,128)(2,1)S(1)}, u32[]{:S(2)}) copy-start(bf16[256,1024]{1,0:T(8,128)(2,1)S(1)} %shard_map.75.rest_0_.mine.own_cols) | copy-start | bytes 1572868
  153.3 62.9 %collective-permute-start.13 = (bf16[256,1024]{1,0:T(8,128)(2,1)S(1)}, bf16[256,1024]{1,0:T(8,128)(2,1)S(1)}, u32[]{:S(2)}, u32[]{:S(2)}) collective-permute-start(bf16[256,1024]{1,0:T(8,128)(2,1)S(1)} %shard_map.75.rest_0_.mine.own_cols), channel_id=1, source_target_pairs={{0,4},{4,0},{1,5},{5,1},{2,6},{6,2},{3,7},{7,3},{8,12},{12,8},{9,1... | collective-permute-start | bytes 1572872 | tf_op jit(solution)/shard_map/ppermute | solution.py:223
  171.3 6.2 %copy-start.36 = (bf16[256,1024]{1,0:T(8,128)(2,1)}, bf16[256,1024]{1,0:T(8,128)(2,1)S(1)}, u32[]{:S(2)}) copy-start(bf16[256,1024]{1,0:T(8,128)(2,1)S(1)} %collective-permute-done.9.rest_2_.theirs) | copy-start | bytes 1572868
  171.3 6.3 %copy-start.5 = (bf16[2,4,2,128,1024]{4,3,2,1,0:T(8,128)(2,1)S(1)}, bf16[2,4,2,128,1024]{4,3,2,1,0:T(8,128)(2,1)}, u32[]{:S(2)}) copy-start(bf16[2,4,2,128,1024]{4,3,2,1,0:T(8,128)(2,1)} %copy-done.4) | copy-start | bytes 12582916
  171.3 52.7 %collective-permute-start.14 = (bf16[4,128,512]{2,1,0:T(8,128)(2,1)}, bf16[4,128,512]{2,1,0:T(8,128)(2,1)S(1)}, u32[]{:S(2)}, u32[]{:S(2)}) collective-permute-start(bf16[4,128,512]{2,1,0:T(8,128)(2,1)} %bitcast.5.rest_1_.block), channel_id=1, source_target_pairs={{0,17},{1,16},{2,19},{3,18},{8,25},{9,24},{10,27},{11,26},{16,1},{... | collective-permute-start | bytes 1572872 | tf_op jit(solution)/shard_map/ppermute | solution.py:251
  177.5 60.8 %collective-permute-start.16 = (bf16[4,128,512]{2,1,0:T(8,128)(2,1)}, bf16[4,128,512]{2,1,0:T(8,128)(2,1)}, u32[]{:S(2)}, u32[]{:S(2)}) collective-permute-start(bf16[4,128,512]{2,1,0:T(8,128)(2,1)} %bitcast.5.rest_1_.block), channel_id=1, source_target_pairs={{0,24},{1,25},{2,26},{3,27},{8,16},{9,17},{10,18},{11,19},{16,8},{... | collective-permute-start | bytes 1572872 | tf_op jit(solution)/shard_map/ppermute | solution.py:251
  178.1 2.0 copy-start.6
  182.5 3.4 copy-start.38
  182.5 35.0 %copy-start.7 = (bf16[2,4,2,128,1024]{4,3,2,1,0:T(8,128)(2,1)S(1)}, bf16[2,4,2,128,1024]{4,3,2,1,0:T(8,128)(2,1)}, u32[]{:S(2)}) copy-start(bf16[2,4,2,128,1024]{4,3,2,1,0:T(8,128)(2,1)} %copy-done.6) | copy-start | bytes 12582916
  182.5 49.6 %collective-permute-start.15 = (bf16[256,1024]{1,0:T(8,128)(2,1)}, bf16[256,1024]{1,0:T(8,128)(2,1)}, u32[]{:S(2)}, u32[]{:S(2)}) collective-permute-start(bf16[256,1024]{1,0:T(8,128)(2,1)} %shard_map.77.rest_0_.mine.own_cols), channel_id=1, source_target_pairs={{0,4},{4,0},{1,5},{5,1},{2,6},{6,2},{3,7},{7,3},{8,12},{12,8},{9,1... | collective-permute-start | bytes 1572872 | tf_op jit(solution)/shard_map/ppermute | solution.py:223
  185.9 75.3 %collective-permute-start.17 = (bf16[256,1024]{1,0:T(8,128)(2,1)S(1)}, bf16[256,1024]{1,0:T(8,128)(2,1)}, u32[]{:S(2)}, u32[]{:S(2)}) collective-permute-start(bf16[256,1024]{1,0:T(8,128)(2,1)S(1)} %shard_map.79.rest_0_.mine.own_cols), channel_id=1, source_target_pairs={{0,4},{4,0},{1,5},{5,1},{2,6},{6,2},{3,7},{7,3},{8,12},{12,8},{9,1... | collective-permute-start | bytes 1572872 | tf_op jit(solution)/shard_map/ppermute | solution.py:223
  216.2 7.7 %copy-start.40 = (bf16[256,1024]{1,0:T(8,128)(2,1)}, bf16[256,1024]{1,0:T(8,128)(2,1)S(1)}, u32[]{:S(2)}) copy-start(bf16[256,1024]{1,0:T(8,128)(2,1)S(1)} %collective-permute-done.13.rest_2_.theirs) | copy-start | bytes 1572868
  216.2 48.2 %collective-permute-start.18 = (bf16[4,128,512]{2,1,0:T(8,128)(2,1)}, bf16[4,128,512]{2,1,0:T(8,128)(2,1)}, u32[]{:S(2)}, u32[]{:S(2)}) collective-permute-start(bf16[4,128,512]{2,1,0:T(8,128)(2,1)} %bitcast.5.rest_1_.block), channel_id=1, source_target_pairs={{0,25},{1,24},{2,27},{3,26},{8,17},{9,16},{10,19},{11,18},{16,9},{... | collective-permute-start | bytes 1572872 | tf_op jit(solution)/shard_map/ppermute | solution.py:251
  220.2 5.9 %copy-start.42 = (f32[1024]{0:T(1024)S(1)}, f32[1024]{0:T(1024)}, u32[]{:S(2)}) copy-start(f32[1024]{0:T(1024)} %param.11) | copy-start | bytes 12292
  224.7 59.0 %collective-permute-start.19 = (bf16[256,1024]{1,0:T(8,128)(2,1)}, bf16[256,1024]{1,0:T(8,128)(2,1)}, u32[]{:S(2)}, u32[]{:S(2)}) collective-permute-start(bf16[256,1024]{1,0:T(8,128)(2,1)} %shard_map.81.rest_0_.mine.own_cols), channel_id=1, source_target_pairs={{0,4},{4,0},{1,5},{5,1},{2,6},{6,2},{3,7},{7,3},{8,12},{12,8},{9,1... | collective-permute-start | bytes 1572872 | tf_op jit(solution)/shard_map/ppermute | solution.py:223
  226.3 2.2 copy-start.9
  232.2 6.1 %copy-start.11 = (bf16[2,4,2,128,1024]{4,3,2,1,0:T(8,128)(2,1)S(1)}, bf16[2,4,2,128,1024]{4,3,2,1,0:T(8,128)(2,1)}, u32[]{:S(2)}) copy-start(bf16[2,4,2,128,1024]{4,3,2,1,0:T(8,128)(2,1)} %copy-done.10) | copy-start | bytes 12582916
  235.3 70.8 %collective-permute-start.20 = (bf16[256,1024]{1,0:T(8,128)(2,1)S(1)}, bf16[256,1024]{1,0:T(8,128)(2,1)S(1)}, u32[]{:S(2)}, u32[]{:S(2)}) collective-permute-start(bf16[256,1024]{1,0:T(8,128)(2,1)S(1)} %shard_map.83.rest_0_.mine.own_cols), channel_id=1, source_target_pairs={{0,4},{4,0},{1,5},{5,1},{2,6},{6,2},{3,7},{7,3},{8,12},{12,8},{9,1... | collective-permute-start | bytes 1572872 | tf_op jit(solution)/shard_map/ppermute | solution.py:223
  261.3 3.2 copy-start.13
  264.4 3.7 copy-start.29
  264.4 64.2 %collective-permute-start.21 = (bf16[256,1024]{1,0:T(8,128)(2,1)S(1)}, bf16[256,1024]{1,0:T(8,128)(2,1)S(1)}, u32[]{:S(2)}, u32[]{:S(2)}) collective-permute-start(bf16[256,1024]{1,0:T(8,128)(2,1)S(1)} %shard_map.85.rest_0_.mine.own_cols), channel_id=1, source_target_pairs={{0,4},{4,0},{1,5},{5,1},{2,6},{6,2},{3,7},{7,3},{8,12},{12,8},{9,1... | collective-permute-start | bytes 1572872 | tf_op jit(solution)/shard_map/ppermute | solution.py:223
  272.0 4.5 %copy-start.25 = (bf16[256,1024]{1,0:T(8,128)(2,1)S(1)}, bf16[256,1024]{1,0:T(8,128)(2,1)}, u32[]{:S(2)}) copy-start(bf16[256,1024]{1,0:T(8,128)(2,1)} %copy-done.24) | copy-start | bytes 1572868
  280.5 6.3 %copy-start.31 = (bf16[256,1024]{1,0:T(8,128)(2,1)S(1)}, bf16[256,1024]{1,0:T(8,128)(2,1)}, u32[]{:S(2)}) copy-start(bf16[256,1024]{1,0:T(8,128)(2,1)} %copy-done.30) | copy-start | bytes 1572868
  280.5 6.3 %copy-start.33 = (bf16[256,1024]{1,0:T(8,128)(2,1)S(1)}, bf16[256,1024]{1,0:T(8,128)(2,1)}, u32[]{:S(2)}) copy-start(bf16[256,1024]{1,0:T(8,128)(2,1)} %copy-done.32) | copy-start | bytes 1572868
  286.7 4.0 %copy-start.19 = (bf16[256,1024]{1,0:T(8,128)(2,1)S(1)}, bf16[256,1024]{1,0:T(8,128)(2,1)}, u32[]{:S(2)}) copy-start(bf16[256,1024]{1,0:T(8,128)(2,1)} %copy-done.18) | copy-start | bytes 1572868
  286.7 4.0 %copy-start.35 = (bf16[256,1024]{1,0:T(8,128)(2,1)S(1)}, bf16[256,1024]{1,0:T(8,128)(2,1)}, u32[]{:S(2)}) copy-start(bf16[256,1024]{1,0:T(8,128)(2,1)} %copy-done.34) | copy-start | bytes 1572868
  286.7 58.8 %collective-permute-start.22 = (bf16[256,1024]{1,0:T(8,128)(2,1)S(1)}, bf16[256,1024]{1,0:T(8,128)(2,1)}, u32[]{:S(2)}, u32[]{:S(2)}) collective-permute-start(bf16[256,1024]{1,0:T(8,128)(2,1)S(1)} %shard_map.90.rest_0_.mine.own_cols), channel_id=1, source_target_pairs={{0,4},{4,0},{1,5},{5,1},{2,6},{6,2},{3,7},{7,3},{8,12},{12,8},{9,1... | collective-permute-start | bytes 1572872 | tf_op jit(solution)/shard_map/ppermute | solution.py:223
  290.7 3.9 %copy-start.27 = (bf16[256,1024]{1,0:T(8,128)(2,1)S(1)}, bf16[256,1024]{1,0:T(8,128)(2,1)}, u32[]{:S(2)}) copy-start(bf16[256,1024]{1,0:T(8,128)(2,1)} %copy-done.26) | copy-start | bytes 1572868
  290.7 3.9 %copy-start.37 = (bf16[256,1024]{1,0:T(8,128)(2,1)S(1)}, bf16[256,1024]{1,0:T(8,128)(2,1)}, u32[]{:S(2)}) copy-start(bf16[256,1024]{1,0:T(8,128)(2,1)} %copy-done.36) | copy-start | bytes 1572868
  298.5 10.7 %copy-start.21 = (bf16[256,1024]{1,0:T(8,128)(2,1)S(1)}, bf16[256,1024]{1,0:T(8,128)(2,1)}, u32[]{:S(2)}) copy-start(bf16[256,1024]{1,0:T(8,128)(2,1)} %copy-done.20) | copy-start | bytes 1572868
  298.5 10.7 %copy-start.39 = (bf16[256,1024]{1,0:T(8,128)(2,1)S(1)}, bf16[256,1024]{1,0:T(8,128)(2,1)}, u32[]{:S(2)}) copy-start(bf16[256,1024]{1,0:T(8,128)(2,1)} %copy-done.38) | copy-start | bytes 1572868
  309.1 4.0 %copy-start.23 = (bf16[256,1024]{1,0:T(8,128)(2,1)S(1)}, bf16[256,1024]{1,0:T(8,128)(2,1)}, u32[]{:S(2)}) copy-start(bf16[256,1024]{1,0:T(8,128)(2,1)} %copy-done.22) | copy-start | bytes 1572868
  309.1 4.0 %copy-start.41 = (bf16[256,1024]{1,0:T(8,128)(2,1)S(1)}, bf16[256,1024]{1,0:T(8,128)(2,1)}, u32[]{:S(2)}) copy-start(bf16[256,1024]{1,0:T(8,128)(2,1)} %copy-done.40) | copy-start | bytes 1572868
  309.1 53.3 %collective-permute-start.25 = (bf16[256,1024]{1,0:T(8,128)(2,1)S(1)}, bf16[256,1024]{1,0:T(8,128)(2,1)}, u32[]{:S(2)}, u32[]{:S(2)}) collective-permute-start(bf16[256,1024]{1,0:T(8,128)(2,1)S(1)} %shard_map.94.rest_0_.mine.own_cols), channel_id=1, source_target_pairs={{0,4},{4,0},{1,5},{5,1},{2,6},{6,2},{3,7},{7,3},{8,12},{12,8},{9,1... | collective-permute-start | bytes 1572872 | tf_op jit(solution)/shard_map/ppermute | solution.py:223
  321.4 10.0 %copy-start.15 = (bf16[2,4,2,128,1024]{4,3,2,1,0:T(8,128)(2,1)S(1)}, bf16[2,4,2,128,1024]{4,3,2,1,0:T(8,128)(2,1)}, u32[]{:S(2)}) copy-start(bf16[2,4,2,128,1024]{4,3,2,1,0:T(8,128)(2,1)} %copy-done.14) | copy-start | bytes 12582916
  331.3 36.6 %collective-permute-start.24 = (bf16[128,1024]{1,0:T(8,128)(2,1)S(1)}, bf16[128,1024]{1,0:T(8,128)(2,1)S(1)}, u32[]{:S(2)}, u32[]{:S(2)}) collective-permute-start(bf16[128,1024]{1,0:T(8,128)(2,1)S(1)} %shard_map.98.rest_0_.mine.own_cols), channel_id=1, source_target_pairs={{0,4},{4,0},{1,5},{5,1},{2,6},{6,2},{3,7},{7,3},{8,12},{12,8},{9,1... | collective-permute-start | bytes 786440 | tf_op jit(solution)/shard_map/ppermute | solution.py:223
  348.2 24.1 %collective-permute-start.23 = (bf16[128,1024]{1,0:T(8,128)(2,1)S(1)}, bf16[128,1024]{1,0:T(8,128)(2,1)S(1)}, u32[]{:S(2)}, u32[]{:S(2)}) collective-permute-start(bf16[128,1024]{1,0:T(8,128)(2,1)S(1)} %shard_map.102.mine.rest_0_), channel_id=1, source_target_pairs={{0,4},{4,0},{1,5},{5,1},{2,6},{6,2},{3,7},{7,3},{8,12},{12,8},{9,1... | collective-permute-start | bytes 786440 | tf_op jit(solution)/shard_map/ppermute | solution.py:223
  (9 other events, 15.5 us)
